TPU v7x, 32 devices: a whole 2x2x4 slice. The times are simulated.
32 devices in a mesh: grp: 2 (over y), gx: 4 (over x, core), gy: 4 (over z).
Axes of the slice: x: 2, y: 2, z: 4, core: 2. Of those that a mesh axis runs over, the one named last changes fastest.
Arguments:
- hidden: bfloat16 [1536, 14336], P(('grp', 'gy'), 'gx'), parts along dimension 0, may hold values from -6 to 6
- parents: int32 [1536], P('grp'), parts along dimension 0, may hold values from 0 to 767, as said below
- depth_table: bfloat16 [256, 14336], P(None, 'gx'), may hold values from -6 to 6
- weight: bfloat16 [14336, 36864], P('gx', 'gy'), may hold values from -0.046875 to 0.046875
Outputs:
- activated: bfloat16 [1536, 36864], P(('grp', 'gx'), 'gy'), parts along dimension 0
There are 2 independent parts, one for each index of `grp`. A program takes and returns all parts, laid end to end along the dimension named above; an argument that names none is the same for every part. Nothing has to cross between parts.
Inputs may be any that keep to these rules, and one draw needn't show every extreme that they name: `parents`: rows come in 3 trees of 256 rows; the first row of each tree is its root and names itself; every other row names an earlier row of its own tree.
All inputs are finite; a program needn't handle non-finite values.
Results may differ from a plain program's by a relative error of at most 0.012.
Values may be sent and summed in bfloat16 or wider, within the bound.
No kernel may reach another device: no remote copies, remote signals or barrier semaphores. Data moves between devices by JAX's collectives and lax.ppermute only.
A program may use at most 192 MiB of HBM per device.

v0:
```python
import jax
import jax.numpy as jnp
from jax import lax
from jax.sharding import PartitionSpec as P


def tree_depth(parents, steps):
    index = jnp.arange(parents.shape[0], dtype=jnp.int32)
    depth = (parents != index).astype(jnp.int32)
    pointer = parents
    for level in range(steps):
        depth = depth + depth[pointer]
        pointer = pointer[pointer]
    return depth


def local(hidden, parents, depth_table, weight):
    tree_rows = depth_table.shape[0]
    depth = tree_depth(parents, tree_rows.bit_length())
    local_rows = hidden.shape[0]
    start_row = lax.axis_index("gy") * local_rows
    depth_here = lax.dynamic_slice_in_dim(depth, start_row, local_rows, 0)
    onehot = (depth_here[:, None] == jnp.arange(tree_rows, dtype=jnp.int32)[None, :]).astype(
        jnp.bfloat16
    )
    looked = jnp.dot(onehot, depth_table, preferred_element_type=jnp.float32)
    rows_in = (hidden.astype(jnp.float32) + looked).astype(jnp.bfloat16)
    gathered = lax.all_gather(rows_in, "gy", axis=0, tiled=True)
    summed = lax.psum_scatter(
        jnp.dot(gathered, weight, preferred_element_type=jnp.float32).astype(jnp.bfloat16),
        "gx",
        scatter_dimension=0,
        tiled=True,
    ).astype(jnp.float32)
    return jax.nn.gelu(summed, approximate=True).astype(jnp.bfloat16)


def solution(mesh):
    return jax.shard_map(
        local,
        mesh=mesh,
        in_specs=(P(("grp", "gy"), "gx"), P("grp"), P(None, "gx"), P("gx", "gy")),
        out_specs=P(("grp", "gx"), "gy"),
        check_vma=False,
    )
```

profile of v0, /device:TPU:0, one launch (start us, length us, event | category | flops | bytes accessed | tf_op | source)
XLA Modules:
  0.0 349.7 jit_solution(16385777152701385864)
XLA Ops:
  6.5 0.0 copy-start
  6.5 0.8 fusion.8
  7.4 0.7 compare_select_fusion.8
  8.1 4.4 %gather_fusion.1 = s32[768]{0:T(1024)S(1)} fusion(s32[768]{0:T(1024)} %param.5, s32[1024]{0:T(1024)S(1)} %pad_clamp_fusion.8), kind=kCustom, calls=%fused_computation.1 | custom fusion | bytes 9216 | tf_op jit(solution)/shard_map/gather | solution.py:13
  12.5 3.2 gather_fusion
  15.8 3.2 gather_fusion.3
  19.0 3.2 gather_fusion.2
  22.2 3.2 gather_fusion.5
  25.4 3.2 gather_fusion.4
  28.7 3.2 gather_fusion.7
  31.8 3.2 gather_fusion.6
  35.1 3.2 gather_fusion.9
  38.3 3.2 gather_fusion.8
  41.5 3.2 gather_fusion.11
  44.7 3.2 gather_fusion.10
  48.0 3.2 gather_fusion.13
  51.2 3.2 gather_fusion.12
  54.4 0.0 copy-start.3
  54.4 3.2 gather_fusion.15
  57.6 3.2 gather_fusion.14
  60.9 3.2 gather_fusion.16
  64.1 0.1 dynamic_slice.3
  64.2 1.6 fusion.6
  65.8 0.0 all-gather.2.cloned.1.call-update
  65.8 0.0 reduce-scatter.2.cloned.1.call-start
  65.9 105.2 %all-gather.2.cloned.1.call-done = bf16[768,3584]{1,0:T(8,128)(2,1)} async-done(((bf16[192,3584]{1,0:T(8,128)(2,1)}), bf16[768,3584]{1,0:T(8,128)(2,1)}) %all-gather.2.cloned.1.call-update) | async-done | bytes 5505040 | tf_op jit(solution)/shard_map/all_gather | solution.py:28
  171.1 58.6 %convolution_convert_fusion = bf16[768,9216]{1,0:T(8,128)(2,1)} fusion(bf16[768,3584]{1,0:T(8,128)(2,1)} %all-gather.2.cloned.1.call-done, bf16[3584,9216]{1,0:T(8,128)(2,1)} %param.7), kind=kOutput, calls=%fused_computation.17 | convolution fusion | flops 50741379072 | bytes 85721088 | tf_op jit(solution)/shard_map/dot_general | solution.py:30
  229.7 0.0 reduce-scatter.2.cloned.1.call-update
  229.7 0.0 copy-start.1
  229.7 108.0 %reduce-scatter.2.cloned.1.call-done = bf16[192,9216]{1,0:T(8,128)(2,1)} async-done(((bf16[768,9216]{1,0:T(8,128)(2,1)}), bf16[192,9216]{1,0:T(8,128)(2,1)}) %reduce-scatter.2.cloned.1.call-update) | async-done | bytes 3538960 | tf_op jit(solution)/shard_map/reduce_scatter | solution.py:29
  337.7 5.1 %fusion.5 = bf16[192,9216]{1,0:T(8,128)(2,1)} fusion(bf16[192,9216]{1,0:T(8,128)(2,1)} %reduce-scatter.2.cloned.1.call-done), kind=kLoop, calls=%fused_computation.27 | loop fusion | flops 17694720 | bytes 7077888 | tf_op jit(solution)/shard_map/convert_element_type | solution.py:35
  342.8 0.0 copy-done.1
  (31 shorter events, 0.2 us)
Async XLA Ops:
  6.5 57.6 %copy-start = (bf16[256,3584]{1,0:T(8,128)(2,1)S(1)}, bf16[256,3584]{1,0:T(8,128)(2,1)}, u32[]{:S(2)}) copy-start(bf16[256,3584]{1,0:T(8,128)(2,1)} %param.6) | copy-start | bytes 5505028
  6.5 9.2 %copy-start.2 = (s32[768]{0:T(1024)S(1)}, s32[768]{0:T(1024)}, u32[]{:S(2)}) copy-start(s32[768]{0:T(1024)} %param.5) | copy-start | bytes 9220
  6.5 164.5 %all-gather.2.cloned.1.call-start = ((), (), s32[]{:S(2)}) async-start(), calls=%async_computation.1 | async-start | bytes 6881280 | tf_op jit(solution)/shard_map/all_gather | solution.py:28
  54.4 9.8 %copy-start.3 = (bf16[192,3584]{1,0:T(8,128)(2,1)S(1)}, bf16[192,3584]{1,0:T(8,128)(2,1)}, u32[]{:S(2)}) copy-start(bf16[192,3584]{1,0:T(8,128)(2,1)} %param.4) | copy-start | bytes 4128772
  65.8 271.9 %reduce-scatter.2.cloned.1.call-start = ((), (), s32[]{:S(2)}) async-start(), calls=%async_computation.2 | async-start | bytes 17694720 | tf_op jit(solution)/shard_map/reduce_scatter | solution.py:29
  229.7 113.1 %copy-start.1 = (bf16[256,3584]{1,0:T(8,128)(2,1)S(1)}, bf16[256,3584]{1,0:T(8,128)(2,1)}, u32[]{:S(2)}) copy-start(bf16[256,3584]{1,0:T(8,128)(2,1)} %param.6) | copy-start | bytes 5505028
Sparse Core Ops, SparseCore 0:
  65.9 105.0 all-gather.1
  229.8 107.8 reduce-scatter.1
where the time goes:
time: 350 us
  waiting for transfers between devices  213 us (61%)
  matrix products  60.3 us (17%)
  local copies, waits for them, and re-layouts  55.5 us (16%)
  between operations  13.7 us (4%)
  other arithmetic  6.85 us (2%)
    reduce_scatter x1, waiting for transfers between devices, local(): lax.psum_scatter(jnp.dot(gathered, weight, preferred_element_type=jnp.flo...  108 us
    all_gather x1, waiting for transfers between devices, local(): gathered = lax.all_gather(rows_in, 'gy', axis=0, tiled=True)  105 us
    dot_general x1, matrix products, local(): jnp.dot(gathered, weight, preferred_element_type=jnp.float32)  58.6 us
    gather x9, local copies, waits for them, and re-layouts, tree_depth(): depth = depth + depth[pointer]  28.7 us
    gather x8, local copies, waits for them, and re-layouts, tree_depth(): pointer = pointer[pointer]  26.8 us
  transfers between devices with their start and end apart: 2, of which 2 were waited for; matrix products, arithmetic and copies ran while one was open for 0% of the time, Pallas kernels for 0%

commit v1 on v0

v1 whole, which is shorter than its diff:
```python
import functools

import jax
import jax.numpy as jnp
from jax import lax
from jax.experimental import pallas as pl
from jax.experimental.pallas import tpu as pltpu
from jax.sharding import PartitionSpec as P

BF16 = jnp.bfloat16
F32 = jnp.float32
MIB = 1024 * 1024


def onehot_kernel(tree, parents_ref, onehot_ref):
    lanes = lax.broadcasted_iota(jnp.int32, (tree, tree), 1)
    rows = lax.broadcasted_iota(jnp.int32, (tree, 1), 0)
    for first in range(0, onehot_ref.shape[0], tree):
        parent = parents_ref[first:first + tree, :] - first
        jump = (parent == lanes).astype(BF16)
        depth = jnp.broadcast_to((parent != rows).astype(F32), (tree, 128))
        for level in range((tree - 1).bit_length()):
            depth = depth + jnp.dot(jump, depth.astype(BF16), preferred_element_type=F32)
            jump = jnp.dot(jump, jump, preferred_element_type=F32).astype(BF16)
        onehot_ref[first:first + tree, :] = (depth[:, :1].astype(jnp.int32) == lanes).astype(BF16)


def depth_onehot(parents, tree):
    rows = parents.shape[0]
    return pl.pallas_call(
        functools.partial(onehot_kernel, tree),
        out_shape=jax.ShapeDtypeStruct((rows, tree), BF16),
        compiler_params=pltpu.CompilerParams(vmem_limit_bytes=16 * MIB),
        cost_estimate=pl.CostEstimate(flops=48 * rows * tree * tree, bytes_accessed=8 * rows * tree, transcendentals=0),
    )(parents[:, None])


def embed_kernel(n_gx, n_gy, first, size, place_ref, onehot_ref, table_ref, hidden_ref, rows_ref):
    chips = n_gx // 2
    block = onehot_ref.shape[0] // n_gy
    x, core = place_ref[0] // 2, place_ref[0] % 2
    for dest in range(n_gx):
        ahead = lax.rem(dest // 2 - x + 2 * chips - 1, chips)
        slot = jnp.where(core == dest % 2, chips, 0) + ahead
        here = dest * block + first
        looked = jnp.dot(onehot_ref[here:here + size, :], table_ref[...], preferred_element_type=F32)
        total = hidden_ref[dest * size:(dest + 1) * size, :].astype(F32) + looked
        rows_ref[pl.ds(pl.multiple_of(slot * size, size), size), :] = total.astype(BF16)


def embed(n_gx, n_gy, first, size, place, onehot, table, hidden):
    rows, depth = hidden.shape
    vmem = pl.BlockSpec(memory_space=pltpu.VMEM)
    return pl.pallas_call(
        functools.partial(embed_kernel, n_gx, n_gy, first, size),
        out_shape=jax.ShapeDtypeStruct((rows, depth), BF16),
        in_specs=[pl.BlockSpec(memory_space=pltpu.SMEM)] + [vmem] * 3,
        out_specs=vmem,
        compiler_params=pltpu.CompilerParams(vmem_limit_bytes=24 * MIB),
        cost_estimate=pl.CostEstimate(flops=2 * rows * 256 * depth, bytes_accessed=6 * rows * depth, transcendentals=0),
    )(place, onehot, table, hidden)


def product_kernel(rows_ref, weight_ref, out_ref):
    out_ref[...] = jnp.dot(rows_ref[...], weight_ref[...], preferred_element_type=F32).astype(BF16)


def product(rows, weight, start, width, tile):
    height, depth = rows.shape
    return pl.pallas_call(
        product_kernel,
        grid=(width // tile,),
        out_shape=jax.ShapeDtypeStruct((height, width), BF16),
        in_specs=[
            pl.BlockSpec((height, depth), lambda j: (0, 0)),
            pl.BlockSpec((depth, tile), lambda j: (0, start // tile + j)),
        ],
        out_specs=pl.BlockSpec((height, tile), lambda j: (0, j)),
        compiler_params=pltpu.CompilerParams(vmem_limit_bytes=32 * MIB),
        cost_estimate=pl.CostEstimate(
            flops=2 * height * depth * width,
            bytes_accessed=2 * (height * depth + depth * width + height * width),
            transcendentals=0,
        ),
    )(rows, weight)


def row_chunks(block):
    for parts in (4, 3, 2):
        if block % (16 * parts) == 0:
            return [block // parts] * parts
    return [block]


def pieces_of(columns, count):
    while columns % (count * 256):
        count -= 1
    return count


def local(n_gx, n_gy, hidden, parents, depth_table, weight):
    tree = depth_table.shape[0]
    columns = weight.shape[1]
    block = hidden.shape[0]
    chips = n_gx // 2
    place = lax.axis_index("gx").astype(jnp.int32)[None]

    sizes = row_chunks(block)
    gathered, first = [], 0
    for size in sizes:
        gathered.append(lax.all_gather(hidden[first:first + size], "gy", axis=0, tiled=True))
        first += size

    onehot = depth_onehot(parents, tree)
    sibling = [(g, g ^ 1) for g in range(n_gx)]

    def across(ahead):
        return [(g, (g // 2 + ahead) % chips * 2 + g % 2) for g in range(n_gx)]

    parts, first = [], 0
    for index, size in enumerate(sizes):
        rows = embed(n_gx, n_gy, first, size, place, onehot, depth_table, gathered[index])
        first += size
        count = pieces_of(columns, 4 if index == len(sizes) - 1 else 2)
        width = columns // count
        tile = 512 if width % 512 == 0 else 256
        done = []
        for piece in range(count):
            out = product(rows, weight, piece * width, width, tile)
            got = lax.ppermute(out[:chips * size], "gx", sibling)
            pair = (out[chips * size:].astype(F32) + got.astype(F32)).astype(BF16)
            total = pair[(chips - 1) * size:].astype(F32)
            for ahead in range(1, chips):
                total = total + lax.ppermute(pair[(ahead - 1) * size:ahead * size], "gx", across(ahead)).astype(F32)
            done.append(jax.nn.gelu(total, approximate=True).astype(BF16))
        parts.append(jnp.concatenate(done, axis=1))
    return jnp.concatenate(parts, axis=0)


def solution(mesh):
    return jax.shard_map(
        functools.partial(local, mesh.shape["gx"], mesh.shape["gy"]),
        mesh=mesh,
        in_specs=(P(("grp", "gy"), "gx"), P("grp"), P(None, "gx"), P("gx", "gy")),
        out_specs=P(("grp", "gx"), "gy"),
        check_vma=False,
    )
```

time: 350 us -> 342 us (0.977)
  Pallas kernels: 0 us -> 144 us
  waiting for transfers between devices: 213 us -> 101 us
  matrix products: 60.3 us -> 0 us
  other arithmetic: 6.85 us -> 45.6 us
  local copies, waits for them, and re-layouts: 55.5 us -> 19.5 us
  starting transfers between devices: 0.04 us -> 16.1 us
    pallas_call x0 -> x15, Pallas kernels: none -> 144 us  [the longest x10 135 us: product(): pl.pallas_call(product_kernel, grid=(width // tile,), out_shape=jax.Shape...]
    reduce_scatter x1 -> x0, waiting for transfers between devices: 108 us -> none  [local(): lax.psum_scatter(jnp.dot(gathered, weight, preferred_element_type=jnp.flo...]
    all_gather x1 -> x4, waiting for transfers between devices: 105 us -> 30.2 us  [local(): lax.all_gather(hidden[first:first + size], 'gy', axis=0, tiled=True)]
    ppermute x0 -> x20, waiting for transfers between devices: none -> 68.7 us  [the longest x10 68.7 us: local(): lax.ppermute(pair[(ahead - 1) * size:ahead * size], 'gx', across(ahead))]
    dot_general x2 -> x0, matrix products: 60.3 us -> none  [the longest x1 58.6 us: local(): jnp.dot(gathered, weight, preferred_element_type=jnp.float32)]
    gather x17 -> x0, local copies, waits for them, and re-layouts: 55.4 us -> none  [the longest x9 28.7 us: tree_depth(): depth = depth + depth[pointer]]
    concatenate x0 -> x1, other arithmetic: none -> 35.7 us  [local(): return jnp.concatenate(parts, axis=0)]
    ppermute x0 -> x20, starting transfers between devices: none -> 15.9 us  [the longest x10 13.1 us: local(): lax.ppermute(pair[(ahead - 1) * size:ahead * size], 'gx', across(ahead))]
  transfers between devices with their start and end apart: 2 -> 24, of which waited for: 2 -> 11; matrix products, arithmetic and copies ran while one was open for 0% -> 5% of each run, Pallas kernels for 0% -> 42%
where the time goes in v1:
time: 342 us; the launch traced here: 340 us
  Pallas kernels  144 us (42%)
  waiting for transfers between devices  101 us (30%)
  other arithmetic  45.6 us (13%)
  local copies, waits for them, and re-layouts  19.5 us (6%)
  starting transfers between devices  16.1 us (5%)
  between operations  13.7 us (4%)
    pallas_call x10, Pallas kernels, product(): pl.pallas_call(product_kernel, grid=(width // tile,), out_shape=jax.Shape...  135 us
    ppermute x10, waiting for transfers between devices, local(): lax.ppermute(pair[(ahead - 1) * size:ahead * size], 'gx', across(ahead))  68.7 us
    concatenate x1, other arithmetic, local(): return jnp.concatenate(parts, axis=0)  35.7 us
    all_gather x4, waiting for transfers between devices, local(): lax.all_gather(hidden[first:first + size], 'gy', axis=0, tiled=True)  30.2 us
    ppermute x10, starting transfers between devices, local(): lax.ppermute(pair[(ahead - 1) * size:ahead * size], 'gx', across(ahead))  13.1 us
    unnamed x46, local copies, waits for them, and re-layouts  10 us
    convert_element_type x10, other arithmetic, local(): pair = (out[chips * size:].astype(F32) + got.astype(F32)).astype(BF16)  7 us
  transfers between devices with their start and end apart: 24, of which 11 were waited for; matrix products, arithmetic and copies ran while one was open for 5% of the time, Pallas kernels for 42%

profile of v1, /device:TPU:0, one launch (start us, length us, event | category | flops | bytes accessed | tf_op | source)
XLA Modules:
  0.0 340.1 jit_solution(6511263209793802777)
XLA Ops:
  6.5 2.4 fusion.80
  11.2 4.3 %shard_map.46.onehot_ref = bf16[768,256]{1,0:T(8,128)(2,1)S(1)} custom-call(s32[768,1]{1,0:T(8,128)S(1)} %broadcast_in_dim.8.parents_ref), custom_call_target="tpu_custom_call" | custom-call | flops 2415919104 | bytes 1572864 | tf_op jit(solution)/shard_map/pallas_call | solution.py:30
  15.5 30.2 %all-gather.11.cloned.1.call-done.hidden_ref = bf16[192,3584]{1,0:T(8,128)(2,1)} async-done(((bf16[48,3584]{1,0:T(8,128)(2,1)}), bf16[192,3584]{1,0:T(8,128)(2,1)}) %all-gather.11.cloned.1.call-update) | async-done | bytes 1376272 | tf_op jit(solution)/shard_map/all_gather | solution.py:111
  48.4 10.7 %shard_map.60 = bf16[192,2304]{1,0:T(8,128)(2,1)S(1)} custom-call(bf16[192,3584]{1,0:T(8,128)(2,1)S(1)} %shard_map.56.rows_ref, bf16[3584,9216]{1,0:T(8,128)(2,1)} %weight_ref.19), custom_call_target="tpu_custom_call" | custom-call | flops 3170893824 | bytes 18776064 | tf_op jit(solution)/shard_map/pallas_call | solution.py:70
  59.2 10.8 %shard_map.59 = bf16[192,2304]{1,0:T(8,128)(2,1)S(1)} custom-call(bf16[192,3584]{1,0:T(8,128)(2,1)S(1)} %shard_map.56.rows_ref, bf16[3584,9216]{1,0:T(8,128)(2,1)} %weight_ref.19), custom_call_target="tpu_custom_call" | custom-call | flops 3170893824 | bytes 18776064 | tf_op jit(solution)/shard_map/pallas_call | solution.py:70
  70.0 10.8 %shard_map.58 = bf16[192,2304]{1,0:T(8,128)(2,1)S(1)} custom-call(bf16[192,3584]{1,0:T(8,128)(2,1)S(1)} %shard_map.56.rows_ref, bf16[3584,9216]{1,0:T(8,128)(2,1)} %weight_ref.19), custom_call_target="tpu_custom_call" | custom-call | flops 3170893824 | bytes 18776064 | tf_op jit(solution)/shard_map/pallas_call | solution.py:70
  80.8 10.9 %shard_map.57 = bf16[192,2304]{1,0:T(8,128)(2,1)S(1)} custom-call(bf16[192,3584]{1,0:T(8,128)(2,1)S(1)} %shard_map.56.rows_ref, bf16[3584,9216]{1,0:T(8,128)(2,1)} %weight_ref.19), custom_call_target="tpu_custom_call" | custom-call | flops 3170893824 | bytes 18776064 | tf_op jit(solution)/shard_map/pallas_call | solution.py:70
  98.0 15.2 %shard_map.55 = bf16[192,4608]{1,0:T(8,128)(2,1)S(1)} custom-call(bf16[192,3584]{1,0:T(8,128)(2,1)S(1)} %shard_map.53.rows_ref, bf16[3584,9216]{1,0:T(8,128)(2,1)} %weight_ref.19), custom_call_target="tpu_custom_call" | custom-call | flops 6341787648 | bytes 36175872 | tf_op jit(solution)/shard_map/pallas_call | solution.py:70
  114.7 15.3 %shard_map.54 = bf16[192,4608]{1,0:T(8,128)(2,1)S(1)} custom-call(bf16[192,3584]{1,0:T(8,128)(2,1)S(1)} %shard_map.53.rows_ref, bf16[3584,9216]{1,0:T(8,128)(2,1)} %weight_ref.19), custom_call_target="tpu_custom_call" | custom-call | flops 6341787648 | bytes 36175872 | tf_op jit(solution)/shard_map/pallas_call | solution.py:70
  135.1 15.2 %shard_map.52 = bf16[192,4608]{1,0:T(8,128)(2,1)S(1)} custom-call(bf16[192,3584]{1,0:T(8,128)(2,1)S(1)} %shard_map.50.rows_ref, bf16[3584,9216]{1,0:T(8,128)(2,1)} %weight_ref.19), custom_call_target="tpu_custom_call" | custom-call | flops 6341787648 | bytes 36175872 | tf_op jit(solution)/shard_map/pallas_call | solution.py:70
  152.5 15.1 %shard_map.51 = bf16[192,4608]{1,0:T(8,128)(2,1)S(1)} custom-call(bf16[192,3584]{1,0:T(8,128)(2,1)S(1)} %shard_map.50.rows_ref, bf16[3584,9216]{1,0:T(8,128)(2,1)} %weight_ref.19), custom_call_target="tpu_custom_call" | custom-call | flops 6341787648 | bytes 36175872 | tf_op jit(solution)/shard_map/pallas_call | solution.py:70
  172.7 15.1 %shard_map.49 = bf16[192,4608]{1,0:T(8,128)(2,1)S(1)} custom-call(bf16[192,3584]{1,0:T(8,128)(2,1)S(1)} %shard_map.47.rows_ref, bf16[3584,9216]{1,0:T(8,128)(2,1)} %weight_ref.19), custom_call_target="tpu_custom_call" | custom-call | flops 6341787648 | bytes 36175872 | tf_op jit(solution)/shard_map/pallas_call | solution.py:70
  187.9 15.4 %shard_map.48 = bf16[192,4608]{1,0:T(8,128)(2,1)S(1)} custom-call(bf16[192,3584]{1,0:T(8,128)(2,1)S(1)} %shard_map.47.rows_ref, bf16[3584,9216]{1,0:T(8,128)(2,1)} %weight_ref.19), custom_call_target="tpu_custom_call" | custom-call | flops 6341787648 | bytes 36175872 | tf_op jit(solution)/shard_map/pallas_call | solution.py:70
  208.7 1.5 collective-permute-start.19
  211.4 5.2 %collective-permute-done.19 = bf16[48,2304]{1,0:T(8,128)(2,1)S(1)} collective-permute-done((bf16[48,2304]{1,0:T(8,128)(2,1)S(1)}, bf16[48,2304]{1,0:T(8,128)(2,1)S(1)}, u32[]{:S(2)}, u32[]{:S(2)}) %collective-permute-start.19) | collective-permute-done | bytes 221216 | tf_op jit(solution)/shard_map/ppermute | solution.py:134
  216.6 1.4 collective-permute-start.17
  218.2 5.4 %collective-permute-done.17 = bf16[48,2304]{1,0:T(8,128)(2,1)S(1)} collective-permute-done((bf16[48,2304]{1,0:T(8,128)(2,1)S(1)}, bf16[48,2304]{1,0:T(8,128)(2,1)S(1)}, u32[]{:S(2)}, u32[]{:S(2)}) %collective-permute-start.17) | collective-permute-done | bytes 221216 | tf_op jit(solution)/shard_map/ppermute | solution.py:134
  223.6 1.4 collective-permute-start.15
  225.2 4.5 %collective-permute-done.15 = bf16[48,2304]{1,0:T(8,128)(2,1)S(1)} collective-permute-done((bf16[48,2304]{1,0:T(8,128)(2,1)S(1)}, bf16[48,2304]{1,0:T(8,128)(2,1)S(1)}, u32[]{:S(2)}, u32[]{:S(2)}) %collective-permute-start.15) | collective-permute-done | bytes 221216 | tf_op jit(solution)/shard_map/ppermute | solution.py:134
  229.7 1.4 collective-permute-start.13
  231.4 4.3 %collective-permute-done.13 = bf16[48,2304]{1,0:T(8,128)(2,1)S(1)} collective-permute-done((bf16[48,2304]{1,0:T(8,128)(2,1)S(1)}, bf16[48,2304]{1,0:T(8,128)(2,1)S(1)}, u32[]{:S(2)}, u32[]{:S(2)}) %collective-permute-start.13) | collective-permute-done | bytes 221216 | tf_op jit(solution)/shard_map/ppermute | solution.py:134
  237.9 1.5 collective-permute-start.11
  240.6 1.5 collective-permute-start.7
  243.2 1.5 collective-permute-start.3
  245.0 6.0 %collective-permute-done.11 = bf16[48,4608]{1,0:T(8,128)(2,1)S(1)} collective-permute-done((bf16[48,4608]{1,0:T(8,128)(2,1)S(1)}, bf16[48,4608]{1,0:T(8,128)(2,1)S(1)}, u32[]{:S(2)}, u32[]{:S(2)}) %collective-permute-start.11) | collective-permute-done | bytes 442400 | tf_op jit(solution)/shard_map/ppermute | solution.py:134
  251.0 1.4 collective-permute-start.1
  252.8 7.7 %collective-permute-done.9 = bf16[48,4608]{1,0:T(8,128)(2,1)S(1)} collective-permute-done((bf16[48,4608]{1,0:T(8,128)(2,1)S(1)}, bf16[48,4608]{1,0:T(8,128)(2,1)S(1)}, u32[]{:S(2)}, u32[]{:S(2)}) %collective-permute-start.9) | collective-permute-done | bytes 442400 | tf_op jit(solution)/shard_map/ppermute | solution.py:134
  260.8 9.1 %collective-permute-done.7 = bf16[48,4608]{1,0:T(8,128)(2,1)S(1)} collective-permute-done((bf16[48,4608]{1,0:T(8,128)(2,1)S(1)}, bf16[48,4608]{1,0:T(8,128)(2,1)S(1)}, u32[]{:S(2)}, u32[]{:S(2)}) %collective-permute-start.7) | collective-permute-done | bytes 442400 | tf_op jit(solution)/shard_map/ppermute | solution.py:134
  270.3 9.1 %collective-permute-done.5 = bf16[48,4608]{1,0:T(8,128)(2,1)S(1)} collective-permute-done((bf16[48,4608]{1,0:T(8,128)(2,1)S(1)}, bf16[48,4608]{1,0:T(8,128)(2,1)S(1)}, u32[]{:S(2)}, u32[]{:S(2)}) %collective-permute-start.5) | collective-permute-done | bytes 442400 | tf_op jit(solution)/shard_map/ppermute | solution.py:134
  279.8 9.1 %collective-permute-done.3 = bf16[48,4608]{1,0:T(8,128)(2,1)S(1)} collective-permute-done((bf16[48,4608]{1,0:T(8,128)(2,1)S(1)}, bf16[48,4608]{1,0:T(8,128)(2,1)S(1)}, u32[]{:S(2)}, u32[]{:S(2)}) %collective-permute-start.3) | collective-permute-done | bytes 442400 | tf_op jit(solution)/shard_map/ppermute | solution.py:134
  289.3 8.3 %collective-permute-done.1 = bf16[48,4608]{1,0:T(8,128)(2,1)S(1)} collective-permute-done((bf16[48,4608]{1,0:T(8,128)(2,1)S(1)}, bf16[48,4608]{1,0:T(8,128)(2,1)S(1)}, u32[]{:S(2)}, u32[]{:S(2)}) %collective-permute-start.1) | collective-permute-done | bytes 442400 | tf_op jit(solution)/shard_map/ppermute | solution.py:134
  297.9 35.7 %maximum_maximum_fusion = bf16[192,9216]{1,0:T(8,128)(2,1)} fusion(bf16[48,2304]{1,0:T(8,128)(2,1)S(1)} %fusion.79, bf16[48,2304]{1,0:T(8,128)(2,1)S(1)} %fusion.71, bf16[48,2304]{1,0:T(8,128)(2,1)S(1)} %fusion.63, bf16[48,2304]{1,0:T(8,128)(2,1)S(1)} %fusion.55, bf16[48,4608]{1,0:T(8,128)(2,1)S(1)} %fusion.47, bf16[48,4608]{1,0:T(8,128)(2,1)S(1)} %fusion.39, ...), kind=kLoop, calls=%fused_computation | loop fusion | flops 35389440 | bytes 7077888 | tf_op jit(solution)/shard_map/concatenate | solution.py:137
  (124 shorter events, 39.0 us)
Async XLA Ops:
  6.5 4.5 %copy-start.22 = (s32[768]{0:T(1024)S(1)}, s32[768]{0:T(1024)}, u32[]{:S(2)}) copy-start(s32[768]{0:T(1024)} %param.5) | copy-start | bytes 9220
  6.5 39.1 %all-gather.11.cloned.1.call-start = ((), (), s32[]{:S(2)}) async-start(), calls=%async_computation.3 | async-start | bytes 1720320 | tf_op jit(solution)/shard_map/all_gather | solution.py:111
  9.0 86.3 %all-gather.9.cloned.1.call-start = ((), (), s32[]{:S(2)}) async-start(), calls=%async_computation.2 | async-start | bytes 1720320 | tf_op jit(solution)/shard_map/all_gather | solution.py:111
  9.7 122.6 %all-gather.7.cloned.1.call-start = ((), (), s32[]{:S(2)}) async-start(), calls=%async_computation.1 | async-start | bytes 1720320 | tf_op jit(solution)/shard_map/all_gather | solution.py:111
  10.5 159.4 %all-gather.5.cloned.1.call-start = ((), (), s32[]{:S(2)}) async-start(), calls=%async_computation | async-start | bytes 1720320 | tf_op jit(solution)/shard_map/all_gather | solution.py:111
  11.2 34.4 %copy-start = (bf16[256,3584]{1,0:T(8,128)(2,1)S(1)}, bf16[256,3584]{1,0:T(8,128)(2,1)}, u32[]{:S(2)}) copy-start(bf16[256,3584]{1,0:T(8,128)(2,1)} %table_ref.7) | copy-start | bytes 5505028
  59.1 32.5 %copy-start.13 = (bf16[192,2304]{1,0:T(8,128)(2,1)}, bf16[192,2304]{1,0:T(8,128)(2,1)S(1)}, u32[]{:S(2)}) copy-start(bf16[192,2304]{1,0:T(8,128)(2,1)S(1)} %shard_map.60) | copy-start | bytes 2654212
  70.0 22.5 %copy-start.11 = (bf16[192,2304]{1,0:T(8,128)(2,1)}, bf16[192,2304]{1,0:T(8,128)(2,1)S(1)}, u32[]{:S(2)}) copy-start(bf16[192,2304]{1,0:T(8,128)(2,1)S(1)} %shard_map.59) | copy-start | bytes 2654212
  80.8 13.0 %copy-start.9 = (bf16[192,2304]{1,0:T(8,128)(2,1)}, bf16[192,2304]{1,0:T(8,128)(2,1)S(1)}, u32[]{:S(2)}) copy-start(bf16[192,2304]{1,0:T(8,128)(2,1)S(1)} %shard_map.58) | copy-start | bytes 2654212
  92.5 110.9 %collective-permute-start.18 = (bf16[96,2304]{1,0:T(8,128)(2,1)}, bf16[96,2304]{1,0:T(8,128)(2,1)}, u32[]{:S(2)}, u32[]{:S(2)}) collective-permute-start(bf16[96,2304]{1,0:T(8,128)(2,1)} %slice.213), channel_id=1, source_target_pairs={{0,4},{4,0},{8,12},{12,8},{1,5},{5,1},{9,13},{13,9},{2,6},{6,2},{1... | collective-permute-start | bytes 1327112 | tf_op jit(solution)/shard_map/ppermute | solution.py:130
  93.3 112.5 %collective-permute-start.16 = (bf16[96,2304]{1,0:T(8,128)(2,1)}, bf16[96,2304]{1,0:T(8,128)(2,1)}, u32[]{:S(2)}, u32[]{:S(2)}) collective-permute-start(bf16[96,2304]{1,0:T(8,128)(2,1)} %slice.209), channel_id=1, source_target_pairs={{0,4},{4,0},{8,12},{12,8},{1,5},{5,1},{9,13},{13,9},{2,6},{6,2},{1... | collective-permute-start | bytes 1327112 | tf_op jit(solution)/shard_map/ppermute | solution.py:130
  94.6 112.8 %collective-permute-start.14 = (bf16[96,2304]{1,0:T(8,128)(2,1)}, bf16[96,2304]{1,0:T(8,128)(2,1)}, u32[]{:S(2)}, u32[]{:S(2)}) collective-permute-start(bf16[96,2304]{1,0:T(8,128)(2,1)} %slice.205), channel_id=1, source_target_pairs={{0,4},{4,0},{8,12},{12,8},{1,5},{5,1},{9,13},{13,9},{2,6},{6,2},{1... | collective-permute-start | bytes 1327112 | tf_op jit(solution)/shard_map/ppermute | solution.py:130
  94.7 114.0 %collective-permute-start.12 = (bf16[96,2304]{1,0:T(8,128)(2,1)S(1)}, bf16[96,2304]{1,0:T(8,128)(2,1)}, u32[]{:S(2)}, u32[]{:S(2)}) collective-permute-start(bf16[96,2304]{1,0:T(8,128)(2,1)S(1)} %slice.201), channel_id=1, source_target_pairs={{0,4},{4,0},{8,12},{12,8},{1,5},{5,1},{9,13},{13,9},{2,6},{6,2},{1... | collective-permute-start | bytes 1327112 | tf_op jit(solution)/shard_map/ppermute | solution.py:130
  114.7 121.2 %collective-permute-start.10 = (bf16[96,4608]{1,0:T(8,128)(2,1)}, bf16[96,4608]{1,0:T(8,128)(2,1)}, u32[]{:S(2)}, u32[]{:S(2)}) collective-permute-start(bf16[96,4608]{1,0:T(8,128)(2,1)} %slice.197), channel_id=1, source_target_pairs={{0,4},{4,0},{8,12},{12,8},{1,5},{5,1},{9,13},{13,9},{2,6},{6,2},{1... | collective-permute-start | bytes 2654216 | tf_op jit(solution)/shard_map/ppermute | solution.py:130
  187.9 15.5 %copy-start.21 = (bf16[96,4608]{1,0:T(8,128)(2,1)S(1)}, bf16[96,4608]{1,0:T(8,128)(2,1)}, u32[]{:S(2)}) copy-start(bf16[96,4608]{1,0:T(8,128)(2,1)} %slice.193) | copy-start | bytes 2654212
  203.4 4.2 %copy-start.10 = (bf16[192,2304]{1,0:T(8,128)(2,1)S(1)}, bf16[192,2304]{1,0:T(8,128)(2,1)}, u32[]{:S(2)}) copy-start(bf16[192,2304]{1,0:T(8,128)(2,1)} %copy-done.9) | copy-start | bytes 2654212
  203.4 34.5 %collective-permute-start.8 = (bf16[96,4608]{1,0:T(8,128)(2,1)S(1)}, bf16[96,4608]{1,0:T(8,128)(2,1)S(1)}, u32[]{:S(2)}, u32[]{:S(2)}) collective-permute-start(bf16[96,4608]{1,0:T(8,128)(2,1)S(1)} %copy-done.21), channel_id=1, source_target_pairs={{0,4},{4,0},{8,12},{12,8},{1,5},{5,1},{9,13},{13,9},{2,6},{6,2},{1... | collective-permute-start | bytes 2654216 | tf_op jit(solution)/shard_map/ppermute | solution.py:130
  205.8 33.9 %collective-permute-start.6 = (bf16[96,4608]{1,0:T(8,128)(2,1)S(1)}, bf16[96,4608]{1,0:T(8,128)(2,1)S(1)}, u32[]{:S(2)}, u32[]{:S(2)}) collective-permute-start(bf16[96,4608]{1,0:T(8,128)(2,1)S(1)} %copy-done.20), channel_id=1, source_target_pairs={{0,4},{4,0},{8,12},{12,8},{1,5},{5,1},{9,13},{13,9},{2,6},{6,2},{1... | collective-permute-start | bytes 2654216 | tf_op jit(solution)/shard_map/ppermute | solution.py:130
  207.5 33.1 %collective-permute-start.4 = (bf16[96,4608]{1,0:T(8,128)(2,1)S(1)}, bf16[96,4608]{1,0:T(8,128)(2,1)S(1)}, u32[]{:S(2)}, u32[]{:S(2)}) collective-permute-start(bf16[96,4608]{1,0:T(8,128)(2,1)S(1)} %copy-done.19), channel_id=1, source_target_pairs={{0,4},{4,0},{8,12},{12,8},{1,5},{5,1},{9,13},{13,9},{2,6},{6,2},{1... | collective-permute-start | bytes 2654216 | tf_op jit(solution)/shard_map/ppermute | solution.py:130
  208.7 7.9 %collective-permute-start.19 = (bf16[48,2304]{1,0:T(8,128)(2,1)S(1)}, bf16[48,2304]{1,0:T(8,128)(2,1)S(1)}, u32[]{:S(2)}, u32[]{:S(2)}) collective-permute-start(bf16[48,2304]{1,0:T(8,128)(2,1)S(1)} %slice.215), channel_id=1, source_target_pairs={{0,8},{4,12},{8,0},{12,4},{1,9},{5,13},{9,1},{13,5},{2,10},{6,14},... | collective-permute-start | bytes 663560 | tf_op jit(solution)/shard_map/ppermute | solution.py:134
  211.3 25.1 %copy-start.8 = (bf16[192,4608]{1,0:T(8,128)(2,1)S(1)}, bf16[192,4608]{1,0:T(8,128)(2,1)}, u32[]{:S(2)}) copy-start(bf16[192,4608]{1,0:T(8,128)(2,1)} %copy-done.7) | copy-start | bytes 5308420
  216.6 7.0 %collective-permute-start.17 = (bf16[48,2304]{1,0:T(8,128)(2,1)S(1)}, bf16[48,2304]{1,0:T(8,128)(2,1)S(1)}, u32[]{:S(2)}, u32[]{:S(2)}) collective-permute-start(bf16[48,2304]{1,0:T(8,128)(2,1)S(1)} %slice.211), channel_id=1, source_target_pairs={{0,8},{4,12},{8,0},{12,4},{1,9},{5,13},{9,1},{13,5},{2,10},{6,14},... | collective-permute-start | bytes 663560 | tf_op jit(solution)/shard_map/ppermute | solution.py:134
  223.6 6.1 %collective-permute-start.15 = (bf16[48,2304]{1,0:T(8,128)(2,1)S(1)}, bf16[48,2304]{1,0:T(8,128)(2,1)S(1)}, u32[]{:S(2)}, u32[]{:S(2)}) collective-permute-start(bf16[48,2304]{1,0:T(8,128)(2,1)S(1)} %slice.207), channel_id=1, source_target_pairs={{0,8},{4,12},{8,0},{12,4},{1,9},{5,13},{9,1},{13,5},{2,10},{6,14},... | collective-permute-start | bytes 663560 | tf_op jit(solution)/shard_map/ppermute | solution.py:134
  229.7 5.9 %collective-permute-start.13 = (bf16[48,2304]{1,0:T(8,128)(2,1)S(1)}, bf16[48,2304]{1,0:T(8,128)(2,1)S(1)}, u32[]{:S(2)}, u32[]{:S(2)}) collective-permute-start(bf16[48,2304]{1,0:T(8,128)(2,1)S(1)} %slice.203), channel_id=1, source_target_pairs={{0,8},{4,12},{8,0},{12,4},{1,9},{5,13},{9,1},{13,5},{2,10},{6,14},... | collective-permute-start | bytes 663560 | tf_op jit(solution)/shard_map/ppermute | solution.py:134
  235.7 6.7 %collective-permute-start.2 = (bf16[96,4608]{1,0:T(8,128)(2,1)S(1)}, bf16[96,4608]{1,0:T(8,128)(2,1)S(1)}, u32[]{:S(2)}, u32[]{:S(2)}) collective-permute-start(bf16[96,4608]{1,0:T(8,128)(2,1)S(1)} %slice.181), channel_id=1, source_target_pairs={{0,4},{4,0},{8,12},{12,8},{1,5},{5,1},{9,13},{13,9},{2,6},{6,2},{1... | collective-permute-start | bytes 2654216 | tf_op jit(solution)/shard_map/ppermute | solution.py:130
  235.9 7.4 %collective-permute-start = (bf16[96,4608]{1,0:T(8,128)(2,1)S(1)}, bf16[96,4608]{1,0:T(8,128)(2,1)S(1)}, u32[]{:S(2)}, u32[]{:S(2)}) collective-permute-start(bf16[96,4608]{1,0:T(8,128)(2,1)S(1)} %slice.177), channel_id=1, source_target_pairs={{0,4},{4,0},{8,12},{12,8},{1,5},{5,1},{9,13},{13,9},{2,6},{6,2},{1... | collective-permute-start | bytes 2654216 | tf_op jit(solution)/shard_map/ppermute | solution.py:130
  237.9 13.1 %collective-permute-start.11 = (bf16[48,4608]{1,0:T(8,128)(2,1)S(1)}, bf16[48,4608]{1,0:T(8,128)(2,1)S(1)}, u32[]{:S(2)}, u32[]{:S(2)}) collective-permute-start(bf16[48,4608]{1,0:T(8,128)(2,1)S(1)} %slice.199), channel_id=1, source_target_pairs={{0,8},{4,12},{8,0},{12,4},{1,9},{5,13},{9,1},{13,5},{2,10},{6,14},... | collective-permute-start | bytes 1327112 | tf_op jit(solution)/shard_map/ppermute | solution.py:134
  239.7 20.8 %collective-permute-start.9 = (bf16[48,4608]{1,0:T(8,128)(2,1)S(1)}, bf16[48,4608]{1,0:T(8,128)(2,1)S(1)}, u32[]{:S(2)}, u32[]{:S(2)}) collective-permute-start(bf16[48,4608]{1,0:T(8,128)(2,1)S(1)} %slice.195), channel_id=1, source_target_pairs={{0,8},{4,12},{8,0},{12,4},{1,9},{5,13},{9,1},{13,5},{2,10},{6,14},... | collective-permute-start | bytes 1327112 | tf_op jit(solution)/shard_map/ppermute | solution.py:134
  240.6 29.4 %collective-permute-start.7 = (bf16[48,4608]{1,0:T(8,128)(2,1)S(1)}, bf16[48,4608]{1,0:T(8,128)(2,1)S(1)}, u32[]{:S(2)}, u32[]{:S(2)}) collective-permute-start(bf16[48,4608]{1,0:T(8,128)(2,1)S(1)} %slice.191), channel_id=1, source_target_pairs={{0,8},{4,12},{8,0},{12,4},{1,9},{5,13},{9,1},{13,5},{2,10},{6,14},... | collective-permute-start | bytes 1327112 | tf_op jit(solution)/shard_map/ppermute | solution.py:134
  242.3 37.1 %collective-permute-start.5 = (bf16[48,4608]{1,0:T(8,128)(2,1)S(1)}, bf16[48,4608]{1,0:T(8,128)(2,1)S(1)}, u32[]{:S(2)}, u32[]{:S(2)}) collective-permute-start(bf16[48,4608]{1,0:T(8,128)(2,1)S(1)} %slice.187), channel_id=1, source_target_pairs={{0,8},{4,12},{8,0},{12,4},{1,9},{5,13},{9,1},{13,5},{2,10},{6,14},... | collective-permute-start | bytes 1327112 | tf_op jit(solution)/shard_map/ppermute | solution.py:134
  243.2 45.6 %collective-permute-start.3 = (bf16[48,4608]{1,0:T(8,128)(2,1)S(1)}, bf16[48,4608]{1,0:T(8,128)(2,1)S(1)}, u32[]{:S(2)}, u32[]{:S(2)}) collective-permute-start(bf16[48,4608]{1,0:T(8,128)(2,1)S(1)} %slice.183), channel_id=1, source_target_pairs={{0,8},{4,12},{8,0},{12,4},{1,9},{5,13},{9,1},{13,5},{2,10},{6,14},... | collective-permute-start | bytes 1327112 | tf_op jit(solution)/shard_map/ppermute | solution.py:134
  251.0 46.6 %collective-permute-start.1 = (bf16[48,4608]{1,0:T(8,128)(2,1)S(1)}, bf16[48,4608]{1,0:T(8,128)(2,1)S(1)}, u32[]{:S(2)}, u32[]{:S(2)}) collective-permute-start(bf16[48,4608]{1,0:T(8,128)(2,1)S(1)} %slice.179), channel_id=1, source_target_pairs={{0,8},{4,12},{8,0},{12,4},{1,9},{5,13},{9,1},{13,5},{2,10},{6,14},... | collective-permute-start | bytes 1327112 | tf_op jit(solution)/shard_map/ppermute | solution.py:134
  (15 other events, 29.7 us)
Sparse Core Ops, SparseCore 0:
  9.1 36.5 all-gather.10
  47.2 32.8 all-gather.8
  81.7 32.6 all-gather.6
  115.8 32.7 all-gather.4

commit v2 on v0

v2 whole, which is shorter than its diff:
```python
import functools

import jax
import jax.numpy as jnp
from jax import lax
from jax.experimental import pallas as pl
from jax.experimental.pallas import tpu as pltpu
from jax.sharding import PartitionSpec as P

BF16 = jnp.bfloat16
F32 = jnp.float32
MIB = 1024 * 1024
ANY = pl.BlockSpec(memory_space=pl.ANY)
VMEM = pl.BlockSpec(memory_space=pltpu.VMEM)
SMEM = pl.BlockSpec(memory_space=pltpu.SMEM)


def params(limit):
    return pltpu.CompilerParams(vmem_limit_bytes=limit * MIB)


def cost(flops, accessed):
    return pl.CostEstimate(flops=8 * flops, bytes_accessed=8 * accessed, transcendentals=0)


def divisor(extent, choices):
    for choice in choices:
        if extent % choice == 0:
            return choice
    return extent


def onehot_kernel(tree, parents_ref, onehot_ref):
    lanes = lax.broadcasted_iota(jnp.int32, (tree, tree), 1)
    rows = lax.broadcasted_iota(jnp.int32, (tree, 1), 0)
    for first in range(0, onehot_ref.shape[0], tree):
        parent = parents_ref[first:first + tree, :] - first
        jump = (parent == lanes).astype(BF16)
        depth = jnp.broadcast_to((parent != rows).astype(F32), (tree, 128))
        for level in range((tree - 1).bit_length()):
            depth = depth + jnp.dot(jump, depth.astype(BF16), preferred_element_type=F32)
            jump = jnp.dot(jump, jump, preferred_element_type=F32).astype(BF16)
        onehot_ref[first:first + tree, :] = (depth[:, :1].astype(jnp.int32) == lanes).astype(BF16)


def depth_onehot(parents, tree):
    rows = parents.shape[0]
    return pl.pallas_call(
        functools.partial(onehot_kernel, tree),
        name="onehot",
        out_shape=jax.ShapeDtypeStruct((rows, tree), BF16),
        compiler_params=params(16),
        cost_estimate=cost(48 * rows * tree * tree, 8 * rows * tree),
    )(parents[:, None])


def forward_kernel(place_ref, near_ref, far_ref, *refs):
    out_ref = refs[-1]
    outer = jnp.logical_or(place_ref[1] == 0, place_ref[1] == 3)

    @pl.when(outer)
    def _():
        out_ref[...] = near_ref[...]

    @pl.when(jnp.logical_not(outer))
    def _():
        out_ref[...] = far_ref[...]


def forward(place, near, far, after):
    return pl.pallas_call(
        forward_kernel,
        name="forward",
        out_shape=jax.ShapeDtypeStruct(near.shape, near.dtype),
        in_specs=[SMEM, VMEM, VMEM] + [ANY] * len(after),
        out_specs=VMEM,
        compiler_params=params(8),
        cost_estimate=cost(0, 6 * near.size),
    )(place, near, far, *after)


def embed_kernel(count, chips, block, first, exclusive, place_ref, onehot_ref, table_ref, *refs):
    rows_ref = refs[-1]
    size = rows_ref.shape[0] // count
    x, core = place_ref[0] // 2, lax.rem(place_ref[0], 2)
    for held in range(count):
        dest = lax.bitwise_xor(place_ref[1], held) if exclusive else held
        ahead = lax.rem(dest // 2 - x + 2 * chips - 1, chips)
        slot = jnp.where(core == lax.rem(dest, 2), chips, 0) + ahead
        here = pl.ds(pl.multiple_of(dest * block + first, 16), size)
        looked = jnp.dot(onehot_ref[here, :], table_ref[...], preferred_element_type=F32)
        total = refs[held][...].astype(F32) + looked
        rows_ref[pl.ds(pl.multiple_of(slot * size, 16), size), :] = total.astype(BF16)


def embed(chips, block, first, exclusive, place, onehot, table, held, after):
    count = len(held)
    size, depth = held[0].shape
    tile = divisor(depth, (896, 512, 256, 128))
    piece = pl.BlockSpec((size, tile), lambda j: (0, j))
    return pl.pallas_call(
        functools.partial(embed_kernel, count, chips, block, first, exclusive),
        name="embed",
        grid=(depth // tile,),
        out_shape=jax.ShapeDtypeStruct((count * size, depth), BF16),
        in_specs=[SMEM, pl.BlockSpec(onehot.shape, lambda j: (0, 0)), pl.BlockSpec((table.shape[0], tile), lambda j: (0, j))]
        + [piece] * count + [ANY] * len(after),
        out_specs=pl.BlockSpec((count * size, tile), lambda j: (0, j)),
        compiler_params=params(16),
        cost_estimate=cost(2 * count * size * table.shape[0] * depth, 6 * count * size * depth),
    )(place, onehot, table, *held, *after)


def product_kernel(start, tile, steps, slots, rows_ref, weight_ref, *refs):
    send_ref, keep_ref, held, arrived = refs[-4:]
    half = send_ref.shape[0]
    step = pl.program_id(0)

    def fetch(index):
        column = pl.multiple_of(start + index * tile, 128)
        slot = lax.rem(index, slots)
        return pltpu.make_async_copy(weight_ref.at[:, pl.ds(column, tile)], held.at[slot], arrived.at[slot])

    @pl.when(step == 0)
    def _():
        for index in range(min(slots - 1, steps)):
            fetch(index).start()

    @pl.when(step + slots - 1 < steps)
    def _():
        fetch(step + slots - 1).start()

    fetch(step).wait()
    out = jnp.dot(rows_ref[...], held[lax.rem(step, slots)], preferred_element_type=F32)
    send_ref[...] = out[:half].astype(BF16)
    keep_ref[...] = out[half:].astype(BF16)


def product(rows, weight, start, width, after):
    height, depth = rows.shape
    tile = divisor(width, (512, 384, 256, 128))
    slots = 4
    half = jax.ShapeDtypeStruct((height // 2, width), BF16)
    return pl.pallas_call(
        functools.partial(product_kernel, start, tile, width // tile, slots),
        name="product",
        grid=(width // tile,),
        out_shape=[half, half],
        in_specs=[pl.BlockSpec((height, depth), lambda j: (0, 0))] + [ANY] * (1 + len(after)),
        out_specs=[pl.BlockSpec((height // 2, tile), lambda j: (0, j))] * 2,
        scratch_shapes=[pltpu.VMEM((slots, depth, tile), BF16), pltpu.SemaphoreType.DMA((slots,))],
        compiler_params=params(32),
        cost_estimate=cost(2 * height * depth * width, 2 * (height * depth + depth * width + height * width)),
    )(rows, weight, *after)


def pair_kernel(keep_ref, got_ref, *refs):
    away_ref, stay_ref = refs[-2:]
    cut = away_ref.shape[0]
    total = keep_ref[...].astype(F32) + got_ref[...].astype(F32)
    away_ref[...] = total[:cut].astype(BF16)
    stay_ref[...] = total[cut:].astype(BF16)


def pair(chips, keep, got, after):
    height, width = keep.shape
    size = height // chips
    tile = divisor(width, (1536, 1152, 768, 512, 384, 256, 128))
    spec = lambda rows: pl.BlockSpec((rows, tile), lambda j: (0, j))
    return pl.pallas_call(
        pair_kernel,
        name="pair",
        grid=(width // tile,),
        out_shape=[jax.ShapeDtypeStruct((height - size, width), BF16), jax.ShapeDtypeStruct((size, width), BF16)],
        in_specs=[spec(height), spec(height)] + [ANY] * len(after),
        out_specs=[spec(height - size), spec(size)],
        compiler_params=params(16),
        cost_estimate=cost(height * width, 6 * height * width),
    )(keep, got, *after)


def finish_kernel(count, *refs):
    total = refs[0][...].astype(F32)
    for index in range(1, count):
        total = total + refs[index][...].astype(F32)
    out_ref, token_ref = refs[-2:]
    out_ref[...] = jax.nn.gelu(total, approximate=True).astype(BF16)
    token_ref[...] = jnp.zeros_like(token_ref)


def finish(shape, step, rows, terms, held, after):
    index, start, width = step
    tile = divisor(width, (1536, 1152, 768, 512, 384, 256, 128))
    aliases = {} if held is None else {len(terms): 0}
    return pl.pallas_call(
        functools.partial(finish_kernel, len(terms)),
        name="finish",
        grid=(width // tile,),
        out_shape=[jax.ShapeDtypeStruct(shape, BF16), jax.ShapeDtypeStruct((8, 128), F32)],
        in_specs=[pl.BlockSpec((rows, tile), lambda j: (0, j))] * len(terms) + [ANY] * (len(aliases) + len(after)),
        out_specs=[
            pl.BlockSpec((rows, tile), lambda j: (index, start // tile + j)),
            pl.BlockSpec((8, 128), lambda j: (0, 0)),
        ],
        input_output_aliases=aliases,
        compiler_params=params(16),
        cost_estimate=cost(12 * rows * width, 6 * rows * width),
    )(*terms, *([] if held is None else [held]), *after)


EARLY = (1, 1)
LAG = 3
LAST = (1, 1, 2, 2)


def column_pieces(columns, shares):
    unit, start, pieces = columns // sum(shares), 0, []
    for share in shares:
        pieces.append((start, share * unit))
        start += share * unit
    return pieces


def local(n_gx, n_gy, hidden, parents, depth_table, weight):
    tree = depth_table.shape[0]
    columns = weight.shape[1]
    block = hidden.shape[0]
    chips = n_gx // 2
    place = jnp.stack([lax.axis_index("gx"), lax.axis_index("gy")]).astype(jnp.int32)
    onehot = depth_onehot(parents, tree)

    parts = divisor(block // 16, (3, 4, 2))
    size = block // parts
    own = [hidden[index * size:(index + 1) * size] for index in range(parts)]

    exclusive = n_gy == 4
    if exclusive:
        near = [None] * parts
        far = [None] * parts
        rest = [None] * parts

        def swap(array, distance):
            return lax.ppermute(array, "gy", [(k, k ^ distance) for k in range(n_gy)])

        near[0], far[0] = swap(own[0], 1), swap(own[0], 2)
        if parts > 1:
            near[1] = swap(own[1], 1)
    else:
        gathered = [lax.all_gather(rows, "gy", axis=0) for rows in own]

    def pass_on(index, after):
        if not exclusive or index >= parts:
            return []
        given = forward(place, near[index], far[index], after)
        rest[index] = lax.ppermute(given, "gy", [(0, 2), (1, 0), (2, 3), (3, 1)])
        if index == 0 and parts > 1:
            far[1] = swap(lax.optimization_barrier((own[1], given))[0], 2)
        return [given]

    sibling = [(g, g ^ 1) for g in range(n_gx)]

    def across(ahead):
        return [(g, (g // 2 + ahead) % chips * 2 + g % 2) for g in range(n_gx)]

    def exchange(away, stay):
        return [stay] + [
            lax.ppermute(away[(ahead - 1) * size:ahead * size], "gx", across(ahead)) for ahead in range(1, chips)
        ]

    steps = [
        (index, start, width)
        for index in range(parts)
        for start, width in column_pieces(columns, LAST if index == parts - 1 else EARLY)
    ]
    out = None
    products, sums = [], []
    pass_on(0, [])
    for step, (index, start, width) in enumerate(steps):
        after = [products[-1][0]] if products else []
        before = []
        if start == 0:
            if exclusive:
                held = [own[index], near[index], far[index], rest[index]]
            else:
                held = [gathered[index][k] for k in range(n_gy)]
            rows = embed(chips, block, index * size, exclusive, place, onehot, depth_table, held, after)
        elif start == steps[step - 1][2] and index + 1 < parts:
            before += pass_on(index + 1, after)
        if step >= 2:
            away, stay = pair(chips, *products[step - 2], after)
            before.append(stay)
            sums.append(exchange(away, stay))
        if step >= LAG:
            out, token = finish((block, columns), steps[step - LAG], size, sums[step - LAG], out, after)
            before.append(token)
        send, keep = product(rows, weight, start, width, before)
        products.append((keep, lax.ppermute(send, "gx", sibling)))
        if exclusive and start > 0 and index + 2 < parts and near[index + 2] is None:
            rows_on, _ = lax.optimization_barrier((own[index + 2], keep))
            near[index + 2], far[index + 2] = swap(rows_on, 1), swap(rows_on, 2)
    token = []
    for step in range(len(steps) - LAG, len(steps)):
        for ready in range(len(sums), min(step + 2, len(steps))):
            sums.append(exchange(*pair(chips, *products[ready], token)))
        out, done = finish((block, columns), steps[step], size, sums[step], out, [])
        token = [done]
    return out


def solution(mesh):
    return jax.shard_map(
        functools.partial(local, mesh.shape["gx"], mesh.shape["gy"]),
        mesh=mesh,
        in_specs=(P(("grp", "gy"), "gx"), P("grp"), P(None, "gx"), P("gx", "gy")),
        out_specs=P(("grp", "gx"), "gy"),
        check_vma=False,
    )
```

time: 350 us -> 201 us (0.57)
  waiting for transfers between devices: 213 us -> 67.1 us
  Pallas kernels: 0 us -> 107 us
  matrix products: 60.3 us -> 0 us
  local copies, waits for them, and re-layouts: 55.5 us -> 2.33 us
  starting transfers between devices: 0.04 us -> 24.8 us
  between operations: 13.7 us -> 0.33 us
  other arithmetic: 6.85 us -> 0.08 us
    reduce_scatter x1 -> x0, waiting for transfers between devices: 108 us -> none  [local(): lax.psum_scatter(jnp.dot(gathered, weight, preferred_element_type=jnp.flo...]
    pallas_call x0 -> x31, Pallas kernels: none -> 107 us  [the longest x8 78.4 us: product(): pl.pallas_call(functools.partial(product_kernel, start, tile, width // ti...]
    all_gather x1 -> x0, waiting for transfers between devices: 105 us -> none  [local(): gathered = lax.all_gather(rows_in, 'gy', axis=0, tiled=True)]
    ppermute x0 -> x25, waiting for transfers between devices: none -> 67.1 us  [the longest x8 29.7 us: exchange(): lax.ppermute(away[(ahead - 1) * size:ahead * size], 'gx', across(ahead))]
    dot_general x2 -> x0, matrix products: 60.3 us -> none  [the longest x1 58.6 us: local(): jnp.dot(gathered, weight, preferred_element_type=jnp.float32)]
    gather x17 -> x0, local copies, waits for them, and re-layouts: 55.4 us -> none  [the longest x9 28.7 us: tree_depth(): depth = depth + depth[pointer]]
    ppermute x0 -> x25, starting transfers between devices: none -> 24.8 us  [the longest x6 10.9 us: swap(): return lax.ppermute(array, 'gy', [(k, k ^ distance) for k in range(n_gy)])]
    convert_element_type x2 -> x0, other arithmetic: 5.93 us -> none  [the longest x1 5.1 us: local(): return jax.nn.gelu(summed, approximate=True).astype(jnp.bfloat16)]
  transfers between devices with their start and end apart: 2 -> 25, of which waited for: 2 -> 11; matrix products, arithmetic and copies ran while one was open for 0% -> 0% of each run, Pallas kernels for 0% -> 52%
where the time goes in v2:
time: 201 us
  Pallas kernels  107 us (53%)
  waiting for transfers between devices  67.1 us (33%)
  starting transfers between devices  24.8 us (12%)
  local copies, waits for them, and re-layouts  2.33 us (1%)
    pallas_call x8, Pallas kernels, product(): pl.pallas_call(functools.partial(product_kernel, start, tile, width // ti...  78.4 us
    ppermute x8, waiting for transfers between devices, exchange(): lax.ppermute(away[(ahead - 1) * size:ahead * size], 'gx', across(ahead))  29.7 us
    ppermute x6, waiting for transfers between devices, swap(): return lax.ppermute(array, 'gy', [(k, k ^ distance) for k in range(n_gy)])  26 us
    ppermute x3, waiting for transfers between devices, pass_on(): rest[index] = lax.ppermute(given, 'gy', [(0, 2), (1, 0), (2, 3), (3, 1)])  11.4 us
    pallas_call x8, Pallas kernels, finish(): pl.pallas_call(functools.partial(finish_kernel, len(terms)), name='finish...  11 us
    ppermute x6, starting transfers between devices, swap(): return lax.ppermute(array, 'gy', [(k, k ^ distance) for k in range(n_gy)])  10.9 us
    ppermute x8, starting transfers between devices, exchange(): lax.ppermute(away[(ahead - 1) * size:ahead * size], 'gx', across(ahead))  9.56 us
    pallas_call x3, Pallas kernels, embed(): pl.pallas_call(functools.partial(embed_kernel, count, chips, block, first...  7.86 us
  transfers between devices with their start and end apart: 25, of which 11 were waited for; matrix products, arithmetic and copies ran while one was open for 0% of the time, Pallas kernels for 52%

profile of v2, /device:TPU:0, one launch (start us, length us, event | category | flops | bytes accessed | tf_op | source)
XLA Modules:
  0.0 201.3 jit_solution(12886815466124238522)
XLA Ops:
  0.0 2.2 %fusion = (bf16[64,3584]{1,0:T(8,128)(2,1)S(1)}, bf16[64,3584]{1,0:T(8,128)(2,1)}, bf16[64,3584]{1,0:T(8,128)(2,1)S(1)}) fusion(bf16[192,3584]{1,0:T(8,128)(2,1)} %param.4), kind=kLoop, calls=%fused_computation.1 | loop fusion | bytes 2752512 | tf_op jit(solution)/shard_map/slice | solution.py:234
  2.2 3.0 %collective-permute-start = (bf16[64,3584]{1,0:T(8,128)(2,1)S(1)}, bf16[64,3584]{1,0:T(8,128)(2,1)S(1)}, u32[]{:S(2)}, u32[]{:S(2)}) collective-permute-start(bf16[64,3584]{1,0:T(8,128)(2,1)S(1)} %get-tuple-element.103.refs_0_), channel_id=1, source_target_pairs={{0,1},{1,0},{2,3},{3,2},{4,5},{5,4},{6,7},{7,6},{8,9},{9,8},{10,11... | collective-permute-start | bytes 1376264 | tf_op jit(solution)/shard_map/ppermute | solution.py:243
  5.2 2.6 %collective-permute-start.1 = (bf16[64,3584]{1,0:T(8,128)(2,1)S(1)}, bf16[64,3584]{1,0:T(8,128)(2,1)S(1)}, u32[]{:S(2)}, u32[]{:S(2)}) collective-permute-start(bf16[64,3584]{1,0:T(8,128)(2,1)S(1)} %get-tuple-element.103.refs_0_), channel_id=1, source_target_pairs={{0,2},{1,3},{2,0},{3,1},{4,6},{5,7},{6,4},{7,5},{8,10},{9,11},{10,... | collective-permute-start | bytes 1376264 | tf_op jit(solution)/shard_map/ppermute | solution.py:243
  8.5 17.8 %collective-permute-done.near_ref.refs_1_ = bf16[64,3584]{1,0:T(8,128)(2,1)S(1)} collective-permute-done((bf16[64,3584]{1,0:T(8,128)(2,1)S(1)}, bf16[64,3584]{1,0:T(8,128)(2,1)S(1)}, u32[]{:S(2)}, u32[]{:S(2)}) %collective-permute-start) | collective-permute-done | bytes 458784 | tf_op jit(solution)/shard_map/ppermute | solution.py:243
  27.6 2.5 %collective-permute-start.2 = (bf16[64,3584]{1,0:T(8,128)(2,1)S(1)}, bf16[64,3584]{1,0:T(8,128)(2,1)S(1)}, u32[]{:S(2)}, u32[]{:S(2)}) collective-permute-start(bf16[64,3584]{1,0:T(8,128)(2,1)S(1)} %forward.3), channel_id=1, source_target_pairs={{0,2},{1,0},{2,3},{3,1},{4,6},{5,4},{6,7},{7,5},{8,10},{9,8},{10,1... | collective-permute-start | bytes 1376264 | tf_op jit(solution)/shard_map/ppermute | solution.py:255
  30.0 4.3 %onehot.1.onehot_ref = bf16[768,256]{1,0:T(8,128)(2,1)S(1)} custom-call(s32[768,1]{1,0:T(8,128)S(1)} %broadcast_in_dim.4.parents_ref), custom_call_target="tpu_custom_call" | custom-call | flops 19327352832 | bytes 12582912 | tf_op jit(solution)/shard_map/onehot/pallas_call | solution.py:48
  34.3 1.8 collective-permute-start.4
  36.1 11.4 %collective-permute-done.2.refs_3_ = bf16[64,3584]{1,0:T(8,128)(2,1)S(1)} collective-permute-done((bf16[64,3584]{1,0:T(8,128)(2,1)S(1)}, bf16[64,3584]{1,0:T(8,128)(2,1)S(1)}, u32[]{:S(2)}, u32[]{:S(2)}) %collective-permute-start.2) | collective-permute-done | bytes 458784 | tf_op jit(solution)/shard_map/ppermute | solution.py:255
  47.5 2.6 %embed.3.rows_ref = bf16[256,3584]{1,0:T(8,128)(2,1)S(1)} custom-call(s32[2]{0:T(128)S(1)} %pad_add_fusion.place_ref, bf16[768,256]{1,0:T(8,128)(2,1)S(1)} %onehot.1.onehot_ref, bf16[256,3584]{1,0:T(8,128)(2,1)S(1)} %copy-done.1, bf16[64,3584]{1,0:T(8,128)(2,1)S(1)} %get-tuple-element.103.refs_0_, ...), custom_call_target="tpu_custom_call" | custom-call | flops 3758096384 | bytes 44040192 | tf_op jit(solution)/shard_map/embed/pallas_call | solution.py:101
  50.1 12.4 %product.8 = (bf16[128,4608]{1,0:T(8,128)(2,1)S(1)}, bf16[128,4608]{1,0:T(8,128)(2,1)S(1)}) custom-call(bf16[256,3584]{1,0:T(8,128)(2,1)S(1)} %embed.3.rows_ref, bf16[3584,9216]{1,0:T(8,128)(2,1)} %weight_ref.15), custom_call_target="tpu_custom_call" | custom-call | flops 67645734912 | bytes 297795584 | tf_op jit(solution)/shard_map/product/pallas_call | solution.py:144
  62.5 2.4 %collective-permute-done.4.far_ref.refs_2_ = bf16[64,3584]{1,0:T(8,128)(2,1)S(1)} collective-permute-done((bf16[64,3584]{1,0:T(8,128)(2,1)S(1)}, bf16[64,3584]{1,0:T(8,128)(2,1)S(1)}, u32[]{:S(2)}, u32[]{:S(2)}) %collective-permute-start.4) | collective-permute-done | bytes 458784 | tf_op jit(solution)/shard_map/ppermute | solution.py:243
  65.7 12.4 %product.9 = (bf16[128,4608]{1,0:T(8,128)(2,1)S(1)}, bf16[128,4608]{1,0:T(8,128)(2,1)S(1)}) custom-call(bf16[256,3584]{1,0:T(8,128)(2,1)S(1)} %embed.3.rows_ref, bf16[3584,9216]{1,0:T(8,128)(2,1)} %weight_ref.15, bf16[64,3584]{1,0:T(8,128)(2,1)S(1)} %forward.4.refs_0_), custom_call_target="tpu_custom_call" | custom-call | flops 67645734912 | bytes 297795584 | tf_op jit(solution)/shard_map/product/pallas_call | solution.py:144
  78.1 2.0 collective-permute-start.5
  81.3 2.6 %embed.4.rows_ref = bf16[256,3584]{1,0:T(8,128)(2,1)S(1)} custom-call(s32[2]{0:T(128)S(1)} %pad_add_fusion.place_ref, bf16[768,256]{1,0:T(8,128)(2,1)S(1)} %onehot.1.onehot_ref, bf16[256,3584]{1,0:T(8,128)(2,1)S(1)} %copy-done.1, bf16[64,3584]{1,0:T(8,128)(2,1)S(1)} %get-tuple-element.53.refs_0_, ...), custom_call_target="tpu_custom_call" | custom-call | flops 3758096384 | bytes 44040192 | tf_op jit(solution)/shard_map/embed/pallas_call | solution.py:101
  86.1 12.3 %product.10 = (bf16[128,4608]{1,0:T(8,128)(2,1)S(1)}, bf16[128,4608]{1,0:T(8,128)(2,1)S(1)}) custom-call(bf16[256,3584]{1,0:T(8,128)(2,1)S(1)} %embed.4.rows_ref, bf16[3584,9216]{1,0:T(8,128)(2,1)} %weight_ref.15, bf16[64,4608]{1,0:T(8,128)(2,1)S(1)} %get-tuple-element.58.refs_0_), custom_call_target="tpu_custom_call" | custom-call | flops 67645734912 | bytes 297795584 | tf_op jit(solution)/shard_map/product/pallas_call | solution.py:144
  98.5 2.4 %collective-permute-done.5.near_ref.refs_1_ = bf16[64,3584]{1,0:T(8,128)(2,1)S(1)} collective-permute-done((bf16[64,3584]{1,0:T(8,128)(2,1)S(1)}, bf16[64,3584]{1,0:T(8,128)(2,1)S(1)}, u32[]{:S(2)}, u32[]{:S(2)}) %collective-permute-start.5) | collective-permute-done | bytes 458784 | tf_op jit(solution)/shard_map/ppermute | solution.py:243
  100.9 2.6 %collective-permute-done.6.far_ref.refs_2_ = bf16[64,3584]{1,0:T(8,128)(2,1)S(1)} collective-permute-done((bf16[64,3584]{1,0:T(8,128)(2,1)S(1)}, bf16[64,3584]{1,0:T(8,128)(2,1)S(1)}, u32[]{:S(2)}, u32[]{:S(2)}) %collective-permute-start.6) | collective-permute-done | bytes 458784 | tf_op jit(solution)/shard_map/ppermute | solution.py:243
  106.8 1.8 finish.8
  108.6 12.4 %product.11 = (bf16[128,4608]{1,0:T(8,128)(2,1)S(1)}, bf16[128,4608]{1,0:T(8,128)(2,1)S(1)}) custom-call(bf16[256,3584]{1,0:T(8,128)(2,1)S(1)} %embed.4.rows_ref, bf16[3584,9216]{1,0:T(8,128)(2,1)} %weight_ref.15, bf16[64,3584]{1,0:T(8,128)(2,1)S(1)} %forward.5.refs_0_, bf16[64,4608]{1,0:T(8,128)(2,1)S(1)} %get-tuple-element.61.refs_1_.refs_0_, ...), custom_call_target="tpu_custom_call" | custom-call | flops 67645734912 | bytes 297795584 | tf_op jit(solution)/shard_map/product/pallas_call | solution.py:144
  121.3 1.8 finish.9
  123.1 2.6 %embed.5.rows_ref = bf16[256,3584]{1,0:T(8,128)(2,1)S(1)} custom-call(s32[2]{0:T(128)S(1)} %pad_add_fusion.place_ref, bf16[768,256]{1,0:T(8,128)(2,1)S(1)} %onehot.1.onehot_ref, bf16[256,3584]{1,0:T(8,128)(2,1)S(1)} %copy-done.1, bf16[64,3584]{1,0:T(8,128)(2,1)S(1)} %copy-done, bf16[64,3584]{1,0:T(8,128)(2,1)S(1)} %collective-permute-done.5.near_ref.refs_1_, ...), custom_call_target="tpu_custom_call" | custom-call | flops 3758096384 | bytes 44040192 | tf_op jit(solution)/shard_map/embed/pallas_call | solution.py:101
  127.6 5.5 %product.12 = (bf16[128,1536]{1,0:T(8,128)(2,1)S(1)}, bf16[128,1536]{1,0:T(8,128)(2,1)S(1)}) custom-call(bf16[256,3584]{1,0:T(8,128)(2,1)S(1)} %embed.5.rows_ref, bf16[3584,9216]{1,0:T(8,128)(2,1)} %weight_ref.15, bf16[64,4608]{1,0:T(8,128)(2,1)S(1)} %get-tuple-element.67.refs_0_, f32[8,128]{1,0:T(8,128)S(1)} %get-tuple-element.70.refs_1_), custom_call_target="tpu_custom_call" | custom-call | flops 22548578304 | bytes 109051904 | tf_op jit(solution)/shard_map/product/pallas_call | solution.py:144
  134.7 7.9 %collective-permute-done.15.refs_1_ = bf16[64,4608]{1,0:T(8,128)(2,1)S(1)} collective-permute-done((bf16[64,4608]{1,0:T(8,128)(2,1)S(1)}, bf16[64,4608]{1,0:T(8,128)(2,1)S(1)}, u32[]{:S(2)}, u32[]{:S(2)}) %collective-permute-start.15) | collective-permute-done | bytes 589856 | tf_op jit(solution)/shard_map/ppermute | solution.py:267
  142.6 1.8 finish.10
  144.3 5.5 %product.13 = (bf16[128,1536]{1,0:T(8,128)(2,1)S(1)}, bf16[128,1536]{1,0:T(8,128)(2,1)S(1)}) custom-call(bf16[256,3584]{1,0:T(8,128)(2,1)S(1)} %embed.5.rows_ref, bf16[3584,9216]{1,0:T(8,128)(2,1)} %weight_ref.15, bf16[64,4608]{1,0:T(8,128)(2,1)S(1)} %get-tuple-element.72.refs_0_, f32[8,128]{1,0:T(8,128)S(1)} %get-tuple-element.75.refs_1_), custom_call_target="tpu_custom_call" | custom-call | flops 22548578304 | bytes 109051904 | tf_op jit(solution)/shard_map/product/pallas_call | solution.py:144
  151.4 3.8 %collective-permute-done.18.refs_1_ = bf16[64,4608]{1,0:T(8,128)(2,1)S(1)} collective-permute-done((bf16[64,4608]{1,0:T(8,128)(2,1)S(1)}, bf16[64,4608]{1,0:T(8,128)(2,1)S(1)}, u32[]{:S(2)}, u32[]{:S(2)}) %collective-permute-start.18) | collective-permute-done | bytes 589856 | tf_op jit(solution)/shard_map/ppermute | solution.py:267
  155.2 1.8 finish.11
  157.0 8.9 %product.14 = (bf16[128,3072]{1,0:T(8,128)(2,1)S(1)}, bf16[128,3072]{1,0:T(8,128)(2,1)S(1)}) custom-call(bf16[256,3584]{1,0:T(8,128)(2,1)S(1)} %embed.5.rows_ref, bf16[3584,9216]{1,0:T(8,128)(2,1)} %weight_ref.15, bf16[64,1536]{1,0:T(8,128)(2,1)S(1)} %get-tuple-element.79.refs_0_, f32[8,128]{1,0:T(8,128)S(1)} %get-tuple-element.82.refs_1_), custom_call_target="tpu_custom_call" | custom-call | flops 45097156608 | bytes 203423744 | tf_op jit(solution)/shard_map/product/pallas_call | solution.py:144
  166.9 8.9 %product.15 = (bf16[128,3072]{1,0:T(8,128)(2,1)S(1)}, bf16[128,3072]{1,0:T(8,128)(2,1)S(1)}) custom-call(bf16[256,3584]{1,0:T(8,128)(2,1)S(1)} %embed.5.rows_ref, bf16[3584,9216]{1,0:T(8,128)(2,1)} %weight_ref.15, bf16[64,1536]{1,0:T(8,128)(2,1)S(1)} %get-tuple-element.84.refs_0_, f32[8,128]{1,0:T(8,128)S(1)} %get-tuple-element.87.refs_1_), custom_call_target="tpu_custom_call" | custom-call | flops 45097156608 | bytes 203423744 | tf_op jit(solution)/shard_map/product/pallas_call | solution.py:144
  178.9 5.3 %collective-permute-done.21.refs_1_ = bf16[64,1536]{1,0:T(8,128)(2,1)S(1)} collective-permute-done((bf16[64,1536]{1,0:T(8,128)(2,1)S(1)}, bf16[64,1536]{1,0:T(8,128)(2,1)S(1)}, u32[]{:S(2)}, u32[]{:S(2)}) %collective-permute-start.21) | collective-permute-done | bytes 196640 | tf_op jit(solution)/shard_map/ppermute | solution.py:267
  186.2 6.4 %collective-permute-done.24.refs_1_ = bf16[64,3072]{1,0:T(8,128)(2,1)S(1)} collective-permute-done((bf16[64,3072]{1,0:T(8,128)(2,1)S(1)}, bf16[64,3072]{1,0:T(8,128)(2,1)S(1)}, u32[]{:S(2)}, u32[]{:S(2)}) %collective-permute-start.24) | collective-permute-done | bytes 393248 | tf_op jit(solution)/shard_map/ppermute | solution.py:267
  193.7 6.4 %collective-permute-done.22.refs_1_ = bf16[64,3072]{1,0:T(8,128)(2,1)S(1)} collective-permute-done((bf16[64,3072]{1,0:T(8,128)(2,1)S(1)}, bf16[64,3072]{1,0:T(8,128)(2,1)S(1)}, u32[]{:S(2)}, u32[]{:S(2)}) %collective-permute-start.22) | collective-permute-done | bytes 393248 | tf_op jit(solution)/shard_map/ppermute | solution.py:267
  (58 shorter events, 23.0 us)
Async XLA Ops:
  0.0 8.2 %copy-start.2 = (s32[768]{0:T(1024)S(1)}, s32[768]{0:T(1024)}, u32[]{:S(2)}) copy-start(s32[768]{0:T(1024)} %param.5) | copy-start | bytes 9220
  2.2 24.1 %collective-permute-start = (bf16[64,3584]{1,0:T(8,128)(2,1)S(1)}, bf16[64,3584]{1,0:T(8,128)(2,1)S(1)}, u32[]{:S(2)}, u32[]{:S(2)}) collective-permute-start(bf16[64,3584]{1,0:T(8,128)(2,1)S(1)} %get-tuple-element.103.refs_0_), channel_id=1, source_target_pairs={{0,1},{1,0},{2,3},{3,2},{4,5},{5,4},{6,7},{7,6},{8,9},{9,8},{10,11... | collective-permute-start | bytes 1376264 | tf_op jit(solution)/shard_map/ppermute | solution.py:243
  5.2 21.8 %collective-permute-start.1 = (bf16[64,3584]{1,0:T(8,128)(2,1)S(1)}, bf16[64,3584]{1,0:T(8,128)(2,1)S(1)}, u32[]{:S(2)}, u32[]{:S(2)}) collective-permute-start(bf16[64,3584]{1,0:T(8,128)(2,1)S(1)} %get-tuple-element.103.refs_0_), channel_id=1, source_target_pairs={{0,2},{1,3},{2,0},{3,1},{4,6},{5,7},{6,4},{7,5},{8,10},{9,11},{10,... | collective-permute-start | bytes 1376264 | tf_op jit(solution)/shard_map/ppermute | solution.py:243
  7.8 54.7 %collective-permute-start.3 = (bf16[64,3584]{1,0:T(8,128)(2,1)S(1)}, bf16[64,3584]{1,0:T(8,128)(2,1)S(1)}, u32[]{:S(2)}, u32[]{:S(2)}) collective-permute-start(bf16[64,3584]{1,0:T(8,128)(2,1)S(1)} %get-tuple-element.53.refs_0_), channel_id=1, source_target_pairs={{0,1},{1,0},{2,3},{3,2},{4,5},{5,4},{6,7},{7,6},{8,9},{9,8},{10,11... | collective-permute-start | bytes 1376264 | tf_op jit(solution)/shard_map/ppermute | solution.py:243
  27.5 19.9 %copy-start.1 = (bf16[256,3584]{1,0:T(8,128)(2,1)S(1)}, bf16[256,3584]{1,0:T(8,128)(2,1)}, u32[]{:S(2)}) copy-start(bf16[256,3584]{1,0:T(8,128)(2,1)} %table_ref.5) | copy-start | bytes 5505028
  27.6 19.9 %collective-permute-start.2 = (bf16[64,3584]{1,0:T(8,128)(2,1)S(1)}, bf16[64,3584]{1,0:T(8,128)(2,1)S(1)}, u32[]{:S(2)}, u32[]{:S(2)}) collective-permute-start(bf16[64,3584]{1,0:T(8,128)(2,1)S(1)} %forward.3), channel_id=1, source_target_pairs={{0,2},{1,0},{2,3},{3,1},{4,6},{5,4},{6,7},{7,5},{8,10},{9,8},{10,1... | collective-permute-start | bytes 1376264 | tf_op jit(solution)/shard_map/ppermute | solution.py:255
  34.3 30.6 %collective-permute-start.4 = (bf16[64,3584]{1,0:T(8,128)(2,1)S(1)}, bf16[64,3584]{1,0:T(8,128)(2,1)S(1)}, u32[]{:S(2)}, u32[]{:S(2)}) collective-permute-start(bf16[64,3584]{1,0:T(8,128)(2,1)S(1)} %get-tuple-element.53.refs_0_), channel_id=1, source_target_pairs={{0,2},{1,3},{2,0},{3,1},{4,6},{5,7},{6,4},{7,5},{8,10},{9,11},{10,... | collective-permute-start | bytes 1376264 | tf_op jit(solution)/shard_map/ppermute | solution.py:243
  65.5 15.8 %collective-permute-start.7 = (bf16[64,3584]{1,0:T(8,128)(2,1)S(1)}, bf16[64,3584]{1,0:T(8,128)(2,1)S(1)}, u32[]{:S(2)}, u32[]{:S(2)}) collective-permute-start(bf16[64,3584]{1,0:T(8,128)(2,1)S(1)} %forward.4.refs_0_), channel_id=1, source_target_pairs={{0,2},{1,0},{2,3},{3,1},{4,6},{5,4},{6,7},{7,5},{8,10},{9,8},{10,1... | collective-permute-start | bytes 1376264 | tf_op jit(solution)/shard_map/ppermute | solution.py:255
  65.6 12.5 %copy-start = (bf16[64,3584]{1,0:T(8,128)(2,1)S(1)}, bf16[64,3584]{1,0:T(8,128)(2,1)}, u32[]{:S(2)}) copy-start(bf16[64,3584]{1,0:T(8,128)(2,1)} %get-tuple-element.56.refs_0_) | copy-start | bytes 1376260
  65.6 18.4 %collective-permute-start.8 = (bf16[128,4608]{1,0:T(8,128)(2,1)S(1)}, bf16[128,4608]{1,0:T(8,128)(2,1)S(1)}, u32[]{:S(2)}, u32[]{:S(2)}) collective-permute-start(bf16[128,4608]{1,0:T(8,128)(2,1)S(1)} %get-tuple-element.57), channel_id=1, source_target_pairs={{0,4},{4,0},{8,12},{12,8},{1,5},{5,1},{9,13},{13,9},{2,6},{6,2},{1... | collective-permute-start | bytes 3538952 | tf_op jit(solution)/shard_map/ppermute | solution.py:297
  78.1 22.8 %collective-permute-start.5 = (bf16[64,3584]{1,0:T(8,128)(2,1)S(1)}, bf16[64,3584]{1,0:T(8,128)(2,1)S(1)}, u32[]{:S(2)}, u32[]{:S(2)}) collective-permute-start(bf16[64,3584]{1,0:T(8,128)(2,1)S(1)} %copy-done), channel_id=1, source_target_pairs={{0,1},{1,0},{2,3},{3,2},{4,5},{5,4},{6,7},{7,6},{8,9},{9,8},{10,11... | collective-permute-start | bytes 1376264 | tf_op jit(solution)/shard_map/ppermute | solution.py:243
  80.1 23.4 %collective-permute-start.6 = (bf16[64,3584]{1,0:T(8,128)(2,1)S(1)}, bf16[64,3584]{1,0:T(8,128)(2,1)S(1)}, u32[]{:S(2)}, u32[]{:S(2)}) collective-permute-start(bf16[64,3584]{1,0:T(8,128)(2,1)S(1)} %copy-done), channel_id=1, source_target_pairs={{0,2},{1,3},{2,0},{3,1},{4,6},{5,7},{6,4},{7,5},{8,10},{9,11},{10,... | collective-permute-start | bytes 1376264 | tf_op jit(solution)/shard_map/ppermute | solution.py:243
  81.2 23.5 %collective-permute-start.10 = (bf16[128,4608]{1,0:T(8,128)(2,1)S(1)}, bf16[128,4608]{1,0:T(8,128)(2,1)S(1)}, u32[]{:S(2)}, u32[]{:S(2)}) collective-permute-start(bf16[128,4608]{1,0:T(8,128)(2,1)S(1)} %get-tuple-element.60), channel_id=1, source_target_pairs={{0,4},{4,0},{8,12},{12,8},{1,5},{5,1},{9,13},{13,9},{2,6},{6,2},{1... | collective-permute-start | bytes 3538952 | tf_op jit(solution)/shard_map/ppermute | solution.py:297
  84.6 22.2 %collective-permute-start.11 = (bf16[64,4608]{1,0:T(8,128)(2,1)S(1)}, bf16[64,4608]{1,0:T(8,128)(2,1)S(1)}, u32[]{:S(2)}, u32[]{:S(2)}) collective-permute-start(bf16[64,4608]{1,0:T(8,128)(2,1)S(1)} %get-tuple-element.62), channel_id=1, source_target_pairs={{0,8},{4,12},{8,0},{12,4},{1,9},{5,13},{9,1},{13,5},{2,10},{6,14},... | collective-permute-start | bytes 1769480 | tf_op jit(solution)/shard_map/ppermute | solution.py:267
  104.1 19.0 %collective-permute-start.9 = (bf16[64,3584]{1,0:T(8,128)(2,1)S(1)}, bf16[64,3584]{1,0:T(8,128)(2,1)S(1)}, u32[]{:S(2)}, u32[]{:S(2)}) collective-permute-start(bf16[64,3584]{1,0:T(8,128)(2,1)S(1)} %forward.5.refs_0_), channel_id=1, source_target_pairs={{0,2},{1,0},{2,3},{3,1},{4,6},{5,4},{6,7},{7,5},{8,10},{9,8},{10,1... | collective-permute-start | bytes 1376264 | tf_op jit(solution)/shard_map/ppermute | solution.py:255
  104.7 21.0 %collective-permute-start.13 = (bf16[128,4608]{1,0:T(8,128)(2,1)S(1)}, bf16[128,4608]{1,0:T(8,128)(2,1)S(1)}, u32[]{:S(2)}, u32[]{:S(2)}) collective-permute-start(bf16[128,4608]{1,0:T(8,128)(2,1)S(1)} %get-tuple-element.66), channel_id=1, source_target_pairs={{0,4},{4,0},{8,12},{12,8},{1,5},{5,1},{9,13},{13,9},{2,6},{6,2},{1... | collective-permute-start | bytes 3538952 | tf_op jit(solution)/shard_map/ppermute | solution.py:297
  105.3 16.0 %collective-permute-start.14 = (bf16[64,4608]{1,0:T(8,128)(2,1)S(1)}, bf16[64,4608]{1,0:T(8,128)(2,1)S(1)}, u32[]{:S(2)}, u32[]{:S(2)}) collective-permute-start(bf16[64,4608]{1,0:T(8,128)(2,1)S(1)} %get-tuple-element.68), channel_id=1, source_target_pairs={{0,8},{4,12},{8,0},{12,4},{1,9},{5,13},{9,1},{13,5},{2,10},{6,14},... | collective-permute-start | bytes 1769480 | tf_op jit(solution)/shard_map/ppermute | solution.py:267
  121.0 12.2 %collective-permute-start.12 = (bf16[128,4608]{1,0:T(8,128)(2,1)S(1)}, bf16[128,4608]{1,0:T(8,128)(2,1)S(1)}, u32[]{:S(2)}, u32[]{:S(2)}) collective-permute-start(bf16[128,4608]{1,0:T(8,128)(2,1)S(1)} %get-tuple-element.65), channel_id=1, source_target_pairs={{0,4},{4,0},{8,12},{12,8},{1,5},{5,1},{9,13},{13,9},{2,6},{6,2},{1... | collective-permute-start | bytes 3538952 | tf_op jit(solution)/shard_map/ppermute | solution.py:297
  126.3 16.2 %collective-permute-start.15 = (bf16[64,4608]{1,0:T(8,128)(2,1)S(1)}, bf16[64,4608]{1,0:T(8,128)(2,1)S(1)}, u32[]{:S(2)}, u32[]{:S(2)}) collective-permute-start(bf16[64,4608]{1,0:T(8,128)(2,1)S(1)} %get-tuple-element.73), channel_id=1, source_target_pairs={{0,8},{4,12},{8,0},{12,4},{1,9},{5,13},{9,1},{13,5},{2,10},{6,14},... | collective-permute-start | bytes 1769480 | tf_op jit(solution)/shard_map/ppermute | solution.py:267
  133.1 16.8 %collective-permute-start.17 = (bf16[128,1536]{1,0:T(8,128)(2,1)S(1)}, bf16[128,1536]{1,0:T(8,128)(2,1)S(1)}, u32[]{:S(2)}, u32[]{:S(2)}) collective-permute-start(bf16[128,1536]{1,0:T(8,128)(2,1)S(1)} %get-tuple-element.78), channel_id=1, source_target_pairs={{0,4},{4,0},{8,12},{12,8},{1,5},{5,1},{9,13},{13,9},{2,6},{6,2},{1... | collective-permute-start | bytes 1179656 | tf_op jit(solution)/shard_map/ppermute | solution.py:297
  133.8 21.4 %collective-permute-start.18 = (bf16[64,4608]{1,0:T(8,128)(2,1)S(1)}, bf16[64,4608]{1,0:T(8,128)(2,1)S(1)}, u32[]{:S(2)}, u32[]{:S(2)}) collective-permute-start(bf16[64,4608]{1,0:T(8,128)(2,1)S(1)} %get-tuple-element.80), channel_id=1, source_target_pairs={{0,8},{4,12},{8,0},{12,4},{1,9},{5,13},{9,1},{13,5},{2,10},{6,14},... | collective-permute-start | bytes 1769480 | tf_op jit(solution)/shard_map/ppermute | solution.py:267
  149.8 16.1 %collective-permute-start.16 = (bf16[128,1536]{1,0:T(8,128)(2,1)S(1)}, bf16[128,1536]{1,0:T(8,128)(2,1)S(1)}, u32[]{:S(2)}, u32[]{:S(2)}) collective-permute-start(bf16[128,1536]{1,0:T(8,128)(2,1)S(1)} %get-tuple-element.77), channel_id=1, source_target_pairs={{0,4},{4,0},{8,12},{12,8},{1,5},{5,1},{9,13},{13,9},{2,6},{6,2},{1... | collective-permute-start | bytes 1179656 | tf_op jit(solution)/shard_map/ppermute | solution.py:297
  150.0 16.1 %collective-permute-start.19 = (bf16[64,1536]{1,0:T(8,128)(2,1)S(1)}, bf16[64,1536]{1,0:T(8,128)(2,1)S(1)}, u32[]{:S(2)}, u32[]{:S(2)}) collective-permute-start(bf16[64,1536]{1,0:T(8,128)(2,1)S(1)} %get-tuple-element.85), channel_id=1, source_target_pairs={{0,8},{4,12},{8,0},{12,4},{1,9},{5,13},{9,1},{13,5},{2,10},{6,14},... | collective-permute-start | bytes 589832 | tf_op jit(solution)/shard_map/ppermute | solution.py:267
  165.9 11.3 %collective-permute-start.23 = (bf16[128,3072]{1,0:T(8,128)(2,1)S(1)}, bf16[128,3072]{1,0:T(8,128)(2,1)S(1)}, u32[]{:S(2)}, u32[]{:S(2)}) collective-permute-start(bf16[128,3072]{1,0:T(8,128)(2,1)S(1)} %get-tuple-element.95), channel_id=1, source_target_pairs={{0,4},{4,0},{8,12},{12,8},{1,5},{5,1},{9,13},{13,9},{2,6},{6,2},{1... | collective-permute-start | bytes 2359304 | tf_op jit(solution)/shard_map/ppermute | solution.py:297
  175.8 9.2 %collective-permute-start.20 = (bf16[128,3072]{1,0:T(8,128)(2,1)S(1)}, bf16[128,3072]{1,0:T(8,128)(2,1)S(1)}, u32[]{:S(2)}, u32[]{:S(2)}) collective-permute-start(bf16[128,3072]{1,0:T(8,128)(2,1)S(1)} %get-tuple-element.89), channel_id=1, source_target_pairs={{0,4},{4,0},{8,12},{12,8},{1,5},{5,1},{9,13},{13,9},{2,6},{6,2},{1... | collective-permute-start | bytes 2359304 | tf_op jit(solution)/shard_map/ppermute | solution.py:297
  176.4 7.8 %collective-permute-start.21 = (bf16[64,1536]{1,0:T(8,128)(2,1)S(1)}, bf16[64,1536]{1,0:T(8,128)(2,1)S(1)}, u32[]{:S(2)}, u32[]{:S(2)}) collective-permute-start(bf16[64,1536]{1,0:T(8,128)(2,1)S(1)} %get-tuple-element.90), channel_id=1, source_target_pairs={{0,8},{4,12},{8,0},{12,4},{1,9},{5,13},{9,1},{13,5},{2,10},{6,14},... | collective-permute-start | bytes 589832 | tf_op jit(solution)/shard_map/ppermute | solution.py:267
  177.5 15.0 %collective-permute-start.24 = (bf16[64,3072]{1,0:T(8,128)(2,1)S(1)}, bf16[64,3072]{1,0:T(8,128)(2,1)S(1)}, u32[]{:S(2)}, u32[]{:S(2)}) collective-permute-start(bf16[64,3072]{1,0:T(8,128)(2,1)S(1)} %get-tuple-element.97), channel_id=1, source_target_pairs={{0,8},{4,12},{8,0},{12,4},{1,9},{5,13},{9,1},{13,5},{2,10},{6,14},... | collective-permute-start | bytes 1179656 | tf_op jit(solution)/shard_map/ppermute | solution.py:267
  185.4 14.7 %collective-permute-start.22 = (bf16[64,3072]{1,0:T(8,128)(2,1)S(1)}, bf16[64,3072]{1,0:T(8,128)(2,1)S(1)}, u32[]{:S(2)}, u32[]{:S(2)}) collective-permute-start(bf16[64,3072]{1,0:T(8,128)(2,1)S(1)} %get-tuple-element.94), channel_id=1, source_target_pairs={{0,8},{4,12},{8,0},{12,4},{1,9},{5,13},{9,1},{13,5},{2,10},{6,14},... | collective-permute-start | bytes 1179656 | tf_op jit(solution)/shard_map/ppermute | solution.py:267

commit v3 on v2

v3 whole, which is shorter than its diff:
```python
import functools

import jax
import jax.numpy as jnp
from jax import lax
from jax.experimental import pallas as pl
from jax.experimental.pallas import tpu as pltpu
from jax.sharding import PartitionSpec as P

BF16 = jnp.bfloat16
F32 = jnp.float32
MIB = 1024 * 1024
ANY = pl.BlockSpec(memory_space=pl.ANY)
VMEM = pl.BlockSpec(memory_space=pltpu.VMEM)
SMEM = pl.BlockSpec(memory_space=pltpu.SMEM)


def params(limit):
    return pltpu.CompilerParams(vmem_limit_bytes=limit * MIB)


def cost(flops, accessed):
    return pl.CostEstimate(flops=8 * flops, bytes_accessed=8 * accessed, transcendentals=0)


def divisor(extent, choices):
    for choice in choices:
        if extent % choice == 0:
            return choice
    return extent


def onehot_kernel(tree, parents_ref, onehot_ref):
    lanes = lax.broadcasted_iota(jnp.int32, (tree, tree), 1)
    rows = lax.broadcasted_iota(jnp.int32, (tree, 1), 0)
    firsts = range(0, onehot_ref.shape[0], tree)
    parents = [parents_ref[first:first + tree, :] - first for first in firsts]
    jumps = [(parent == lanes).astype(BF16) for parent in parents]
    depths = [jnp.broadcast_to((parent != rows).astype(F32), (tree, 128)) for parent in parents]
    for level in range((tree - 1).bit_length()):
        depths = [
            depth + jnp.dot(jump, depth.astype(BF16), preferred_element_type=F32)
            for depth, jump in zip(depths, jumps)
        ]
        jumps = [jnp.dot(jump, jump, preferred_element_type=F32).astype(BF16) for jump in jumps]
    for first, depth in zip(firsts, depths):
        onehot_ref[first:first + tree, :] = (depth[:, :1].astype(jnp.int32) == lanes).astype(BF16)


def depth_onehot(parents, tree):
    rows = parents.shape[0]
    return pl.pallas_call(
        functools.partial(onehot_kernel, tree),
        name="onehot",
        out_shape=jax.ShapeDtypeStruct((rows, tree), BF16),
        compiler_params=params(16),
        cost_estimate=cost(48 * rows * tree * tree, 8 * rows * tree),
    )(parents[:, None])


def forward_kernel(place_ref, near_ref, far_ref, *refs):
    out_ref = refs[-1]
    outer = jnp.logical_or(place_ref[1] == 0, place_ref[1] == 3)

    @pl.when(outer)
    def _():
        out_ref[...] = near_ref[...]

    @pl.when(jnp.logical_not(outer))
    def _():
        out_ref[...] = far_ref[...]


def forward(place, near, far, after):
    return pl.pallas_call(
        forward_kernel,
        name="forward",
        out_shape=jax.ShapeDtypeStruct(near.shape, near.dtype),
        in_specs=[SMEM, VMEM, VMEM] + [ANY] * len(after),
        out_specs=VMEM,
        compiler_params=params(8),
        cost_estimate=cost(0, 6 * near.size),
    )(place, near, far, *after)


def slot_of(dest, chips, gx):
    ahead = lax.rem(dest // 2 - gx // 2 + 2 * chips - 1, chips)
    return jnp.where(lax.rem(gx, 2) == lax.rem(dest, 2), chips, 0) + ahead


def embed_kernel(count, chips, block, first, exclusive, place_ref, onehot_ref, table_ref, *refs):
    rows_ref = refs[-1]
    size = rows_ref.shape[0] // count
    for held in range(count):
        dest = lax.bitwise_xor(place_ref[1], held) if exclusive else held
        slot = slot_of(dest, chips, place_ref[0])
        here = pl.ds(pl.multiple_of(dest * block + first, 16), size)
        looked = jnp.dot(onehot_ref[here, :], table_ref[...], preferred_element_type=F32)
        total = refs[held][...].astype(F32) + looked
        rows_ref[pl.ds(pl.multiple_of(slot * size, 16), size), :] = total.astype(BF16)


def embed(chips, block, first, exclusive, place, onehot, table, held, after):
    count = len(held)
    size, depth = held[0].shape
    tile = divisor(depth, (896, 512, 256, 128))
    piece = pl.BlockSpec((size, tile), lambda j: (0, j))
    return pl.pallas_call(
        functools.partial(embed_kernel, count, chips, block, first, exclusive),
        name="embed",
        grid=(depth // tile,),
        out_shape=jax.ShapeDtypeStruct((count * size, depth), BF16),
        in_specs=[SMEM, pl.BlockSpec(onehot.shape, lambda j: (0, 0)), pl.BlockSpec((table.shape[0], tile), lambda j: (0, j))]
        + [piece] * count + [ANY] * len(after),
        out_specs=pl.BlockSpec((count * size, tile), lambda j: (0, j)),
        compiler_params=params(16),
        cost_estimate=cost(2 * count * size * table.shape[0] * depth, 6 * count * size * depth),
    )(place, onehot, table, *held, *after)


def embed_own_kernel(block, first, place_ref, onehot_ref, table_ref, hidden_ref, *refs):
    start = place_ref[1] * block
    for rows_ref in refs:
        size = rows_ref.shape[0]
        here = pl.ds(pl.multiple_of(start + first, 16), size)
        looked = jnp.dot(onehot_ref[here, :], table_ref[...], preferred_element_type=F32)
        rows_ref[...] = (hidden_ref[first:first + size, :].astype(F32) + looked).astype(BF16)
        first += size


def embed_own(first, size, count, place, onehot, table, hidden):
    block, depth = hidden.shape
    tile = divisor(depth, (896, 512, 256, 128))
    column = lambda j: (0, j)
    return pl.pallas_call(
        functools.partial(embed_own_kernel, block, first),
        name="own",
        grid=(depth // tile,),
        out_shape=[jax.ShapeDtypeStruct((size, depth), BF16)] * count,
        in_specs=[
            SMEM,
            pl.BlockSpec(onehot.shape, lambda j: (0, 0)),
            pl.BlockSpec((table.shape[0], tile), column),
            pl.BlockSpec((block, tile), column),
        ],
        out_specs=[pl.BlockSpec((size, tile), column)] * count,
        compiler_params=params(16),
        cost_estimate=cost(2 * count * size * table.shape[0] * depth, 6 * count * size * depth),
    )(place, onehot, table, hidden)


def gelu_sum(terms):
    total = terms[0].astype(F32)
    for term in terms[1:]:
        total = total + term.astype(F32)
    return jax.nn.gelu(total, approximate=True).astype(BF16)


def product_kernel(start, tile, steps, slots, chips, count, exclusive, ending, place_ref, weight_ref, *refs):
    blocks = refs[:count]
    terms = refs[count:count + ending[3]]
    outs = 2 if not ending[3] else 3
    scratch = len(refs) - (4 if not ending[3] else 8)
    send_ref, keep_ref = refs[scratch - outs:scratch - outs + 2]
    rows, held, arrived, filled = refs[scratch:scratch + 4]
    half = send_ref.shape[0]
    step = pl.program_id(0)

    def fetch(index):
        column = pl.multiple_of(start + index * tile, 128)
        slot = lax.rem(index, slots)
        return pltpu.make_async_copy(weight_ref.at[:, pl.ds(column, tile)], held.at[slot], arrived.at[slot])

    def fill(index):
        if count == 1:
            return pltpu.make_async_copy(blocks[0], rows, filled.at[0])
        size = rows.shape[0] // count
        dest = lax.bitwise_xor(place_ref[1], index) if exclusive else index
        first = pl.multiple_of(slot_of(dest, chips, place_ref[0]) * size, 16)
        return pltpu.make_async_copy(blocks[index], rows.at[pl.ds(first, size), :], filled.at[index])

    if ending[3]:
        out_ref = refs[scratch - 1]
        term_buffer, out_buffer, term_sems, out_sem = refs[scratch + 4:]
        row, column, width, number = ending
        given = [pltpu.make_async_copy(terms[n], term_buffer.at[n], term_sems.at[n]) for n in range(number)]
        place_out = out_ref.at[row:row + out_buffer.shape[0], column:column + width]
        taken = pltpu.make_async_copy(out_buffer, place_out, out_sem.at[0])

    @pl.when(step == 0)
    def _():
        fetch(0).start()
        for index in range(count):
            fill(index).start()
        for index in range(1, min(slots - 1, steps)):
            fetch(index).start()
        if ending[3]:
            for copy in given:
                copy.start()
        for index in range(count):
            fill(index).wait()

    @pl.when(step + slots - 1 < steps)
    def _():
        fetch(step + slots - 1).start()

    fetch(step).wait()
    out = jnp.dot(rows[...], held[lax.rem(step, slots)], preferred_element_type=F32)
    send_ref[...] = out[:half].astype(BF16)
    keep_ref[...] = out[half:].astype(BF16)

    if ending[3]:
        @pl.when(step == 0)
        def _():
            for copy in given:
                copy.wait()
            part = divisor(width, (512, 384, 256, 128))

            @pl.loop(0, width // part)
            def _(index):
                here = pl.ds(pl.multiple_of(index * part, 128), part)
                out_buffer[:, here] = gelu_sum([term_buffer[n, :, here] for n in range(number)])

            taken.start()

        @pl.when(step == steps - 1)
        def _():
            taken.wait()


def product(chips, exclusive, place, blocks, weight, start, width, after, ending=None, terms=(), out=None, shape=None):
    count = len(blocks)
    height, depth = count * blocks[0].shape[0], blocks[0].shape[1]
    tile = divisor(width, (512, 384, 256, 128))
    slots = 4
    half = jax.ShapeDtypeStruct((height // 2, width), BF16)
    outs = [half, half]
    out_specs = [pl.BlockSpec((height // 2, tile), lambda j: (0, j))] * 2
    scratch = [
        pltpu.VMEM((height, depth), BF16),
        pltpu.VMEM((slots, depth, tile), BF16),
        pltpu.SemaphoreType.DMA((slots,)),
        pltpu.SemaphoreType.DMA((count,)),
    ]
    operands = [place, weight, *blocks, *terms]
    aliases = {}
    ending = (0, 0, 0, 0) if not terms else (*ending, terms[0].shape[1], len(terms))
    if terms:
        outs.append(jax.ShapeDtypeStruct(shape, BF16))
        out_specs.append(ANY)
        scratch += [
            pltpu.VMEM((len(terms), *terms[0].shape), BF16),
            pltpu.VMEM(terms[0].shape, BF16),
            pltpu.SemaphoreType.DMA((len(terms),)),
            pltpu.SemaphoreType.DMA((1,)),
        ]
        if out is not None:
            aliases = {len(operands): 2}
            operands.append(out)
    operands += after
    return pl.pallas_call(
        functools.partial(product_kernel, start, tile, width // tile, slots, chips, count, exclusive, ending),
        name="product",
        grid=(width // tile,),
        out_shape=outs,
        in_specs=[SMEM] + [ANY] * (len(operands) - 1),
        out_specs=out_specs,
        scratch_shapes=scratch,
        input_output_aliases=aliases,
        compiler_params=params(40),
        cost_estimate=cost(2 * height * depth * width, 2 * (height * depth + depth * width + height * width)),
    )(*operands)


def pair_kernel(keep_ref, got_ref, *refs):
    away_ref, stay_ref = refs[-2:]
    cut = away_ref.shape[0]
    total = keep_ref[...].astype(F32) + got_ref[...].astype(F32)
    away_ref[...] = total[:cut].astype(BF16)
    stay_ref[...] = total[cut:].astype(BF16)


def pair(chips, keep, got, after):
    height, width = keep.shape
    size = height // chips
    tile = divisor(width, (1536, 1152, 768, 512, 384, 256, 128))
    spec = lambda rows: pl.BlockSpec((rows, tile), lambda j: (0, j))
    return pl.pallas_call(
        pair_kernel,
        name="pair",
        grid=(width // tile,),
        out_shape=[jax.ShapeDtypeStruct((height - size, width), BF16), jax.ShapeDtypeStruct((size, width), BF16)],
        in_specs=[spec(height), spec(height)] + [ANY] * len(after),
        out_specs=[spec(height - size), spec(size)],
        compiler_params=params(16),
        cost_estimate=cost(height * width, 6 * height * width),
    )(keep, got, *after)


def finish_kernel(count, *refs):
    out_ref, token_ref = refs[-2:]
    out_ref[...] = gelu_sum([refs[index][...] for index in range(count)])
    token_ref[...] = jnp.zeros_like(token_ref)


def finish(shape, step, rows, terms, held, after):
    index, start, width = step
    tile = divisor(width, (1536, 1152, 768, 512, 384, 256, 128))
    aliases = {} if held is None else {len(terms): 0}
    return pl.pallas_call(
        functools.partial(finish_kernel, len(terms)),
        name="finish",
        grid=(width // tile,),
        out_shape=[jax.ShapeDtypeStruct(shape, BF16), jax.ShapeDtypeStruct((8, 128), F32)],
        in_specs=[pl.BlockSpec((rows, tile), lambda j: (0, j))] * len(terms) + [ANY] * (len(aliases) + len(after)),
        out_specs=[
            pl.BlockSpec((rows, tile), lambda j: (index, start // tile + j)),
            pl.BlockSpec((8, 128), lambda j: (0, 0)),
        ],
        input_output_aliases=aliases,
        compiler_params=params(16),
        cost_estimate=cost(12 * rows * width, 6 * rows * width),
    )(*terms, *([] if held is None else [held]), *after)


def column_pieces(columns, shares):
    unit, start, pieces = columns // sum(shares), 0, []
    for share in shares:
        pieces.append((start, share * unit))
        start += share * unit
    return pieces


SHARES = ((3, 3), (3, 3), (2, 2, 2))

ORDER = "f0 p00 f1 p01 t2 s00 p10 s01 f2 p11-00 s10 p20-01 s11 p21-10 s20 p22-11 s21 g20 s22 g21 g22".split()


def local(n_gx, n_gy, hidden, parents, depth_table, weight):
    tree = depth_table.shape[0]
    columns = weight.shape[1]
    block = hidden.shape[0]
    chips = n_gx // 2
    parts = len(SHARES)
    size = block // parts
    place = jnp.stack([lax.axis_index("gx"), lax.axis_index("gy")]).astype(jnp.int32)

    exclusive = n_gy == 4

    def swap(array, distance):
        return lax.ppermute(array, "gy", [(k, k ^ distance) for k in range(n_gy)])

    def later(array, token):
        return lax.optimization_barrier((array, token))[0]

    def take(index, token):
        if not exclusive:
            whole = lax.all_gather(own[index], "gy", axis=0)
            held[index] = [whole[k] for k in range(n_gy)]
        else:
            rows = own[index] if token is None else later(own[index], token)
            held[index] = [own[index], swap(rows, 1), swap(rows, 2)]

    own, held = [hidden[:size]], [None] * parts
    take(0, None)
    onehot = depth_onehot(parents, tree)
    own += embed_own(size, size, parts - 1, place, onehot, depth_table, hidden)

    sibling = [(g, g ^ 1) for g in range(n_gx)]

    def across(ahead):
        return [(g, (g // 2 + ahead) % chips * 2 + g % 2) for g in range(n_gx)]

    out, after = None, own[1:2]
    pieces = [column_pieces(columns, shares) for shares in SHARES]
    products, sums = {}, {}
    for item in ORDER:
        kind, index, piece = item[0], int(item[1]), item[1:3]
        if kind == "f":
            if exclusive:
                given = forward(place, held[index][1], held[index][2], after)
                held[index].append(lax.ppermute(given, "gy", [(0, 2), (1, 0), (2, 3), (3, 1)]))
                after = [given]
            if index == 0:
                take(1, after[0] if after else None)
                rows = embed(chips, block, 0, exclusive, place, onehot, depth_table, held[0], after)
                held[0] = [rows]
        if kind == "t":
            take(index, after[0])
        if kind == "p":
            start, width = pieces[index][int(item[2])]
            extra = {}
            if len(item) > 3:
                done = item[4:]
                ending = (int(done[0]) * size, pieces[int(done[0])][int(done[1])][0])
                extra = dict(ending=ending, terms=sums[done], out=out, shape=(block, columns))
            send, keep, *rest = product(chips, exclusive, place, held[index], weight, start, width, after, **extra)
            out = rest[0] if rest else out
            products[piece] = (keep, lax.ppermute(send, "gx", sibling))
            after = [keep]
        if kind == "s":
            away, stay = pair(chips, *products[piece], after)
            sums[piece] = [stay] + [
                lax.ppermute(away[(ahead - 1) * size:ahead * size], "gx", across(ahead)) for ahead in range(1, chips)
            ]
            after = [stay]
        if kind == "g":
            start, width = pieces[index][int(item[2])]
            out, token = finish((block, columns), (index, start, width), size, sums[piece], out, after)
            after = [token]
    return out


def solution(mesh):
    return jax.shard_map(
        functools.partial(local, mesh.shape["gx"], mesh.shape["gy"]),
        mesh=mesh,
        in_specs=(P(("grp", "gy"), "gx"), P("grp"), P(None, "gx"), P("gx", "gy")),
        out_specs=P(("grp", "gx"), "gy"),
        check_vma=False,
    )
```

time: 201 us -> 185 us (0.920)
  waiting for transfers between devices: 67.1 us -> 58.3 us
  Pallas kernels: 107 us -> 99 us
    pallas_call x8 -> x3, Pallas kernels: 11 us -> 3.34 us  [finish(): pl.pallas_call(functools.partial(finish_kernel, len(terms)), name='finish...]
    ppermute x19 -> x17, waiting for transfers between devices: 41.2 us -> 35.5 us  [the longest x7 26.3 us: local(): lax.ppermute(away[(ahead - 1) * size:ahead * size], 'gx', across(ahead))]
    pallas_call x8 -> x7, Pallas kernels: 78.4 us -> 83.8 us  [product(): pl.pallas_call(functools.partial(product_kernel, start, tile, width // ti...]
    pallas_call x3 -> x1, Pallas kernels: 7.86 us -> 2.62 us  [embed(): pl.pallas_call(functools.partial(embed_kernel, count, chips, block, first...]
    ppermute x6, waiting for transfers between devices: 26 us -> 22.8 us  [swap(): return lax.ppermute(array, 'gy', [(k, k ^ distance) for k in range(n_gy)])]
    pallas_call x1, Pallas kernels: 4.26 us -> 2 us  [depth_onehot(): pl.pallas_call(functools.partial(onehot_kernel, tree), name='onehot', out...]
    ppermute x19 -> x17, starting transfers between devices: 14 us -> 13 us  [the longest x7 8.32 us: local(): lax.ppermute(away[(ahead - 1) * size:ahead * size], 'gx', across(ahead))]
  transfers between devices with their start and end apart: 25 -> 23, of which waited for: 11 -> 10; matrix products, arithmetic and copies ran while one was open for 0% -> 0% of each run, Pallas kernels for 52% -> 52%
where the time goes in v3:
time: 185 us
  Pallas kernels  99 us (54%)
  waiting for transfers between devices  58.3 us (32%)
  starting transfers between devices  23.6 us (13%)
  local copies, waits for them, and re-layouts  3.39 us (2%)
    pallas_call x7, Pallas kernels, product(): pl.pallas_call(functools.partial(product_kernel, start, tile, width // ti...  83.8 us
    ppermute x7, waiting for transfers between devices, local(): lax.ppermute(away[(ahead - 1) * size:ahead * size], 'gx', across(ahead))  26.3 us
    ppermute x6, waiting for transfers between devices, swap(): return lax.ppermute(array, 'gy', [(k, k ^ distance) for k in range(n_gy)])  22.8 us
    ppermute x6, starting transfers between devices, swap(): return lax.ppermute(array, 'gy', [(k, k ^ distance) for k in range(n_gy)])  10.6 us
    ppermute x3, waiting for transfers between devices, local(): lax.ppermute(given, 'gy', [(0, 2), (1, 0), (2, 3), (3, 1)])  9.15 us
    ppermute x7, starting transfers between devices, local(): lax.ppermute(away[(ahead - 1) * size:ahead * size], 'gx', across(ahead))  8.32 us
    ppermute x3, starting transfers between devices, local(): lax.ppermute(given, 'gy', [(0, 2), (1, 0), (2, 3), (3, 1)])  3.78 us
  transfers between devices with their start and end apart: 23, of which 10 were waited for; matrix products, arithmetic and copies ran while one was open for 0% of the time, Pallas kernels for 52%

profile of v3, /device:TPU:0, one launch (start us, length us, event | category | flops | bytes accessed | tf_op | source)
XLA Modules:
  0.0 184.6 jit_solution(1261890909171190329)
XLA Ops:
  1.1 4.1 %collective-permute-start.1 = (bf16[64,3584]{1,0:T(8,128)(2,1)S(1)}, bf16[64,3584]{1,0:T(8,128)(2,1)S(1)}, u32[]{:S(2)}, u32[]{:S(2)}) collective-permute-start(bf16[64,3584]{1,0:T(8,128)(2,1)S(1)} %slice.3.refs_0_), channel_id=1, source_target_pairs={{0,2},{1,3},{2,0},{3,1},{4,6},{5,7},{6,4},{7,5},{8,10},{9,11},{10,... | collective-permute-start | bytes 1376264 | tf_op jit(solution)/shard_map/ppermute | solution.py:351
  5.2 1.6 collective-permute-start
  7.6 2.0 %onehot.1.onehot_ref = bf16[768,256]{1,0:T(8,128)(2,1)S(1)} custom-call(s32[768,1]{1,0:T(8,128)S(1)} %broadcast_in_dim.4.parents_ref), custom_call_target="tpu_custom_call" | custom-call | flops 19327352832 | bytes 12582912 | tf_op jit(solution)/shard_map/onehot/pallas_call | solution.py:52
  9.7 1.5 copy-done.1
  11.2 1.9 %own.1 = (bf16[64,3584]{1,0:T(8,128)(2,1)S(1)}, bf16[64,3584]{1,0:T(8,128)(2,1)S(1)}) custom-call(s32[2]{0:T(128)S(1)} %pad_add_fusion.place_ref, bf16[768,256]{1,0:T(8,128)(2,1)S(1)} %onehot.1.onehot_ref, bf16[256,3584]{1,0:T(8,128)(2,1)S(1)} %copy-done.1, bf16[192,3584]{1,0:T(8,128)(2,1)S(1)} %copy-done), custom_call_target="tpu_custom_call" | custom-call | flops 1879048192 | bytes 22020096 | tf_op jit(solution)/shard_map/own/pallas_call | solution.py:135
  13.1 12.5 %collective-permute-done.1.far_ref.refs_2_ = bf16[64,3584]{1,0:T(8,128)(2,1)S(1)} collective-permute-done((bf16[64,3584]{1,0:T(8,128)(2,1)S(1)}, bf16[64,3584]{1,0:T(8,128)(2,1)S(1)}, u32[]{:S(2)}, u32[]{:S(2)}) %collective-permute-start.1) | collective-permute-done | bytes 458784 | tf_op jit(solution)/shard_map/ppermute | solution.py:351
  26.4 1.4 collective-permute-start.2
  27.8 2.4 %collective-permute-start.4 = (bf16[64,3584]{1,0:T(8,128)(2,1)S(1)}, bf16[64,3584]{1,0:T(8,128)(2,1)S(1)}, u32[]{:S(2)}, u32[]{:S(2)}) collective-permute-start(bf16[64,3584]{1,0:T(8,128)(2,1)S(1)} %get-tuple-element.48.refs_0_), channel_id=1, source_target_pairs={{0,2},{1,3},{2,0},{3,1},{4,6},{5,7},{6,4},{7,5},{8,10},{9,11},{10,... | collective-permute-start | bytes 1376264 | tf_op jit(solution)/shard_map/ppermute | solution.py:351
  30.9 9.1 %collective-permute-done.2.refs_3_ = bf16[64,3584]{1,0:T(8,128)(2,1)S(1)} collective-permute-done((bf16[64,3584]{1,0:T(8,128)(2,1)S(1)}, bf16[64,3584]{1,0:T(8,128)(2,1)S(1)}, u32[]{:S(2)}, u32[]{:S(2)}) %collective-permute-start.2) | collective-permute-done | bytes 458784 | tf_op jit(solution)/shard_map/ppermute | solution.py:382
  40.0 2.6 %embed.1.refs_0_ = bf16[256,3584]{1,0:T(8,128)(2,1)S(1)} custom-call(s32[2]{0:T(128)S(1)} %pad_add_fusion.place_ref, bf16[768,256]{1,0:T(8,128)(2,1)S(1)} %onehot.1.onehot_ref, bf16[256,3584]{1,0:T(8,128)(2,1)S(1)} %copy-done.1, bf16[64,3584]{1,0:T(8,128)(2,1)S(1)} %slice.3.refs_0_, bf16[64,3584]{1,0:T(8,128)(2,1)S(1)} %collective-permute-done.near_ref.refs_1_, ...), custom_call_target="tpu_custom_call" | custom-call | flops 3758096384 | bytes 44040192 | tf_op jit(solution)/shard_map/embed/pallas_call | solution.py:108
  42.6 13.0 %product.7 = (bf16[128,4608]{1,0:T(8,128)(2,1)S(1)}, bf16[128,4608]{1,0:T(8,128)(2,1)S(1)}) custom-call(s32[2]{0:T(128)S(1)} %pad_add_fusion.place_ref, bf16[3584,9216]{1,0:T(8,128)(2,1)} %weight_ref.13, bf16[256,3584]{1,0:T(8,128)(2,1)S(1)} %embed.1.refs_0_, bf16[64,3584]{1,0:T(8,128)(2,1)S(1)} %forward.3.refs_4_.refs_1_), custom_call_target="tpu_custom_call" | custom-call | flops 67645734912 | bytes 297795584 | tf_op jit(solution)/shard_map/product/pallas_call | solution.py:261
  55.6 4.4 %collective-permute-done.4.far_ref.refs_2_ = bf16[64,3584]{1,0:T(8,128)(2,1)S(1)} collective-permute-done((bf16[64,3584]{1,0:T(8,128)(2,1)S(1)}, bf16[64,3584]{1,0:T(8,128)(2,1)S(1)}, u32[]{:S(2)}, u32[]{:S(2)}) %collective-permute-start.4) | collective-permute-done | bytes 458784 | tf_op jit(solution)/shard_map/ppermute | solution.py:351
  61.3 13.0 %product.8 = (bf16[128,4608]{1,0:T(8,128)(2,1)S(1)}, bf16[128,4608]{1,0:T(8,128)(2,1)S(1)}) custom-call(s32[2]{0:T(128)S(1)} %pad_add_fusion.place_ref, bf16[3584,9216]{1,0:T(8,128)(2,1)} %weight_ref.13, bf16[256,3584]{1,0:T(8,128)(2,1)S(1)} %embed.1.refs_0_, bf16[64,3584]{1,0:T(8,128)(2,1)S(1)} %forward.4.refs_1_), custom_call_target="tpu_custom_call" | custom-call | flops 67645734912 | bytes 297795584 | tf_op jit(solution)/shard_map/product/pallas_call | solution.py:261
  74.3 1.8 collective-permute-start.6
  76.9 1.6 collective-permute-start.11
  78.5 13.3 %product.9 = (bf16[128,4608]{1,0:T(8,128)(2,1)S(1)}, bf16[128,4608]{1,0:T(8,128)(2,1)S(1)}) custom-call(s32[2]{0:T(128)S(1)} %pad_add_fusion.place_ref, bf16[3584,9216]{1,0:T(8,128)(2,1)} %weight_ref.13, bf16[64,3584]{1,0:T(8,128)(2,1)S(1)} %get-tuple-element.48.refs_0_, bf16[64,3584]{1,0:T(8,128)(2,1)S(1)} %collective-permute-done.3.near_ref.refs_1_, ...), custom_call_target="tpu_custom_call" | custom-call | flops 67645734912 | bytes 297795584 | tf_op jit(solution)/shard_map/product/pallas_call | solution.py:261
  92.4 5.7 %collective-permute-done.6.far_ref.refs_2_ = bf16[64,3584]{1,0:T(8,128)(2,1)S(1)} collective-permute-done((bf16[64,3584]{1,0:T(8,128)(2,1)S(1)}, bf16[64,3584]{1,0:T(8,128)(2,1)S(1)}, u32[]{:S(2)}, u32[]{:S(2)}) %collective-permute-start.6) | collective-permute-done | bytes 458784 | tf_op jit(solution)/shard_map/ppermute | solution.py:351
  98.7 1.7 collective-permute-start.10
  100.3 1.5 collective-permute-start.13
  101.8 13.8 %product.10 = (bf16[128,4608]{1,0:T(8,128)(2,1)S(1)}, bf16[128,4608]{1,0:T(8,128)(2,1)S(1)}, bf16[192,9216]{1,0:T(8,128)(2,1)}) custom-call(s32[2]{0:T(128)S(1)} %pad_add_fusion.place_ref, bf16[3584,9216]{1,0:T(8,128)(2,1)} %weight_ref.13, bf16[64,3584]{1,0:T(8,128)(2,1)S(1)} %get-tuple-element.48.refs_0_, ...), custom_call_target="tpu_custom_call" | custom-call | flops 67645734912 | bytes 297795584 | tf_op jit(solution)/shard_map/product/pallas_call | solution.py:261
  117.4 10.3 %product.11 = (bf16[128,3072]{1,0:T(8,128)(2,1)S(1)}, bf16[128,3072]{1,0:T(8,128)(2,1)S(1)}, bf16[192,9216]{1,0:T(8,128)(2,1)}) custom-call(s32[2]{0:T(128)S(1)} %pad_add_fusion.place_ref, bf16[3584,9216]{1,0:T(8,128)(2,1)} %weight_ref.13, bf16[64,3584]{1,0:T(8,128)(2,1)S(1)} %get-tuple-element.51.refs_0_, ...), custom_call_target="tpu_custom_call", output_to_operand_aliasing={{2}: (8, {})} | custom-call | flops 45097156608 | bytes 203423744 | tf_op jit(solution)/shard_map/product/pallas_call | solution.py:261
  128.4 1.6 collective-permute-start.15
  129.9 2.8 %collective-permute-done.16.refs_5_ = bf16[64,4608]{1,0:T(8,128)(2,1)S(1)} collective-permute-done((bf16[64,4608]{1,0:T(8,128)(2,1)S(1)}, bf16[64,4608]{1,0:T(8,128)(2,1)S(1)}, u32[]{:S(2)}, u32[]{:S(2)}) %collective-permute-start.16) | collective-permute-done | bytes 589856 | tf_op jit(solution)/shard_map/ppermute | solution.py:404
  132.7 10.3 %product.12 = (bf16[128,3072]{1,0:T(8,128)(2,1)S(1)}, bf16[128,3072]{1,0:T(8,128)(2,1)S(1)}, bf16[192,9216]{1,0:T(8,128)(2,1)}) custom-call(s32[2]{0:T(128)S(1)} %pad_add_fusion.place_ref, bf16[3584,9216]{1,0:T(8,128)(2,1)} %weight_ref.13, bf16[64,3584]{1,0:T(8,128)(2,1)S(1)} %get-tuple-element.51.refs_0_, ...), custom_call_target="tpu_custom_call", output_to_operand_aliasing={{2}: (8, {})} | custom-call | flops 45097156608 | bytes 203423744 | tf_op jit(solution)/shard_map/product/pallas_call | solution.py:261
  143.5 1.3 collective-permute-done.15.refs_5_
  144.8 10.3 %product.13 = (bf16[128,3072]{1,0:T(8,128)(2,1)S(1)}, bf16[128,3072]{1,0:T(8,128)(2,1)S(1)}, bf16[192,9216]{1,0:T(8,128)(2,1)}) custom-call(s32[2]{0:T(128)S(1)} %pad_add_fusion.place_ref, bf16[3584,9216]{1,0:T(8,128)(2,1)} %weight_ref.13, bf16[64,3584]{1,0:T(8,128)(2,1)S(1)} %get-tuple-element.51.refs_0_, ...), custom_call_target="tpu_custom_call", output_to_operand_aliasing={{2}: (8, {})} | custom-call | flops 45097156608 | bytes 203423744 | tf_op jit(solution)/shard_map/product/pallas_call | solution.py:261
  156.4 1.2 collective-permute-start.22
  157.7 9.4 %collective-permute-done.19.refs_1_ = bf16[64,3072]{1,0:T(8,128)(2,1)S(1)} collective-permute-done((bf16[64,3072]{1,0:T(8,128)(2,1)S(1)}, bf16[64,3072]{1,0:T(8,128)(2,1)S(1)}, u32[]{:S(2)}, u32[]{:S(2)}) %collective-permute-start.19) | collective-permute-done | bytes 393248 | tf_op jit(solution)/shard_map/ppermute | solution.py:404
  169.5 6.0 %collective-permute-done.22.refs_1_ = bf16[64,3072]{1,0:T(8,128)(2,1)S(1)} collective-permute-done((bf16[64,3072]{1,0:T(8,128)(2,1)S(1)}, bf16[64,3072]{1,0:T(8,128)(2,1)S(1)}, u32[]{:S(2)}, u32[]{:S(2)}) %collective-permute-start.22) | collective-permute-done | bytes 393248 | tf_op jit(solution)/shard_map/ppermute | solution.py:404
  175.5 1.1 finish.4
  176.6 6.9 %collective-permute-done.21.refs_1_ = bf16[64,3072]{1,0:T(8,128)(2,1)S(1)} collective-permute-done((bf16[64,3072]{1,0:T(8,128)(2,1)S(1)}, bf16[64,3072]{1,0:T(8,128)(2,1)S(1)}, u32[]{:S(2)}, u32[]{:S(2)}) %collective-permute-start.21) | collective-permute-done | bytes 393248 | tf_op jit(solution)/shard_map/ppermute | solution.py:404
  183.5 1.1 finish.5
  (44 shorter events, 13.3 us)
Async XLA Ops:
  1.1 24.6 %collective-permute-start.1 = (bf16[64,3584]{1,0:T(8,128)(2,1)S(1)}, bf16[64,3584]{1,0:T(8,128)(2,1)S(1)}, u32[]{:S(2)}, u32[]{:S(2)}) collective-permute-start(bf16[64,3584]{1,0:T(8,128)(2,1)S(1)} %slice.3.refs_0_), channel_id=1, source_target_pairs={{0,2},{1,3},{2,0},{3,1},{4,6},{5,7},{6,4},{7,5},{8,10},{9,11},{10,... | collective-permute-start | bytes 1376264 | tf_op jit(solution)/shard_map/ppermute | solution.py:351
  5.2 20.6 %collective-permute-start = (bf16[64,3584]{1,0:T(8,128)(2,1)S(1)}, bf16[64,3584]{1,0:T(8,128)(2,1)S(1)}, u32[]{:S(2)}, u32[]{:S(2)}) collective-permute-start(bf16[64,3584]{1,0:T(8,128)(2,1)S(1)} %slice.3.refs_0_), channel_id=1, source_target_pairs={{0,1},{1,0},{2,3},{3,2},{4,5},{5,4},{6,7},{7,6},{8,9},{9,8},{10,11... | collective-permute-start | bytes 1376264 | tf_op jit(solution)/shard_map/ppermute | solution.py:351
  7.6 2.1 %copy-start = (bf16[192,3584]{1,0:T(8,128)(2,1)S(1)}, bf16[192,3584]{1,0:T(8,128)(2,1)}, u32[]{:S(2)}) copy-start(bf16[192,3584]{1,0:T(8,128)(2,1)} %hidden_ref.1) | copy-start | bytes 4128772
  9.7 1.5 copy-start.1
  26.4 13.6 %collective-permute-start.2 = (bf16[64,3584]{1,0:T(8,128)(2,1)S(1)}, bf16[64,3584]{1,0:T(8,128)(2,1)S(1)}, u32[]{:S(2)}, u32[]{:S(2)}) collective-permute-start(bf16[64,3584]{1,0:T(8,128)(2,1)S(1)} %forward.3.refs_4_.refs_1_), channel_id=1, source_target_pairs={{0,2},{1,0},{2,3},{3,1},{4,6},{5,4},{6,7},{7,5},{8,10},{9,8},{10,1... | collective-permute-start | bytes 1376264 | tf_op jit(solution)/shard_map/ppermute | solution.py:382
  27.8 32.2 %collective-permute-start.4 = (bf16[64,3584]{1,0:T(8,128)(2,1)S(1)}, bf16[64,3584]{1,0:T(8,128)(2,1)S(1)}, u32[]{:S(2)}, u32[]{:S(2)}) collective-permute-start(bf16[64,3584]{1,0:T(8,128)(2,1)S(1)} %get-tuple-element.48.refs_0_), channel_id=1, source_target_pairs={{0,2},{1,3},{2,0},{3,1},{4,6},{5,7},{6,4},{7,5},{8,10},{9,11},{10,... | collective-permute-start | bytes 1376264 | tf_op jit(solution)/shard_map/ppermute | solution.py:351
  30.2 29.8 %collective-permute-start.3 = (bf16[64,3584]{1,0:T(8,128)(2,1)S(1)}, bf16[64,3584]{1,0:T(8,128)(2,1)S(1)}, u32[]{:S(2)}, u32[]{:S(2)}) collective-permute-start(bf16[64,3584]{1,0:T(8,128)(2,1)S(1)} %get-tuple-element.48.refs_0_), channel_id=1, source_target_pairs={{0,1},{1,0},{2,3},{3,2},{4,5},{5,4},{6,7},{7,6},{8,9},{9,8},{10,11... | collective-permute-start | bytes 1376264 | tf_op jit(solution)/shard_map/ppermute | solution.py:351
  60.6 17.9 %collective-permute-start.8 = (bf16[64,3584]{1,0:T(8,128)(2,1)S(1)}, bf16[64,3584]{1,0:T(8,128)(2,1)S(1)}, u32[]{:S(2)}, u32[]{:S(2)}) collective-permute-start(bf16[64,3584]{1,0:T(8,128)(2,1)S(1)} %forward.4.refs_1_), channel_id=1, source_target_pairs={{0,2},{1,0},{2,3},{3,1},{4,6},{5,4},{6,7},{7,5},{8,10},{9,8},{10,1... | collective-permute-start | bytes 1376264 | tf_op jit(solution)/shard_map/ppermute | solution.py:382
  61.3 15.0 %collective-permute-start.9 = (bf16[128,4608]{1,0:T(8,128)(2,1)S(1)}, bf16[128,4608]{1,0:T(8,128)(2,1)S(1)}, u32[]{:S(2)}, u32[]{:S(2)}) collective-permute-start(bf16[128,4608]{1,0:T(8,128)(2,1)S(1)} %get-tuple-element.53), channel_id=1, source_target_pairs={{0,4},{4,0},{8,12},{12,8},{1,5},{5,1},{9,13},{13,9},{2,6},{6,2},{1... | collective-permute-start | bytes 3538952 | tf_op jit(solution)/shard_map/ppermute | solution.py:399
  74.3 23.7 %collective-permute-start.6 = (bf16[64,3584]{1,0:T(8,128)(2,1)S(1)}, bf16[64,3584]{1,0:T(8,128)(2,1)S(1)}, u32[]{:S(2)}, u32[]{:S(2)}) collective-permute-start(bf16[64,3584]{1,0:T(8,128)(2,1)S(1)} %get-tuple-element.51.refs_0_), channel_id=1, source_target_pairs={{0,2},{1,3},{2,0},{3,1},{4,6},{5,7},{6,4},{7,5},{8,10},{9,11},{10,... | collective-permute-start | bytes 1376264 | tf_op jit(solution)/shard_map/ppermute | solution.py:351
  76.1 22.0 %collective-permute-start.5 = (bf16[64,3584]{1,0:T(8,128)(2,1)S(1)}, bf16[64,3584]{1,0:T(8,128)(2,1)S(1)}, u32[]{:S(2)}, u32[]{:S(2)}) collective-permute-start(bf16[64,3584]{1,0:T(8,128)(2,1)S(1)} %get-tuple-element.51.refs_0_), channel_id=1, source_target_pairs={{0,1},{1,0},{2,3},{3,2},{4,5},{5,4},{6,7},{7,6},{8,9},{9,8},{10,11... | collective-permute-start | bytes 1376264 | tf_op jit(solution)/shard_map/ppermute | solution.py:351
  76.2 15.6 %collective-permute-start.7 = (bf16[128,4608]{1,0:T(8,128)(2,1)S(1)}, bf16[128,4608]{1,0:T(8,128)(2,1)S(1)}, u32[]{:S(2)}, u32[]{:S(2)}) collective-permute-start(bf16[128,4608]{1,0:T(8,128)(2,1)S(1)} %get-tuple-element.52), channel_id=1, source_target_pairs={{0,4},{4,0},{8,12},{12,8},{1,5},{5,1},{9,13},{13,9},{2,6},{6,2},{1... | collective-permute-start | bytes 3538952 | tf_op jit(solution)/shard_map/ppermute | solution.py:399
  76.9 24.9 %collective-permute-start.11 = (bf16[64,4608]{1,0:T(8,128)(2,1)S(1)}, bf16[64,4608]{1,0:T(8,128)(2,1)S(1)}, u32[]{:S(2)}, u32[]{:S(2)}) collective-permute-start(bf16[64,4608]{1,0:T(8,128)(2,1)S(1)} %get-tuple-element.57), channel_id=1, source_target_pairs={{0,8},{4,12},{8,0},{12,4},{1,9},{5,13},{9,1},{13,5},{2,10},{6,14},... | collective-permute-start | bytes 1769480 | tf_op jit(solution)/shard_map/ppermute | solution.py:404
  98.7 18.7 %collective-permute-start.10 = (bf16[64,3584]{1,0:T(8,128)(2,1)S(1)}, bf16[64,3584]{1,0:T(8,128)(2,1)S(1)}, u32[]{:S(2)}, u32[]{:S(2)}) collective-permute-start(bf16[64,3584]{1,0:T(8,128)(2,1)S(1)} %forward.5.refs_6_), channel_id=1, source_target_pairs={{0,2},{1,0},{2,3},{3,1},{4,6},{5,4},{6,7},{7,5},{8,10},{9,8},{10,1... | collective-permute-start | bytes 1376264 | tf_op jit(solution)/shard_map/ppermute | solution.py:382
  100.3 17.0 %collective-permute-start.13 = (bf16[64,4608]{1,0:T(8,128)(2,1)S(1)}, bf16[64,4608]{1,0:T(8,128)(2,1)S(1)}, u32[]{:S(2)}, u32[]{:S(2)}) collective-permute-start(bf16[64,4608]{1,0:T(8,128)(2,1)S(1)} %get-tuple-element.60), channel_id=1, source_target_pairs={{0,8},{4,12},{8,0},{12,4},{1,9},{5,13},{9,1},{13,5},{2,10},{6,14},... | collective-permute-start | bytes 1769480 | tf_op jit(solution)/shard_map/ppermute | solution.py:404
  101.8 14.4 %collective-permute-start.14 = (bf16[128,4608]{1,0:T(8,128)(2,1)S(1)}, bf16[128,4608]{1,0:T(8,128)(2,1)S(1)}, u32[]{:S(2)}, u32[]{:S(2)}) collective-permute-start(bf16[128,4608]{1,0:T(8,128)(2,1)S(1)} %get-tuple-element.62), channel_id=1, source_target_pairs={{0,4},{4,0},{8,12},{12,8},{1,5},{5,1},{9,13},{13,9},{2,6},{6,2},{1... | collective-permute-start | bytes 3538952 | tf_op jit(solution)/shard_map/ppermute | solution.py:399
  115.6 12.1 %collective-permute-start.12 = (bf16[128,4608]{1,0:T(8,128)(2,1)S(1)}, bf16[128,4608]{1,0:T(8,128)(2,1)S(1)}, u32[]{:S(2)}, u32[]{:S(2)}) collective-permute-start(bf16[128,4608]{1,0:T(8,128)(2,1)S(1)} %get-tuple-element.59), channel_id=1, source_target_pairs={{0,4},{4,0},{8,12},{12,8},{1,5},{5,1},{9,13},{13,9},{2,6},{6,2},{1... | collective-permute-start | bytes 3538952 | tf_op jit(solution)/shard_map/ppermute | solution.py:399
  116.8 15.9 %collective-permute-start.16 = (bf16[64,4608]{1,0:T(8,128)(2,1)S(1)}, bf16[64,4608]{1,0:T(8,128)(2,1)S(1)}, u32[]{:S(2)}, u32[]{:S(2)}) collective-permute-start(bf16[64,4608]{1,0:T(8,128)(2,1)S(1)} %get-tuple-element.67), channel_id=1, source_target_pairs={{0,8},{4,12},{8,0},{12,4},{1,9},{5,13},{9,1},{13,5},{2,10},{6,14},... | collective-permute-start | bytes 1769480 | tf_op jit(solution)/shard_map/ppermute | solution.py:404
  127.7 15.4 %collective-permute-start.17 = (bf16[128,3072]{1,0:T(8,128)(2,1)S(1)}, bf16[128,3072]{1,0:T(8,128)(2,1)S(1)}, u32[]{:S(2)}, u32[]{:S(2)}) collective-permute-start(bf16[128,3072]{1,0:T(8,128)(2,1)S(1)} %get-tuple-element.70), channel_id=1, source_target_pairs={{0,4},{4,0},{8,12},{12,8},{1,5},{5,1},{9,13},{13,9},{2,6},{6,2},{1... | collective-permute-start | bytes 2359304 | tf_op jit(solution)/shard_map/ppermute | solution.py:399
  128.4 16.4 %collective-permute-start.15 = (bf16[64,4608]{1,0:T(8,128)(2,1)S(1)}, bf16[64,4608]{1,0:T(8,128)(2,1)S(1)}, u32[]{:S(2)}, u32[]{:S(2)}) collective-permute-start(bf16[64,4608]{1,0:T(8,128)(2,1)S(1)} %get-tuple-element.66), channel_id=1, source_target_pairs={{0,8},{4,12},{8,0},{12,4},{1,9},{5,13},{9,1},{13,5},{2,10},{6,14},... | collective-permute-start | bytes 1769480 | tf_op jit(solution)/shard_map/ppermute | solution.py:404
  142.9 13.1 %collective-permute-start.20 = (bf16[128,3072]{1,0:T(8,128)(2,1)S(1)}, bf16[128,3072]{1,0:T(8,128)(2,1)S(1)}, u32[]{:S(2)}, u32[]{:S(2)}) collective-permute-start(bf16[128,3072]{1,0:T(8,128)(2,1)S(1)} %get-tuple-element.77), channel_id=1, source_target_pairs={{0,4},{4,0},{8,12},{12,8},{1,5},{5,1},{9,13},{13,9},{2,6},{6,2},{1... | collective-permute-start | bytes 2359304 | tf_op jit(solution)/shard_map/ppermute | solution.py:399
  155.0 13.2 %collective-permute-start.18 = (bf16[128,3072]{1,0:T(8,128)(2,1)S(1)}, bf16[128,3072]{1,0:T(8,128)(2,1)S(1)}, u32[]{:S(2)}, u32[]{:S(2)}) collective-permute-start(bf16[128,3072]{1,0:T(8,128)(2,1)S(1)} %get-tuple-element.74), channel_id=1, source_target_pairs={{0,4},{4,0},{8,12},{12,8},{1,5},{5,1},{9,13},{13,9},{2,6},{6,2},{1... | collective-permute-start | bytes 2359304 | tf_op jit(solution)/shard_map/ppermute | solution.py:399
  155.1 12.0 %collective-permute-start.19 = (bf16[64,3072]{1,0:T(8,128)(2,1)S(1)}, bf16[64,3072]{1,0:T(8,128)(2,1)S(1)}, u32[]{:S(2)}, u32[]{:S(2)}) collective-permute-start(bf16[64,3072]{1,0:T(8,128)(2,1)S(1)} %get-tuple-element.75), channel_id=1, source_target_pairs={{0,8},{4,12},{8,0},{12,4},{1,9},{5,13},{9,1},{13,5},{2,10},{6,14},... | collective-permute-start | bytes 1179656 | tf_op jit(solution)/shard_map/ppermute | solution.py:404
  156.4 19.1 %collective-permute-start.22 = (bf16[64,3072]{1,0:T(8,128)(2,1)S(1)}, bf16[64,3072]{1,0:T(8,128)(2,1)S(1)}, u32[]{:S(2)}, u32[]{:S(2)}) collective-permute-start(bf16[64,3072]{1,0:T(8,128)(2,1)S(1)} %get-tuple-element.82), channel_id=1, source_target_pairs={{0,8},{4,12},{8,0},{12,4},{1,9},{5,13},{9,1},{13,5},{2,10},{6,14},... | collective-permute-start | bytes 1179656 | tf_op jit(solution)/shard_map/ppermute | solution.py:404
  168.6 14.9 %collective-permute-start.21 = (bf16[64,3072]{1,0:T(8,128)(2,1)S(1)}, bf16[64,3072]{1,0:T(8,128)(2,1)S(1)}, u32[]{:S(2)}, u32[]{:S(2)}) collective-permute-start(bf16[64,3072]{1,0:T(8,128)(2,1)S(1)} %get-tuple-element.81), channel_id=1, source_target_pairs={{0,8},{4,12},{8,0},{12,4},{1,9},{5,13},{9,1},{13,5},{2,10},{6,14},... | collective-permute-start | bytes 1179656 | tf_op jit(solution)/shard_map/ppermute | solution.py:404

commit v4 on v3

--- a/solution.py
+++ b/solution.py
@@ -19,8 +19,9 @@
     return pltpu.CompilerParams(vmem_limit_bytes=limit * MIB)
 
 
-def cost(flops, accessed):
-    return pl.CostEstimate(flops=8 * flops, bytes_accessed=8 * accessed, transcendentals=0)
+def cost(flops, accessed, long=False):
+    factor = 1000 if long else 8
+    return pl.CostEstimate(flops=factor * flops, bytes_accessed=factor * accessed, transcendentals=0)
 
 
 def divisor(extent, choices):
@@ -71,7 +72,7 @@
         out_ref[...] = far_ref[...]
 
 
-def forward(place, near, far, after):
+def forward(place, near, far, after, long):
     return pl.pallas_call(
         forward_kernel,
         name="forward",
@@ -79,7 +80,7 @@
         in_specs=[SMEM, VMEM, VMEM] + [ANY] * len(after),
         out_specs=VMEM,
         compiler_params=params(8),
-        cost_estimate=cost(0, 6 * near.size),
+        cost_estimate=cost(0, 6 * near.size, long),
     )(place, near, far, *after)
 
 
@@ -160,28 +161,22 @@
     blocks = refs[:count]
     terms = refs[count:count + ending[3]]
     outs = 2 if not ending[3] else 3
-    scratch = len(refs) - (4 if not ending[3] else 8)
+    scratch = len(refs) - (3 if not ending[3] else 7)
     send_ref, keep_ref = refs[scratch - outs:scratch - outs + 2]
-    rows, held, arrived, filled = refs[scratch:scratch + 4]
+    rows, held, arrived = refs[scratch:scratch + 3]
     half = send_ref.shape[0]
     step = pl.program_id(0)
+    lanes = held.shape[3]
 
     def fetch(index):
-        column = pl.multiple_of(start + index * tile, 128)
         slot = lax.rem(index, slots)
-        return pltpu.make_async_copy(weight_ref.at[:, pl.ds(column, tile)], held.at[slot], arrived.at[slot])
-
-    def fill(index):
-        if count == 1:
-            return pltpu.make_async_copy(blocks[0], rows, filled.at[0])
-        size = rows.shape[0] // count
-        dest = lax.bitwise_xor(place_ref[1], index) if exclusive else index
-        first = pl.multiple_of(slot_of(dest, chips, place_ref[0]) * size, 16)
-        return pltpu.make_async_copy(blocks[index], rows.at[pl.ds(first, size), :], filled.at[index])
+        for side in range(tile // lanes):
+            column = pl.multiple_of(start + index * tile + side * lanes, 128)
+            yield pltpu.make_async_copy(weight_ref.at[:, pl.ds(column, lanes)], held.at[slot, side], arrived.at[slot, side])
 
     if ending[3]:
         out_ref = refs[scratch - 1]
-        term_buffer, out_buffer, term_sems, out_sem = refs[scratch + 4:]
+        term_buffer, out_buffer, term_sems, out_sem = refs[scratch + 3:]
         row, column, width, number = ending
         given = [pltpu.make_async_copy(terms[n], term_buffer.at[n], term_sems.at[n]) for n in range(number)]
         place_out = out_ref.at[row:row + out_buffer.shape[0], column:column + width]
@@ -189,25 +184,31 @@
 
     @pl.when(step == 0)
     def _():
-        fetch(0).start()
-        for index in range(count):
-            fill(index).start()
-        for index in range(1, min(slots - 1, steps)):
-            fetch(index).start()
+        for index in range(min(slots - 1, steps)):
+            for copy in fetch(index):
+                copy.start()
         if ending[3]:
             for copy in given:
                 copy.start()
+        size = rows.shape[0] // count
         for index in range(count):
-            fill(index).wait()
+            first = 0
+            if count > 1:
+                dest = lax.bitwise_xor(place_ref[1], index) if exclusive else index
+                first = pl.multiple_of(slot_of(dest, chips, place_ref[0]) * size, 16)
+            rows[pl.ds(first, size), :] = blocks[index][...]
 
     @pl.when(step + slots - 1 < steps)
     def _():
-        fetch(step + slots - 1).start()
-
-    fetch(step).wait()
-    out = jnp.dot(rows[...], held[lax.rem(step, slots)], preferred_element_type=F32)
-    send_ref[...] = out[:half].astype(BF16)
-    keep_ref[...] = out[half:].astype(BF16)
+        for copy in fetch(step + slots - 1):
+            copy.start()
+
+    for side, copy in enumerate(fetch(step)):
+        copy.wait()
+        out = jnp.dot(rows[...], held[lax.rem(step, slots), side], preferred_element_type=F32)
+        here = slice(side * lanes, (side + 1) * lanes)
+        send_ref[:, here] = out[:half].astype(BF16)
+        keep_ref[:, here] = out[half:].astype(BF16)
 
     if ending[3]:
         @pl.when(step == 0)
@@ -232,15 +233,15 @@
     count = len(blocks)
     height, depth = count * blocks[0].shape[0], blocks[0].shape[1]
     tile = divisor(width, (512, 384, 256, 128))
+    lanes = divisor(tile, (256, 128))
     slots = 4
     half = jax.ShapeDtypeStruct((height // 2, width), BF16)
     outs = [half, half]
     out_specs = [pl.BlockSpec((height // 2, tile), lambda j: (0, j))] * 2
     scratch = [
         pltpu.VMEM((height, depth), BF16),
-        pltpu.VMEM((slots, depth, tile), BF16),
-        pltpu.SemaphoreType.DMA((slots,)),
-        pltpu.SemaphoreType.DMA((count,)),
+        pltpu.VMEM((slots, tile // lanes, depth, lanes), BF16),
+        pltpu.SemaphoreType.DMA((slots, tile // lanes)),
     ]
     operands = [place, weight, *blocks, *terms]
     aliases = {}
@@ -263,7 +264,7 @@
         name="product",
         grid=(width // tile,),
         out_shape=outs,
-        in_specs=[SMEM] + [ANY] * (len(operands) - 1),
+        in_specs=[SMEM, ANY] + [VMEM] * count + [ANY] * (len(operands) - 2 - count),
         out_specs=out_specs,
         scratch_shapes=scratch,
         input_output_aliases=aliases,
@@ -280,7 +281,7 @@
     stay_ref[...] = total[cut:].astype(BF16)
 
 
-def pair(chips, keep, got, after):
+def pair(chips, keep, got, after, long):
     height, width = keep.shape
     size = height // chips
     tile = divisor(width, (1536, 1152, 768, 512, 384, 256, 128))
@@ -293,7 +294,7 @@
         in_specs=[spec(height), spec(height)] + [ANY] * len(after),
         out_specs=[spec(height - size), spec(size)],
         compiler_params=params(16),
-        cost_estimate=cost(height * width, 6 * height * width),
+        cost_estimate=cost(height * width, 6 * height * width, long),
     )(keep, got, *after)
 
 
@@ -303,7 +304,7 @@
     token_ref[...] = jnp.zeros_like(token_ref)
 
 
-def finish(shape, step, rows, terms, held, after):
+def finish(shape, step, rows, terms, held, after, long):
     index, start, width = step
     tile = divisor(width, (1536, 1152, 768, 512, 384, 256, 128))
     aliases = {} if held is None else {len(terms): 0}
@@ -319,7 +320,7 @@
         ],
         input_output_aliases=aliases,
         compiler_params=params(16),
-        cost_estimate=cost(12 * rows * width, 6 * rows * width),
+        cost_estimate=cost(12 * rows * width, 6 * rows * width, long),
     )(*terms, *([] if held is None else [held]), *after)
 
 
@@ -333,7 +334,12 @@
 
 SHARES = ((3, 3), (3, 3), (2, 2, 2))
 
-ORDER = "f0 p00 f1 p01 t2 s00 p10 s01 f2 p11-00 s10 p20-01 s11 p21-10 s20 p22-11 s21 g20 s22 g21 g22".split()
+ORDER = (
+    ("f0", "p00", "f1", "p01", "t2", "s00"),
+    ("p10", "s01", "f2", "p11-00", "s10"),
+    ("p20-01", "s11", "p21-10", "s20", "p22-11+", "g20!"),
+    ("s21!", "s22", "g21", "g22"),
+)
 
 
 def local(n_gx, n_gy, hidden, parents, depth_table, weight):
@@ -373,12 +379,15 @@
 
     out, after = None, own[1:2]
     pieces = [column_pieces(columns, shares) for shares in SHARES]
-    products, sums = {}, {}
-    for item in ORDER:
+    products, sums, waiting = {}, {}, {}
+    for item in sum(ORDER, ()):
+        long = item.endswith("!")
+        late = item.endswith("+")
+        item = item.rstrip("!+")
         kind, index, piece = item[0], int(item[1]), item[1:3]
         if kind == "f":
             if exclusive:
-                given = forward(place, held[index][1], held[index][2], after)
+                given = forward(place, held[index][1], held[index][2], after, long)
                 held[index].append(lax.ppermute(given, "gy", [(0, 2), (1, 0), (2, 3), (3, 1)]))
                 after = [given]
             if index == 0:
@@ -396,18 +405,24 @@
                 extra = dict(ending=ending, terms=sums[done], out=out, shape=(block, columns))
             send, keep, *rest = product(chips, exclusive, place, held[index], weight, start, width, after, **extra)
             out = rest[0] if rest else out
-            products[piece] = (keep, lax.ppermute(send, "gx", sibling))
             after = [keep]
+            if late:
+                waiting[piece] = keep, send
+            else:
+                products[piece] = keep, lax.ppermute(send, "gx", sibling)
         if kind == "s":
-            away, stay = pair(chips, *products[piece], after)
+            away, stay = pair(chips, *products[piece], after, long)
             sums[piece] = [stay] + [
                 lax.ppermute(away[(ahead - 1) * size:ahead * size], "gx", across(ahead)) for ahead in range(1, chips)
             ]
             after = [stay]
         if kind == "g":
             start, width = pieces[index][int(item[2])]
-            out, token = finish((block, columns), (index, start, width), size, sums[piece], out, after)
+            out, token = finish((block, columns), (index, start, width), size, sums[piece], out, after, long)
             after = [token]
+            for name, (keep, send) in waiting.items():
+                products[name] = keep, lax.ppermute(later(send, token), "gx", sibling)
+            waiting = {}
     return out
 
 

time: 185 us -> 220 us (1.19)
  Pallas kernels: 99 us -> 153 us
  waiting for transfers between devices: 58.3 us -> 39.1 us
    pallas_call x7, Pallas kernels: 83.8 us -> 138 us  [product(): pl.pallas_call(functools.partial(product_kernel, start, tile, width // ti...]
    ppermute x7, waiting for transfers between devices: 26.3 us -> 16 us  [local(): lax.ppermute(away[(ahead - 1) * size:ahead * size], 'gx', across(ahead))]
    ppermute x6, waiting for transfers between devices: 22.8 us -> 12.7 us  [swap(): return lax.ppermute(array, 'gy', [(k, k ^ distance) for k in range(n_gy)])]
  transfers between devices with their start and end apart: 23 -> 23, of which waited for: 10 -> 6; matrix products, arithmetic and copies ran while one was open for 0% -> 0% of each run, Pallas kernels for 52% -> 69%
where the time goes in v4:
time: 220 us
  Pallas kernels  153 us (70%)
  waiting for transfers between devices  39.1 us (18%)
  starting transfers between devices  24 us (11%)
  local copies, waits for them, and re-layouts  3.39 us (2%)
    pallas_call x7, Pallas kernels, product(): pl.pallas_call(functools.partial(product_kernel, start, tile, width // ti...  138 us
    ppermute x7, waiting for transfers between devices, local(): lax.ppermute(away[(ahead - 1) * size:ahead * size], 'gx', across(ahead))  16 us
    ppermute x6, waiting for transfers between devices, swap(): return lax.ppermute(array, 'gy', [(k, k ^ distance) for k in range(n_gy)])  12.7 us
    ppermute x6, starting transfers between devices, swap(): return lax.ppermute(array, 'gy', [(k, k ^ distance) for k in range(n_gy)])  11.8 us
    ppermute x3, waiting for transfers between devices, local(): lax.ppermute(given, 'gy', [(0, 2), (1, 0), (2, 3), (3, 1)])  9.15 us
    ppermute x7, starting transfers between devices, local(): lax.ppermute(away[(ahead - 1) * size:ahead * size], 'gx', across(ahead))  7.01 us
  transfers between devices with their start and end apart: 23, of which 6 were waited for; matrix products, arithmetic and copies ran while one was open for 0% of the time, Pallas kernels for 69%

profile of v4, /device:TPU:0, one launch (start us, length us, event | category | flops | bytes accessed | tf_op | source)
XLA Modules:
  0.0 220.3 jit_solution(882804213419934183)
XLA Ops:
  0.0 1.0 slice.3.refs_0_
  1.1 4.1 %collective-permute-start.1 = (bf16[64,3584]{1,0:T(8,128)(2,1)S(1)}, bf16[64,3584]{1,0:T(8,128)(2,1)S(1)}, u32[]{:S(2)}, u32[]{:S(2)}) collective-permute-start(bf16[64,3584]{1,0:T(8,128)(2,1)S(1)} %slice.3.refs_0_), channel_id=1, source_target_pairs={{0,2},{1,3},{2,0},{3,1},{4,6},{5,7},{6,4},{7,5},{8,10},{9,11},{10,... | collective-permute-start | bytes 1376264 | tf_op jit(solution)/shard_map/ppermute | solution.py:357
  5.2 1.6 collective-permute-start
  6.7 0.8 broadcast_in_dim.4.parents_ref
  7.6 2.0 onehot.1.onehot_ref
  9.7 1.5 copy-done.1
  11.2 1.9 own.1
  13.1 12.5 %collective-permute-done.1.far_ref.refs_2_ = bf16[64,3584]{1,0:T(8,128)(2,1)S(1)} collective-permute-done((bf16[64,3584]{1,0:T(8,128)(2,1)S(1)}, bf16[64,3584]{1,0:T(8,128)(2,1)S(1)}, u32[]{:S(2)}, u32[]{:S(2)}) %collective-permute-start.1) | collective-permute-done | bytes 458784 | tf_op jit(solution)/shard_map/ppermute | solution.py:357
  26.4 1.4 collective-permute-start.2
  27.8 2.4 %collective-permute-start.4 = (bf16[64,3584]{1,0:T(8,128)(2,1)S(1)}, bf16[64,3584]{1,0:T(8,128)(2,1)S(1)}, u32[]{:S(2)}, u32[]{:S(2)}) collective-permute-start(bf16[64,3584]{1,0:T(8,128)(2,1)S(1)} %get-tuple-element.49.refs_0_), channel_id=1, source_target_pairs={{0,2},{1,3},{2,0},{3,1},{4,6},{5,7},{6,4},{7,5},{8,10},{9,11},{10,... | collective-permute-start | bytes 1376264 | tf_op jit(solution)/shard_map/ppermute | solution.py:357
  30.2 0.6 collective-permute-start.3
  30.9 9.1 %collective-permute-done.2.refs_3_ = bf16[64,3584]{1,0:T(8,128)(2,1)S(1)} collective-permute-done((bf16[64,3584]{1,0:T(8,128)(2,1)S(1)}, bf16[64,3584]{1,0:T(8,128)(2,1)S(1)}, u32[]{:S(2)}, u32[]{:S(2)}) %collective-permute-start.2) | collective-permute-done | bytes 458784 | tf_op jit(solution)/shard_map/ppermute | solution.py:391
  40.0 2.6 %embed.1.refs_0_ = bf16[256,3584]{1,0:T(8,128)(2,1)S(1)} custom-call(s32[2]{0:T(128)S(1)} %pad_add_fusion.place_ref, bf16[768,256]{1,0:T(8,128)(2,1)S(1)} %onehot.1.onehot_ref, bf16[256,3584]{1,0:T(8,128)(2,1)S(1)} %copy-done.1, bf16[64,3584]{1,0:T(8,128)(2,1)S(1)} %slice.3.refs_0_, bf16[64,3584]{1,0:T(8,128)(2,1)S(1)} %collective-permute-done.near_ref.refs_1_, ...), custom_call_target="tpu_custom_call" | custom-call | flops 3758096384 | bytes 44040192 | tf_op jit(solution)/shard_map/embed/pallas_call | solution.py:109
  42.6 22.2 %product.7 = (bf16[128,4608]{1,0:T(8,128)(2,1)S(1)}, bf16[128,4608]{1,0:T(8,128)(2,1)S(1)}) custom-call(s32[2]{0:T(128)S(1)} %pad_add_fusion.place_ref, bf16[3584,9216]{1,0:T(8,128)(2,1)} %weight_ref.13, bf16[256,3584]{1,0:T(8,128)(2,1)S(1)} %embed.1.refs_0_, bf16[64,3584]{1,0:T(8,128)(2,1)S(1)} %forward.3.refs_4_.refs_1_), custom_call_target="tpu_custom_call" | custom-call | flops 67645734912 | bytes 297795584 | tf_op jit(solution)/shard_map/product/pallas_call | solution.py:262
  65.4 2.3 %collective-permute-start.8 = (bf16[64,3584]{1,0:T(8,128)(2,1)S(1)}, bf16[64,3584]{1,0:T(8,128)(2,1)S(1)}, u32[]{:S(2)}, u32[]{:S(2)}) collective-permute-start(bf16[64,3584]{1,0:T(8,128)(2,1)S(1)} %forward.4.refs_1_), channel_id=1, source_target_pairs={{0,2},{1,0},{2,3},{3,1},{4,6},{5,4},{6,7},{7,5},{8,10},{9,8},{10,1... | collective-permute-start | bytes 1376264 | tf_op jit(solution)/shard_map/ppermute | solution.py:391
  67.8 22.2 %product.8 = (bf16[128,4608]{1,0:T(8,128)(2,1)S(1)}, bf16[128,4608]{1,0:T(8,128)(2,1)S(1)}) custom-call(s32[2]{0:T(128)S(1)} %pad_add_fusion.place_ref, bf16[3584,9216]{1,0:T(8,128)(2,1)} %weight_ref.13, bf16[256,3584]{1,0:T(8,128)(2,1)S(1)} %embed.1.refs_0_, bf16[64,3584]{1,0:T(8,128)(2,1)S(1)} %forward.4.refs_1_), custom_call_target="tpu_custom_call" | custom-call | flops 67645734912 | bytes 297795584 | tf_op jit(solution)/shard_map/product/pallas_call | solution.py:262
  89.9 1.5 collective-permute-start.6
  91.5 1.5 collective-permute-start.5
  93.6 1.6 collective-permute-start.11
  95.2 22.2 %product.9 = (bf16[128,4608]{1,0:T(8,128)(2,1)S(1)}, bf16[128,4608]{1,0:T(8,128)(2,1)S(1)}) custom-call(s32[2]{0:T(128)S(1)} %pad_add_fusion.place_ref, bf16[3584,9216]{1,0:T(8,128)(2,1)} %weight_ref.13, bf16[64,3584]{1,0:T(8,128)(2,1)S(1)} %get-tuple-element.49.refs_0_, bf16[64,3584]{1,0:T(8,128)(2,1)S(1)} %collective-permute-done.3.near_ref.refs_1_, ...), custom_call_target="tpu_custom_call" | custom-call | flops 67645734912 | bytes 297795584 | tf_op jit(solution)/shard_map/product/pallas_call | solution.py:262
  119.7 23.0 %product.10 = (bf16[128,4608]{1,0:T(8,128)(2,1)S(1)}, bf16[128,4608]{1,0:T(8,128)(2,1)S(1)}, bf16[192,9216]{1,0:T(8,128)(2,1)}) custom-call(s32[2]{0:T(128)S(1)} %pad_add_fusion.place_ref, bf16[3584,9216]{1,0:T(8,128)(2,1)} %weight_ref.13, bf16[64,3584]{1,0:T(8,128)(2,1)S(1)} %get-tuple-element.49.refs_0_, ...), custom_call_target="tpu_custom_call" | custom-call | flops 67645734912 | bytes 297795584 | tf_op jit(solution)/shard_map/product/pallas_call | solution.py:262
  143.8 1.6 collective-permute-start.16
  145.4 16.2 %product.11 = (bf16[128,3072]{1,0:T(8,128)(2,1)S(1)}, bf16[128,3072]{1,0:T(8,128)(2,1)S(1)}, bf16[192,9216]{1,0:T(8,128)(2,1)}) custom-call(s32[2]{0:T(128)S(1)} %pad_add_fusion.place_ref, bf16[3584,9216]{1,0:T(8,128)(2,1)} %weight_ref.13, bf16[64,3584]{1,0:T(8,128)(2,1)S(1)} %get-tuple-element.52.refs_0_, ...), custom_call_target="tpu_custom_call", output_to_operand_aliasing={{2}: (8, {})} | custom-call | flops 45097156608 | bytes 203423744 | tf_op jit(solution)/shard_map/product/pallas_call | solution.py:262
  162.9 16.2 %product.12 = (bf16[128,3072]{1,0:T(8,128)(2,1)S(1)}, bf16[128,3072]{1,0:T(8,128)(2,1)S(1)}, bf16[192,9216]{1,0:T(8,128)(2,1)}) custom-call(s32[2]{0:T(128)S(1)} %pad_add_fusion.place_ref, bf16[3584,9216]{1,0:T(8,128)(2,1)} %weight_ref.13, bf16[64,3584]{1,0:T(8,128)(2,1)S(1)} %get-tuple-element.52.refs_0_, ...), custom_call_target="tpu_custom_call", output_to_operand_aliasing={{2}: (8, {})} | custom-call | flops 45097156608 | bytes 203423744 | tf_op jit(solution)/shard_map/product/pallas_call | solution.py:262
  179.8 1.6 collective-permute-start.18
  181.4 16.2 %product.13 = (bf16[128,3072]{1,0:T(8,128)(2,1)S(1)}, bf16[128,3072]{1,0:T(8,128)(2,1)S(1)}, bf16[192,9216]{1,0:T(8,128)(2,1)}) custom-call(s32[2]{0:T(128)S(1)} %pad_add_fusion.place_ref, bf16[3584,9216]{1,0:T(8,128)(2,1)} %weight_ref.13, bf16[64,3584]{1,0:T(8,128)(2,1)S(1)} %get-tuple-element.52.refs_0_, ...), custom_call_target="tpu_custom_call", output_to_operand_aliasing={{2}: (8, {})} | custom-call | flops 45097156608 | bytes 203423744 | tf_op jit(solution)/shard_map/product/pallas_call | solution.py:262
  197.6 1.1 finish.3
  199.8 1.2 collective-permute-done.19.got_ref
  202.0 9.1 %collective-permute-done.22.refs_1_ = bf16[64,3072]{1,0:T(8,128)(2,1)S(1)} collective-permute-done((bf16[64,3072]{1,0:T(8,128)(2,1)S(1)}, bf16[64,3072]{1,0:T(8,128)(2,1)S(1)}, u32[]{:S(2)}, u32[]{:S(2)}) %collective-permute-start.22) | collective-permute-done | bytes 393248 | tf_op jit(solution)/shard_map/ppermute | solution.py:416
  211.1 1.1 finish.4
  212.2 6.9 %collective-permute-done.21.refs_1_ = bf16[64,3072]{1,0:T(8,128)(2,1)S(1)} collective-permute-done((bf16[64,3072]{1,0:T(8,128)(2,1)S(1)}, bf16[64,3072]{1,0:T(8,128)(2,1)S(1)}, u32[]{:S(2)}, u32[]{:S(2)}) %collective-permute-start.21) | collective-permute-done | bytes 393248 | tf_op jit(solution)/shard_map/ppermute | solution.py:416
  219.1 1.1 finish.5
  (44 shorter events, 9.4 us)
Async XLA Ops:
  1.1 24.6 %collective-permute-start.1 = (bf16[64,3584]{1,0:T(8,128)(2,1)S(1)}, bf16[64,3584]{1,0:T(8,128)(2,1)S(1)}, u32[]{:S(2)}, u32[]{:S(2)}) collective-permute-start(bf16[64,3584]{1,0:T(8,128)(2,1)S(1)} %slice.3.refs_0_), channel_id=1, source_target_pairs={{0,2},{1,3},{2,0},{3,1},{4,6},{5,7},{6,4},{7,5},{8,10},{9,11},{10,... | collective-permute-start | bytes 1376264 | tf_op jit(solution)/shard_map/ppermute | solution.py:357
  5.2 20.6 %collective-permute-start = (bf16[64,3584]{1,0:T(8,128)(2,1)S(1)}, bf16[64,3584]{1,0:T(8,128)(2,1)S(1)}, u32[]{:S(2)}, u32[]{:S(2)}) collective-permute-start(bf16[64,3584]{1,0:T(8,128)(2,1)S(1)} %slice.3.refs_0_), channel_id=1, source_target_pairs={{0,1},{1,0},{2,3},{3,2},{4,5},{5,4},{6,7},{7,6},{8,9},{9,8},{10,11... | collective-permute-start | bytes 1376264 | tf_op jit(solution)/shard_map/ppermute | solution.py:357
  7.6 2.1 copy-start
  9.7 1.5 copy-start.1
  26.4 13.6 %collective-permute-start.2 = (bf16[64,3584]{1,0:T(8,128)(2,1)S(1)}, bf16[64,3584]{1,0:T(8,128)(2,1)S(1)}, u32[]{:S(2)}, u32[]{:S(2)}) collective-permute-start(bf16[64,3584]{1,0:T(8,128)(2,1)S(1)} %forward.3.refs_4_.refs_1_), channel_id=1, source_target_pairs={{0,2},{1,0},{2,3},{3,1},{4,6},{5,4},{6,7},{7,5},{8,10},{9,8},{10,1... | collective-permute-start | bytes 1376264 | tf_op jit(solution)/shard_map/ppermute | solution.py:391
  27.8 37.0 %collective-permute-start.4 = (bf16[64,3584]{1,0:T(8,128)(2,1)S(1)}, bf16[64,3584]{1,0:T(8,128)(2,1)S(1)}, u32[]{:S(2)}, u32[]{:S(2)}) collective-permute-start(bf16[64,3584]{1,0:T(8,128)(2,1)S(1)} %get-tuple-element.49.refs_0_), channel_id=1, source_target_pairs={{0,2},{1,3},{2,0},{3,1},{4,6},{5,7},{6,4},{7,5},{8,10},{9,11},{10,... | collective-permute-start | bytes 1376264 | tf_op jit(solution)/shard_map/ppermute | solution.py:357
  30.2 34.6 %collective-permute-start.3 = (bf16[64,3584]{1,0:T(8,128)(2,1)S(1)}, bf16[64,3584]{1,0:T(8,128)(2,1)S(1)}, u32[]{:S(2)}, u32[]{:S(2)}) collective-permute-start(bf16[64,3584]{1,0:T(8,128)(2,1)S(1)} %get-tuple-element.49.refs_0_), channel_id=1, source_target_pairs={{0,1},{1,0},{2,3},{3,2},{4,5},{5,4},{6,7},{7,6},{8,9},{9,8},{10,11... | collective-permute-start | bytes 1376264 | tf_op jit(solution)/shard_map/ppermute | solution.py:357
  65.4 29.7 %collective-permute-start.8 = (bf16[64,3584]{1,0:T(8,128)(2,1)S(1)}, bf16[64,3584]{1,0:T(8,128)(2,1)S(1)}, u32[]{:S(2)}, u32[]{:S(2)}) collective-permute-start(bf16[64,3584]{1,0:T(8,128)(2,1)S(1)} %forward.4.refs_1_), channel_id=1, source_target_pairs={{0,2},{1,0},{2,3},{3,1},{4,6},{5,4},{6,7},{7,5},{8,10},{9,8},{10,1... | collective-permute-start | bytes 1376264 | tf_op jit(solution)/shard_map/ppermute | solution.py:391
  67.8 25.3 %collective-permute-start.9 = (bf16[128,4608]{1,0:T(8,128)(2,1)S(1)}, bf16[128,4608]{1,0:T(8,128)(2,1)S(1)}, u32[]{:S(2)}, u32[]{:S(2)}) collective-permute-start(bf16[128,4608]{1,0:T(8,128)(2,1)S(1)} %get-tuple-element.54), channel_id=1, source_target_pairs={{0,4},{4,0},{8,12},{12,8},{1,5},{5,1},{9,13},{13,9},{2,6},{6,2},{1... | collective-permute-start | bytes 3538952 | tf_op jit(solution)/shard_map/ppermute | solution.py:412
  89.9 28.1 %collective-permute-start.6 = (bf16[64,3584]{1,0:T(8,128)(2,1)S(1)}, bf16[64,3584]{1,0:T(8,128)(2,1)S(1)}, u32[]{:S(2)}, u32[]{:S(2)}) collective-permute-start(bf16[64,3584]{1,0:T(8,128)(2,1)S(1)} %get-tuple-element.52.refs_0_), channel_id=1, source_target_pairs={{0,2},{1,3},{2,0},{3,1},{4,6},{5,7},{6,4},{7,5},{8,10},{9,11},{10,... | collective-permute-start | bytes 1376264 | tf_op jit(solution)/shard_map/ppermute | solution.py:357
  91.5 26.5 %collective-permute-start.5 = (bf16[64,3584]{1,0:T(8,128)(2,1)S(1)}, bf16[64,3584]{1,0:T(8,128)(2,1)S(1)}, u32[]{:S(2)}, u32[]{:S(2)}) collective-permute-start(bf16[64,3584]{1,0:T(8,128)(2,1)S(1)} %get-tuple-element.52.refs_0_), channel_id=1, source_target_pairs={{0,1},{1,0},{2,3},{3,2},{4,5},{5,4},{6,7},{7,6},{8,9},{9,8},{10,11... | collective-permute-start | bytes 1376264 | tf_op jit(solution)/shard_map/ppermute | solution.py:357
  93.0 24.4 %collective-permute-start.7 = (bf16[128,4608]{1,0:T(8,128)(2,1)S(1)}, bf16[128,4608]{1,0:T(8,128)(2,1)S(1)}, u32[]{:S(2)}, u32[]{:S(2)}) collective-permute-start(bf16[128,4608]{1,0:T(8,128)(2,1)S(1)} %get-tuple-element.53), channel_id=1, source_target_pairs={{0,4},{4,0},{8,12},{12,8},{1,5},{5,1},{9,13},{13,9},{2,6},{6,2},{1... | collective-permute-start | bytes 3538952 | tf_op jit(solution)/shard_map/ppermute | solution.py:412
  93.6 26.1 %collective-permute-start.11 = (bf16[64,4608]{1,0:T(8,128)(2,1)S(1)}, bf16[64,4608]{1,0:T(8,128)(2,1)S(1)}, u32[]{:S(2)}, u32[]{:S(2)}) collective-permute-start(bf16[64,4608]{1,0:T(8,128)(2,1)S(1)} %get-tuple-element.58), channel_id=1, source_target_pairs={{0,8},{4,12},{8,0},{12,4},{1,9},{5,13},{9,1},{13,5},{2,10},{6,14},... | collective-permute-start | bytes 1769480 | tf_op jit(solution)/shard_map/ppermute | solution.py:416
  118.6 26.8 %collective-permute-start.10 = (bf16[64,3584]{1,0:T(8,128)(2,1)S(1)}, bf16[64,3584]{1,0:T(8,128)(2,1)S(1)}, u32[]{:S(2)}, u32[]{:S(2)}) collective-permute-start(bf16[64,3584]{1,0:T(8,128)(2,1)S(1)} %forward.5.refs_6_), channel_id=1, source_target_pairs={{0,2},{1,0},{2,3},{3,1},{4,6},{5,4},{6,7},{7,5},{8,10},{9,8},{10,1... | collective-permute-start | bytes 1376264 | tf_op jit(solution)/shard_map/ppermute | solution.py:391
  119.1 26.2 %collective-permute-start.13 = (bf16[64,4608]{1,0:T(8,128)(2,1)S(1)}, bf16[64,4608]{1,0:T(8,128)(2,1)S(1)}, u32[]{:S(2)}, u32[]{:S(2)}) collective-permute-start(bf16[64,4608]{1,0:T(8,128)(2,1)S(1)} %get-tuple-element.61), channel_id=1, source_target_pairs={{0,8},{4,12},{8,0},{12,4},{1,9},{5,13},{9,1},{13,5},{2,10},{6,14},... | collective-permute-start | bytes 1769480 | tf_op jit(solution)/shard_map/ppermute | solution.py:416
  119.7 23.6 %collective-permute-start.14 = (bf16[128,4608]{1,0:T(8,128)(2,1)S(1)}, bf16[128,4608]{1,0:T(8,128)(2,1)S(1)}, u32[]{:S(2)}, u32[]{:S(2)}) collective-permute-start(bf16[128,4608]{1,0:T(8,128)(2,1)S(1)} %get-tuple-element.63), channel_id=1, source_target_pairs={{0,4},{4,0},{8,12},{12,8},{1,5},{5,1},{9,13},{13,9},{2,6},{6,2},{1... | collective-permute-start | bytes 3538952 | tf_op jit(solution)/shard_map/ppermute | solution.py:412
  142.7 19.0 %collective-permute-start.12 = (bf16[128,4608]{1,0:T(8,128)(2,1)S(1)}, bf16[128,4608]{1,0:T(8,128)(2,1)S(1)}, u32[]{:S(2)}, u32[]{:S(2)}) collective-permute-start(bf16[128,4608]{1,0:T(8,128)(2,1)S(1)} %get-tuple-element.60), channel_id=1, source_target_pairs={{0,4},{4,0},{8,12},{12,8},{1,5},{5,1},{9,13},{13,9},{2,6},{6,2},{1... | collective-permute-start | bytes 3538952 | tf_op jit(solution)/shard_map/ppermute | solution.py:412
  143.8 19.1 %collective-permute-start.16 = (bf16[64,4608]{1,0:T(8,128)(2,1)S(1)}, bf16[64,4608]{1,0:T(8,128)(2,1)S(1)}, u32[]{:S(2)}, u32[]{:S(2)}) collective-permute-start(bf16[64,4608]{1,0:T(8,128)(2,1)S(1)} %get-tuple-element.68), channel_id=1, source_target_pairs={{0,8},{4,12},{8,0},{12,4},{1,9},{5,13},{9,1},{13,5},{2,10},{6,14},... | collective-permute-start | bytes 1769480 | tf_op jit(solution)/shard_map/ppermute | solution.py:416
  161.6 17.8 %collective-permute-start.17 = (bf16[128,3072]{1,0:T(8,128)(2,1)S(1)}, bf16[128,3072]{1,0:T(8,128)(2,1)S(1)}, u32[]{:S(2)}, u32[]{:S(2)}) collective-permute-start(bf16[128,3072]{1,0:T(8,128)(2,1)S(1)} %get-tuple-element.71), channel_id=1, source_target_pairs={{0,4},{4,0},{8,12},{12,8},{1,5},{5,1},{9,13},{13,9},{2,6},{6,2},{1... | collective-permute-start | bytes 2359304 | tf_op jit(solution)/shard_map/ppermute | solution.py:412
  162.3 19.1 %collective-permute-start.15 = (bf16[64,4608]{1,0:T(8,128)(2,1)S(1)}, bf16[64,4608]{1,0:T(8,128)(2,1)S(1)}, u32[]{:S(2)}, u32[]{:S(2)}) collective-permute-start(bf16[64,4608]{1,0:T(8,128)(2,1)S(1)} %get-tuple-element.67), channel_id=1, source_target_pairs={{0,8},{4,12},{8,0},{12,4},{1,9},{5,13},{9,1},{13,5},{2,10},{6,14},... | collective-permute-start | bytes 1769480 | tf_op jit(solution)/shard_map/ppermute | solution.py:416
  179.1 19.6 %collective-permute-start.20 = (bf16[128,3072]{1,0:T(8,128)(2,1)S(1)}, bf16[128,3072]{1,0:T(8,128)(2,1)S(1)}, u32[]{:S(2)}, u32[]{:S(2)}) collective-permute-start(bf16[128,3072]{1,0:T(8,128)(2,1)S(1)} %get-tuple-element.80), channel_id=1, source_target_pairs={{0,4},{4,0},{8,12},{12,8},{1,5},{5,1},{9,13},{13,9},{2,6},{6,2},{1... | collective-permute-start | bytes 2359304 | tf_op jit(solution)/shard_map/ppermute | solution.py:412
  179.8 17.8 %collective-permute-start.18 = (bf16[64,3072]{1,0:T(8,128)(2,1)S(1)}, bf16[64,3072]{1,0:T(8,128)(2,1)S(1)}, u32[]{:S(2)}, u32[]{:S(2)}) collective-permute-start(bf16[64,3072]{1,0:T(8,128)(2,1)S(1)} %get-tuple-element.76), channel_id=1, source_target_pairs={{0,8},{4,12},{8,0},{12,4},{1,9},{5,13},{9,1},{13,5},{2,10},{6,14},... | collective-permute-start | bytes 1179656 | tf_op jit(solution)/shard_map/ppermute | solution.py:416
  198.7 2.3 %collective-permute-start.19 = (bf16[128,3072]{1,0:T(8,128)(2,1)S(1)}, bf16[128,3072]{1,0:T(8,128)(2,1)S(1)}, u32[]{:S(2)}, u32[]{:S(2)}) collective-permute-start(bf16[128,3072]{1,0:T(8,128)(2,1)S(1)} %get-tuple-element.79), channel_id=1, source_target_pairs={{0,4},{4,0},{8,12},{12,8},{1,5},{5,1},{9,13},{13,9},{2,6},{6,2},{1... | collective-permute-start | bytes 2359304 | tf_op jit(solution)/shard_map/ppermute | solution.py:424
  199.2 12.0 %collective-permute-start.22 = (bf16[64,3072]{1,0:T(8,128)(2,1)S(1)}, bf16[64,3072]{1,0:T(8,128)(2,1)S(1)}, u32[]{:S(2)}, u32[]{:S(2)}) collective-permute-start(bf16[64,3072]{1,0:T(8,128)(2,1)S(1)} %get-tuple-element.84), channel_id=1, source_target_pairs={{0,8},{4,12},{8,0},{12,4},{1,9},{5,13},{9,1},{13,5},{2,10},{6,14},... | collective-permute-start | bytes 1179656 | tf_op jit(solution)/shard_map/ppermute | solution.py:416
  201.4 17.7 %collective-permute-start.21 = (bf16[64,3072]{1,0:T(8,128)(2,1)S(1)}, bf16[64,3072]{1,0:T(8,128)(2,1)S(1)}, u32[]{:S(2)}, u32[]{:S(2)}) collective-permute-start(bf16[64,3072]{1,0:T(8,128)(2,1)S(1)} %get-tuple-element.83), channel_id=1, source_target_pairs={{0,8},{4,12},{8,0},{12,4},{1,9},{5,13},{9,1},{13,5},{2,10},{6,14},... | collective-permute-start | bytes 1179656 | tf_op jit(solution)/shard_map/ppermute | solution.py:416

commit v5 on v4

--- a/solution.py
+++ b/solution.py
@@ -166,13 +166,11 @@
     rows, held, arrived = refs[scratch:scratch + 3]
     half = send_ref.shape[0]
     step = pl.program_id(0)
-    lanes = held.shape[3]
 
     def fetch(index):
+        column = pl.multiple_of(start + index * tile, 128)
         slot = lax.rem(index, slots)
-        for side in range(tile // lanes):
-            column = pl.multiple_of(start + index * tile + side * lanes, 128)
-            yield pltpu.make_async_copy(weight_ref.at[:, pl.ds(column, lanes)], held.at[slot, side], arrived.at[slot, side])
+        return pltpu.make_async_copy(weight_ref.at[:, pl.ds(column, tile)], held.at[slot], arrived.at[slot])
 
     if ending[3]:
         out_ref = refs[scratch - 1]
@@ -185,8 +183,7 @@
     @pl.when(step == 0)
     def _():
         for index in range(min(slots - 1, steps)):
-            for copy in fetch(index):
-                copy.start()
+            fetch(index).start()
         if ending[3]:
             for copy in given:
                 copy.start()
@@ -200,15 +197,12 @@
 
     @pl.when(step + slots - 1 < steps)
     def _():
-        for copy in fetch(step + slots - 1):
-            copy.start()
-
-    for side, copy in enumerate(fetch(step)):
-        copy.wait()
-        out = jnp.dot(rows[...], held[lax.rem(step, slots), side], preferred_element_type=F32)
-        here = slice(side * lanes, (side + 1) * lanes)
-        send_ref[:, here] = out[:half].astype(BF16)
-        keep_ref[:, here] = out[half:].astype(BF16)
+        fetch(step + slots - 1).start()
+
+    fetch(step).wait()
+    out = jnp.dot(rows[...], held[lax.rem(step, slots)], preferred_element_type=F32)
+    send_ref[...] = out[:half].astype(BF16)
+    keep_ref[...] = out[half:].astype(BF16)
 
     if ending[3]:
         @pl.when(step == 0)
@@ -233,15 +227,14 @@
     count = len(blocks)
     height, depth = count * blocks[0].shape[0], blocks[0].shape[1]
     tile = divisor(width, (512, 384, 256, 128))
-    lanes = divisor(tile, (256, 128))
     slots = 4
     half = jax.ShapeDtypeStruct((height // 2, width), BF16)
     outs = [half, half]
     out_specs = [pl.BlockSpec((height // 2, tile), lambda j: (0, j))] * 2
     scratch = [
         pltpu.VMEM((height, depth), BF16),
-        pltpu.VMEM((slots, tile // lanes, depth, lanes), BF16),
-        pltpu.SemaphoreType.DMA((slots, tile // lanes)),
+        pltpu.VMEM((slots, depth, tile), BF16),
+        pltpu.SemaphoreType.DMA((slots,)),
     ]
     operands = [place, weight, *blocks, *terms]
     aliases = {}
@@ -284,7 +277,7 @@
 def pair(chips, keep, got, after, long):
     height, width = keep.shape
     size = height // chips
-    tile = divisor(width, (1536, 1152, 768, 512, 384, 256, 128))
+    tile = width // 2 if width % 256 == 0 else width
     spec = lambda rows: pl.BlockSpec((rows, tile), lambda j: (0, j))
     return pl.pallas_call(
         pair_kernel,
@@ -332,7 +325,7 @@
     return pieces
 
 
-SHARES = ((3, 3), (3, 3), (2, 2, 2))
+SHARES = ((11, 7), (11, 7), (6, 6, 6))
 
 ORDER = (
     ("f0", "p00", "f1", "p01", "t2", "s00"),

time: 220 us -> 184 us (0.84)
  Pallas kernels: 153 us -> 98.6 us
  waiting for transfers between devices: 39.1 us -> 57.6 us
    pallas_call x7, Pallas kernels: 138 us -> 83.5 us  [product(): pl.pallas_call(functools.partial(product_kernel, start, tile, width // ti...]
    ppermute x3, waiting for transfers between devices: 9.15 us -> 18.9 us  [local(): lax.ppermute(given, 'gy', [(0, 2), (1, 0), (2, 3), (3, 1)])]
    ppermute x7, waiting for transfers between devices: 16 us -> 22.7 us  [local(): lax.ppermute(away[(ahead - 1) * size:ahead * size], 'gx', across(ahead))]
    ppermute x6, waiting for transfers between devices: 12.7 us -> 15 us  [swap(): return lax.ppermute(array, 'gy', [(k, k ^ distance) for k in range(n_gy)])]
  transfers between devices with their start and end apart: 23 -> 23, of which waited for: 6 -> 9; matrix products, arithmetic and copies ran while one was open for 0% -> 0% of each run, Pallas kernels for 69% -> 53%
where the time goes in v5:
time: 184 us
  Pallas kernels  98.6 us (54%)
  waiting for transfers between devices  57.6 us (31%)
  starting transfers between devices  23.6 us (13%)
  local copies, waits for them, and re-layouts  3.39 us (2%)
    pallas_call x7, Pallas kernels, product(): pl.pallas_call(functools.partial(product_kernel, start, tile, width // ti...  83.5 us
    ppermute x7, waiting for transfers between devices, local(): lax.ppermute(away[(ahead - 1) * size:ahead * size], 'gx', across(ahead))  22.7 us
    ppermute x3, waiting for transfers between devices, local(): lax.ppermute(given, 'gy', [(0, 2), (1, 0), (2, 3), (3, 1)])  18.9 us
    ppermute x6, waiting for transfers between devices, swap(): return lax.ppermute(array, 'gy', [(k, k ^ distance) for k in range(n_gy)])  15 us
    ppermute x6, starting transfers between devices, swap(): return lax.ppermute(array, 'gy', [(k, k ^ distance) for k in range(n_gy)])  11.6 us
    ppermute x7, starting transfers between devices, local(): lax.ppermute(away[(ahead - 1) * size:ahead * size], 'gx', across(ahead))  7.49 us
    ppermute x3, starting transfers between devices, local(): lax.ppermute(given, 'gy', [(0, 2), (1, 0), (2, 3), (3, 1)])  3.69 us
  transfers between devices with their start and end apart: 23, of which 9 were waited for; matrix products, arithmetic and copies ran while one was open for 0% of the time, Pallas kernels for 53%

profile of v5, /device:TPU:0, one launch (start us, length us, event | category | flops | bytes accessed | tf_op | source)
XLA Modules:
  0.0 183.5 jit_solution(14260125135645657613)
XLA Ops:
  0.0 1.0 slice.3.refs_0_
  1.1 3.1 %collective-permute-start = (bf16[64,3584]{1,0:T(8,128)(2,1)S(1)}, bf16[64,3584]{1,0:T(8,128)(2,1)S(1)}, u32[]{:S(2)}, u32[]{:S(2)}) collective-permute-start(bf16[64,3584]{1,0:T(8,128)(2,1)S(1)} %slice.3.refs_0_), channel_id=1, source_target_pairs={{0,1},{1,0},{2,3},{3,2},{4,5},{5,4},{6,7},{7,6},{8,9},{9,8},{10,11... | collective-permute-start | bytes 1376264 | tf_op jit(solution)/shard_map/ppermute | solution.py:350
  4.1 2.6 %collective-permute-start.1 = (bf16[64,3584]{1,0:T(8,128)(2,1)S(1)}, bf16[64,3584]{1,0:T(8,128)(2,1)S(1)}, u32[]{:S(2)}, u32[]{:S(2)}) collective-permute-start(bf16[64,3584]{1,0:T(8,128)(2,1)S(1)} %slice.3.refs_0_), channel_id=1, source_target_pairs={{0,2},{1,3},{2,0},{3,1},{4,6},{5,7},{6,4},{7,5},{8,10},{9,11},{10,... | collective-permute-start | bytes 1376264 | tf_op jit(solution)/shard_map/ppermute | solution.py:350
  7.6 2.0 %onehot.1.onehot_ref = bf16[768,256]{1,0:T(8,128)(2,1)S(1)} custom-call(s32[768,1]{1,0:T(8,128)S(1)} %broadcast_in_dim.4.parents_ref), custom_call_target="tpu_custom_call" | custom-call | flops 19327352832 | bytes 12582912 | tf_op jit(solution)/shard_map/onehot/pallas_call | solution.py:53
  9.7 1.5 copy-done.1
  11.2 1.9 %own.1 = (bf16[64,3584]{1,0:T(8,128)(2,1)S(1)}, bf16[64,3584]{1,0:T(8,128)(2,1)S(1)}) custom-call(s32[2]{0:T(128)S(1)} %pad_add_fusion.place_ref, bf16[768,256]{1,0:T(8,128)(2,1)S(1)} %onehot.1.onehot_ref, bf16[256,3584]{1,0:T(8,128)(2,1)S(1)} %copy-done.1, bf16[192,3584]{1,0:T(8,128)(2,1)S(1)} %copy-done), custom_call_target="tpu_custom_call" | custom-call | flops 1879048192 | bytes 22020096 | tf_op jit(solution)/shard_map/own/pallas_call | solution.py:136
  13.1 11.3 %collective-permute-done.near_ref.refs_1_ = bf16[64,3584]{1,0:T(8,128)(2,1)S(1)} collective-permute-done((bf16[64,3584]{1,0:T(8,128)(2,1)S(1)}, bf16[64,3584]{1,0:T(8,128)(2,1)S(1)}, u32[]{:S(2)}, u32[]{:S(2)}) %collective-permute-start) | collective-permute-done | bytes 458784 | tf_op jit(solution)/shard_map/ppermute | solution.py:350
  24.4 2.5 %collective-permute-done.1.far_ref.refs_2_ = bf16[64,3584]{1,0:T(8,128)(2,1)S(1)} collective-permute-done((bf16[64,3584]{1,0:T(8,128)(2,1)S(1)}, bf16[64,3584]{1,0:T(8,128)(2,1)S(1)}, u32[]{:S(2)}, u32[]{:S(2)}) %collective-permute-start.1) | collective-permute-done | bytes 458784 | tf_op jit(solution)/shard_map/ppermute | solution.py:350
  27.9 1.7 collective-permute-start.3
  29.6 1.3 collective-permute-start.4
  30.9 18.9 %collective-permute-done.2.refs_3_ = bf16[64,3584]{1,0:T(8,128)(2,1)S(1)} collective-permute-done((bf16[64,3584]{1,0:T(8,128)(2,1)S(1)}, bf16[64,3584]{1,0:T(8,128)(2,1)S(1)}, u32[]{:S(2)}, u32[]{:S(2)}) %collective-permute-start.2) | collective-permute-done | bytes 458784 | tf_op jit(solution)/shard_map/ppermute | solution.py:384
  49.8 2.6 %embed.1.refs_0_ = bf16[256,3584]{1,0:T(8,128)(2,1)S(1)} custom-call(s32[2]{0:T(128)S(1)} %pad_add_fusion.place_ref, bf16[768,256]{1,0:T(8,128)(2,1)S(1)} %onehot.1.onehot_ref, bf16[256,3584]{1,0:T(8,128)(2,1)S(1)} %copy-done.1, bf16[64,3584]{1,0:T(8,128)(2,1)S(1)} %slice.3.refs_0_, bf16[64,3584]{1,0:T(8,128)(2,1)S(1)} %collective-permute-done.near_ref.refs_1_, ...), custom_call_target="tpu_custom_call" | custom-call | flops 3758096384 | bytes 44040192 | tf_op jit(solution)/shard_map/embed/pallas_call | solution.py:109
  52.5 15.3 %product.7 = (bf16[128,5632]{1,0:T(8,128)(2,1)S(1)}, bf16[128,5632]{1,0:T(8,128)(2,1)S(1)}) custom-call(s32[2]{0:T(128)S(1)} %pad_add_fusion.place_ref, bf16[3584,9216]{1,0:T(8,128)(2,1)} %weight_ref.13, bf16[256,3584]{1,0:T(8,128)(2,1)S(1)} %embed.1.refs_0_, bf16[64,3584]{1,0:T(8,128)(2,1)S(1)} %forward.3.refs_4_.refs_1_), custom_call_target="tpu_custom_call" | custom-call | flops 82678120448 | bytes 360710144 | tf_op jit(solution)/shard_map/product/pallas_call | solution.py:255
  68.4 1.2 collective-permute-start.8
  69.7 10.7 %product.8 = (bf16[128,3584]{1,0:T(8,128)(2,1)S(1)}, bf16[128,3584]{1,0:T(8,128)(2,1)S(1)}) custom-call(s32[2]{0:T(128)S(1)} %pad_add_fusion.place_ref, bf16[3584,9216]{1,0:T(8,128)(2,1)} %weight_ref.13, bf16[256,3584]{1,0:T(8,128)(2,1)S(1)} %embed.1.refs_0_, bf16[64,3584]{1,0:T(8,128)(2,1)S(1)} %forward.4.refs_1_), custom_call_target="tpu_custom_call" | custom-call | flops 52613349376 | bytes 234881024 | tf_op jit(solution)/shard_map/product/pallas_call | solution.py:255
  81.3 2.0 %collective-permute-start.6 = (bf16[64,3584]{1,0:T(8,128)(2,1)S(1)}, bf16[64,3584]{1,0:T(8,128)(2,1)S(1)}, u32[]{:S(2)}, u32[]{:S(2)}) collective-permute-start(bf16[64,3584]{1,0:T(8,128)(2,1)S(1)} %get-tuple-element.52.refs_0_), channel_id=1, source_target_pairs={{0,2},{1,3},{2,0},{3,1},{4,6},{5,7},{6,4},{7,5},{8,10},{9,11},{10,... | collective-permute-start | bytes 1376264 | tf_op jit(solution)/shard_map/ppermute | solution.py:350
  83.9 1.6 collective-permute-start.11
  85.5 15.4 %product.9 = (bf16[128,5632]{1,0:T(8,128)(2,1)S(1)}, bf16[128,5632]{1,0:T(8,128)(2,1)S(1)}) custom-call(s32[2]{0:T(128)S(1)} %pad_add_fusion.place_ref, bf16[3584,9216]{1,0:T(8,128)(2,1)} %weight_ref.13, bf16[64,3584]{1,0:T(8,128)(2,1)S(1)} %get-tuple-element.49.refs_0_, bf16[64,3584]{1,0:T(8,128)(2,1)S(1)} %collective-permute-done.3.near_ref.refs_1_, ...), custom_call_target="tpu_custom_call" | custom-call | flops 82678120448 | bytes 360710144 | tf_op jit(solution)/shard_map/product/pallas_call | solution.py:255
  101.6 1.2 collective-permute-done.5.near_ref.refs_1_
  103.5 2.1 %collective-permute-start.10 = (bf16[64,3584]{1,0:T(8,128)(2,1)S(1)}, bf16[64,3584]{1,0:T(8,128)(2,1)S(1)}, u32[]{:S(2)}, u32[]{:S(2)}) collective-permute-start(bf16[64,3584]{1,0:T(8,128)(2,1)S(1)} %forward.5.refs_6_), channel_id=1, source_target_pairs={{0,2},{1,0},{2,3},{3,1},{4,6},{5,4},{6,7},{7,5},{8,10},{9,8},{10,1... | collective-permute-start | bytes 1376264 | tf_op jit(solution)/shard_map/ppermute | solution.py:384
  105.5 1.5 collective-permute-start.13
  107.0 11.6 %product.10 = (bf16[128,3584]{1,0:T(8,128)(2,1)S(1)}, bf16[128,3584]{1,0:T(8,128)(2,1)S(1)}, bf16[192,9216]{1,0:T(8,128)(2,1)}) custom-call(s32[2]{0:T(128)S(1)} %pad_add_fusion.place_ref, bf16[3584,9216]{1,0:T(8,128)(2,1)} %weight_ref.13, bf16[64,3584]{1,0:T(8,128)(2,1)S(1)} %get-tuple-element.49.refs_0_, ...), custom_call_target="tpu_custom_call" | custom-call | flops 52613349376 | bytes 234881024 | tf_op jit(solution)/shard_map/product/pallas_call | solution.py:255
  120.0 10.1 %product.11 = (bf16[128,3072]{1,0:T(8,128)(2,1)S(1)}, bf16[128,3072]{1,0:T(8,128)(2,1)S(1)}, bf16[192,9216]{1,0:T(8,128)(2,1)}) custom-call(s32[2]{0:T(128)S(1)} %pad_add_fusion.place_ref, bf16[3584,9216]{1,0:T(8,128)(2,1)} %weight_ref.13, bf16[64,3584]{1,0:T(8,128)(2,1)S(1)} %get-tuple-element.52.refs_0_, ...), custom_call_target="tpu_custom_call", output_to_operand_aliasing={{2}: (8, {})} | custom-call | flops 45097156608 | bytes 203423744 | tf_op jit(solution)/shard_map/product/pallas_call | solution.py:255
  130.9 1.6 collective-permute-start.15
  132.4 6.0 %collective-permute-done.16.refs_5_ = bf16[64,5632]{1,0:T(8,128)(2,1)S(1)} collective-permute-done((bf16[64,5632]{1,0:T(8,128)(2,1)S(1)}, bf16[64,5632]{1,0:T(8,128)(2,1)S(1)}, u32[]{:S(2)}, u32[]{:S(2)}) %collective-permute-start.16) | collective-permute-done | bytes 720928 | tf_op jit(solution)/shard_map/ppermute | solution.py:409
  138.4 10.4 %product.12 = (bf16[128,3072]{1,0:T(8,128)(2,1)S(1)}, bf16[128,3072]{1,0:T(8,128)(2,1)S(1)}, bf16[192,9216]{1,0:T(8,128)(2,1)}) custom-call(s32[2]{0:T(128)S(1)} %pad_add_fusion.place_ref, bf16[3584,9216]{1,0:T(8,128)(2,1)} %weight_ref.13, bf16[64,3584]{1,0:T(8,128)(2,1)S(1)} %get-tuple-element.52.refs_0_, ...), custom_call_target="tpu_custom_call", output_to_operand_aliasing={{2}: (8, {})} | custom-call | flops 45097156608 | bytes 203423744 | tf_op jit(solution)/shard_map/product/pallas_call | solution.py:255
  149.9 10.1 %product.13 = (bf16[128,3072]{1,0:T(8,128)(2,1)S(1)}, bf16[128,3072]{1,0:T(8,128)(2,1)S(1)}, bf16[192,9216]{1,0:T(8,128)(2,1)}) custom-call(s32[2]{0:T(128)S(1)} %pad_add_fusion.place_ref, bf16[3584,9216]{1,0:T(8,128)(2,1)} %weight_ref.13, bf16[64,3584]{1,0:T(8,128)(2,1)S(1)} %get-tuple-element.52.refs_0_, ...), custom_call_target="tpu_custom_call", output_to_operand_aliasing={{2}: (8, {})} | custom-call | flops 45097156608 | bytes 203423744 | tf_op jit(solution)/shard_map/product/pallas_call | solution.py:255
  160.9 1.1 finish.3
  165.4 8.9 %collective-permute-done.22.refs_1_ = bf16[64,3072]{1,0:T(8,128)(2,1)S(1)} collective-permute-done((bf16[64,3072]{1,0:T(8,128)(2,1)S(1)}, bf16[64,3072]{1,0:T(8,128)(2,1)S(1)}, u32[]{:S(2)}, u32[]{:S(2)}) %collective-permute-start.22) | collective-permute-done | bytes 393248 | tf_op jit(solution)/shard_map/ppermute | solution.py:409
  174.4 1.1 finish.4
  175.5 6.9 %collective-permute-done.21.refs_1_ = bf16[64,3072]{1,0:T(8,128)(2,1)S(1)} collective-permute-done((bf16[64,3072]{1,0:T(8,128)(2,1)S(1)}, bf16[64,3072]{1,0:T(8,128)(2,1)S(1)}, u32[]{:S(2)}, u32[]{:S(2)}) %collective-permute-start.21) | collective-permute-done | bytes 393248 | tf_op jit(solution)/shard_map/ppermute | solution.py:409
  182.4 1.1 finish.5
  (44 shorter events, 12.9 us)
Async XLA Ops:
  1.1 23.3 %collective-permute-start = (bf16[64,3584]{1,0:T(8,128)(2,1)S(1)}, bf16[64,3584]{1,0:T(8,128)(2,1)S(1)}, u32[]{:S(2)}, u32[]{:S(2)}) collective-permute-start(bf16[64,3584]{1,0:T(8,128)(2,1)S(1)} %slice.3.refs_0_), channel_id=1, source_target_pairs={{0,1},{1,0},{2,3},{3,2},{4,5},{5,4},{6,7},{7,6},{8,9},{9,8},{10,11... | collective-permute-start | bytes 1376264 | tf_op jit(solution)/shard_map/ppermute | solution.py:350
  4.1 22.8 %collective-permute-start.1 = (bf16[64,3584]{1,0:T(8,128)(2,1)S(1)}, bf16[64,3584]{1,0:T(8,128)(2,1)S(1)}, u32[]{:S(2)}, u32[]{:S(2)}) collective-permute-start(bf16[64,3584]{1,0:T(8,128)(2,1)S(1)} %slice.3.refs_0_), channel_id=1, source_target_pairs={{0,2},{1,3},{2,0},{3,1},{4,6},{5,7},{6,4},{7,5},{8,10},{9,11},{10,... | collective-permute-start | bytes 1376264 | tf_op jit(solution)/shard_map/ppermute | solution.py:350
  7.6 2.1 %copy-start = (bf16[192,3584]{1,0:T(8,128)(2,1)S(1)}, bf16[192,3584]{1,0:T(8,128)(2,1)}, u32[]{:S(2)}) copy-start(bf16[192,3584]{1,0:T(8,128)(2,1)} %hidden_ref.1) | copy-start | bytes 4128772
  9.7 1.5 copy-start.1
  27.5 22.3 %collective-permute-start.2 = (bf16[64,3584]{1,0:T(8,128)(2,1)S(1)}, bf16[64,3584]{1,0:T(8,128)(2,1)S(1)}, u32[]{:S(2)}, u32[]{:S(2)}) collective-permute-start(bf16[64,3584]{1,0:T(8,128)(2,1)S(1)} %forward.3.refs_4_.refs_1_), channel_id=1, source_target_pairs={{0,2},{1,0},{2,3},{3,1},{4,6},{5,4},{6,7},{7,5},{8,10},{9,8},{10,1... | collective-permute-start | bytes 1376264 | tf_op jit(solution)/shard_map/ppermute | solution.py:384
  27.9 40.0 %collective-permute-start.3 = (bf16[64,3584]{1,0:T(8,128)(2,1)S(1)}, bf16[64,3584]{1,0:T(8,128)(2,1)S(1)}, u32[]{:S(2)}, u32[]{:S(2)}) collective-permute-start(bf16[64,3584]{1,0:T(8,128)(2,1)S(1)} %get-tuple-element.49.refs_0_), channel_id=1, source_target_pairs={{0,1},{1,0},{2,3},{3,2},{4,5},{5,4},{6,7},{7,6},{8,9},{9,8},{10,11... | collective-permute-start | bytes 1376264 | tf_op jit(solution)/shard_map/ppermute | solution.py:350
  29.6 38.3 %collective-permute-start.4 = (bf16[64,3584]{1,0:T(8,128)(2,1)S(1)}, bf16[64,3584]{1,0:T(8,128)(2,1)S(1)}, u32[]{:S(2)}, u32[]{:S(2)}) collective-permute-start(bf16[64,3584]{1,0:T(8,128)(2,1)S(1)} %get-tuple-element.49.refs_0_), channel_id=1, source_target_pairs={{0,2},{1,3},{2,0},{3,1},{4,6},{5,7},{6,4},{7,5},{8,10},{9,11},{10,... | collective-permute-start | bytes 1376264 | tf_op jit(solution)/shard_map/ppermute | solution.py:350
  67.7 15.5 %collective-permute-start.9 = (bf16[128,5632]{1,0:T(8,128)(2,1)S(1)}, bf16[128,5632]{1,0:T(8,128)(2,1)S(1)}, u32[]{:S(2)}, u32[]{:S(2)}) collective-permute-start(bf16[128,5632]{1,0:T(8,128)(2,1)S(1)} %get-tuple-element.54), channel_id=1, source_target_pairs={{0,4},{4,0},{8,12},{12,8},{1,5},{5,1},{9,13},{13,9},{2,6},{6,2},{1... | collective-permute-start | bytes 4325384 | tf_op jit(solution)/shard_map/ppermute | solution.py:405
  68.4 17.1 %collective-permute-start.8 = (bf16[64,3584]{1,0:T(8,128)(2,1)S(1)}, bf16[64,3584]{1,0:T(8,128)(2,1)S(1)}, u32[]{:S(2)}, u32[]{:S(2)}) collective-permute-start(bf16[64,3584]{1,0:T(8,128)(2,1)S(1)} %forward.4.refs_1_), channel_id=1, source_target_pairs={{0,2},{1,0},{2,3},{3,1},{4,6},{5,4},{6,7},{7,5},{8,10},{9,8},{10,1... | collective-permute-start | bytes 1376264 | tf_op jit(solution)/shard_map/ppermute | solution.py:384
  80.4 22.5 %collective-permute-start.5 = (bf16[64,3584]{1,0:T(8,128)(2,1)S(1)}, bf16[64,3584]{1,0:T(8,128)(2,1)S(1)}, u32[]{:S(2)}, u32[]{:S(2)}) collective-permute-start(bf16[64,3584]{1,0:T(8,128)(2,1)S(1)} %get-tuple-element.52.refs_0_), channel_id=1, source_target_pairs={{0,1},{1,0},{2,3},{3,2},{4,5},{5,4},{6,7},{7,6},{8,9},{9,8},{10,11... | collective-permute-start | bytes 1376264 | tf_op jit(solution)/shard_map/ppermute | solution.py:350
  81.3 21.6 %collective-permute-start.6 = (bf16[64,3584]{1,0:T(8,128)(2,1)S(1)}, bf16[64,3584]{1,0:T(8,128)(2,1)S(1)}, u32[]{:S(2)}, u32[]{:S(2)}) collective-permute-start(bf16[64,3584]{1,0:T(8,128)(2,1)S(1)} %get-tuple-element.52.refs_0_), channel_id=1, source_target_pairs={{0,2},{1,3},{2,0},{3,1},{4,6},{5,7},{6,4},{7,5},{8,10},{9,11},{10,... | collective-permute-start | bytes 1376264 | tf_op jit(solution)/shard_map/ppermute | solution.py:350
  83.3 17.9 %collective-permute-start.7 = (bf16[128,3584]{1,0:T(8,128)(2,1)S(1)}, bf16[128,3584]{1,0:T(8,128)(2,1)S(1)}, u32[]{:S(2)}, u32[]{:S(2)}) collective-permute-start(bf16[128,3584]{1,0:T(8,128)(2,1)S(1)} %get-tuple-element.53), channel_id=1, source_target_pairs={{0,4},{4,0},{8,12},{12,8},{1,5},{5,1},{9,13},{13,9},{2,6},{6,2},{1... | collective-permute-start | bytes 2752520 | tf_op jit(solution)/shard_map/ppermute | solution.py:405
  83.9 23.1 %collective-permute-start.11 = (bf16[64,5632]{1,0:T(8,128)(2,1)S(1)}, bf16[64,5632]{1,0:T(8,128)(2,1)S(1)}, u32[]{:S(2)}, u32[]{:S(2)}) collective-permute-start(bf16[64,5632]{1,0:T(8,128)(2,1)S(1)} %get-tuple-element.58), channel_id=1, source_target_pairs={{0,8},{4,12},{8,0},{12,4},{1,9},{5,13},{9,1},{13,5},{2,10},{6,14},... | collective-permute-start | bytes 2162696 | tf_op jit(solution)/shard_map/ppermute | solution.py:409
  100.9 17.8 %collective-permute-start.14 = (bf16[128,5632]{1,0:T(8,128)(2,1)S(1)}, bf16[128,5632]{1,0:T(8,128)(2,1)S(1)}, u32[]{:S(2)}, u32[]{:S(2)}) collective-permute-start(bf16[128,5632]{1,0:T(8,128)(2,1)S(1)} %get-tuple-element.63), channel_id=1, source_target_pairs={{0,4},{4,0},{8,12},{12,8},{1,5},{5,1},{9,13},{13,9},{2,6},{6,2},{1... | collective-permute-start | bytes 4325384 | tf_op jit(solution)/shard_map/ppermute | solution.py:405
  103.5 16.5 %collective-permute-start.10 = (bf16[64,3584]{1,0:T(8,128)(2,1)S(1)}, bf16[64,3584]{1,0:T(8,128)(2,1)S(1)}, u32[]{:S(2)}, u32[]{:S(2)}) collective-permute-start(bf16[64,3584]{1,0:T(8,128)(2,1)S(1)} %forward.5.refs_6_), channel_id=1, source_target_pairs={{0,2},{1,0},{2,3},{3,1},{4,6},{5,4},{6,7},{7,5},{8,10},{9,8},{10,1... | collective-permute-start | bytes 1376264 | tf_op jit(solution)/shard_map/ppermute | solution.py:384
  105.5 14.5 %collective-permute-start.13 = (bf16[64,3584]{1,0:T(8,128)(2,1)S(1)}, bf16[64,3584]{1,0:T(8,128)(2,1)S(1)}, u32[]{:S(2)}, u32[]{:S(2)}) collective-permute-start(bf16[64,3584]{1,0:T(8,128)(2,1)S(1)} %get-tuple-element.61), channel_id=1, source_target_pairs={{0,8},{4,12},{8,0},{12,4},{1,9},{5,13},{9,1},{13,5},{2,10},{6,14},... | collective-permute-start | bytes 1376264 | tf_op jit(solution)/shard_map/ppermute | solution.py:409
  118.6 11.8 %collective-permute-start.12 = (bf16[128,3584]{1,0:T(8,128)(2,1)S(1)}, bf16[128,3584]{1,0:T(8,128)(2,1)S(1)}, u32[]{:S(2)}, u32[]{:S(2)}) collective-permute-start(bf16[128,3584]{1,0:T(8,128)(2,1)S(1)} %get-tuple-element.60), channel_id=1, source_target_pairs={{0,4},{4,0},{8,12},{12,8},{1,5},{5,1},{9,13},{13,9},{2,6},{6,2},{1... | collective-permute-start | bytes 2752520 | tf_op jit(solution)/shard_map/ppermute | solution.py:405
  119.4 19.0 %collective-permute-start.16 = (bf16[64,5632]{1,0:T(8,128)(2,1)S(1)}, bf16[64,5632]{1,0:T(8,128)(2,1)S(1)}, u32[]{:S(2)}, u32[]{:S(2)}) collective-permute-start(bf16[64,5632]{1,0:T(8,128)(2,1)S(1)} %get-tuple-element.68), channel_id=1, source_target_pairs={{0,8},{4,12},{8,0},{12,4},{1,9},{5,13},{9,1},{13,5},{2,10},{6,14},... | collective-permute-start | bytes 2162696 | tf_op jit(solution)/shard_map/ppermute | solution.py:409
  130.1 18.7 %collective-permute-start.17 = (bf16[128,3072]{1,0:T(8,128)(2,1)S(1)}, bf16[128,3072]{1,0:T(8,128)(2,1)S(1)}, u32[]{:S(2)}, u32[]{:S(2)}) collective-permute-start(bf16[128,3072]{1,0:T(8,128)(2,1)S(1)} %get-tuple-element.71), channel_id=1, source_target_pairs={{0,4},{4,0},{8,12},{12,8},{1,5},{5,1},{9,13},{13,9},{2,6},{6,2},{1... | collective-permute-start | bytes 2359304 | tf_op jit(solution)/shard_map/ppermute | solution.py:405
  130.9 19.0 %collective-permute-start.15 = (bf16[64,3584]{1,0:T(8,128)(2,1)S(1)}, bf16[64,3584]{1,0:T(8,128)(2,1)S(1)}, u32[]{:S(2)}, u32[]{:S(2)}) collective-permute-start(bf16[64,3584]{1,0:T(8,128)(2,1)S(1)} %get-tuple-element.67), channel_id=1, source_target_pairs={{0,8},{4,12},{8,0},{12,4},{1,9},{5,13},{9,1},{13,5},{2,10},{6,14},... | collective-permute-start | bytes 1376264 | tf_op jit(solution)/shard_map/ppermute | solution.py:409
  148.8 13.2 %collective-permute-start.20 = (bf16[128,3072]{1,0:T(8,128)(2,1)S(1)}, bf16[128,3072]{1,0:T(8,128)(2,1)S(1)}, u32[]{:S(2)}, u32[]{:S(2)}) collective-permute-start(bf16[128,3072]{1,0:T(8,128)(2,1)S(1)} %get-tuple-element.80), channel_id=1, source_target_pairs={{0,4},{4,0},{8,12},{12,8},{1,5},{5,1},{9,13},{13,9},{2,6},{6,2},{1... | collective-permute-start | bytes 2359304 | tf_op jit(solution)/shard_map/ppermute | solution.py:405
  149.3 11.6 %collective-permute-start.18 = (bf16[64,3072]{1,0:T(8,128)(2,1)S(1)}, bf16[64,3072]{1,0:T(8,128)(2,1)S(1)}, u32[]{:S(2)}, u32[]{:S(2)}) collective-permute-start(bf16[64,3072]{1,0:T(8,128)(2,1)S(1)} %get-tuple-element.76), channel_id=1, source_target_pairs={{0,8},{4,12},{8,0},{12,4},{1,9},{5,13},{9,1},{13,5},{2,10},{6,14},... | collective-permute-start | bytes 1179656 | tf_op jit(solution)/shard_map/ppermute | solution.py:409
  162.0 2.3 %collective-permute-start.19 = (bf16[128,3072]{1,0:T(8,128)(2,1)S(1)}, bf16[128,3072]{1,0:T(8,128)(2,1)S(1)}, u32[]{:S(2)}, u32[]{:S(2)}) collective-permute-start(bf16[128,3072]{1,0:T(8,128)(2,1)S(1)} %get-tuple-element.79), channel_id=1, source_target_pairs={{0,4},{4,0},{8,12},{12,8},{1,5},{5,1},{9,13},{13,9},{2,6},{6,2},{1... | collective-permute-start | bytes 2359304 | tf_op jit(solution)/shard_map/ppermute | solution.py:417
  162.4 12.0 %collective-permute-start.22 = (bf16[64,3072]{1,0:T(8,128)(2,1)S(1)}, bf16[64,3072]{1,0:T(8,128)(2,1)S(1)}, u32[]{:S(2)}, u32[]{:S(2)}) collective-permute-start(bf16[64,3072]{1,0:T(8,128)(2,1)S(1)} %get-tuple-element.84), channel_id=1, source_target_pairs={{0,8},{4,12},{8,0},{12,4},{1,9},{5,13},{9,1},{13,5},{2,10},{6,14},... | collective-permute-start | bytes 1179656 | tf_op jit(solution)/shard_map/ppermute | solution.py:409
  164.7 17.7 %collective-permute-start.21 = (bf16[64,3072]{1,0:T(8,128)(2,1)S(1)}, bf16[64,3072]{1,0:T(8,128)(2,1)S(1)}, u32[]{:S(2)}, u32[]{:S(2)}) collective-permute-start(bf16[64,3072]{1,0:T(8,128)(2,1)S(1)} %get-tuple-element.83), channel_id=1, source_target_pairs={{0,8},{4,12},{8,0},{12,4},{1,9},{5,13},{9,1},{13,5},{2,10},{6,14},... | collective-permute-start | bytes 1179656 | tf_op jit(solution)/shard_map/ppermute | solution.py:409

commit v6 on v5

--- a/solution.py
+++ b/solution.py
@@ -89,34 +89,57 @@
     return jnp.where(lax.rem(gx, 2) == lax.rem(dest, 2), chips, 0) + ahead
 
 
-def embed_kernel(count, chips, block, first, exclusive, place_ref, onehot_ref, table_ref, *refs):
+def look_kernel(count, chips, block, first, exclusive, place_ref, onehot_ref, table_ref, *refs):
+    looked_ref = refs[-1]
+    size = looked_ref.shape[0] // count
+    for dest in range(count):
+        here = pl.ds(dest * block + first, size)
+        looked = jnp.dot(onehot_ref[here, :], table_ref[...], preferred_element_type=F32)
+        slot = pl.multiple_of(slot_of(dest, chips, place_ref[0]) * size, 16)
+        looked_ref[pl.ds(slot, size), :] = looked.astype(BF16)
+
+
+def look(chips, count, block, first, size, exclusive, place, onehot, table, after):
+    depth = table.shape[1]
+    tile = divisor(depth, (896, 512, 256, 128))
+    return pl.pallas_call(
+        functools.partial(look_kernel, count, chips, block, first, exclusive),
+        name="look",
+        grid=(depth // tile,),
+        out_shape=jax.ShapeDtypeStruct((count * size, depth), BF16),
+        in_specs=[SMEM, pl.BlockSpec(onehot.shape, lambda j: (0, 0)), pl.BlockSpec((table.shape[0], tile), lambda j: (0, j))]
+        + [ANY] * len(after),
+        out_specs=pl.BlockSpec((count * size, tile), lambda j: (0, j)),
+        compiler_params=params(16),
+        cost_estimate=cost(2 * count * size * table.shape[0] * depth, 4 * count * size * depth),
+    )(place, onehot, table, *after)
+
+
+def arrange_kernel(count, chips, exclusive, added, place_ref, *refs):
     rows_ref = refs[-1]
     size = rows_ref.shape[0] // count
     for held in range(count):
         dest = lax.bitwise_xor(place_ref[1], held) if exclusive else held
-        slot = slot_of(dest, chips, place_ref[0])
-        here = pl.ds(pl.multiple_of(dest * block + first, 16), size)
-        looked = jnp.dot(onehot_ref[here, :], table_ref[...], preferred_element_type=F32)
-        total = refs[held][...].astype(F32) + looked
-        rows_ref[pl.ds(pl.multiple_of(slot * size, 16), size), :] = total.astype(BF16)
-
-
-def embed(chips, block, first, exclusive, place, onehot, table, held, after):
+        here = pl.ds(pl.multiple_of(slot_of(dest, chips, place_ref[0]) * size, 16), size)
+        if added:
+            rows_ref[here, :] = (refs[held][...].astype(F32) + refs[count][here, :].astype(F32)).astype(BF16)
+        else:
+            rows_ref[here, :] = refs[held][...]
+
+
+def arrange(chips, exclusive, place, held, looked, after):
     count = len(held)
     size, depth = held[0].shape
-    tile = divisor(depth, (896, 512, 256, 128))
-    piece = pl.BlockSpec((size, tile), lambda j: (0, j))
-    return pl.pallas_call(
-        functools.partial(embed_kernel, count, chips, block, first, exclusive),
-        name="embed",
-        grid=(depth // tile,),
+    added = [] if looked is None else [looked]
+    return pl.pallas_call(
+        functools.partial(arrange_kernel, count, chips, exclusive, bool(added)),
+        name="arrange",
         out_shape=jax.ShapeDtypeStruct((count * size, depth), BF16),
-        in_specs=[SMEM, pl.BlockSpec(onehot.shape, lambda j: (0, 0)), pl.BlockSpec((table.shape[0], tile), lambda j: (0, j))]
-        + [piece] * count + [ANY] * len(after),
-        out_specs=pl.BlockSpec((count * size, tile), lambda j: (0, j)),
-        compiler_params=params(16),
-        cost_estimate=cost(2 * count * size * table.shape[0] * depth, 6 * count * size * depth),
-    )(place, onehot, table, *held, *after)
+        in_specs=[SMEM] + [VMEM] * (count + len(added)) + [ANY] * len(after),
+        out_specs=VMEM,
+        compiler_params=params(16),
+        cost_estimate=cost(count * size * depth, 6 * count * size * depth),
+    )(place, *held, *added, *after)
 
 
 def embed_own_kernel(block, first, place_ref, onehot_ref, table_ref, hidden_ref, *refs):
@@ -157,13 +180,12 @@
     return jax.nn.gelu(total, approximate=True).astype(BF16)
 
 
-def product_kernel(start, tile, steps, slots, chips, count, exclusive, ending, place_ref, weight_ref, *refs):
-    blocks = refs[:count]
-    terms = refs[count:count + ending[3]]
+def product_kernel(start, tile, steps, slots, ending, rows_ref, weight_ref, *refs):
+    terms = refs[:ending[3]]
     outs = 2 if not ending[3] else 3
-    scratch = len(refs) - (3 if not ending[3] else 7)
+    scratch = len(refs) - (2 if not ending[3] else 6)
     send_ref, keep_ref = refs[scratch - outs:scratch - outs + 2]
-    rows, held, arrived = refs[scratch:scratch + 3]
+    held, arrived = refs[scratch:scratch + 2]
     half = send_ref.shape[0]
     step = pl.program_id(0)
 
@@ -174,7 +196,7 @@
 
     if ending[3]:
         out_ref = refs[scratch - 1]
-        term_buffer, out_buffer, term_sems, out_sem = refs[scratch + 3:]
+        term_buffer, out_buffer, term_sems, out_sem = refs[scratch + 2:]
         row, column, width, number = ending
         given = [pltpu.make_async_copy(terms[n], term_buffer.at[n], term_sems.at[n]) for n in range(number)]
         place_out = out_ref.at[row:row + out_buffer.shape[0], column:column + width]
@@ -187,20 +209,13 @@
         if ending[3]:
             for copy in given:
                 copy.start()
-        size = rows.shape[0] // count
-        for index in range(count):
-            first = 0
-            if count > 1:
-                dest = lax.bitwise_xor(place_ref[1], index) if exclusive else index
-                first = pl.multiple_of(slot_of(dest, chips, place_ref[0]) * size, 16)
-            rows[pl.ds(first, size), :] = blocks[index][...]
 
     @pl.when(step + slots - 1 < steps)
     def _():
         fetch(step + slots - 1).start()
 
     fetch(step).wait()
-    out = jnp.dot(rows[...], held[lax.rem(step, slots)], preferred_element_type=F32)
+    out = jnp.dot(rows_ref[...], held[lax.rem(step, slots)], preferred_element_type=F32)
     send_ref[...] = out[:half].astype(BF16)
     keep_ref[...] = out[half:].astype(BF16)
 
@@ -223,20 +238,18 @@
             taken.wait()
 
 
-def product(chips, exclusive, place, blocks, weight, start, width, after, ending=None, terms=(), out=None, shape=None):
-    count = len(blocks)
-    height, depth = count * blocks[0].shape[0], blocks[0].shape[1]
+def product(rows, weight, start, width, after, ending=None, terms=(), out=None, shape=None):
+    height, depth = rows.shape
     tile = divisor(width, (512, 384, 256, 128))
     slots = 4
     half = jax.ShapeDtypeStruct((height // 2, width), BF16)
     outs = [half, half]
     out_specs = [pl.BlockSpec((height // 2, tile), lambda j: (0, j))] * 2
     scratch = [
-        pltpu.VMEM((height, depth), BF16),
         pltpu.VMEM((slots, depth, tile), BF16),
         pltpu.SemaphoreType.DMA((slots,)),
     ]
-    operands = [place, weight, *blocks, *terms]
+    operands = [rows, weight, *terms]
     aliases = {}
     ending = (0, 0, 0, 0) if not terms else (*ending, terms[0].shape[1], len(terms))
     if terms:
@@ -253,11 +266,11 @@
             operands.append(out)
     operands += after
     return pl.pallas_call(
-        functools.partial(product_kernel, start, tile, width // tile, slots, chips, count, exclusive, ending),
+        functools.partial(product_kernel, start, tile, width // tile, slots, ending),
         name="product",
         grid=(width // tile,),
         out_shape=outs,
-        in_specs=[SMEM, ANY] + [VMEM] * count + [ANY] * (len(operands) - 2 - count),
+        in_specs=[VMEM] + [ANY] * (len(operands) - 1),
         out_specs=out_specs,
         scratch_shapes=scratch,
         input_output_aliases=aliases,
@@ -328,9 +341,9 @@
 SHARES = ((11, 7), (11, 7), (6, 6, 6))
 
 ORDER = (
-    ("f0", "p00", "f1", "p01", "t2", "s00"),
-    ("p10", "s01", "f2", "p11-00", "s10"),
-    ("p20-01", "s11", "p21-10", "s20", "p22-11+", "g20!"),
+    ("f0", "a0", "p00", "f1", "p01", "t2", "s00"),
+    ("a1", "p10", "s01", "f2", "p11-00", "s10"),
+    ("a2", "p20-01", "s11", "p21-10", "s20", "p22-11+", "g20!"),
     ("s21!", "s22", "g21", "g22"),
 )
 
@@ -358,7 +371,7 @@
             held[index] = [whole[k] for k in range(n_gy)]
         else:
             rows = own[index] if token is None else later(own[index], token)
-            held[index] = [own[index], swap(rows, 1), swap(rows, 2)]
+            held[index] = [own[index], None if index == 1 else swap(rows, 1), swap(rows, 2)]
 
     own, held = [hidden[:size]], [None] * parts
     take(0, None)
@@ -385,10 +398,14 @@
                 after = [given]
             if index == 0:
                 take(1, after[0] if after else None)
-                rows = embed(chips, block, 0, exclusive, place, onehot, depth_table, held[0], after)
-                held[0] = [rows]
+                looked = look(chips, n_gx, block, 0, size, exclusive, place, onehot, depth_table, after)
         if kind == "t":
             take(index, after[0])
+        if kind == "a":
+            rows = arrange(chips, exclusive, place, held[index], None if index else looked, after)
+            after = [rows]
+            if exclusive and index == 0:
+                held[1][1] = swap(later(own[1], rows), 1)
         if kind == "p":
             start, width = pieces[index][int(item[2])]
             extra = {}
@@ -396,7 +413,7 @@
                 done = item[4:]
                 ending = (int(done[0]) * size, pieces[int(done[0])][int(done[1])][0])
                 extra = dict(ending=ending, terms=sums[done], out=out, shape=(block, columns))
-            send, keep, *rest = product(chips, exclusive, place, held[index], weight, start, width, after, **extra)
+            send, keep, *rest = product(rows, weight, start, width, after, **extra)
             out = rest[0] if rest else out
             after = [keep]
             if late:

time: 184 us -> 173 us (0.940)
  waiting for transfers between devices: 57.6 us -> 49.4 us
  Pallas kernels: 98.6 us -> 96.2 us
    ppermute x3, waiting for transfers between devices: 18.9 us -> 5.83 us  [local(): lax.ppermute(given, 'gy', [(0, 2), (1, 0), (2, 3), (3, 1)])]
    pallas_call x7, Pallas kernels: 83.5 us -> 78.9 us  [product(): pl.pallas_call(functools.partial(product_kernel, start, tile, width // ti...]
    ppermute x6, waiting for transfers between devices: 15 us -> 18.8 us  [swap(): return lax.ppermute(array, 'gy', [(k, k ^ distance) for k in range(n_gy)])]
    ppermute x6, starting transfers between devices: 11.6 us -> 14.4 us  [swap(): return lax.ppermute(array, 'gy', [(k, k ^ distance) for k in range(n_gy)])]
    ppermute x3, starting transfers between devices: 3.69 us -> 1.18 us  [local(): lax.ppermute(given, 'gy', [(0, 2), (1, 0), (2, 3), (3, 1)])]
    pallas_call x1 -> x4, Pallas kernels: 2.62 us -> 4.82 us  [the longest x1 2.47 us: look(): pl.pallas_call(functools.partial(look_kernel, count, chips, block, first,...]
  transfers between devices with their start and end apart: 23 -> 23, of which waited for: 9 -> 11; matrix products, arithmetic and copies ran while one was open for 0% -> 1% of each run, Pallas kernels for 53% -> 55%
where the time goes in v6:
time: 173 us
  Pallas kernels  96.2 us (56%)
  waiting for transfers between devices  49.4 us (29%)
  starting transfers between devices  23.3 us (13%)
  local copies, waits for them, and re-layouts  3.39 us (2%)
    pallas_call x7, Pallas kernels, product(): pl.pallas_call(functools.partial(product_kernel, start, tile, width // ti...  78.9 us
    ppermute x7, waiting for transfers between devices, local(): lax.ppermute(away[(ahead - 1) * size:ahead * size], 'gx', across(ahead))  23.4 us
    ppermute x6, waiting for transfers between devices, swap(): return lax.ppermute(array, 'gy', [(k, k ^ distance) for k in range(n_gy)])  18.8 us
    ppermute x6, starting transfers between devices, swap(): return lax.ppermute(array, 'gy', [(k, k ^ distance) for k in range(n_gy)])  14.4 us
    ppermute x7, starting transfers between devices, local(): lax.ppermute(away[(ahead - 1) * size:ahead * size], 'gx', across(ahead))  7 us
    ppermute x3, waiting for transfers between devices, local(): lax.ppermute(given, 'gy', [(0, 2), (1, 0), (2, 3), (3, 1)])  5.83 us
  transfers between devices with their start and end apart: 23, of which 11 were waited for; matrix products, arithmetic and copies ran while one was open for 1% of the time, Pallas kernels for 55%

profile of v6, /device:TPU:0, one launch (start us, length us, event | category | flops | bytes accessed | tf_op | source)
XLA Modules:
  0.0 172.6 jit_solution(8658300494291549982)
XLA Ops:
  1.1 3.1 %collective-permute-start = (bf16[64,3584]{1,0:T(8,128)(2,1)S(1)}, bf16[64,3584]{1,0:T(8,128)(2,1)S(1)}, u32[]{:S(2)}, u32[]{:S(2)}) collective-permute-start(bf16[64,3584]{1,0:T(8,128)(2,1)S(1)} %slice.3.refs_0_), channel_id=1, source_target_pairs={{0,1},{1,0},{2,3},{3,2},{4,5},{5,4},{6,7},{7,6},{8,9},{9,8},{10,11... | collective-permute-start | bytes 1376264 | tf_op jit(solution)/shard_map/ppermute | solution.py:363
  4.1 2.6 %collective-permute-start.1 = (bf16[64,3584]{1,0:T(8,128)(2,1)S(1)}, bf16[64,3584]{1,0:T(8,128)(2,1)S(1)}, u32[]{:S(2)}, u32[]{:S(2)}) collective-permute-start(bf16[64,3584]{1,0:T(8,128)(2,1)S(1)} %slice.3.refs_0_), channel_id=1, source_target_pairs={{0,2},{1,3},{2,0},{3,1},{4,6},{5,7},{6,4},{7,5},{8,10},{9,11},{10,... | collective-permute-start | bytes 1376264 | tf_op jit(solution)/shard_map/ppermute | solution.py:363
  7.6 2.0 %onehot.1.onehot_ref = bf16[768,256]{1,0:T(8,128)(2,1)S(1)} custom-call(s32[768,1]{1,0:T(8,128)S(1)} %broadcast_in_dim.4.parents_ref), custom_call_target="tpu_custom_call" | custom-call | flops 19327352832 | bytes 12582912 | tf_op jit(solution)/shard_map/onehot/pallas_call | solution.py:53
  9.7 1.5 copy-done.1
  11.2 1.9 %own.1 = (bf16[64,3584]{1,0:T(8,128)(2,1)S(1)}, bf16[64,3584]{1,0:T(8,128)(2,1)S(1)}) custom-call(s32[2]{0:T(128)S(1)} %pad_add_fusion.place_ref, bf16[768,256]{1,0:T(8,128)(2,1)S(1)} %onehot.1.onehot_ref, bf16[256,3584]{1,0:T(8,128)(2,1)S(1)} %copy-done.1, bf16[192,3584]{1,0:T(8,128)(2,1)S(1)} %copy-done), custom_call_target="tpu_custom_call" | custom-call | flops 1879048192 | bytes 22020096 | tf_op jit(solution)/shard_map/own/pallas_call | solution.py:159
  13.1 11.3 %collective-permute-done.near_ref.refs_1_ = bf16[64,3584]{1,0:T(8,128)(2,1)S(1)} collective-permute-done((bf16[64,3584]{1,0:T(8,128)(2,1)S(1)}, bf16[64,3584]{1,0:T(8,128)(2,1)S(1)}, u32[]{:S(2)}, u32[]{:S(2)}) %collective-permute-start) | collective-permute-done | bytes 458784 | tf_op jit(solution)/shard_map/ppermute | solution.py:363
  24.4 2.5 %collective-permute-done.1.far_ref.refs_2_ = bf16[64,3584]{1,0:T(8,128)(2,1)S(1)} collective-permute-done((bf16[64,3584]{1,0:T(8,128)(2,1)S(1)}, bf16[64,3584]{1,0:T(8,128)(2,1)S(1)}, u32[]{:S(2)}, u32[]{:S(2)}) %collective-permute-start.1) | collective-permute-done | bytes 458784 | tf_op jit(solution)/shard_map/ppermute | solution.py:363
  27.9 2.7 %collective-permute-start.4 = (bf16[64,3584]{1,0:T(8,128)(2,1)S(1)}, bf16[64,3584]{1,0:T(8,128)(2,1)S(1)}, u32[]{:S(2)}, u32[]{:S(2)}) collective-permute-start(bf16[64,3584]{1,0:T(8,128)(2,1)S(1)} %get-tuple-element.51.refs_0_), channel_id=1, source_target_pairs={{0,2},{1,3},{2,0},{3,1},{4,6},{5,7},{6,4},{7,5},{8,10},{9,11},{10,... | collective-permute-start | bytes 1376264 | tf_op jit(solution)/shard_map/ppermute | solution.py:363
  30.6 2.5 %look.1.refs_4_ = bf16[256,3584]{1,0:T(8,128)(2,1)S(1)} custom-call(s32[2]{0:T(128)S(1)} %pad_add_fusion.place_ref, bf16[768,256]{1,0:T(8,128)(2,1)S(1)} %onehot.1.onehot_ref, bf16[256,3584]{1,0:T(8,128)(2,1)S(1)} %copy-done.1, bf16[64,3584]{1,0:T(8,128)(2,1)S(1)} %forward.3.refs_0_.refs_5_), custom_call_target="tpu_custom_call" | custom-call | flops 3758096384 | bytes 29360128 | tf_op jit(solution)/shard_map/look/pallas_call | solution.py:105
  33.1 5.8 %collective-permute-done.2.refs_3_ = bf16[64,3584]{1,0:T(8,128)(2,1)S(1)} collective-permute-done((bf16[64,3584]{1,0:T(8,128)(2,1)S(1)}, bf16[64,3584]{1,0:T(8,128)(2,1)S(1)}, u32[]{:S(2)}, u32[]{:S(2)}) %collective-permute-start.2) | collective-permute-done | bytes 458784 | tf_op jit(solution)/shard_map/ppermute | solution.py:397
  39.9 3.6 %collective-permute-start.3 = (bf16[64,3584]{1,0:T(8,128)(2,1)S(1)}, bf16[64,3584]{1,0:T(8,128)(2,1)S(1)}, u32[]{:S(2)}, u32[]{:S(2)}) collective-permute-start(bf16[64,3584]{1,0:T(8,128)(2,1)S(1)} %get-tuple-element.51.refs_0_), channel_id=1, source_target_pairs={{0,1},{1,0},{2,3},{3,2},{4,5},{5,4},{6,7},{7,6},{8,9},{9,8},{10,11... | collective-permute-start | bytes 1376264 | tf_op jit(solution)/shard_map/ppermute | solution.py:363
  43.4 14.6 %product.7 = (bf16[128,5632]{1,0:T(8,128)(2,1)S(1)}, bf16[128,5632]{1,0:T(8,128)(2,1)S(1)}) custom-call(bf16[256,3584]{1,0:T(8,128)(2,1)S(1)} %arrange.3.rows_ref.refs_0_, bf16[3584,9216]{1,0:T(8,128)(2,1)} %weight_ref.13, bf16[256,3584]{1,0:T(8,128)(2,1)S(1)} %arrange.3.rows_ref.refs_0_), custom_call_target="tpu_custom_call" | custom-call | flops 82678120448 | bytes 360710144 | tf_op jit(solution)/shard_map/product/pallas_call | solution.py:268
  58.2 1.3 collective-permute-done.4.far_ref.refs_2_
  60.6 10.1 %product.8 = (bf16[128,3584]{1,0:T(8,128)(2,1)S(1)}, bf16[128,3584]{1,0:T(8,128)(2,1)S(1)}) custom-call(bf16[256,3584]{1,0:T(8,128)(2,1)S(1)} %arrange.3.rows_ref.refs_0_, bf16[3584,9216]{1,0:T(8,128)(2,1)} %weight_ref.13, bf16[64,3584]{1,0:T(8,128)(2,1)S(1)} %forward.4.refs_0_), custom_call_target="tpu_custom_call" | custom-call | flops 52613349376 | bytes 234881024 | tf_op jit(solution)/shard_map/product/pallas_call | solution.py:268
  70.7 1.9 %collective-permute-start.5 = (bf16[64,3584]{1,0:T(8,128)(2,1)S(1)}, bf16[64,3584]{1,0:T(8,128)(2,1)S(1)}, u32[]{:S(2)}, u32[]{:S(2)}) collective-permute-start(bf16[64,3584]{1,0:T(8,128)(2,1)S(1)} %get-tuple-element.54.refs_0_), channel_id=1, source_target_pairs={{0,1},{1,0},{2,3},{3,2},{4,5},{5,4},{6,7},{7,6},{8,9},{9,8},{10,11... | collective-permute-start | bytes 1376264 | tf_op jit(solution)/shard_map/ppermute | solution.py:363
  73.7 1.6 collective-permute-start.12
  76.0 14.6 %product.9 = (bf16[128,5632]{1,0:T(8,128)(2,1)S(1)}, bf16[128,5632]{1,0:T(8,128)(2,1)S(1)}) custom-call(bf16[256,3584]{1,0:T(8,128)(2,1)S(1)} %arrange.4.rows_ref.refs_0_, bf16[3584,9216]{1,0:T(8,128)(2,1)} %weight_ref.13, bf16[256,3584]{1,0:T(8,128)(2,1)S(1)} %arrange.4.rows_ref.refs_0_), custom_call_target="tpu_custom_call" | custom-call | flops 82678120448 | bytes 360710144 | tf_op jit(solution)/shard_map/product/pallas_call | solution.py:268
  91.4 3.4 %collective-permute-done.6.far_ref.refs_2_ = bf16[64,3584]{1,0:T(8,128)(2,1)S(1)} collective-permute-done((bf16[64,3584]{1,0:T(8,128)(2,1)S(1)}, bf16[64,3584]{1,0:T(8,128)(2,1)S(1)}, u32[]{:S(2)}, u32[]{:S(2)}) %collective-permute-start.6) | collective-permute-done | bytes 458784 | tf_op jit(solution)/shard_map/ppermute | solution.py:363
  96.0 1.5 collective-permute-start.14
  97.5 10.9 %product.10 = (bf16[128,3584]{1,0:T(8,128)(2,1)S(1)}, bf16[128,3584]{1,0:T(8,128)(2,1)S(1)}, bf16[192,9216]{1,0:T(8,128)(2,1)}) custom-call(bf16[256,3584]{1,0:T(8,128)(2,1)S(1)} %arrange.4.rows_ref.refs_0_, bf16[3584,9216]{1,0:T(8,128)(2,1)} %weight_ref.13, bf16[64,5632]{1,0:T(8,128)(2,1)S(1)} %get-tuple-element.57.refs_4_.refs_0_, ...), custom_call_target="tpu_custom_call" | custom-call | flops 52613349376 | bytes 234881024 | tf_op jit(solution)/shard_map/product/pallas_call | solution.py:268
  110.5 9.5 %product.11 = (bf16[128,3072]{1,0:T(8,128)(2,1)S(1)}, bf16[128,3072]{1,0:T(8,128)(2,1)S(1)}, bf16[192,9216]{1,0:T(8,128)(2,1)}) custom-call(bf16[256,3584]{1,0:T(8,128)(2,1)S(1)} %arrange.5.rows_ref.refs_3_, bf16[3584,9216]{1,0:T(8,128)(2,1)} %weight_ref.13, bf16[64,3584]{1,0:T(8,128)(2,1)S(1)} %get-tuple-element.59.refs_0_, ...), custom_call_target="tpu_custom_call", output_to_operand_aliasing={{2}: (4, {})} | custom-call | flops 45097156608 | bytes 203423744 | tf_op jit(solution)/shard_map/product/pallas_call | solution.py:268
  120.7 1.6 collective-permute-start.15
  122.3 5.9 %collective-permute-done.16.refs_1_ = bf16[64,5632]{1,0:T(8,128)(2,1)S(1)} collective-permute-done((bf16[64,5632]{1,0:T(8,128)(2,1)S(1)}, bf16[64,5632]{1,0:T(8,128)(2,1)S(1)}, u32[]{:S(2)}, u32[]{:S(2)}) %collective-permute-start.16) | collective-permute-done | bytes 720928 | tf_op jit(solution)/shard_map/ppermute | solution.py:426
  128.2 9.7 %product.12 = (bf16[128,3072]{1,0:T(8,128)(2,1)S(1)}, bf16[128,3072]{1,0:T(8,128)(2,1)S(1)}, bf16[192,9216]{1,0:T(8,128)(2,1)}) custom-call(bf16[256,3584]{1,0:T(8,128)(2,1)S(1)} %arrange.5.rows_ref.refs_3_, bf16[3584,9216]{1,0:T(8,128)(2,1)} %weight_ref.13, bf16[64,5632]{1,0:T(8,128)(2,1)S(1)} %get-tuple-element.63.refs_4_.refs_0_, ...), custom_call_target="tpu_custom_call", output_to_operand_aliasing={{2}: (4, {})} | custom-call | flops 45097156608 | bytes 203423744 | tf_op jit(solution)/shard_map/product/pallas_call | solution.py:268
  139.0 9.5 %product.13 = (bf16[128,3072]{1,0:T(8,128)(2,1)S(1)}, bf16[128,3072]{1,0:T(8,128)(2,1)S(1)}, bf16[192,9216]{1,0:T(8,128)(2,1)}) custom-call(bf16[256,3584]{1,0:T(8,128)(2,1)S(1)} %arrange.5.rows_ref.refs_3_, bf16[3584,9216]{1,0:T(8,128)(2,1)} %weight_ref.13, bf16[64,3584]{1,0:T(8,128)(2,1)S(1)} %get-tuple-element.68.refs_3_.refs_0_, ...), custom_call_target="tpu_custom_call", output_to_operand_aliasing={{2}: (4, {})} | custom-call | flops 45097156608 | bytes 203423744 | tf_op jit(solution)/shard_map/product/pallas_call | solution.py:268
  148.5 1.5 collective-permute-done.18.refs_1_
  150.0 1.1 finish.3
  152.1 1.3 collective-permute-done.19.got_ref
  154.4 9.1 %collective-permute-done.22.refs_1_ = bf16[64,3072]{1,0:T(8,128)(2,1)S(1)} collective-permute-done((bf16[64,3072]{1,0:T(8,128)(2,1)S(1)}, bf16[64,3072]{1,0:T(8,128)(2,1)S(1)}, u32[]{:S(2)}, u32[]{:S(2)}) %collective-permute-start.22) | collective-permute-done | bytes 393248 | tf_op jit(solution)/shard_map/ppermute | solution.py:426
  163.5 1.1 finish.4
  164.6 6.9 %collective-permute-done.21.refs_1_ = bf16[64,3072]{1,0:T(8,128)(2,1)S(1)} collective-permute-done((bf16[64,3072]{1,0:T(8,128)(2,1)S(1)}, bf16[64,3072]{1,0:T(8,128)(2,1)S(1)}, u32[]{:S(2)}, u32[]{:S(2)}) %collective-permute-start.21) | collective-permute-done | bytes 393248 | tf_op jit(solution)/shard_map/ppermute | solution.py:426
  171.5 1.1 finish.5
  (47 shorter events, 14.7 us)
Async XLA Ops:
  1.1 23.3 %collective-permute-start = (bf16[64,3584]{1,0:T(8,128)(2,1)S(1)}, bf16[64,3584]{1,0:T(8,128)(2,1)S(1)}, u32[]{:S(2)}, u32[]{:S(2)}) collective-permute-start(bf16[64,3584]{1,0:T(8,128)(2,1)S(1)} %slice.3.refs_0_), channel_id=1, source_target_pairs={{0,1},{1,0},{2,3},{3,2},{4,5},{5,4},{6,7},{7,6},{8,9},{9,8},{10,11... | collective-permute-start | bytes 1376264 | tf_op jit(solution)/shard_map/ppermute | solution.py:363
  4.1 22.8 %collective-permute-start.1 = (bf16[64,3584]{1,0:T(8,128)(2,1)S(1)}, bf16[64,3584]{1,0:T(8,128)(2,1)S(1)}, u32[]{:S(2)}, u32[]{:S(2)}) collective-permute-start(bf16[64,3584]{1,0:T(8,128)(2,1)S(1)} %slice.3.refs_0_), channel_id=1, source_target_pairs={{0,2},{1,3},{2,0},{3,1},{4,6},{5,7},{6,4},{7,5},{8,10},{9,11},{10,... | collective-permute-start | bytes 1376264 | tf_op jit(solution)/shard_map/ppermute | solution.py:363
  7.6 2.1 %copy-start = (bf16[192,3584]{1,0:T(8,128)(2,1)S(1)}, bf16[192,3584]{1,0:T(8,128)(2,1)}, u32[]{:S(2)}) copy-start(bf16[192,3584]{1,0:T(8,128)(2,1)} %hidden_ref.1) | copy-start | bytes 4128772
  9.7 1.5 copy-start.1
  27.5 11.4 %collective-permute-start.2 = (bf16[64,3584]{1,0:T(8,128)(2,1)S(1)}, bf16[64,3584]{1,0:T(8,128)(2,1)S(1)}, u32[]{:S(2)}, u32[]{:S(2)}) collective-permute-start(bf16[64,3584]{1,0:T(8,128)(2,1)S(1)} %forward.3.refs_0_.refs_5_), channel_id=1, source_target_pairs={{0,2},{1,0},{2,3},{3,1},{4,6},{5,4},{6,7},{7,5},{8,10},{9,8},{10,1... | collective-permute-start | bytes 1376264 | tf_op jit(solution)/shard_map/ppermute | solution.py:397
  27.9 31.6 %collective-permute-start.4 = (bf16[64,3584]{1,0:T(8,128)(2,1)S(1)}, bf16[64,3584]{1,0:T(8,128)(2,1)S(1)}, u32[]{:S(2)}, u32[]{:S(2)}) collective-permute-start(bf16[64,3584]{1,0:T(8,128)(2,1)S(1)} %get-tuple-element.51.refs_0_), channel_id=1, source_target_pairs={{0,2},{1,3},{2,0},{3,1},{4,6},{5,7},{6,4},{7,5},{8,10},{9,11},{10,... | collective-permute-start | bytes 1376264 | tf_op jit(solution)/shard_map/ppermute | solution.py:363
  39.9 19.9 %collective-permute-start.3 = (bf16[64,3584]{1,0:T(8,128)(2,1)S(1)}, bf16[64,3584]{1,0:T(8,128)(2,1)S(1)}, u32[]{:S(2)}, u32[]{:S(2)}) collective-permute-start(bf16[64,3584]{1,0:T(8,128)(2,1)S(1)} %get-tuple-element.51.refs_0_), channel_id=1, source_target_pairs={{0,1},{1,0},{2,3},{3,2},{4,5},{5,4},{6,7},{7,6},{8,9},{9,8},{10,11... | collective-permute-start | bytes 1376264 | tf_op jit(solution)/shard_map/ppermute | solution.py:363
  58.1 15.0 %collective-permute-start.9 = (bf16[128,5632]{1,0:T(8,128)(2,1)S(1)}, bf16[128,5632]{1,0:T(8,128)(2,1)S(1)}, u32[]{:S(2)}, u32[]{:S(2)}) collective-permute-start(bf16[128,5632]{1,0:T(8,128)(2,1)S(1)} %get-tuple-element.56), channel_id=1, source_target_pairs={{0,4},{4,0},{8,12},{12,8},{1,5},{5,1},{9,13},{13,9},{2,6},{6,2},{1... | collective-permute-start | bytes 4325384 | tf_op jit(solution)/shard_map/ppermute | solution.py:422
  60.3 15.0 %collective-permute-start.8 = (bf16[64,3584]{1,0:T(8,128)(2,1)S(1)}, bf16[64,3584]{1,0:T(8,128)(2,1)S(1)}, u32[]{:S(2)}, u32[]{:S(2)}) collective-permute-start(bf16[64,3584]{1,0:T(8,128)(2,1)S(1)} %forward.4.refs_0_), channel_id=1, source_target_pairs={{0,2},{1,0},{2,3},{3,1},{4,6},{5,4},{6,7},{7,5},{8,10},{9,8},{10,1... | collective-permute-start | bytes 1376264 | tf_op jit(solution)/shard_map/ppermute | solution.py:397
  70.7 20.7 %collective-permute-start.5 = (bf16[64,3584]{1,0:T(8,128)(2,1)S(1)}, bf16[64,3584]{1,0:T(8,128)(2,1)S(1)}, u32[]{:S(2)}, u32[]{:S(2)}) collective-permute-start(bf16[64,3584]{1,0:T(8,128)(2,1)S(1)} %get-tuple-element.54.refs_0_), channel_id=1, source_target_pairs={{0,1},{1,0},{2,3},{3,2},{4,5},{5,4},{6,7},{7,6},{8,9},{9,8},{10,11... | collective-permute-start | bytes 1376264 | tf_op jit(solution)/shard_map/ppermute | solution.py:363
  72.6 22.3 %collective-permute-start.6 = (bf16[64,3584]{1,0:T(8,128)(2,1)S(1)}, bf16[64,3584]{1,0:T(8,128)(2,1)S(1)}, u32[]{:S(2)}, u32[]{:S(2)}) collective-permute-start(bf16[64,3584]{1,0:T(8,128)(2,1)S(1)} %get-tuple-element.54.refs_0_), channel_id=1, source_target_pairs={{0,2},{1,3},{2,0},{3,1},{4,6},{5,7},{6,4},{7,5},{8,10},{9,11},{10,... | collective-permute-start | bytes 1376264 | tf_op jit(solution)/shard_map/ppermute | solution.py:363
  73.0 17.9 %collective-permute-start.7 = (bf16[128,3584]{1,0:T(8,128)(2,1)S(1)}, bf16[128,3584]{1,0:T(8,128)(2,1)S(1)}, u32[]{:S(2)}, u32[]{:S(2)}) collective-permute-start(bf16[128,3584]{1,0:T(8,128)(2,1)S(1)} %get-tuple-element.55), channel_id=1, source_target_pairs={{0,4},{4,0},{8,12},{12,8},{1,5},{5,1},{9,13},{13,9},{2,6},{6,2},{1... | collective-permute-start | bytes 2752520 | tf_op jit(solution)/shard_map/ppermute | solution.py:422
  73.7 23.8 %collective-permute-start.12 = (bf16[64,5632]{1,0:T(8,128)(2,1)S(1)}, bf16[64,5632]{1,0:T(8,128)(2,1)S(1)}, u32[]{:S(2)}, u32[]{:S(2)}) collective-permute-start(bf16[64,5632]{1,0:T(8,128)(2,1)S(1)} %get-tuple-element.61), channel_id=1, source_target_pairs={{0,8},{4,12},{8,0},{12,4},{1,9},{5,13},{9,1},{13,5},{2,10},{6,14},... | collective-permute-start | bytes 2162696 | tf_op jit(solution)/shard_map/ppermute | solution.py:426
  90.6 17.9 %collective-permute-start.11 = (bf16[128,5632]{1,0:T(8,128)(2,1)S(1)}, bf16[128,5632]{1,0:T(8,128)(2,1)S(1)}, u32[]{:S(2)}, u32[]{:S(2)}) collective-permute-start(bf16[128,5632]{1,0:T(8,128)(2,1)S(1)} %get-tuple-element.60), channel_id=1, source_target_pairs={{0,4},{4,0},{8,12},{12,8},{1,5},{5,1},{9,13},{13,9},{2,6},{6,2},{1... | collective-permute-start | bytes 4325384 | tf_op jit(solution)/shard_map/ppermute | solution.py:422
  95.4 14.4 %collective-permute-start.10 = (bf16[64,3584]{1,0:T(8,128)(2,1)S(1)}, bf16[64,3584]{1,0:T(8,128)(2,1)S(1)}, u32[]{:S(2)}, u32[]{:S(2)}) collective-permute-start(bf16[64,3584]{1,0:T(8,128)(2,1)S(1)} %forward.5.refs_2_), channel_id=1, source_target_pairs={{0,2},{1,0},{2,3},{3,1},{4,6},{5,4},{6,7},{7,5},{8,10},{9,8},{10,1... | collective-permute-start | bytes 1376264 | tf_op jit(solution)/shard_map/ppermute | solution.py:397
  96.0 14.5 %collective-permute-start.14 = (bf16[64,3584]{1,0:T(8,128)(2,1)S(1)}, bf16[64,3584]{1,0:T(8,128)(2,1)S(1)}, u32[]{:S(2)}, u32[]{:S(2)}) collective-permute-start(bf16[64,3584]{1,0:T(8,128)(2,1)S(1)} %get-tuple-element.65), channel_id=1, source_target_pairs={{0,8},{4,12},{8,0},{12,4},{1,9},{5,13},{9,1},{13,5},{2,10},{6,14},... | collective-permute-start | bytes 1376264 | tf_op jit(solution)/shard_map/ppermute | solution.py:426
  108.4 11.9 %collective-permute-start.13 = (bf16[128,3584]{1,0:T(8,128)(2,1)S(1)}, bf16[128,3584]{1,0:T(8,128)(2,1)S(1)}, u32[]{:S(2)}, u32[]{:S(2)}) collective-permute-start(bf16[128,3584]{1,0:T(8,128)(2,1)S(1)} %get-tuple-element.64), channel_id=1, source_target_pairs={{0,4},{4,0},{8,12},{12,8},{1,5},{5,1},{9,13},{13,9},{2,6},{6,2},{1... | collective-permute-start | bytes 2752520 | tf_op jit(solution)/shard_map/ppermute | solution.py:422
  109.2 19.0 %collective-permute-start.16 = (bf16[64,5632]{1,0:T(8,128)(2,1)S(1)}, bf16[64,5632]{1,0:T(8,128)(2,1)S(1)}, u32[]{:S(2)}, u32[]{:S(2)}) collective-permute-start(bf16[64,5632]{1,0:T(8,128)(2,1)S(1)} %get-tuple-element.70), channel_id=1, source_target_pairs={{0,8},{4,12},{8,0},{12,4},{1,9},{5,13},{9,1},{13,5},{2,10},{6,14},... | collective-permute-start | bytes 2162696 | tf_op jit(solution)/shard_map/ppermute | solution.py:426
  120.0 18.0 %collective-permute-start.17 = (bf16[128,3072]{1,0:T(8,128)(2,1)S(1)}, bf16[128,3072]{1,0:T(8,128)(2,1)S(1)}, u32[]{:S(2)}, u32[]{:S(2)}) collective-permute-start(bf16[128,3072]{1,0:T(8,128)(2,1)S(1)} %get-tuple-element.73), channel_id=1, source_target_pairs={{0,4},{4,0},{8,12},{12,8},{1,5},{5,1},{9,13},{13,9},{2,6},{6,2},{1... | collective-permute-start | bytes 2359304 | tf_op jit(solution)/shard_map/ppermute | solution.py:422
  120.7 18.3 %collective-permute-start.15 = (bf16[64,3584]{1,0:T(8,128)(2,1)S(1)}, bf16[64,3584]{1,0:T(8,128)(2,1)S(1)}, u32[]{:S(2)}, u32[]{:S(2)}) collective-permute-start(bf16[64,3584]{1,0:T(8,128)(2,1)S(1)} %get-tuple-element.69), channel_id=1, source_target_pairs={{0,8},{4,12},{8,0},{12,4},{1,9},{5,13},{9,1},{13,5},{2,10},{6,14},... | collective-permute-start | bytes 1376264 | tf_op jit(solution)/shard_map/ppermute | solution.py:426
  137.9 13.2 %collective-permute-start.20 = (bf16[128,3072]{1,0:T(8,128)(2,1)S(1)}, bf16[128,3072]{1,0:T(8,128)(2,1)S(1)}, u32[]{:S(2)}, u32[]{:S(2)}) collective-permute-start(bf16[128,3072]{1,0:T(8,128)(2,1)S(1)} %get-tuple-element.82), channel_id=1, source_target_pairs={{0,4},{4,0},{8,12},{12,8},{1,5},{5,1},{9,13},{13,9},{2,6},{6,2},{1... | collective-permute-start | bytes 2359304 | tf_op jit(solution)/shard_map/ppermute | solution.py:422
  138.4 11.6 %collective-permute-start.18 = (bf16[64,3072]{1,0:T(8,128)(2,1)S(1)}, bf16[64,3072]{1,0:T(8,128)(2,1)S(1)}, u32[]{:S(2)}, u32[]{:S(2)}) collective-permute-start(bf16[64,3072]{1,0:T(8,128)(2,1)S(1)} %get-tuple-element.78), channel_id=1, source_target_pairs={{0,8},{4,12},{8,0},{12,4},{1,9},{5,13},{9,1},{13,5},{2,10},{6,14},... | collective-permute-start | bytes 1179656 | tf_op jit(solution)/shard_map/ppermute | solution.py:426
  151.1 2.3 %collective-permute-start.19 = (bf16[128,3072]{1,0:T(8,128)(2,1)S(1)}, bf16[128,3072]{1,0:T(8,128)(2,1)S(1)}, u32[]{:S(2)}, u32[]{:S(2)}) collective-permute-start(bf16[128,3072]{1,0:T(8,128)(2,1)S(1)} %get-tuple-element.81), channel_id=1, source_target_pairs={{0,4},{4,0},{8,12},{12,8},{1,5},{5,1},{9,13},{13,9},{2,6},{6,2},{1... | collective-permute-start | bytes 2359304 | tf_op jit(solution)/shard_map/ppermute | solution.py:434
  151.5 12.0 %collective-permute-start.22 = (bf16[64,3072]{1,0:T(8,128)(2,1)S(1)}, bf16[64,3072]{1,0:T(8,128)(2,1)S(1)}, u32[]{:S(2)}, u32[]{:S(2)}) collective-permute-start(bf16[64,3072]{1,0:T(8,128)(2,1)S(1)} %get-tuple-element.86), channel_id=1, source_target_pairs={{0,8},{4,12},{8,0},{12,4},{1,9},{5,13},{9,1},{13,5},{2,10},{6,14},... | collective-permute-start | bytes 1179656 | tf_op jit(solution)/shard_map/ppermute | solution.py:426
  153.8 17.7 %collective-permute-start.21 = (bf16[64,3072]{1,0:T(8,128)(2,1)S(1)}, bf16[64,3072]{1,0:T(8,128)(2,1)S(1)}, u32[]{:S(2)}, u32[]{:S(2)}) collective-permute-start(bf16[64,3072]{1,0:T(8,128)(2,1)S(1)} %get-tuple-element.85), channel_id=1, source_target_pairs={{0,8},{4,12},{8,0},{12,4},{1,9},{5,13},{9,1},{13,5},{2,10},{6,14},... | collective-permute-start | bytes 1179656 | tf_op jit(solution)/shard_map/ppermute | solution.py:426

commit v7 on v6

--- a/solution.py
+++ b/solution.py
@@ -152,24 +152,24 @@
         first += size
 
 
-def embed_own(first, size, count, place, onehot, table, hidden):
+def embed_own(sizes, place, onehot, table, hidden):
     block, depth = hidden.shape
     tile = divisor(depth, (896, 512, 256, 128))
     column = lambda j: (0, j)
     return pl.pallas_call(
-        functools.partial(embed_own_kernel, block, first),
+        functools.partial(embed_own_kernel, block, block - sum(sizes)),
         name="own",
         grid=(depth // tile,),
-        out_shape=[jax.ShapeDtypeStruct((size, depth), BF16)] * count,
+        out_shape=[jax.ShapeDtypeStruct((size, depth), BF16) for size in sizes],
         in_specs=[
             SMEM,
             pl.BlockSpec(onehot.shape, lambda j: (0, 0)),
             pl.BlockSpec((table.shape[0], tile), column),
             pl.BlockSpec((block, tile), column),
         ],
-        out_specs=[pl.BlockSpec((size, tile), column)] * count,
-        compiler_params=params(16),
-        cost_estimate=cost(2 * count * size * table.shape[0] * depth, 6 * count * size * depth),
+        out_specs=[pl.BlockSpec((size, tile), column) for size in sizes],
+        compiler_params=params(16),
+        cost_estimate=cost(2 * sum(sizes) * table.shape[0] * depth, 6 * sum(sizes) * depth),
     )(place, onehot, table, hidden)
 
 
@@ -180,7 +180,7 @@
     return jax.nn.gelu(total, approximate=True).astype(BF16)
 
 
-def product_kernel(start, tile, steps, slots, ending, rows_ref, weight_ref, *refs):
+def product_kernel(start, tile, steps, slots, ending, rows_ref, lead_ref, weight_ref, *refs):
     terms = refs[:ending[3]]
     outs = 2 if not ending[3] else 3
     scratch = len(refs) - (2 if not ending[3] else 6)
@@ -204,7 +204,7 @@
 
     @pl.when(step == 0)
     def _():
-        for index in range(min(slots - 1, steps)):
+        for index in range(1, min(slots - 1, steps)):
             fetch(index).start()
         if ending[3]:
             for copy in given:
@@ -214,10 +214,19 @@
     def _():
         fetch(step + slots - 1).start()
 
-    fetch(step).wait()
-    out = jnp.dot(rows_ref[...], held[lax.rem(step, slots)], preferred_element_type=F32)
-    send_ref[...] = out[:half].astype(BF16)
-    keep_ref[...] = out[half:].astype(BF16)
+    def multiply(tile_ref):
+        out = jnp.dot(rows_ref[...], tile_ref[...], preferred_element_type=F32)
+        send_ref[...] = out[:half].astype(BF16)
+        keep_ref[...] = out[half:].astype(BF16)
+
+    @pl.when(step == 0)
+    def _():
+        multiply(lead_ref)
+
+    @pl.when(step > 0)
+    def _():
+        fetch(step).wait()
+        multiply(held.at[lax.rem(step, slots)])
 
     if ending[3]:
         @pl.when(step == 0)
@@ -249,7 +258,7 @@
         pltpu.VMEM((slots, depth, tile), BF16),
         pltpu.SemaphoreType.DMA((slots,)),
     ]
-    operands = [rows, weight, *terms]
+    operands = [rows, weight[:, start:start + tile], weight, *terms]
     aliases = {}
     ending = (0, 0, 0, 0) if not terms else (*ending, terms[0].shape[1], len(terms))
     if terms:
@@ -270,11 +279,11 @@
         name="product",
         grid=(width // tile,),
         out_shape=outs,
-        in_specs=[VMEM] + [ANY] * (len(operands) - 1),
+        in_specs=[VMEM] * 2 + [ANY] * (len(operands) - 2),
         out_specs=out_specs,
         scratch_shapes=scratch,
         input_output_aliases=aliases,
-        compiler_params=params(40),
+        compiler_params=params(24),
         cost_estimate=cost(2 * height * depth * width, 2 * (height * depth + depth * width + height * width)),
     )(*operands)
 
@@ -338,12 +347,19 @@
     return pieces
 
 
-SHARES = ((11, 7), (11, 7), (6, 6, 6))
+SHARES = ((9, 9), (6, 6, 6), (6, 6, 6))
+
+
+def chunk_sizes(block):
+    if block % 192 == 0:
+        return [block // 4, block * 5 // 12, block // 3]
+    return [block // 3] * 3
+
 
 ORDER = (
-    ("f0", "a0", "p00", "f1", "p01", "t2", "s00"),
-    ("a1", "p10", "s01", "f2", "p11-00", "s10"),
-    ("a2", "p20-01", "s11", "p21-10", "s20", "p22-11+", "g20!"),
+    ("f0", "a0", "p00", "p01", "s00", "f1", "s01"),
+    ("a1", "t2", "p10", "p11-00", "f2", "s10", "p12-01", "s11"),
+    ("a2", "p20-10", "s12", "p21-11", "s20", "p22-12+", "g20!"),
     ("s21!", "s22", "g21", "g22"),
 )
 
@@ -353,8 +369,9 @@
     columns = weight.shape[1]
     block = hidden.shape[0]
     chips = n_gx // 2
-    parts = len(SHARES)
-    size = block // parts
+    sizes = chunk_sizes(block)
+    firsts = [sum(sizes[:index]) for index in range(len(sizes))]
+    parts = len(sizes)
     place = jnp.stack([lax.axis_index("gx"), lax.axis_index("gy")]).astype(jnp.int32)
 
     exclusive = n_gy == 4
@@ -373,10 +390,10 @@
             rows = own[index] if token is None else later(own[index], token)
             held[index] = [own[index], None if index == 1 else swap(rows, 1), swap(rows, 2)]
 
-    own, held = [hidden[:size]], [None] * parts
+    own, held = [hidden[:sizes[0]]], [None] * parts
     take(0, None)
     onehot = depth_onehot(parents, tree)
-    own += embed_own(size, size, parts - 1, place, onehot, depth_table, hidden)
+    own += embed_own(sizes[1:], place, onehot, depth_table, hidden)
 
     sibling = [(g, g ^ 1) for g in range(n_gx)]
 
@@ -398,7 +415,7 @@
                 after = [given]
             if index == 0:
                 take(1, after[0] if after else None)
-                looked = look(chips, n_gx, block, 0, size, exclusive, place, onehot, depth_table, after)
+                looked = look(chips, n_gx, block, 0, sizes[0], exclusive, place, onehot, depth_table, after)
         if kind == "t":
             take(index, after[0])
         if kind == "a":
@@ -411,7 +428,7 @@
             extra = {}
             if len(item) > 3:
                 done = item[4:]
-                ending = (int(done[0]) * size, pieces[int(done[0])][int(done[1])][0])
+                ending = (firsts[int(done[0])], pieces[int(done[0])][int(done[1])][0])
                 extra = dict(ending=ending, terms=sums[done], out=out, shape=(block, columns))
             send, keep, *rest = product(rows, weight, start, width, after, **extra)
             out = rest[0] if rest else out
@@ -422,13 +439,14 @@
                 products[piece] = keep, lax.ppermute(send, "gx", sibling)
         if kind == "s":
             away, stay = pair(chips, *products[piece], after, long)
+            size = sizes[index]
             sums[piece] = [stay] + [
                 lax.ppermute(away[(ahead - 1) * size:ahead * size], "gx", across(ahead)) for ahead in range(1, chips)
             ]
             after = [stay]
         if kind == "g":
             start, width = pieces[index][int(item[2])]
-            out, token = finish((block, columns), (index, start, width), size, sums[piece], out, after, long)
+            out, token = finish((block, columns), (firsts[index] // sizes[index], start, width), sizes[index], sums[piece], out, after, long)
             after = [token]
             for name, (keep, send) in waiting.items():
                 products[name] = keep, lax.ppermute(later(send, token), "gx", sibling)

time: 173 us -> 169 us (0.977)
  local copies, waits for them, and re-layouts: 3.39 us -> 9.27 us
  Pallas kernels: 96.2 us -> 91.4 us
  waiting for transfers between devices: 49.4 us -> 44.9 us
    ppermute x6, waiting for transfers between devices: 18.8 us -> 11.1 us  [swap(): return lax.ppermute(array, 'gy', [(k, k ^ distance) for k in range(n_gy)])]
    slice x1 -> x2, local copies, waits for them, and re-layouts: 1.05 us -> 6.93 us  [the longest x1 5.93 us: product(): operands = [rows, weight[:, start:start + tile], weight, *terms]]
    ppermute x3, waiting for transfers between devices: 5.83 us -> 10.8 us  [local(): lax.ppermute(given, 'gy', [(0, 2), (1, 0), (2, 3), (3, 1)])]
    pallas_call x7 -> x8, Pallas kernels: 78.9 us -> 74.2 us  [product(): pl.pallas_call(functools.partial(product_kernel, start, tile, width // ti...]
    ppermute x6, starting transfers between devices: 14.4 us -> 10.8 us  [swap(): return lax.ppermute(array, 'gy', [(k, k ^ distance) for k in range(n_gy)])]
    ppermute x3, starting transfers between devices: 1.18 us -> 3.22 us  [local(): lax.ppermute(given, 'gy', [(0, 2), (1, 0), (2, 3), (3, 1)])]
    ppermute x7 -> x8, waiting for transfers between devices: 23.4 us -> 21.4 us  [local(): lax.ppermute(away[(ahead - 1) * size:ahead * size], 'gx', across(ahead))]
    ppermute x7 -> x8, starting transfers between devices: 7 us -> 6.86 us  [local(): lax.ppermute(away[(ahead - 1) * size:ahead * size], 'gx', across(ahead))]
  transfers between devices with their start and end apart: 23 -> 25, of which waited for: 11 -> 12; matrix products, arithmetic and copies ran while one was open for 1% -> 4% of each run, Pallas kernels for 55% -> 53%
where the time goes in v7:
time: 169 us; the launch traced here: 168 us
  Pallas kernels  91.4 us (54%)
  waiting for transfers between devices  44.9 us (27%)
  starting transfers between devices  22.5 us (13%)
  local copies, waits for them, and re-layouts  9.27 us (5%)
    pallas_call x8, Pallas kernels, product(): pl.pallas_call(functools.partial(product_kernel, start, tile, width // ti...  74.2 us
    ppermute x8, waiting for transfers between devices, local(): lax.ppermute(away[(ahead - 1) * size:ahead * size], 'gx', across(ahead))  21.4 us
    ppermute x6, waiting for transfers between devices, swap(): return lax.ppermute(array, 'gy', [(k, k ^ distance) for k in range(n_gy)])  11.1 us
    ppermute x3, waiting for transfers between devices, local(): lax.ppermute(given, 'gy', [(0, 2), (1, 0), (2, 3), (3, 1)])  10.8 us
    ppermute x6, starting transfers between devices, swap(): return lax.ppermute(array, 'gy', [(k, k ^ distance) for k in range(n_gy)])  10.8 us
    ppermute x8, starting transfers between devices, local(): lax.ppermute(away[(ahead - 1) * size:ahead * size], 'gx', across(ahead))  6.86 us
    slice x1, local copies, waits for them, and re-layouts, product(): operands = [rows, weight[:, start:start + tile], weight, *terms]  5.93 us
    pallas_call x8, Pallas kernels, pair(): pl.pallas_call(pair_kernel, name='pair', grid=(width // tile,), out_shape...  3.52 us
  transfers between devices with their start and end apart: 25, of which 12 were waited for; matrix products, arithmetic and copies ran while one was open for 4% of the time, Pallas kernels for 53%

profile of v7, /device:TPU:0, one launch (start us, length us, event | category | flops | bytes accessed | tf_op | source)
XLA Modules:
  0.0 168.5 jit_solution(3681514320821225461)
XLA Ops:
  1.0 4.1 %collective-permute-start.1 = (bf16[48,3584]{1,0:T(8,128)(2,1)S(1)}, bf16[48,3584]{1,0:T(8,128)(2,1)S(1)}, u32[]{:S(2)}, u32[]{:S(2)}) collective-permute-start(bf16[48,3584]{1,0:T(8,128)(2,1)S(1)} %slice.19.refs_0_), channel_id=1, source_target_pairs={{0,2},{1,3},{2,0},{3,1},{4,6},{5,7},{6,4},{7,5},{8,10},{9,11},{10,... | collective-permute-start | bytes 1032200 | tf_op jit(solution)/shard_map/ppermute | solution.py:380
  5.1 1.6 collective-permute-start
  7.5 2.0 %onehot.1.onehot_ref = bf16[768,256]{1,0:T(8,128)(2,1)S(1)} custom-call(s32[768,1]{1,0:T(8,128)S(1)} %broadcast_in_dim.4.parents_ref), custom_call_target="tpu_custom_call" | custom-call | flops 19327352832 | bytes 12582912 | tf_op jit(solution)/shard_map/onehot/pallas_call | solution.py:53
  9.6 1.5 copy-done.1
  11.1 2.0 %own.1 = (bf16[80,3584]{1,0:T(8,128)(2,1)S(1)}, bf16[64,3584]{1,0:T(8,128)(2,1)S(1)}) custom-call(s32[2]{0:T(128)S(1)} %pad_add_fusion.place_ref, bf16[768,256]{1,0:T(8,128)(2,1)S(1)} %onehot.1.onehot_ref, bf16[256,3584]{1,0:T(8,128)(2,1)S(1)} %copy-done.1, bf16[192,3584]{1,0:T(8,128)(2,1)S(1)} %copy-done), custom_call_target="tpu_custom_call" | custom-call | flops 2113929216 | bytes 24772608 | tf_op jit(solution)/shard_map/own/pallas_call | solution.py:159
  13.1 7.5 %collective-permute-done.1.far_ref.refs_2_ = bf16[48,3584]{1,0:T(8,128)(2,1)S(1)} collective-permute-done((bf16[48,3584]{1,0:T(8,128)(2,1)S(1)}, bf16[48,3584]{1,0:T(8,128)(2,1)S(1)}, u32[]{:S(2)}, u32[]{:S(2)}) %collective-permute-start.1) | collective-permute-done | bytes 344096 | tf_op jit(solution)/shard_map/ppermute | solution.py:380
  21.4 1.4 collective-permute-start.2
  22.8 5.9 %fusion = (bf16[3584,512]{1,0:T(8,128)(2,1)S(1)}, bf16[3584,512]{1,0:T(8,128)(2,1)S(1)}, bf16[3584,512]{1,0:T(8,128)(2,1)S(1)}, bf16[3584,512]{1,0:T(8,128)(2,1)S(1)}) fusion(bf16[3584,9216]{1,0:T(8,128)(2,1)} %weight_ref.15), kind=kLoop, calls=%fused_computation.1 | loop fusion | bytes 29360128 | tf_op jit(solution)/shard_map/slice | solution.py:261
  28.8 2.5 %collective-permute-start.4 = (bf16[80,3584]{1,0:T(8,128)(2,1)S(1)}, bf16[80,3584]{1,0:T(8,128)(2,1)S(1)}, u32[]{:S(2)}, u32[]{:S(2)}) collective-permute-start(bf16[80,3584]{1,0:T(8,128)(2,1)S(1)} %get-tuple-element.56.refs_0_), channel_id=1, source_target_pairs={{0,2},{1,3},{2,0},{3,1},{4,6},{5,7},{6,4},{7,5},{8,10},{9,11},{10,... | collective-permute-start | bytes 1720328 | tf_op jit(solution)/shard_map/ppermute | solution.py:380
  31.3 2.4 %look.1.refs_4_ = bf16[192,3584]{1,0:T(8,128)(2,1)S(1)} custom-call(s32[2]{0:T(128)S(1)} %pad_add_fusion.place_ref, bf16[768,256]{1,0:T(8,128)(2,1)S(1)} %onehot.1.onehot_ref, bf16[256,3584]{1,0:T(8,128)(2,1)S(1)} %copy-done.1, bf16[48,3584]{1,0:T(8,128)(2,1)S(1)} %forward.3.refs_0_.refs_5_), custom_call_target="tpu_custom_call" | custom-call | flops 2818572288 | bytes 22020096 | tf_op jit(solution)/shard_map/look/pallas_call | solution.py:105
  34.6 1.3 collective-permute-start.3
  35.9 10.7 %product.8 = (bf16[96,4608]{1,0:T(8,128)(2,1)S(1)}, bf16[96,4608]{1,0:T(8,128)(2,1)S(1)}) custom-call(bf16[192,3584]{1,0:T(8,128)(2,1)S(1)} %arrange.3.rows_ref.refs_0_, bf16[3584,512]{1,0:T(8,128)(2,1)S(1)} %get-tuple-element.104.lead_ref, bf16[3584,9216]{1,0:T(8,128)(2,1)} %weight_ref.15, bf16[192,3584]{1,0:T(8,128)(2,1)S(1)} %arrange.3.rows_ref.refs_0_), custom_call_target="tpu_custom_call" | custom-call | flops 50734301184 | bytes 289406976 | tf_op jit(solution)/shard_map/product/pallas_call | solution.py:277
  46.7 10.7 %product.9 = (bf16[96,4608]{1,0:T(8,128)(2,1)S(1)}, bf16[96,4608]{1,0:T(8,128)(2,1)S(1)}) custom-call(bf16[192,3584]{1,0:T(8,128)(2,1)S(1)} %arrange.3.rows_ref.refs_0_, bf16[3584,512]{1,0:T(8,128)(2,1)S(1)} %get-tuple-element.103.lead_ref, bf16[3584,9216]{1,0:T(8,128)(2,1)} %weight_ref.15, bf16[96,4608]{1,0:T(8,128)(2,1)S(1)} %get-tuple-element.57.refs_0_.keep_ref), custom_call_target="tpu_custom_call" | custom-call | flops 50734301184 | bytes 289406976 | tf_op jit(solution)/shard_map/product/pallas_call | solution.py:277
  58.4 2.8 %collective-permute-done.3.near_ref.refs_1_ = bf16[80,3584]{1,0:T(8,128)(2,1)S(1)} collective-permute-done((bf16[80,3584]{1,0:T(8,128)(2,1)S(1)}, bf16[80,3584]{1,0:T(8,128)(2,1)S(1)}, u32[]{:S(2)}, u32[]{:S(2)}) %collective-permute-start.3) | collective-permute-done | bytes 573472 | tf_op jit(solution)/shard_map/ppermute | solution.py:380
  61.8 1.6 collective-permute-start.10
  64.4 10.8 %collective-permute-done.6.refs_3_ = bf16[80,3584]{1,0:T(8,128)(2,1)S(1)} collective-permute-done((bf16[80,3584]{1,0:T(8,128)(2,1)S(1)}, bf16[80,3584]{1,0:T(8,128)(2,1)S(1)}, u32[]{:S(2)}, u32[]{:S(2)}) %collective-permute-start.6) | collective-permute-done | bytes 573472 | tf_op jit(solution)/shard_map/ppermute | solution.py:414
  75.9 1.3 collective-permute-start.9
  77.2 9.0 %product.10 = (bf16[160,3072]{1,0:T(8,128)(2,1)S(1)}, bf16[160,3072]{1,0:T(8,128)(2,1)S(1)}) custom-call(bf16[320,3584]{1,0:T(8,128)(2,1)S(1)} %arrange.4.rows_ref.refs_0_, bf16[3584,512]{1,0:T(8,128)(2,1)S(1)} %get-tuple-element.104.lead_ref, bf16[3584,9216]{1,0:T(8,128)(2,1)} %weight_ref.15, bf16[320,3584]{1,0:T(8,128)(2,1)S(1)} %arrange.4.rows_ref.refs_0_), custom_call_target="tpu_custom_call" | custom-call | flops 56371445760 | bytes 210239488 | tf_op jit(solution)/shard_map/product/pallas_call | solution.py:277
  86.4 9.5 %product.11 = (bf16[160,3072]{1,0:T(8,128)(2,1)S(1)}, bf16[160,3072]{1,0:T(8,128)(2,1)S(1)}, bf16[192,9216]{1,0:T(8,128)(2,1)}) custom-call(bf16[320,3584]{1,0:T(8,128)(2,1)S(1)} %arrange.4.rows_ref.refs_0_, bf16[3584,512]{1,0:T(8,128)(2,1)S(1)} %get-tuple-element.102.lead_ref, bf16[3584,9216]{1,0:T(8,128)(2,1)} %weight_ref.15, ...), custom_call_target="tpu_custom_call" | custom-call | flops 56371445760 | bytes 210239488 | tf_op jit(solution)/shard_map/product/pallas_call | solution.py:277
  97.7 1.7 %collective-permute-start.11 = (bf16[64,3584]{1,0:T(8,128)(2,1)S(1)}, bf16[64,3584]{1,0:T(8,128)(2,1)S(1)}, u32[]{:S(2)}, u32[]{:S(2)}) collective-permute-start(bf16[64,3584]{1,0:T(8,128)(2,1)S(1)} %forward.5.refs_0_), channel_id=1, source_target_pairs={{0,2},{1,0},{2,3},{3,1},{4,6},{5,4},{6,7},{7,5},{8,10},{9,8},{10,1... | collective-permute-start | bytes 1376264 | tf_op jit(solution)/shard_map/ppermute | solution.py:414
  99.9 1.6 collective-permute-start.16
  101.5 9.5 %product.12 = (bf16[160,3072]{1,0:T(8,128)(2,1)S(1)}, bf16[160,3072]{1,0:T(8,128)(2,1)S(1)}, bf16[192,9216]{1,0:T(8,128)(2,1)}) custom-call(bf16[320,3584]{1,0:T(8,128)(2,1)S(1)} %arrange.4.rows_ref.refs_0_, bf16[3584,512]{1,0:T(8,128)(2,1)S(1)} %get-tuple-element.101.lead_ref, bf16[3584,9216]{1,0:T(8,128)(2,1)} %weight_ref.15, ...), custom_call_target="tpu_custom_call", output_to_operand_aliasing={{2}: (5, {})} | custom-call | flops 56371445760 | bytes 210239488 | tf_op jit(solution)/shard_map/product/pallas_call | solution.py:277
  112.9 8.2 %product.13 = (bf16[128,3072]{1,0:T(8,128)(2,1)S(1)}, bf16[128,3072]{1,0:T(8,128)(2,1)S(1)}, bf16[192,9216]{1,0:T(8,128)(2,1)}) custom-call(bf16[256,3584]{1,0:T(8,128)(2,1)S(1)} %arrange.5.rows_ref.refs_3_, bf16[3584,512]{1,0:T(8,128)(2,1)S(1)} %get-tuple-element.104.lead_ref, bf16[3584,9216]{1,0:T(8,128)(2,1)} %weight_ref.15, ...), custom_call_target="tpu_custom_call", output_to_operand_aliasing={{2}: (5, {})} | custom-call | flops 45097156608 | bytes 203423744 | tf_op jit(solution)/shard_map/product/pallas_call | solution.py:277
  121.9 1.6 collective-permute-start.17
  123.4 2.1 %collective-permute-done.18.refs_1_ = bf16[80,3072]{1,0:T(8,128)(2,1)S(1)} collective-permute-done((bf16[80,3072]{1,0:T(8,128)(2,1)S(1)}, bf16[80,3072]{1,0:T(8,128)(2,1)S(1)}, u32[]{:S(2)}, u32[]{:S(2)}) %collective-permute-start.18) | collective-permute-done | bytes 491552 | tf_op jit(solution)/shard_map/ppermute | solution.py:444
  125.5 8.2 %product.14 = (bf16[128,3072]{1,0:T(8,128)(2,1)S(1)}, bf16[128,3072]{1,0:T(8,128)(2,1)S(1)}, bf16[192,9216]{1,0:T(8,128)(2,1)}) custom-call(bf16[256,3584]{1,0:T(8,128)(2,1)S(1)} %arrange.5.rows_ref.refs_3_, bf16[3584,512]{1,0:T(8,128)(2,1)S(1)} %get-tuple-element.102.lead_ref, bf16[3584,9216]{1,0:T(8,128)(2,1)} %weight_ref.15, ...), custom_call_target="tpu_custom_call", output_to_operand_aliasing={{2}: (5, {})} | custom-call | flops 45097156608 | bytes 203423744 | tf_op jit(solution)/shard_map/product/pallas_call | solution.py:277
  134.6 1.2 collective-permute-done.17.refs_1_
  135.8 8.2 %product.15 = (bf16[128,3072]{1,0:T(8,128)(2,1)S(1)}, bf16[128,3072]{1,0:T(8,128)(2,1)S(1)}, bf16[192,9216]{1,0:T(8,128)(2,1)}) custom-call(bf16[256,3584]{1,0:T(8,128)(2,1)S(1)} %arrange.5.rows_ref.refs_3_, bf16[3584,512]{1,0:T(8,128)(2,1)S(1)} %get-tuple-element.101.lead_ref, bf16[3584,9216]{1,0:T(8,128)(2,1)} %weight_ref.15, ...), custom_call_target="tpu_custom_call", output_to_operand_aliasing={{2}: (5, {})} | custom-call | flops 45097156608 | bytes 203423744 | tf_op jit(solution)/shard_map/product/pallas_call | solution.py:277
  144.0 1.8 %collective-permute-done.20.refs_1_ = bf16[64,3072]{1,0:T(8,128)(2,1)S(1)} collective-permute-done((bf16[64,3072]{1,0:T(8,128)(2,1)S(1)}, bf16[64,3072]{1,0:T(8,128)(2,1)S(1)}, u32[]{:S(2)}, u32[]{:S(2)}) %collective-permute-start.20) | collective-permute-done | bytes 393248 | tf_op jit(solution)/shard_map/ppermute | solution.py:444
  147.7 1.5 collective-permute-done.21.got_ref
  150.0 9.3 %collective-permute-done.24.refs_1_ = bf16[64,3072]{1,0:T(8,128)(2,1)S(1)} collective-permute-done((bf16[64,3072]{1,0:T(8,128)(2,1)S(1)}, bf16[64,3072]{1,0:T(8,128)(2,1)S(1)}, u32[]{:S(2)}, u32[]{:S(2)}) %collective-permute-start.24) | collective-permute-done | bytes 393248 | tf_op jit(solution)/shard_map/ppermute | solution.py:444
  160.4 6.9 %collective-permute-done.23.refs_1_ = bf16[64,3072]{1,0:T(8,128)(2,1)S(1)} collective-permute-done((bf16[64,3072]{1,0:T(8,128)(2,1)S(1)}, bf16[64,3072]{1,0:T(8,128)(2,1)S(1)}, u32[]{:S(2)}, u32[]{:S(2)}) %collective-permute-start.23) | collective-permute-done | bytes 393248 | tf_op jit(solution)/shard_map/ppermute | solution.py:444
  (54 shorter events, 17.6 us)
Async XLA Ops:
  1.0 19.6 %collective-permute-start.1 = (bf16[48,3584]{1,0:T(8,128)(2,1)S(1)}, bf16[48,3584]{1,0:T(8,128)(2,1)S(1)}, u32[]{:S(2)}, u32[]{:S(2)}) collective-permute-start(bf16[48,3584]{1,0:T(8,128)(2,1)S(1)} %slice.19.refs_0_), channel_id=1, source_target_pairs={{0,2},{1,3},{2,0},{3,1},{4,6},{5,7},{6,4},{7,5},{8,10},{9,11},{10,... | collective-permute-start | bytes 1032200 | tf_op jit(solution)/shard_map/ppermute | solution.py:380
  5.1 15.7 %collective-permute-start = (bf16[48,3584]{1,0:T(8,128)(2,1)S(1)}, bf16[48,3584]{1,0:T(8,128)(2,1)S(1)}, u32[]{:S(2)}, u32[]{:S(2)}) collective-permute-start(bf16[48,3584]{1,0:T(8,128)(2,1)S(1)} %slice.19.refs_0_), channel_id=1, source_target_pairs={{0,1},{1,0},{2,3},{3,2},{4,5},{5,4},{6,7},{7,6},{8,9},{9,8},{10,11... | collective-permute-start | bytes 1032200 | tf_op jit(solution)/shard_map/ppermute | solution.py:380
  7.5 2.1 %copy-start = (bf16[192,3584]{1,0:T(8,128)(2,1)S(1)}, bf16[192,3584]{1,0:T(8,128)(2,1)}, u32[]{:S(2)}) copy-start(bf16[192,3584]{1,0:T(8,128)(2,1)} %hidden_ref.1) | copy-start | bytes 4128772
  9.6 1.5 copy-start.1
  21.4 12.3 %collective-permute-start.2 = (bf16[48,3584]{1,0:T(8,128)(2,1)S(1)}, bf16[48,3584]{1,0:T(8,128)(2,1)S(1)}, u32[]{:S(2)}, u32[]{:S(2)}) collective-permute-start(bf16[48,3584]{1,0:T(8,128)(2,1)S(1)} %forward.3.refs_0_.refs_5_), channel_id=1, source_target_pairs={{0,2},{1,0},{2,3},{3,1},{4,6},{5,4},{6,7},{7,5},{8,10},{9,8},{10,1... | collective-permute-start | bytes 1032200 | tf_op jit(solution)/shard_map/ppermute | solution.py:414
  28.8 29.6 %collective-permute-start.4 = (bf16[80,3584]{1,0:T(8,128)(2,1)S(1)}, bf16[80,3584]{1,0:T(8,128)(2,1)S(1)}, u32[]{:S(2)}, u32[]{:S(2)}) collective-permute-start(bf16[80,3584]{1,0:T(8,128)(2,1)S(1)} %get-tuple-element.56.refs_0_), channel_id=1, source_target_pairs={{0,2},{1,3},{2,0},{3,1},{4,6},{5,7},{6,4},{7,5},{8,10},{9,11},{10,... | collective-permute-start | bytes 1720328 | tf_op jit(solution)/shard_map/ppermute | solution.py:380
  34.6 26.6 %collective-permute-start.3 = (bf16[80,3584]{1,0:T(8,128)(2,1)S(1)}, bf16[80,3584]{1,0:T(8,128)(2,1)S(1)}, u32[]{:S(2)}, u32[]{:S(2)}) collective-permute-start(bf16[80,3584]{1,0:T(8,128)(2,1)S(1)} %get-tuple-element.56.refs_0_), channel_id=1, source_target_pairs={{0,1},{1,0},{2,3},{3,2},{4,5},{5,4},{6,7},{7,6},{8,9},{9,8},{10,11... | collective-permute-start | bytes 1720328 | tf_op jit(solution)/shard_map/ppermute | solution.py:380
  46.6 11.4 %collective-permute-start.5 = (bf16[96,4608]{1,0:T(8,128)(2,1)S(1)}, bf16[96,4608]{1,0:T(8,128)(2,1)S(1)}, u32[]{:S(2)}, u32[]{:S(2)}) collective-permute-start(bf16[96,4608]{1,0:T(8,128)(2,1)S(1)} %get-tuple-element.58), channel_id=1, source_target_pairs={{0,4},{4,0},{8,12},{12,8},{1,5},{5,1},{9,13},{13,9},{2,6},{6,2},{1... | collective-permute-start | bytes 2654216 | tf_op jit(solution)/shard_map/ppermute | solution.py:439
  57.4 6.0 %collective-permute-start.7 = (bf16[96,4608]{1,0:T(8,128)(2,1)S(1)}, bf16[96,4608]{1,0:T(8,128)(2,1)S(1)}, u32[]{:S(2)}, u32[]{:S(2)}) collective-permute-start(bf16[96,4608]{1,0:T(8,128)(2,1)S(1)} %get-tuple-element.61), channel_id=1, source_target_pairs={{0,4},{4,0},{8,12},{12,8},{1,5},{5,1},{9,13},{13,9},{2,6},{6,2},{1... | collective-permute-start | bytes 2654216 | tf_op jit(solution)/shard_map/ppermute | solution.py:439
  61.8 13.5 %collective-permute-start.6 = (bf16[80,3584]{1,0:T(8,128)(2,1)S(1)}, bf16[80,3584]{1,0:T(8,128)(2,1)S(1)}, u32[]{:S(2)}, u32[]{:S(2)}) collective-permute-start(bf16[80,3584]{1,0:T(8,128)(2,1)S(1)} %forward.4.refs_0_), channel_id=1, source_target_pairs={{0,2},{1,0},{2,3},{3,1},{4,6},{5,4},{6,7},{7,5},{8,10},{9,8},{10,1... | collective-permute-start | bytes 1720328 | tf_op jit(solution)/shard_map/ppermute | solution.py:414
  61.8 24.5 %collective-permute-start.10 = (bf16[48,4608]{1,0:T(8,128)(2,1)S(1)}, bf16[48,4608]{1,0:T(8,128)(2,1)S(1)}, u32[]{:S(2)}, u32[]{:S(2)}) collective-permute-start(bf16[48,4608]{1,0:T(8,128)(2,1)S(1)} %get-tuple-element.64), channel_id=1, source_target_pairs={{0,8},{4,12},{8,0},{12,4},{1,9},{5,13},{9,1},{13,5},{2,10},{6,14},... | collective-permute-start | bytes 1327112 | tf_op jit(solution)/shard_map/ppermute | solution.py:444
  63.8 37.6 %collective-permute-start.13 = (bf16[48,4608]{1,0:T(8,128)(2,1)S(1)}, bf16[48,4608]{1,0:T(8,128)(2,1)S(1)}, u32[]{:S(2)}, u32[]{:S(2)}) collective-permute-start(bf16[48,4608]{1,0:T(8,128)(2,1)S(1)} %get-tuple-element.68), channel_id=1, source_target_pairs={{0,8},{4,12},{8,0},{12,4},{1,9},{5,13},{9,1},{13,5},{2,10},{6,14},... | collective-permute-start | bytes 1327112 | tf_op jit(solution)/shard_map/ppermute | solution.py:444
  75.9 20.8 %collective-permute-start.9 = (bf16[64,3584]{1,0:T(8,128)(2,1)S(1)}, bf16[64,3584]{1,0:T(8,128)(2,1)S(1)}, u32[]{:S(2)}, u32[]{:S(2)}) collective-permute-start(bf16[64,3584]{1,0:T(8,128)(2,1)S(1)} %get-tuple-element.63.refs_0_), channel_id=1, source_target_pairs={{0,2},{1,3},{2,0},{3,1},{4,6},{5,7},{6,4},{7,5},{8,10},{9,11},{10,... | collective-permute-start | bytes 1376264 | tf_op jit(solution)/shard_map/ppermute | solution.py:380
  77.2 19.9 %collective-permute-start.8 = (bf16[64,3584]{1,0:T(8,128)(2,1)S(1)}, bf16[64,3584]{1,0:T(8,128)(2,1)S(1)}, u32[]{:S(2)}, u32[]{:S(2)}) collective-permute-start(bf16[64,3584]{1,0:T(8,128)(2,1)S(1)} %get-tuple-element.63.refs_0_), channel_id=1, source_target_pairs={{0,1},{1,0},{2,3},{3,2},{4,5},{5,4},{6,7},{7,6},{8,9},{9,8},{10,11... | collective-permute-start | bytes 1376264 | tf_op jit(solution)/shard_map/ppermute | solution.py:380
  86.3 13.1 %collective-permute-start.14 = (bf16[160,3072]{1,0:T(8,128)(2,1)S(1)}, bf16[160,3072]{1,0:T(8,128)(2,1)S(1)}, u32[]{:S(2)}, u32[]{:S(2)}) collective-permute-start(bf16[160,3072]{1,0:T(8,128)(2,1)S(1)} %get-tuple-element.70), channel_id=1, source_target_pairs={{0,4},{4,0},{8,12},{12,8},{1,5},{5,1},{9,13},{13,9},{2,6},{6,2},{1... | collective-permute-start | bytes 2949128 | tf_op jit(solution)/shard_map/ppermute | solution.py:439
  95.9 15.1 %collective-permute-start.12 = (bf16[160,3072]{1,0:T(8,128)(2,1)S(1)}, bf16[160,3072]{1,0:T(8,128)(2,1)S(1)}, u32[]{:S(2)}, u32[]{:S(2)}) collective-permute-start(bf16[160,3072]{1,0:T(8,128)(2,1)S(1)} %get-tuple-element.67), channel_id=1, source_target_pairs={{0,4},{4,0},{8,12},{12,8},{1,5},{5,1},{9,13},{13,9},{2,6},{6,2},{1... | collective-permute-start | bytes 2949128 | tf_op jit(solution)/shard_map/ppermute | solution.py:439
  97.7 14.5 %collective-permute-start.11 = (bf16[64,3584]{1,0:T(8,128)(2,1)S(1)}, bf16[64,3584]{1,0:T(8,128)(2,1)S(1)}, u32[]{:S(2)}, u32[]{:S(2)}) collective-permute-start(bf16[64,3584]{1,0:T(8,128)(2,1)S(1)} %forward.5.refs_0_), channel_id=1, source_target_pairs={{0,2},{1,0},{2,3},{3,1},{4,6},{5,4},{6,7},{7,5},{8,10},{9,8},{10,1... | collective-permute-start | bytes 1376264 | tf_op jit(solution)/shard_map/ppermute | solution.py:414
  99.9 13.0 %collective-permute-start.16 = (bf16[80,3072]{1,0:T(8,128)(2,1)S(1)}, bf16[80,3072]{1,0:T(8,128)(2,1)S(1)}, u32[]{:S(2)}, u32[]{:S(2)}) collective-permute-start(bf16[80,3072]{1,0:T(8,128)(2,1)S(1)} %get-tuple-element.75), channel_id=1, source_target_pairs={{0,8},{4,12},{8,0},{12,4},{1,9},{5,13},{9,1},{13,5},{2,10},{6,14},... | collective-permute-start | bytes 1474568 | tf_op jit(solution)/shard_map/ppermute | solution.py:444
  111.0 10.4 %collective-permute-start.15 = (bf16[160,3072]{1,0:T(8,128)(2,1)S(1)}, bf16[160,3072]{1,0:T(8,128)(2,1)S(1)}, u32[]{:S(2)}, u32[]{:S(2)}) collective-permute-start(bf16[160,3072]{1,0:T(8,128)(2,1)S(1)} %get-tuple-element.74), channel_id=1, source_target_pairs={{0,4},{4,0},{8,12},{12,8},{1,5},{5,1},{9,13},{13,9},{2,6},{6,2},{1... | collective-permute-start | bytes 2949128 | tf_op jit(solution)/shard_map/ppermute | solution.py:439
  111.6 14.0 %collective-permute-start.18 = (bf16[80,3072]{1,0:T(8,128)(2,1)S(1)}, bf16[80,3072]{1,0:T(8,128)(2,1)S(1)}, u32[]{:S(2)}, u32[]{:S(2)}) collective-permute-start(bf16[80,3072]{1,0:T(8,128)(2,1)S(1)} %get-tuple-element.80), channel_id=1, source_target_pairs={{0,8},{4,12},{8,0},{12,4},{1,9},{5,13},{9,1},{13,5},{2,10},{6,14},... | collective-permute-start | bytes 1474568 | tf_op jit(solution)/shard_map/ppermute | solution.py:444
  121.1 12.7 %collective-permute-start.19 = (bf16[128,3072]{1,0:T(8,128)(2,1)S(1)}, bf16[128,3072]{1,0:T(8,128)(2,1)S(1)}, u32[]{:S(2)}, u32[]{:S(2)}) collective-permute-start(bf16[128,3072]{1,0:T(8,128)(2,1)S(1)} %get-tuple-element.83), channel_id=1, source_target_pairs={{0,4},{4,0},{8,12},{12,8},{1,5},{5,1},{9,13},{13,9},{2,6},{6,2},{1... | collective-permute-start | bytes 2359304 | tf_op jit(solution)/shard_map/ppermute | solution.py:439
  121.9 13.9 %collective-permute-start.17 = (bf16[80,3072]{1,0:T(8,128)(2,1)S(1)}, bf16[80,3072]{1,0:T(8,128)(2,1)S(1)}, u32[]{:S(2)}, u32[]{:S(2)}) collective-permute-start(bf16[80,3072]{1,0:T(8,128)(2,1)S(1)} %get-tuple-element.79), channel_id=1, source_target_pairs={{0,8},{4,12},{8,0},{12,4},{1,9},{5,13},{9,1},{13,5},{2,10},{6,14},... | collective-permute-start | bytes 1474568 | tf_op jit(solution)/shard_map/ppermute | solution.py:444
  133.8 13.2 %collective-permute-start.22 = (bf16[128,3072]{1,0:T(8,128)(2,1)S(1)}, bf16[128,3072]{1,0:T(8,128)(2,1)S(1)}, u32[]{:S(2)}, u32[]{:S(2)}) collective-permute-start(bf16[128,3072]{1,0:T(8,128)(2,1)S(1)} %get-tuple-element.92), channel_id=1, source_target_pairs={{0,4},{4,0},{8,12},{12,8},{1,5},{5,1},{9,13},{13,9},{2,6},{6,2},{1... | collective-permute-start | bytes 2359304 | tf_op jit(solution)/shard_map/ppermute | solution.py:439
  134.3 11.6 %collective-permute-start.20 = (bf16[64,3072]{1,0:T(8,128)(2,1)S(1)}, bf16[64,3072]{1,0:T(8,128)(2,1)S(1)}, u32[]{:S(2)}, u32[]{:S(2)}) collective-permute-start(bf16[64,3072]{1,0:T(8,128)(2,1)S(1)} %get-tuple-element.88), channel_id=1, source_target_pairs={{0,8},{4,12},{8,0},{12,4},{1,9},{5,13},{9,1},{13,5},{2,10},{6,14},... | collective-permute-start | bytes 1179656 | tf_op jit(solution)/shard_map/ppermute | solution.py:444
  146.9 2.3 %collective-permute-start.21 = (bf16[128,3072]{1,0:T(8,128)(2,1)S(1)}, bf16[128,3072]{1,0:T(8,128)(2,1)S(1)}, u32[]{:S(2)}, u32[]{:S(2)}) collective-permute-start(bf16[128,3072]{1,0:T(8,128)(2,1)S(1)} %get-tuple-element.91), channel_id=1, source_target_pairs={{0,4},{4,0},{8,12},{12,8},{1,5},{5,1},{9,13},{13,9},{2,6},{6,2},{1... | collective-permute-start | bytes 2359304 | tf_op jit(solution)/shard_map/ppermute | solution.py:452
  147.4 12.0 %collective-permute-start.24 = (bf16[64,3072]{1,0:T(8,128)(2,1)S(1)}, bf16[64,3072]{1,0:T(8,128)(2,1)S(1)}, u32[]{:S(2)}, u32[]{:S(2)}) collective-permute-start(bf16[64,3072]{1,0:T(8,128)(2,1)S(1)} %get-tuple-element.96), channel_id=1, source_target_pairs={{0,8},{4,12},{8,0},{12,4},{1,9},{5,13},{9,1},{13,5},{2,10},{6,14},... | collective-permute-start | bytes 1179656 | tf_op jit(solution)/shard_map/ppermute | solution.py:444
  149.6 17.7 %collective-permute-start.23 = (bf16[64,3072]{1,0:T(8,128)(2,1)S(1)}, bf16[64,3072]{1,0:T(8,128)(2,1)S(1)}, u32[]{:S(2)}, u32[]{:S(2)}) collective-permute-start(bf16[64,3072]{1,0:T(8,128)(2,1)S(1)} %get-tuple-element.95), channel_id=1, source_target_pairs={{0,8},{4,12},{8,0},{12,4},{1,9},{5,13},{9,1},{13,5},{2,10},{6,14},... | collective-permute-start | bytes 1179656 | tf_op jit(solution)/shard_map/ppermute | solution.py:444

commit v8 on v7

--- a/solution.py
+++ b/solution.py
@@ -247,9 +247,13 @@
             taken.wait()
 
 
-def product(rows, weight, start, width, after, ending=None, terms=(), out=None, shape=None):
+def tile_of(width):
+    return divisor(width, (512, 384, 256, 128))
+
+
+def product(rows, lead, weight, start, width, after, ending=None, terms=(), out=None, shape=None):
     height, depth = rows.shape
-    tile = divisor(width, (512, 384, 256, 128))
+    tile = lead.shape[1]
     slots = 4
     half = jax.ShapeDtypeStruct((height // 2, width), BF16)
     outs = [half, half]
@@ -258,7 +262,7 @@
         pltpu.VMEM((slots, depth, tile), BF16),
         pltpu.SemaphoreType.DMA((slots,)),
     ]
-    operands = [rows, weight[:, start:start + tile], weight, *terms]
+    operands = [rows, lead, weight, *terms]
     aliases = {}
     ending = (0, 0, 0, 0) if not terms else (*ending, terms[0].shape[1], len(terms))
     if terms:
@@ -347,7 +351,7 @@
     return pieces
 
 
-SHARES = ((9, 9), (6, 6, 6), (6, 6, 6))
+SHARES = ((8, 10), (6, 6, 6), (6, 6, 6))
 
 
 def chunk_sizes(block):
@@ -400,8 +404,11 @@
     def across(ahead):
         return [(g, (g // 2 + ahead) % chips * 2 + g % 2) for g in range(n_gx)]
 
-    out, after = None, own[1:2]
     pieces = [column_pieces(columns, shares) for shares in SHARES]
+    cuts = sorted({(start, tile_of(width)) for each in pieces for start, width in each})
+    leads = {(start, tile): weight[:, start:start + tile] for start, tile in cuts}
+
+    out, after = None, own[1:2] + list(leads.values())
     products, sums, waiting = {}, {}, {}
     for item in sum(ORDER, ()):
         long = item.endswith("!")
@@ -430,7 +437,7 @@
                 done = item[4:]
                 ending = (firsts[int(done[0])], pieces[int(done[0])][int(done[1])][0])
                 extra = dict(ending=ending, terms=sums[done], out=out, shape=(block, columns))
-            send, keep, *rest = product(rows, weight, start, width, after, **extra)
+            send, keep, *rest = product(rows, leads[start, tile_of(width)], weight, start, width, after, **extra)
             out = rest[0] if rest else out
             after = [keep]
             if late:

time: 169 us -> 183 us (1.083)
  local copies, waits for them, and re-layouts: 9.27 us -> 19.6 us
  waiting for transfers between devices: 44.9 us -> 50.9 us
  starting transfers between devices: 22.5 us -> 20.6 us
    ppermute x3, waiting for transfers between devices: 10.8 us -> 17.3 us  [local(): lax.ppermute(given, 'gy', [(0, 2), (1, 0), (2, 3), (3, 1)])]
    unnamed x4 -> x20, local copies, waits for them, and re-layouts: 1.51 us -> 6.76 us
    slice x1, local copies, waits for them, and re-layouts: 5.93 us -> 11 us  [local(): weight[:, start:start + tile]]
  transfers between devices with their start and end apart: 25 -> 25, of which waited for: 12 -> 11; matrix products, arithmetic and copies ran while one was open for 4% -> 7% of each run, Pallas kernels for 53% -> 49%
where the time goes in v8:
time: 183 us
  Pallas kernels  91.5 us (50%)
  waiting for transfers between devices  50.9 us (28%)
  starting transfers between devices  20.6 us (11%)
  local copies, waits for them, and re-layouts  19.6 us (11%)
    pallas_call x8, Pallas kernels, product(): pl.pallas_call(functools.partial(product_kernel, start, tile, width // ti...  74.3 us
    ppermute x8, waiting for transfers between devices, local(): lax.ppermute(away[(ahead - 1) * size:ahead * size], 'gx', across(ahead))  21.5 us
    ppermute x3, waiting for transfers between devices, local(): lax.ppermute(given, 'gy', [(0, 2), (1, 0), (2, 3), (3, 1)])  17.3 us
    slice x1, local copies, waits for them, and re-layouts, local(): weight[:, start:start + tile]  11 us
    ppermute x6, waiting for transfers between devices, swap(): return lax.ppermute(array, 'gy', [(k, k ^ distance) for k in range(n_gy)])  10.6 us
    ppermute x6, starting transfers between devices, swap(): return lax.ppermute(array, 'gy', [(k, k ^ distance) for k in range(n_gy)])  10.3 us
    ppermute x8, starting transfers between devices, local(): lax.ppermute(away[(ahead - 1) * size:ahead * size], 'gx', across(ahead))  6.85 us
    unnamed x20, local copies, waits for them, and re-layouts  6.76 us
  transfers between devices with their start and end apart: 25, of which 11 were waited for; matrix products, arithmetic and copies ran while one was open for 7% of the time, Pallas kernels for 49%

profile of v8, /device:TPU:0, one launch (start us, length us, event | category | flops | bytes accessed | tf_op | source)
XLA Modules:
  0.0 183.1 jit_solution(13759022074653249965)
XLA Ops:
  1.0 4.1 %collective-permute-start.1 = (bf16[48,3584]{1,0:T(8,128)(2,1)S(1)}, bf16[48,3584]{1,0:T(8,128)(2,1)S(1)}, u32[]{:S(2)}, u32[]{:S(2)}) collective-permute-start(bf16[48,3584]{1,0:T(8,128)(2,1)S(1)} %slice.15.refs_0_), channel_id=1, source_target_pairs={{0,2},{1,3},{2,0},{3,1},{4,6},{5,7},{6,4},{7,5},{8,10},{9,11},{10,... | collective-permute-start | bytes 1032200 | tf_op jit(solution)/shard_map/ppermute | solution.py:384
  5.1 1.6 collective-permute-start
  7.5 2.0 %onehot.1.onehot_ref = bf16[768,256]{1,0:T(8,128)(2,1)S(1)} custom-call(s32[768,1]{1,0:T(8,128)S(1)} %broadcast_in_dim.4.parents_ref), custom_call_target="tpu_custom_call" | custom-call | flops 19327352832 | bytes 12582912 | tf_op jit(solution)/shard_map/onehot/pallas_call | solution.py:53
  9.6 11.0 %fusion = (bf16[3584,512]{1,0:T(8,128)(2,1)}, bf16[3584,512]{1,0:T(8,128)(2,1)}, bf16[3584,512]{1,0:T(8,128)(2,1)}, bf16[3584,512]{1,0:T(8,128)(2,1)}) fusion(bf16[3584,9216]{1,0:T(8,128)(2,1)} %weight_ref.15), kind=kLoop, calls=%fused_computation.1 | loop fusion | bytes 29360128 | tf_op jit(solution)/shard_map/slice | solution.py:409
  20.7 1.5 copy-done.9
  22.2 2.0 %own.1 = (bf16[80,3584]{1,0:T(8,128)(2,1)S(1)}, bf16[64,3584]{1,0:T(8,128)(2,1)S(1)}) custom-call(s32[2]{0:T(128)S(1)} %pad_add_fusion.place_ref, bf16[768,256]{1,0:T(8,128)(2,1)S(1)} %onehot.1.onehot_ref, bf16[256,3584]{1,0:T(8,128)(2,1)S(1)} %copy-done.9, bf16[192,3584]{1,0:T(8,128)(2,1)S(1)} %copy-done.8), custom_call_target="tpu_custom_call" | custom-call | flops 2113929216 | bytes 24772608 | tf_op jit(solution)/shard_map/own/pallas_call | solution.py:159
  25.3 2.0 %copy-done.4 = bf16[3584,512]{1,0:T(8,128)(2,1)S(1)} copy-done((bf16[3584,512]{1,0:T(8,128)(2,1)S(1)}, bf16[3584,512]{1,0:T(8,128)(2,1)}, u32[]{:S(2)}) %copy-start.4) | copy-done | bytes 3670040
  27.4 2.0 %copy-done.6 = bf16[3584,512]{1,0:T(8,128)(2,1)S(1)} copy-done((bf16[3584,512]{1,0:T(8,128)(2,1)S(1)}, bf16[3584,512]{1,0:T(8,128)(2,1)}, u32[]{:S(2)}) %copy-start.6) | copy-done | bytes 3670040
  30.6 2.4 %look.1.refs_4_ = bf16[192,3584]{1,0:T(8,128)(2,1)S(1)} custom-call(s32[2]{0:T(128)S(1)} %pad_add_fusion.place_ref, bf16[768,256]{1,0:T(8,128)(2,1)S(1)} %onehot.1.onehot_ref, bf16[256,3584]{1,0:T(8,128)(2,1)S(1)} %copy-done.9, bf16[48,3584]{1,0:T(8,128)(2,1)S(1)} %forward.3.refs_0_.refs_5_), custom_call_target="tpu_custom_call" | custom-call | flops 2818572288 | bytes 22020096 | tf_op jit(solution)/shard_map/look/pallas_call | solution.py:105
  33.0 6.4 %collective-permute-done.2.refs_3_ = bf16[48,3584]{1,0:T(8,128)(2,1)S(1)} collective-permute-done((bf16[48,3584]{1,0:T(8,128)(2,1)S(1)}, bf16[48,3584]{1,0:T(8,128)(2,1)S(1)}, u32[]{:S(2)}, u32[]{:S(2)}) %collective-permute-start.2) | collective-permute-done | bytes 344096 | tf_op jit(solution)/shard_map/ppermute | solution.py:421
  40.3 9.8 %product.8 = (bf16[96,4096]{1,0:T(8,128)(2,1)S(1)}, bf16[96,4096]{1,0:T(8,128)(2,1)S(1)}) custom-call(bf16[192,3584]{1,0:T(8,128)(2,1)S(1)} %arrange.3.rows_ref.refs_0_, bf16[3584,512]{1,0:T(8,128)(2,1)S(1)} %copy-done.5, bf16[3584,9216]{1,0:T(8,128)(2,1)} %weight_ref.15, bf16[192,3584]{1,0:T(8,128)(2,1)S(1)} %arrange.3.rows_ref.refs_0_), custom_call_target="tpu_custom_call" | custom-call | flops 45097156608 | bytes 258473984 | tf_op jit(solution)/shard_map/product/pallas_call | solution.py:281
  50.1 3.2 %collective-permute-start.3 = (bf16[80,3584]{1,0:T(8,128)(2,1)S(1)}, bf16[80,3584]{1,0:T(8,128)(2,1)S(1)}, u32[]{:S(2)}, u32[]{:S(2)}) collective-permute-start(bf16[80,3584]{1,0:T(8,128)(2,1)S(1)} %get-tuple-element.56.refs_0_), channel_id=1, source_target_pairs={{0,1},{1,0},{2,3},{3,2},{4,5},{5,4},{6,7},{7,6},{8,9},{9,8},{10,11... | collective-permute-start | bytes 1720328 | tf_op jit(solution)/shard_map/ppermute | solution.py:384
  53.3 11.8 %product.9 = (bf16[96,5120]{1,0:T(8,128)(2,1)S(1)}, bf16[96,5120]{1,0:T(8,128)(2,1)S(1)}) custom-call(bf16[192,3584]{1,0:T(8,128)(2,1)S(1)} %arrange.3.rows_ref.refs_0_, bf16[3584,512]{1,0:T(8,128)(2,1)S(1)} %copy-done.7, bf16[3584,9216]{1,0:T(8,128)(2,1)} %weight_ref.15, bf16[96,4096]{1,0:T(8,128)(2,1)S(1)} %get-tuple-element.57.refs_0_.keep_ref), custom_call_target="tpu_custom_call" | custom-call | flops 56371445760 | bytes 320339968 | tf_op jit(solution)/shard_map/product/pallas_call | solution.py:281
  66.0 9.6 %collective-permute-done.3.near_ref.refs_1_ = bf16[80,3584]{1,0:T(8,128)(2,1)S(1)} collective-permute-done((bf16[80,3584]{1,0:T(8,128)(2,1)S(1)}, bf16[80,3584]{1,0:T(8,128)(2,1)S(1)}, u32[]{:S(2)}, u32[]{:S(2)}) %collective-permute-start.3) | collective-permute-done | bytes 573472 | tf_op jit(solution)/shard_map/ppermute | solution.py:384
  76.3 1.6 collective-permute-start.10
  79.0 10.9 %collective-permute-done.6.refs_3_ = bf16[80,3584]{1,0:T(8,128)(2,1)S(1)} collective-permute-done((bf16[80,3584]{1,0:T(8,128)(2,1)S(1)}, bf16[80,3584]{1,0:T(8,128)(2,1)S(1)}, u32[]{:S(2)}, u32[]{:S(2)}) %collective-permute-start.6) | collective-permute-done | bytes 573472 | tf_op jit(solution)/shard_map/ppermute | solution.py:421
  90.6 1.2 collective-permute-start.9
  91.8 9.0 %product.10 = (bf16[160,3072]{1,0:T(8,128)(2,1)S(1)}, bf16[160,3072]{1,0:T(8,128)(2,1)S(1)}) custom-call(bf16[320,3584]{1,0:T(8,128)(2,1)S(1)} %arrange.4.rows_ref.refs_0_, bf16[3584,512]{1,0:T(8,128)(2,1)S(1)} %copy-done.5, bf16[3584,9216]{1,0:T(8,128)(2,1)} %weight_ref.15, bf16[320,3584]{1,0:T(8,128)(2,1)S(1)} %arrange.4.rows_ref.refs_0_), custom_call_target="tpu_custom_call" | custom-call | flops 56371445760 | bytes 210239488 | tf_op jit(solution)/shard_map/product/pallas_call | solution.py:281
  101.0 9.3 %product.11 = (bf16[160,3072]{1,0:T(8,128)(2,1)S(1)}, bf16[160,3072]{1,0:T(8,128)(2,1)S(1)}, bf16[192,9216]{1,0:T(8,128)(2,1)}) custom-call(bf16[320,3584]{1,0:T(8,128)(2,1)S(1)} %arrange.4.rows_ref.refs_0_, bf16[3584,512]{1,0:T(8,128)(2,1)S(1)} %copy-done.3, bf16[3584,9216]{1,0:T(8,128)(2,1)} %weight_ref.15, ...), custom_call_target="tpu_custom_call" | custom-call | flops 56371445760 | bytes 210239488 | tf_op jit(solution)/shard_map/product/pallas_call | solution.py:281
  112.4 1.5 collective-permute-start.11
  114.3 1.6 collective-permute-start.16
  115.9 9.7 %product.12 = (bf16[160,3072]{1,0:T(8,128)(2,1)S(1)}, bf16[160,3072]{1,0:T(8,128)(2,1)S(1)}, bf16[192,9216]{1,0:T(8,128)(2,1)}) custom-call(bf16[320,3584]{1,0:T(8,128)(2,1)S(1)} %arrange.4.rows_ref.refs_0_, bf16[3584,512]{1,0:T(8,128)(2,1)S(1)} %copy-done.1, bf16[3584,9216]{1,0:T(8,128)(2,1)} %weight_ref.15, ...), custom_call_target="tpu_custom_call", output_to_operand_aliasing={{2}: (5, {})} | custom-call | flops 56371445760 | bytes 210239488 | tf_op jit(solution)/shard_map/product/pallas_call | solution.py:281
  127.5 8.2 %product.13 = (bf16[128,3072]{1,0:T(8,128)(2,1)S(1)}, bf16[128,3072]{1,0:T(8,128)(2,1)S(1)}, bf16[192,9216]{1,0:T(8,128)(2,1)}) custom-call(bf16[256,3584]{1,0:T(8,128)(2,1)S(1)} %arrange.5.rows_ref.refs_3_, bf16[3584,512]{1,0:T(8,128)(2,1)S(1)} %copy-done.5, bf16[3584,9216]{1,0:T(8,128)(2,1)} %weight_ref.15, ...), custom_call_target="tpu_custom_call", output_to_operand_aliasing={{2}: (5, {})} | custom-call | flops 45097156608 | bytes 203423744 | tf_op jit(solution)/shard_map/product/pallas_call | solution.py:281
  136.5 1.6 collective-permute-start.17
  138.1 2.1 %collective-permute-done.18.refs_1_ = bf16[80,3072]{1,0:T(8,128)(2,1)S(1)} collective-permute-done((bf16[80,3072]{1,0:T(8,128)(2,1)S(1)}, bf16[80,3072]{1,0:T(8,128)(2,1)S(1)}, u32[]{:S(2)}, u32[]{:S(2)}) %collective-permute-start.18) | collective-permute-done | bytes 491552 | tf_op jit(solution)/shard_map/ppermute | solution.py:451
  140.2 8.2 %product.14 = (bf16[128,3072]{1,0:T(8,128)(2,1)S(1)}, bf16[128,3072]{1,0:T(8,128)(2,1)S(1)}, bf16[192,9216]{1,0:T(8,128)(2,1)}) custom-call(bf16[256,3584]{1,0:T(8,128)(2,1)S(1)} %arrange.5.rows_ref.refs_3_, bf16[3584,512]{1,0:T(8,128)(2,1)S(1)} %copy-done.3, bf16[3584,9216]{1,0:T(8,128)(2,1)} %weight_ref.15, ...), custom_call_target="tpu_custom_call", output_to_operand_aliasing={{2}: (5, {})} | custom-call | flops 45097156608 | bytes 203423744 | tf_op jit(solution)/shard_map/product/pallas_call | solution.py:281
  149.2 1.2 collective-permute-done.17.refs_1_
  150.4 8.2 %product.15 = (bf16[128,3072]{1,0:T(8,128)(2,1)S(1)}, bf16[128,3072]{1,0:T(8,128)(2,1)S(1)}, bf16[192,9216]{1,0:T(8,128)(2,1)}) custom-call(bf16[256,3584]{1,0:T(8,128)(2,1)S(1)} %arrange.5.rows_ref.refs_3_, bf16[3584,512]{1,0:T(8,128)(2,1)S(1)} %copy-done.1, bf16[3584,9216]{1,0:T(8,128)(2,1)} %weight_ref.15, ...), custom_call_target="tpu_custom_call", output_to_operand_aliasing={{2}: (5, {})} | custom-call | flops 45097156608 | bytes 203423744 | tf_op jit(solution)/shard_map/product/pallas_call | solution.py:281
  158.6 1.9 %collective-permute-done.20.refs_1_ = bf16[64,3072]{1,0:T(8,128)(2,1)S(1)} collective-permute-done((bf16[64,3072]{1,0:T(8,128)(2,1)S(1)}, bf16[64,3072]{1,0:T(8,128)(2,1)S(1)}, u32[]{:S(2)}, u32[]{:S(2)}) %collective-permute-start.20) | collective-permute-done | bytes 393248 | tf_op jit(solution)/shard_map/ppermute | solution.py:451
  162.3 1.5 collective-permute-done.21.got_ref
  164.6 9.3 %collective-permute-done.24.refs_1_ = bf16[64,3072]{1,0:T(8,128)(2,1)S(1)} collective-permute-done((bf16[64,3072]{1,0:T(8,128)(2,1)S(1)}, bf16[64,3072]{1,0:T(8,128)(2,1)S(1)}, u32[]{:S(2)}, u32[]{:S(2)}) %collective-permute-start.24) | collective-permute-done | bytes 393248 | tf_op jit(solution)/shard_map/ppermute | solution.py:451
  175.1 6.9 %collective-permute-done.23.refs_1_ = bf16[64,3072]{1,0:T(8,128)(2,1)S(1)} collective-permute-done((bf16[64,3072]{1,0:T(8,128)(2,1)S(1)}, bf16[64,3072]{1,0:T(8,128)(2,1)S(1)}, u32[]{:S(2)}, u32[]{:S(2)}) %collective-permute-start.23) | collective-permute-done | bytes 393248 | tf_op jit(solution)/shard_map/ppermute | solution.py:451
  (70 shorter events, 19.4 us)
Async XLA Ops:
  1.0 23.2 %collective-permute-start.1 = (bf16[48,3584]{1,0:T(8,128)(2,1)S(1)}, bf16[48,3584]{1,0:T(8,128)(2,1)S(1)}, u32[]{:S(2)}, u32[]{:S(2)}) collective-permute-start(bf16[48,3584]{1,0:T(8,128)(2,1)S(1)} %slice.15.refs_0_), channel_id=1, source_target_pairs={{0,2},{1,3},{2,0},{3,1},{4,6},{5,7},{6,4},{7,5},{8,10},{9,11},{10,... | collective-permute-start | bytes 1032200 | tf_op jit(solution)/shard_map/ppermute | solution.py:384
  5.1 19.1 %collective-permute-start = (bf16[48,3584]{1,0:T(8,128)(2,1)S(1)}, bf16[48,3584]{1,0:T(8,128)(2,1)S(1)}, u32[]{:S(2)}, u32[]{:S(2)}) collective-permute-start(bf16[48,3584]{1,0:T(8,128)(2,1)S(1)} %slice.15.refs_0_), channel_id=1, source_target_pairs={{0,1},{1,0},{2,3},{3,2},{4,5},{5,4},{6,7},{7,6},{8,9},{9,8},{10,11... | collective-permute-start | bytes 1032200 | tf_op jit(solution)/shard_map/ppermute | solution.py:384
  9.6 11.1 %copy-start.8 = (bf16[192,3584]{1,0:T(8,128)(2,1)S(1)}, bf16[192,3584]{1,0:T(8,128)(2,1)}, u32[]{:S(2)}) copy-start(bf16[192,3584]{1,0:T(8,128)(2,1)} %hidden_ref.1) | copy-start | bytes 4128772
  22.2 2.0 %copy-start = (bf16[3584,512]{1,0:T(8,128)(2,1)S(1)}, bf16[3584,512]{1,0:T(8,128)(2,1)}, u32[]{:S(2)}) copy-start(bf16[3584,512]{1,0:T(8,128)(2,1)} %get-tuple-element.101.refs_4_.lead_ref) | copy-start | bytes 11010052
  22.2 3.2 %copy-start.2 = (bf16[3584,512]{1,0:T(8,128)(2,1)S(1)}, bf16[3584,512]{1,0:T(8,128)(2,1)}, u32[]{:S(2)}) copy-start(bf16[3584,512]{1,0:T(8,128)(2,1)} %get-tuple-element.103.refs_2_.lead_ref) | copy-start | bytes 11010052
  30.0 9.4 %collective-permute-start.2 = (bf16[48,3584]{1,0:T(8,128)(2,1)S(1)}, bf16[48,3584]{1,0:T(8,128)(2,1)S(1)}, u32[]{:S(2)}, u32[]{:S(2)}) collective-permute-start(bf16[48,3584]{1,0:T(8,128)(2,1)S(1)} %forward.3.refs_0_.refs_5_), channel_id=1, source_target_pairs={{0,2},{1,0},{2,3},{3,1},{4,6},{5,4},{6,7},{7,5},{8,10},{9,8},{10,1... | collective-permute-start | bytes 1032200 | tf_op jit(solution)/shard_map/ppermute | solution.py:421
  30.4 35.7 %collective-permute-start.4 = (bf16[80,3584]{1,0:T(8,128)(2,1)S(1)}, bf16[80,3584]{1,0:T(8,128)(2,1)S(1)}, u32[]{:S(2)}, u32[]{:S(2)}) collective-permute-start(bf16[80,3584]{1,0:T(8,128)(2,1)S(1)} %get-tuple-element.56.refs_0_), channel_id=1, source_target_pairs={{0,2},{1,3},{2,0},{3,1},{4,6},{5,7},{6,4},{7,5},{8,10},{9,11},{10,... | collective-permute-start | bytes 1720328 | tf_op jit(solution)/shard_map/ppermute | solution.py:384
  33.0 7.3 %copy-start.5 = (bf16[3584,512]{1,0:T(8,128)(2,1)S(1)}, bf16[3584,512]{1,0:T(8,128)(2,1)}, u32[]{:S(2)}) copy-start(bf16[3584,512]{1,0:T(8,128)(2,1)} %get-tuple-element.104.refs_1_.lead_ref) | copy-start | bytes 11010052
  40.3 13.0 %copy-start.7 = (bf16[3584,512]{1,0:T(8,128)(2,1)S(1)}, bf16[3584,512]{1,0:T(8,128)(2,1)}, u32[]{:S(2)}) copy-start(bf16[3584,512]{1,0:T(8,128)(2,1)} %get-tuple-element.102.refs_3_.lead_ref) | copy-start | bytes 11010052
  50.1 25.6 %collective-permute-start.3 = (bf16[80,3584]{1,0:T(8,128)(2,1)S(1)}, bf16[80,3584]{1,0:T(8,128)(2,1)S(1)}, u32[]{:S(2)}, u32[]{:S(2)}) collective-permute-start(bf16[80,3584]{1,0:T(8,128)(2,1)S(1)} %get-tuple-element.56.refs_0_), channel_id=1, source_target_pairs={{0,1},{1,0},{2,3},{3,2},{4,5},{5,4},{6,7},{7,6},{8,9},{9,8},{10,11... | collective-permute-start | bytes 1720328 | tf_op jit(solution)/shard_map/ppermute | solution.py:384
  53.3 12.3 %collective-permute-start.5 = (bf16[96,4096]{1,0:T(8,128)(2,1)S(1)}, bf16[96,4096]{1,0:T(8,128)(2,1)S(1)}, u32[]{:S(2)}, u32[]{:S(2)}) collective-permute-start(bf16[96,4096]{1,0:T(8,128)(2,1)S(1)} %get-tuple-element.58), channel_id=1, source_target_pairs={{0,4},{4,0},{8,12},{12,8},{1,5},{5,1},{9,13},{13,9},{2,6},{6,2},{1... | collective-permute-start | bytes 2359304 | tf_op jit(solution)/shard_map/ppermute | solution.py:446
  65.1 12.8 %collective-permute-start.7 = (bf16[96,5120]{1,0:T(8,128)(2,1)S(1)}, bf16[96,5120]{1,0:T(8,128)(2,1)S(1)}, u32[]{:S(2)}, u32[]{:S(2)}) collective-permute-start(bf16[96,5120]{1,0:T(8,128)(2,1)S(1)} %get-tuple-element.61), channel_id=1, source_target_pairs={{0,4},{4,0},{8,12},{12,8},{1,5},{5,1},{9,13},{13,9},{2,6},{6,2},{1... | collective-permute-start | bytes 2949128 | tf_op jit(solution)/shard_map/ppermute | solution.py:446
  76.2 13.6 %collective-permute-start.6 = (bf16[80,3584]{1,0:T(8,128)(2,1)S(1)}, bf16[80,3584]{1,0:T(8,128)(2,1)S(1)}, u32[]{:S(2)}, u32[]{:S(2)}) collective-permute-start(bf16[80,3584]{1,0:T(8,128)(2,1)S(1)} %forward.4.refs_0_), channel_id=1, source_target_pairs={{0,2},{1,0},{2,3},{3,1},{4,6},{5,4},{6,7},{7,5},{8,10},{9,8},{10,1... | collective-permute-start | bytes 1720328 | tf_op jit(solution)/shard_map/ppermute | solution.py:421
  76.3 24.6 %collective-permute-start.10 = (bf16[48,4096]{1,0:T(8,128)(2,1)S(1)}, bf16[48,4096]{1,0:T(8,128)(2,1)S(1)}, u32[]{:S(2)}, u32[]{:S(2)}) collective-permute-start(bf16[48,4096]{1,0:T(8,128)(2,1)S(1)} %get-tuple-element.64), channel_id=1, source_target_pairs={{0,8},{4,12},{8,0},{12,4},{1,9},{5,13},{9,1},{13,5},{2,10},{6,14},... | collective-permute-start | bytes 1179656 | tf_op jit(solution)/shard_map/ppermute | solution.py:451
  78.4 37.5 %collective-permute-start.13 = (bf16[48,5120]{1,0:T(8,128)(2,1)S(1)}, bf16[48,5120]{1,0:T(8,128)(2,1)S(1)}, u32[]{:S(2)}, u32[]{:S(2)}) collective-permute-start(bf16[48,5120]{1,0:T(8,128)(2,1)S(1)} %get-tuple-element.68), channel_id=1, source_target_pairs={{0,8},{4,12},{8,0},{12,4},{1,9},{5,13},{9,1},{13,5},{2,10},{6,14},... | collective-permute-start | bytes 1474568 | tf_op jit(solution)/shard_map/ppermute | solution.py:451
  90.6 10.4 %copy-start.3 = (bf16[3584,512]{1,0:T(8,128)(2,1)S(1)}, bf16[3584,512]{1,0:T(8,128)(2,1)}, u32[]{:S(2)}) copy-start(bf16[3584,512]{1,0:T(8,128)(2,1)} %get-tuple-element.103.refs_2_.lead_ref) | copy-start | bytes 11010052
  90.6 20.9 %collective-permute-start.9 = (bf16[64,3584]{1,0:T(8,128)(2,1)S(1)}, bf16[64,3584]{1,0:T(8,128)(2,1)S(1)}, u32[]{:S(2)}, u32[]{:S(2)}) collective-permute-start(bf16[64,3584]{1,0:T(8,128)(2,1)S(1)} %get-tuple-element.63.refs_0_), channel_id=1, source_target_pairs={{0,2},{1,3},{2,0},{3,1},{4,6},{5,7},{6,4},{7,5},{8,10},{9,11},{10,... | collective-permute-start | bytes 1376264 | tf_op jit(solution)/shard_map/ppermute | solution.py:384
  91.8 20.0 %collective-permute-start.8 = (bf16[64,3584]{1,0:T(8,128)(2,1)S(1)}, bf16[64,3584]{1,0:T(8,128)(2,1)S(1)}, u32[]{:S(2)}, u32[]{:S(2)}) collective-permute-start(bf16[64,3584]{1,0:T(8,128)(2,1)S(1)} %get-tuple-element.63.refs_0_), channel_id=1, source_target_pairs={{0,1},{1,0},{2,3},{3,2},{4,5},{5,4},{6,7},{7,6},{8,9},{9,8},{10,11... | collective-permute-start | bytes 1376264 | tf_op jit(solution)/shard_map/ppermute | solution.py:384
  100.9 13.0 %collective-permute-start.14 = (bf16[160,3072]{1,0:T(8,128)(2,1)S(1)}, bf16[160,3072]{1,0:T(8,128)(2,1)S(1)}, u32[]{:S(2)}, u32[]{:S(2)}) collective-permute-start(bf16[160,3072]{1,0:T(8,128)(2,1)S(1)} %get-tuple-element.70), channel_id=1, source_target_pairs={{0,4},{4,0},{8,12},{12,8},{1,5},{5,1},{9,13},{13,9},{2,6},{6,2},{1... | collective-permute-start | bytes 2949128 | tf_op jit(solution)/shard_map/ppermute | solution.py:446
  110.3 5.6 %copy-start.1 = (bf16[3584,512]{1,0:T(8,128)(2,1)S(1)}, bf16[3584,512]{1,0:T(8,128)(2,1)}, u32[]{:S(2)}) copy-start(bf16[3584,512]{1,0:T(8,128)(2,1)} %get-tuple-element.101.refs_4_.lead_ref) | copy-start | bytes 11010052
  110.3 15.4 %collective-permute-start.12 = (bf16[160,3072]{1,0:T(8,128)(2,1)S(1)}, bf16[160,3072]{1,0:T(8,128)(2,1)S(1)}, u32[]{:S(2)}, u32[]{:S(2)}) collective-permute-start(bf16[160,3072]{1,0:T(8,128)(2,1)S(1)} %get-tuple-element.67), channel_id=1, source_target_pairs={{0,4},{4,0},{8,12},{12,8},{1,5},{5,1},{9,13},{13,9},{2,6},{6,2},{1... | collective-permute-start | bytes 2949128 | tf_op jit(solution)/shard_map/ppermute | solution.py:446
  112.4 14.4 %collective-permute-start.11 = (bf16[64,3584]{1,0:T(8,128)(2,1)S(1)}, bf16[64,3584]{1,0:T(8,128)(2,1)S(1)}, u32[]{:S(2)}, u32[]{:S(2)}) collective-permute-start(bf16[64,3584]{1,0:T(8,128)(2,1)S(1)} %forward.5.refs_0_), channel_id=1, source_target_pairs={{0,2},{1,0},{2,3},{3,1},{4,6},{5,4},{6,7},{7,5},{8,10},{9,8},{10,1... | collective-permute-start | bytes 1376264 | tf_op jit(solution)/shard_map/ppermute | solution.py:421
  114.3 13.2 %collective-permute-start.16 = (bf16[80,3072]{1,0:T(8,128)(2,1)S(1)}, bf16[80,3072]{1,0:T(8,128)(2,1)S(1)}, u32[]{:S(2)}, u32[]{:S(2)}) collective-permute-start(bf16[80,3072]{1,0:T(8,128)(2,1)S(1)} %get-tuple-element.75), channel_id=1, source_target_pairs={{0,8},{4,12},{8,0},{12,4},{1,9},{5,13},{9,1},{13,5},{2,10},{6,14},... | collective-permute-start | bytes 1474568 | tf_op jit(solution)/shard_map/ppermute | solution.py:451
  125.6 10.4 %collective-permute-start.15 = (bf16[160,3072]{1,0:T(8,128)(2,1)S(1)}, bf16[160,3072]{1,0:T(8,128)(2,1)S(1)}, u32[]{:S(2)}, u32[]{:S(2)}) collective-permute-start(bf16[160,3072]{1,0:T(8,128)(2,1)S(1)} %get-tuple-element.74), channel_id=1, source_target_pairs={{0,4},{4,0},{8,12},{12,8},{1,5},{5,1},{9,13},{13,9},{2,6},{6,2},{1... | collective-permute-start | bytes 2949128 | tf_op jit(solution)/shard_map/ppermute | solution.py:446
  126.2 14.0 %collective-permute-start.18 = (bf16[80,3072]{1,0:T(8,128)(2,1)S(1)}, bf16[80,3072]{1,0:T(8,128)(2,1)S(1)}, u32[]{:S(2)}, u32[]{:S(2)}) collective-permute-start(bf16[80,3072]{1,0:T(8,128)(2,1)S(1)} %get-tuple-element.80), channel_id=1, source_target_pairs={{0,8},{4,12},{8,0},{12,4},{1,9},{5,13},{9,1},{13,5},{2,10},{6,14},... | collective-permute-start | bytes 1474568 | tf_op jit(solution)/shard_map/ppermute | solution.py:451
  135.8 12.7 %collective-permute-start.19 = (bf16[128,3072]{1,0:T(8,128)(2,1)S(1)}, bf16[128,3072]{1,0:T(8,128)(2,1)S(1)}, u32[]{:S(2)}, u32[]{:S(2)}) collective-permute-start(bf16[128,3072]{1,0:T(8,128)(2,1)S(1)} %get-tuple-element.83), channel_id=1, source_target_pairs={{0,4},{4,0},{8,12},{12,8},{1,5},{5,1},{9,13},{13,9},{2,6},{6,2},{1... | collective-permute-start | bytes 2359304 | tf_op jit(solution)/shard_map/ppermute | solution.py:446
  136.5 13.9 %collective-permute-start.17 = (bf16[80,3072]{1,0:T(8,128)(2,1)S(1)}, bf16[80,3072]{1,0:T(8,128)(2,1)S(1)}, u32[]{:S(2)}, u32[]{:S(2)}) collective-permute-start(bf16[80,3072]{1,0:T(8,128)(2,1)S(1)} %get-tuple-element.79), channel_id=1, source_target_pairs={{0,8},{4,12},{8,0},{12,4},{1,9},{5,13},{9,1},{13,5},{2,10},{6,14},... | collective-permute-start | bytes 1474568 | tf_op jit(solution)/shard_map/ppermute | solution.py:451
  148.4 13.2 %collective-permute-start.22 = (bf16[128,3072]{1,0:T(8,128)(2,1)S(1)}, bf16[128,3072]{1,0:T(8,128)(2,1)S(1)}, u32[]{:S(2)}, u32[]{:S(2)}) collective-permute-start(bf16[128,3072]{1,0:T(8,128)(2,1)S(1)} %get-tuple-element.92), channel_id=1, source_target_pairs={{0,4},{4,0},{8,12},{12,8},{1,5},{5,1},{9,13},{13,9},{2,6},{6,2},{1... | collective-permute-start | bytes 2359304 | tf_op jit(solution)/shard_map/ppermute | solution.py:446
  148.9 11.6 %collective-permute-start.20 = (bf16[64,3072]{1,0:T(8,128)(2,1)S(1)}, bf16[64,3072]{1,0:T(8,128)(2,1)S(1)}, u32[]{:S(2)}, u32[]{:S(2)}) collective-permute-start(bf16[64,3072]{1,0:T(8,128)(2,1)S(1)} %get-tuple-element.88), channel_id=1, source_target_pairs={{0,8},{4,12},{8,0},{12,4},{1,9},{5,13},{9,1},{13,5},{2,10},{6,14},... | collective-permute-start | bytes 1179656 | tf_op jit(solution)/shard_map/ppermute | solution.py:451
  161.6 2.3 %collective-permute-start.21 = (bf16[128,3072]{1,0:T(8,128)(2,1)S(1)}, bf16[128,3072]{1,0:T(8,128)(2,1)S(1)}, u32[]{:S(2)}, u32[]{:S(2)}) collective-permute-start(bf16[128,3072]{1,0:T(8,128)(2,1)S(1)} %get-tuple-element.91), channel_id=1, source_target_pairs={{0,4},{4,0},{8,12},{12,8},{1,5},{5,1},{9,13},{13,9},{2,6},{6,2},{1... | collective-permute-start | bytes 2359304 | tf_op jit(solution)/shard_map/ppermute | solution.py:459
  162.0 12.0 %collective-permute-start.24 = (bf16[64,3072]{1,0:T(8,128)(2,1)S(1)}, bf16[64,3072]{1,0:T(8,128)(2,1)S(1)}, u32[]{:S(2)}, u32[]{:S(2)}) collective-permute-start(bf16[64,3072]{1,0:T(8,128)(2,1)S(1)} %get-tuple-element.96), channel_id=1, source_target_pairs={{0,8},{4,12},{8,0},{12,4},{1,9},{5,13},{9,1},{13,5},{2,10},{6,14},... | collective-permute-start | bytes 1179656 | tf_op jit(solution)/shard_map/ppermute | solution.py:451
  164.3 17.7 %collective-permute-start.23 = (bf16[64,3072]{1,0:T(8,128)(2,1)S(1)}, bf16[64,3072]{1,0:T(8,128)(2,1)S(1)}, u32[]{:S(2)}, u32[]{:S(2)}) collective-permute-start(bf16[64,3072]{1,0:T(8,128)(2,1)S(1)} %get-tuple-element.95), channel_id=1, source_target_pairs={{0,8},{4,12},{8,0},{12,4},{1,9},{5,13},{9,1},{13,5},{2,10},{6,14},... | collective-permute-start | bytes 1179656 | tf_op jit(solution)/shard_map/ppermute | solution.py:451
  (3 other events, 5.6 us)

commit v9 on v8

--- a/solution.py
+++ b/solution.py
@@ -351,7 +351,7 @@
     return pieces
 
 
-SHARES = ((8, 10), (6, 6, 6), (6, 6, 6))
+SHARES = ((9, 9), (6, 6, 6), (6, 6, 6))
 
 
 def chunk_sizes(block):
@@ -404,11 +404,8 @@
     def across(ahead):
         return [(g, (g // 2 + ahead) % chips * 2 + g % 2) for g in range(n_gx)]
 
+    out, after = None, own[1:2]
     pieces = [column_pieces(columns, shares) for shares in SHARES]
-    cuts = sorted({(start, tile_of(width)) for each in pieces for start, width in each})
-    leads = {(start, tile): weight[:, start:start + tile] for start, tile in cuts}
-
-    out, after = None, own[1:2] + list(leads.values())
     products, sums, waiting = {}, {}, {}
     for item in sum(ORDER, ()):
         long = item.endswith("!")
@@ -423,6 +420,9 @@
             if index == 0:
                 take(1, after[0] if after else None)
                 looked = look(chips, n_gx, block, 0, sizes[0], exclusive, place, onehot, depth_table, after)
+                cuts = sorted({(start, tile_of(width)) for each in pieces for start, width in each})
+                ready = later(weight, looked)
+                leads = {(start, tile): ready[:, start:start + tile] for start, tile in cuts}
         if kind == "t":
             take(index, after[0])
         if kind == "a":

time: 183 us -> 169 us (0.923)
  local copies, waits for them, and re-layouts: 19.6 us -> 9.27 us
  waiting for transfers between devices: 50.9 us -> 44.9 us
  starting transfers between devices: 20.6 us -> 22.5 us
    ppermute x3, waiting for transfers between devices: 17.3 us -> 10.8 us  [local(): lax.ppermute(given, 'gy', [(0, 2), (1, 0), (2, 3), (3, 1)])]
    unnamed x20 -> x4, local copies, waits for them, and re-layouts: 6.76 us -> 1.51 us
    slice x1, local copies, waits for them, and re-layouts: 11 us -> 5.93 us  [local(): ready[:, start:start + tile]]
  transfers between devices with their start and end apart: 25 -> 25, of which waited for: 11 -> 12; matrix products, arithmetic and copies ran while one was open for 7% -> 4% of each run, Pallas kernels for 49% -> 53%
where the time goes in v9:
time: 169 us; the launch traced here: 168 us
  Pallas kernels  91.4 us (54%)
  waiting for transfers between devices  44.9 us (27%)
  starting transfers between devices  22.5 us (13%)
  local copies, waits for them, and re-layouts  9.27 us (5%)
    pallas_call x8, Pallas kernels, product(): pl.pallas_call(functools.partial(product_kernel, start, tile, width // ti...  74.2 us
    ppermute x8, waiting for transfers between devices, local(): lax.ppermute(away[(ahead - 1) * size:ahead * size], 'gx', across(ahead))  21.5 us
    ppermute x6, waiting for transfers between devices, swap(): return lax.ppermute(array, 'gy', [(k, k ^ distance) for k in range(n_gy)])  11.1 us
    ppermute x3, waiting for transfers between devices, local(): lax.ppermute(given, 'gy', [(0, 2), (1, 0), (2, 3), (3, 1)])  10.8 us
    ppermute x6, starting transfers between devices, swap(): return lax.ppermute(array, 'gy', [(k, k ^ distance) for k in range(n_gy)])  10.7 us
    ppermute x8, starting transfers between devices, local(): lax.ppermute(away[(ahead - 1) * size:ahead * size], 'gx', across(ahead))  6.86 us
    slice x1, local copies, waits for them, and re-layouts, local(): ready[:, start:start + tile]  5.93 us
    pallas_call x8, Pallas kernels, pair(): pl.pallas_call(pair_kernel, name='pair', grid=(width // tile,), out_shape...  3.52 us
  transfers between devices with their start and end apart: 25, of which 12 were waited for; matrix products, arithmetic and copies ran while one was open for 4% of the time, Pallas kernels for 53%

profile of v9, /device:TPU:0, one launch (start us, length us, event | category | flops | bytes accessed | tf_op | source)
XLA Modules:
  0.0 168.5 jit_solution(15702563334841347970)
XLA Ops:
  1.0 4.1 %collective-permute-start.1 = (bf16[48,3584]{1,0:T(8,128)(2,1)S(1)}, bf16[48,3584]{1,0:T(8,128)(2,1)S(1)}, u32[]{:S(2)}, u32[]{:S(2)}) collective-permute-start(bf16[48,3584]{1,0:T(8,128)(2,1)S(1)} %slice.15.refs_0_), channel_id=1, source_target_pairs={{0,2},{1,3},{2,0},{3,1},{4,6},{5,7},{6,4},{7,5},{8,10},{9,11},{10,... | collective-permute-start | bytes 1032200 | tf_op jit(solution)/shard_map/ppermute | solution.py:384
  5.1 1.6 collective-permute-start
  7.5 2.0 %onehot.1.onehot_ref = bf16[768,256]{1,0:T(8,128)(2,1)S(1)} custom-call(s32[768,1]{1,0:T(8,128)S(1)} %broadcast_in_dim.4.parents_ref), custom_call_target="tpu_custom_call" | custom-call | flops 19327352832 | bytes 12582912 | tf_op jit(solution)/shard_map/onehot/pallas_call | solution.py:53
  9.6 1.5 copy-done.1
  11.1 2.0 %own.1 = (bf16[80,3584]{1,0:T(8,128)(2,1)S(1)}, bf16[64,3584]{1,0:T(8,128)(2,1)S(1)}) custom-call(s32[2]{0:T(128)S(1)} %pad_add_fusion.place_ref, bf16[768,256]{1,0:T(8,128)(2,1)S(1)} %onehot.1.onehot_ref, bf16[256,3584]{1,0:T(8,128)(2,1)S(1)} %copy-done.1, bf16[192,3584]{1,0:T(8,128)(2,1)S(1)} %copy-done), custom_call_target="tpu_custom_call" | custom-call | flops 2113929216 | bytes 24772608 | tf_op jit(solution)/shard_map/own/pallas_call | solution.py:159
  13.1 7.5 %collective-permute-done.1.far_ref.refs_2_ = bf16[48,3584]{1,0:T(8,128)(2,1)S(1)} collective-permute-done((bf16[48,3584]{1,0:T(8,128)(2,1)S(1)}, bf16[48,3584]{1,0:T(8,128)(2,1)S(1)}, u32[]{:S(2)}, u32[]{:S(2)}) %collective-permute-start.1) | collective-permute-done | bytes 344096 | tf_op jit(solution)/shard_map/ppermute | solution.py:384
  21.4 1.4 collective-permute-start.2
  22.8 2.4 %look.1.refs_4_ = bf16[192,3584]{1,0:T(8,128)(2,1)S(1)} custom-call(s32[2]{0:T(128)S(1)} %pad_add_fusion.place_ref, bf16[768,256]{1,0:T(8,128)(2,1)S(1)} %onehot.1.onehot_ref, bf16[256,3584]{1,0:T(8,128)(2,1)S(1)} %copy-done.1, bf16[48,3584]{1,0:T(8,128)(2,1)S(1)} %forward.3.refs_0_.refs_5_), custom_call_target="tpu_custom_call" | custom-call | flops 2818572288 | bytes 22020096 | tf_op jit(solution)/shard_map/look/pallas_call | solution.py:105
  25.2 2.5 %collective-permute-start.4 = (bf16[80,3584]{1,0:T(8,128)(2,1)S(1)}, bf16[80,3584]{1,0:T(8,128)(2,1)S(1)}, u32[]{:S(2)}, u32[]{:S(2)}) collective-permute-start(bf16[80,3584]{1,0:T(8,128)(2,1)S(1)} %get-tuple-element.57.refs_0_), channel_id=1, source_target_pairs={{0,2},{1,3},{2,0},{3,1},{4,6},{5,7},{6,4},{7,5},{8,10},{9,11},{10,... | collective-permute-start | bytes 1720328 | tf_op jit(solution)/shard_map/ppermute | solution.py:384
  27.7 5.9 %fusion = (bf16[3584,512]{1,0:T(8,128)(2,1)S(1)}, bf16[3584,512]{1,0:T(8,128)(2,1)S(1)}, bf16[3584,512]{1,0:T(8,128)(2,1)S(1)}, bf16[3584,512]{1,0:T(8,128)(2,1)S(1)}) fusion(bf16[3584,9216]{1,0:T(8,128)(2,1)} %weight_ref.15), kind=kLoop, calls=%fused_computation.1 | loop fusion | bytes 29360128 | tf_op jit(solution)/shard_map/slice | solution.py:425
  34.6 1.3 collective-permute-start.3
  35.9 10.7 %product.8 = (bf16[96,4608]{1,0:T(8,128)(2,1)S(1)}, bf16[96,4608]{1,0:T(8,128)(2,1)S(1)}) custom-call(bf16[192,3584]{1,0:T(8,128)(2,1)S(1)} %arrange.3.rows_ref.refs_0_, bf16[3584,512]{1,0:T(8,128)(2,1)S(1)} %get-tuple-element.106.lead_ref, bf16[3584,9216]{1,0:T(8,128)(2,1)} %weight_ref.15, bf16[192,3584]{1,0:T(8,128)(2,1)S(1)} %arrange.3.rows_ref.refs_0_), custom_call_target="tpu_custom_call" | custom-call | flops 50734301184 | bytes 289406976 | tf_op jit(solution)/shard_map/product/pallas_call | solution.py:281
  46.7 10.7 %product.9 = (bf16[96,4608]{1,0:T(8,128)(2,1)S(1)}, bf16[96,4608]{1,0:T(8,128)(2,1)S(1)}) custom-call(bf16[192,3584]{1,0:T(8,128)(2,1)S(1)} %arrange.3.rows_ref.refs_0_, bf16[3584,512]{1,0:T(8,128)(2,1)S(1)} %get-tuple-element.105.lead_ref, bf16[3584,9216]{1,0:T(8,128)(2,1)} %weight_ref.15, bf16[96,4608]{1,0:T(8,128)(2,1)S(1)} %get-tuple-element.59.refs_0_.keep_ref), custom_call_target="tpu_custom_call" | custom-call | flops 50734301184 | bytes 289406976 | tf_op jit(solution)/shard_map/product/pallas_call | solution.py:281
  58.4 2.8 %collective-permute-done.3.near_ref.refs_1_ = bf16[80,3584]{1,0:T(8,128)(2,1)S(1)} collective-permute-done((bf16[80,3584]{1,0:T(8,128)(2,1)S(1)}, bf16[80,3584]{1,0:T(8,128)(2,1)S(1)}, u32[]{:S(2)}, u32[]{:S(2)}) %collective-permute-start.3) | collective-permute-done | bytes 573472 | tf_op jit(solution)/shard_map/ppermute | solution.py:384
  61.8 1.6 collective-permute-start.10
  64.4 10.8 %collective-permute-done.6.refs_3_ = bf16[80,3584]{1,0:T(8,128)(2,1)S(1)} collective-permute-done((bf16[80,3584]{1,0:T(8,128)(2,1)S(1)}, bf16[80,3584]{1,0:T(8,128)(2,1)S(1)}, u32[]{:S(2)}, u32[]{:S(2)}) %collective-permute-start.6) | collective-permute-done | bytes 573472 | tf_op jit(solution)/shard_map/ppermute | solution.py:418
  75.9 1.2 collective-permute-start.9
  77.2 9.0 %product.10 = (bf16[160,3072]{1,0:T(8,128)(2,1)S(1)}, bf16[160,3072]{1,0:T(8,128)(2,1)S(1)}) custom-call(bf16[320,3584]{1,0:T(8,128)(2,1)S(1)} %arrange.4.rows_ref.refs_0_, bf16[3584,512]{1,0:T(8,128)(2,1)S(1)} %get-tuple-element.106.lead_ref, bf16[3584,9216]{1,0:T(8,128)(2,1)} %weight_ref.15, bf16[320,3584]{1,0:T(8,128)(2,1)S(1)} %arrange.4.rows_ref.refs_0_), custom_call_target="tpu_custom_call" | custom-call | flops 56371445760 | bytes 210239488 | tf_op jit(solution)/shard_map/product/pallas_call | solution.py:281
  86.3 9.5 %product.11 = (bf16[160,3072]{1,0:T(8,128)(2,1)S(1)}, bf16[160,3072]{1,0:T(8,128)(2,1)S(1)}, bf16[192,9216]{1,0:T(8,128)(2,1)}) custom-call(bf16[320,3584]{1,0:T(8,128)(2,1)S(1)} %arrange.4.rows_ref.refs_0_, bf16[3584,512]{1,0:T(8,128)(2,1)S(1)} %get-tuple-element.104.lead_ref, bf16[3584,9216]{1,0:T(8,128)(2,1)} %weight_ref.15, ...), custom_call_target="tpu_custom_call" | custom-call | flops 56371445760 | bytes 210239488 | tf_op jit(solution)/shard_map/product/pallas_call | solution.py:281
  97.6 1.8 %collective-permute-start.11 = (bf16[64,3584]{1,0:T(8,128)(2,1)S(1)}, bf16[64,3584]{1,0:T(8,128)(2,1)S(1)}, u32[]{:S(2)}, u32[]{:S(2)}) collective-permute-start(bf16[64,3584]{1,0:T(8,128)(2,1)S(1)} %forward.5.refs_0_), channel_id=1, source_target_pairs={{0,2},{1,0},{2,3},{3,1},{4,6},{5,4},{6,7},{7,5},{8,10},{9,8},{10,1... | collective-permute-start | bytes 1376264 | tf_op jit(solution)/shard_map/ppermute | solution.py:418
  99.9 1.6 collective-permute-start.16
  101.5 9.5 %product.12 = (bf16[160,3072]{1,0:T(8,128)(2,1)S(1)}, bf16[160,3072]{1,0:T(8,128)(2,1)S(1)}, bf16[192,9216]{1,0:T(8,128)(2,1)}) custom-call(bf16[320,3584]{1,0:T(8,128)(2,1)S(1)} %arrange.4.rows_ref.refs_0_, bf16[3584,512]{1,0:T(8,128)(2,1)S(1)} %get-tuple-element.103.lead_ref, bf16[3584,9216]{1,0:T(8,128)(2,1)} %weight_ref.15, ...), custom_call_target="tpu_custom_call", output_to_operand_aliasing={{2}: (5, {})} | custom-call | flops 56371445760 | bytes 210239488 | tf_op jit(solution)/shard_map/product/pallas_call | solution.py:281
  112.9 8.2 %product.13 = (bf16[128,3072]{1,0:T(8,128)(2,1)S(1)}, bf16[128,3072]{1,0:T(8,128)(2,1)S(1)}, bf16[192,9216]{1,0:T(8,128)(2,1)}) custom-call(bf16[256,3584]{1,0:T(8,128)(2,1)S(1)} %arrange.5.rows_ref.refs_3_, bf16[3584,512]{1,0:T(8,128)(2,1)S(1)} %get-tuple-element.106.lead_ref, bf16[3584,9216]{1,0:T(8,128)(2,1)} %weight_ref.15, ...), custom_call_target="tpu_custom_call", output_to_operand_aliasing={{2}: (5, {})} | custom-call | flops 45097156608 | bytes 203423744 | tf_op jit(solution)/shard_map/product/pallas_call | solution.py:281
  121.9 1.6 collective-permute-start.17
  123.4 2.1 %collective-permute-done.18.refs_1_ = bf16[80,3072]{1,0:T(8,128)(2,1)S(1)} collective-permute-done((bf16[80,3072]{1,0:T(8,128)(2,1)S(1)}, bf16[80,3072]{1,0:T(8,128)(2,1)S(1)}, u32[]{:S(2)}, u32[]{:S(2)}) %collective-permute-start.18) | collective-permute-done | bytes 491552 | tf_op jit(solution)/shard_map/ppermute | solution.py:451
  125.5 8.2 %product.14 = (bf16[128,3072]{1,0:T(8,128)(2,1)S(1)}, bf16[128,3072]{1,0:T(8,128)(2,1)S(1)}, bf16[192,9216]{1,0:T(8,128)(2,1)}) custom-call(bf16[256,3584]{1,0:T(8,128)(2,1)S(1)} %arrange.5.rows_ref.refs_3_, bf16[3584,512]{1,0:T(8,128)(2,1)S(1)} %get-tuple-element.104.lead_ref, bf16[3584,9216]{1,0:T(8,128)(2,1)} %weight_ref.15, ...), custom_call_target="tpu_custom_call", output_to_operand_aliasing={{2}: (5, {})} | custom-call | flops 45097156608 | bytes 203423744 | tf_op jit(solution)/shard_map/product/pallas_call | solution.py:281
  134.6 1.2 collective-permute-done.17.refs_1_
  135.8 8.2 %product.15 = (bf16[128,3072]{1,0:T(8,128)(2,1)S(1)}, bf16[128,3072]{1,0:T(8,128)(2,1)S(1)}, bf16[192,9216]{1,0:T(8,128)(2,1)}) custom-call(bf16[256,3584]{1,0:T(8,128)(2,1)S(1)} %arrange.5.rows_ref.refs_3_, bf16[3584,512]{1,0:T(8,128)(2,1)S(1)} %get-tuple-element.103.lead_ref, bf16[3584,9216]{1,0:T(8,128)(2,1)} %weight_ref.15, ...), custom_call_target="tpu_custom_call", output_to_operand_aliasing={{2}: (5, {})} | custom-call | flops 45097156608 | bytes 203423744 | tf_op jit(solution)/shard_map/product/pallas_call | solution.py:281
  144.0 1.8 %collective-permute-done.20.refs_1_ = bf16[64,3072]{1,0:T(8,128)(2,1)S(1)} collective-permute-done((bf16[64,3072]{1,0:T(8,128)(2,1)S(1)}, bf16[64,3072]{1,0:T(8,128)(2,1)S(1)}, u32[]{:S(2)}, u32[]{:S(2)}) %collective-permute-start.20) | collective-permute-done | bytes 393248 | tf_op jit(solution)/shard_map/ppermute | solution.py:451
  147.7 1.5 collective-permute-done.21.got_ref
  150.0 9.3 %collective-permute-done.24.refs_1_ = bf16[64,3072]{1,0:T(8,128)(2,1)S(1)} collective-permute-done((bf16[64,3072]{1,0:T(8,128)(2,1)S(1)}, bf16[64,3072]{1,0:T(8,128)(2,1)S(1)}, u32[]{:S(2)}, u32[]{:S(2)}) %collective-permute-start.24) | collective-permute-done | bytes 393248 | tf_op jit(solution)/shard_map/ppermute | solution.py:451
  160.4 6.9 %collective-permute-done.23.refs_1_ = bf16[64,3072]{1,0:T(8,128)(2,1)S(1)} collective-permute-done((bf16[64,3072]{1,0:T(8,128)(2,1)S(1)}, bf16[64,3072]{1,0:T(8,128)(2,1)S(1)}, u32[]{:S(2)}, u32[]{:S(2)}) %collective-permute-start.23) | collective-permute-done | bytes 393248 | tf_op jit(solution)/shard_map/ppermute | solution.py:451
  (54 shorter events, 17.5 us)
Async XLA Ops:
  1.0 19.6 %collective-permute-start.1 = (bf16[48,3584]{1,0:T(8,128)(2,1)S(1)}, bf16[48,3584]{1,0:T(8,128)(2,1)S(1)}, u32[]{:S(2)}, u32[]{:S(2)}) collective-permute-start(bf16[48,3584]{1,0:T(8,128)(2,1)S(1)} %slice.15.refs_0_), channel_id=1, source_target_pairs={{0,2},{1,3},{2,0},{3,1},{4,6},{5,7},{6,4},{7,5},{8,10},{9,11},{10,... | collective-permute-start | bytes 1032200 | tf_op jit(solution)/shard_map/ppermute | solution.py:384
  5.1 15.7 %collective-permute-start = (bf16[48,3584]{1,0:T(8,128)(2,1)S(1)}, bf16[48,3584]{1,0:T(8,128)(2,1)S(1)}, u32[]{:S(2)}, u32[]{:S(2)}) collective-permute-start(bf16[48,3584]{1,0:T(8,128)(2,1)S(1)} %slice.15.refs_0_), channel_id=1, source_target_pairs={{0,1},{1,0},{2,3},{3,2},{4,5},{5,4},{6,7},{7,6},{8,9},{9,8},{10,11... | collective-permute-start | bytes 1032200 | tf_op jit(solution)/shard_map/ppermute | solution.py:384
  7.5 2.1 %copy-start = (bf16[192,3584]{1,0:T(8,128)(2,1)S(1)}, bf16[192,3584]{1,0:T(8,128)(2,1)}, u32[]{:S(2)}) copy-start(bf16[192,3584]{1,0:T(8,128)(2,1)} %hidden_ref.1) | copy-start | bytes 4128772
  9.6 1.5 copy-start.1
  21.4 12.3 %collective-permute-start.2 = (bf16[48,3584]{1,0:T(8,128)(2,1)S(1)}, bf16[48,3584]{1,0:T(8,128)(2,1)S(1)}, u32[]{:S(2)}, u32[]{:S(2)}) collective-permute-start(bf16[48,3584]{1,0:T(8,128)(2,1)S(1)} %forward.3.refs_0_.refs_5_), channel_id=1, source_target_pairs={{0,2},{1,0},{2,3},{3,1},{4,6},{5,4},{6,7},{7,5},{8,10},{9,8},{10,1... | collective-permute-start | bytes 1032200 | tf_op jit(solution)/shard_map/ppermute | solution.py:418
  25.2 33.2 %collective-permute-start.4 = (bf16[80,3584]{1,0:T(8,128)(2,1)S(1)}, bf16[80,3584]{1,0:T(8,128)(2,1)S(1)}, u32[]{:S(2)}, u32[]{:S(2)}) collective-permute-start(bf16[80,3584]{1,0:T(8,128)(2,1)S(1)} %get-tuple-element.57.refs_0_), channel_id=1, source_target_pairs={{0,2},{1,3},{2,0},{3,1},{4,6},{5,7},{6,4},{7,5},{8,10},{9,11},{10,... | collective-permute-start | bytes 1720328 | tf_op jit(solution)/shard_map/ppermute | solution.py:384
  34.6 26.6 %collective-permute-start.3 = (bf16[80,3584]{1,0:T(8,128)(2,1)S(1)}, bf16[80,3584]{1,0:T(8,128)(2,1)S(1)}, u32[]{:S(2)}, u32[]{:S(2)}) collective-permute-start(bf16[80,3584]{1,0:T(8,128)(2,1)S(1)} %get-tuple-element.57.refs_0_), channel_id=1, source_target_pairs={{0,1},{1,0},{2,3},{3,2},{4,5},{5,4},{6,7},{7,6},{8,9},{9,8},{10,11... | collective-permute-start | bytes 1720328 | tf_op jit(solution)/shard_map/ppermute | solution.py:384
  46.6 11.4 %collective-permute-start.5 = (bf16[96,4608]{1,0:T(8,128)(2,1)S(1)}, bf16[96,4608]{1,0:T(8,128)(2,1)S(1)}, u32[]{:S(2)}, u32[]{:S(2)}) collective-permute-start(bf16[96,4608]{1,0:T(8,128)(2,1)S(1)} %get-tuple-element.60), channel_id=1, source_target_pairs={{0,4},{4,0},{8,12},{12,8},{1,5},{5,1},{9,13},{13,9},{2,6},{6,2},{1... | collective-permute-start | bytes 2654216 | tf_op jit(solution)/shard_map/ppermute | solution.py:446
  57.4 6.0 %collective-permute-start.7 = (bf16[96,4608]{1,0:T(8,128)(2,1)S(1)}, bf16[96,4608]{1,0:T(8,128)(2,1)S(1)}, u32[]{:S(2)}, u32[]{:S(2)}) collective-permute-start(bf16[96,4608]{1,0:T(8,128)(2,1)S(1)} %get-tuple-element.63), channel_id=1, source_target_pairs={{0,4},{4,0},{8,12},{12,8},{1,5},{5,1},{9,13},{13,9},{2,6},{6,2},{1... | collective-permute-start | bytes 2654216 | tf_op jit(solution)/shard_map/ppermute | solution.py:446
  61.7 13.5 %collective-permute-start.6 = (bf16[80,3584]{1,0:T(8,128)(2,1)S(1)}, bf16[80,3584]{1,0:T(8,128)(2,1)S(1)}, u32[]{:S(2)}, u32[]{:S(2)}) collective-permute-start(bf16[80,3584]{1,0:T(8,128)(2,1)S(1)} %forward.4.refs_0_), channel_id=1, source_target_pairs={{0,2},{1,0},{2,3},{3,1},{4,6},{5,4},{6,7},{7,5},{8,10},{9,8},{10,1... | collective-permute-start | bytes 1720328 | tf_op jit(solution)/shard_map/ppermute | solution.py:418
  61.8 24.5 %collective-permute-start.10 = (bf16[48,4608]{1,0:T(8,128)(2,1)S(1)}, bf16[48,4608]{1,0:T(8,128)(2,1)S(1)}, u32[]{:S(2)}, u32[]{:S(2)}) collective-permute-start(bf16[48,4608]{1,0:T(8,128)(2,1)S(1)} %get-tuple-element.66), channel_id=1, source_target_pairs={{0,8},{4,12},{8,0},{12,4},{1,9},{5,13},{9,1},{13,5},{2,10},{6,14},... | collective-permute-start | bytes 1327112 | tf_op jit(solution)/shard_map/ppermute | solution.py:451
  63.8 37.6 %collective-permute-start.13 = (bf16[48,4608]{1,0:T(8,128)(2,1)S(1)}, bf16[48,4608]{1,0:T(8,128)(2,1)S(1)}, u32[]{:S(2)}, u32[]{:S(2)}) collective-permute-start(bf16[48,4608]{1,0:T(8,128)(2,1)S(1)} %get-tuple-element.70), channel_id=1, source_target_pairs={{0,8},{4,12},{8,0},{12,4},{1,9},{5,13},{9,1},{13,5},{2,10},{6,14},... | collective-permute-start | bytes 1327112 | tf_op jit(solution)/shard_map/ppermute | solution.py:451
  75.9 20.8 %collective-permute-start.9 = (bf16[64,3584]{1,0:T(8,128)(2,1)S(1)}, bf16[64,3584]{1,0:T(8,128)(2,1)S(1)}, u32[]{:S(2)}, u32[]{:S(2)}) collective-permute-start(bf16[64,3584]{1,0:T(8,128)(2,1)S(1)} %get-tuple-element.65.refs_0_), channel_id=1, source_target_pairs={{0,2},{1,3},{2,0},{3,1},{4,6},{5,7},{6,4},{7,5},{8,10},{9,11},{10,... | collective-permute-start | bytes 1376264 | tf_op jit(solution)/shard_map/ppermute | solution.py:384
  77.2 19.8 %collective-permute-start.8 = (bf16[64,3584]{1,0:T(8,128)(2,1)S(1)}, bf16[64,3584]{1,0:T(8,128)(2,1)S(1)}, u32[]{:S(2)}, u32[]{:S(2)}) collective-permute-start(bf16[64,3584]{1,0:T(8,128)(2,1)S(1)} %get-tuple-element.65.refs_0_), channel_id=1, source_target_pairs={{0,1},{1,0},{2,3},{3,2},{4,5},{5,4},{6,7},{7,6},{8,9},{9,8},{10,11... | collective-permute-start | bytes 1376264 | tf_op jit(solution)/shard_map/ppermute | solution.py:384
  86.2 13.2 %collective-permute-start.14 = (bf16[160,3072]{1,0:T(8,128)(2,1)S(1)}, bf16[160,3072]{1,0:T(8,128)(2,1)S(1)}, u32[]{:S(2)}, u32[]{:S(2)}) collective-permute-start(bf16[160,3072]{1,0:T(8,128)(2,1)S(1)} %get-tuple-element.72), channel_id=1, source_target_pairs={{0,4},{4,0},{8,12},{12,8},{1,5},{5,1},{9,13},{13,9},{2,6},{6,2},{1... | collective-permute-start | bytes 2949128 | tf_op jit(solution)/shard_map/ppermute | solution.py:446
  95.9 15.2 %collective-permute-start.12 = (bf16[160,3072]{1,0:T(8,128)(2,1)S(1)}, bf16[160,3072]{1,0:T(8,128)(2,1)S(1)}, u32[]{:S(2)}, u32[]{:S(2)}) collective-permute-start(bf16[160,3072]{1,0:T(8,128)(2,1)S(1)} %get-tuple-element.69), channel_id=1, source_target_pairs={{0,4},{4,0},{8,12},{12,8},{1,5},{5,1},{9,13},{13,9},{2,6},{6,2},{1... | collective-permute-start | bytes 2949128 | tf_op jit(solution)/shard_map/ppermute | solution.py:446
  97.6 14.5 %collective-permute-start.11 = (bf16[64,3584]{1,0:T(8,128)(2,1)S(1)}, bf16[64,3584]{1,0:T(8,128)(2,1)S(1)}, u32[]{:S(2)}, u32[]{:S(2)}) collective-permute-start(bf16[64,3584]{1,0:T(8,128)(2,1)S(1)} %forward.5.refs_0_), channel_id=1, source_target_pairs={{0,2},{1,0},{2,3},{3,1},{4,6},{5,4},{6,7},{7,5},{8,10},{9,8},{10,1... | collective-permute-start | bytes 1376264 | tf_op jit(solution)/shard_map/ppermute | solution.py:418
  99.9 13.0 %collective-permute-start.16 = (bf16[80,3072]{1,0:T(8,128)(2,1)S(1)}, bf16[80,3072]{1,0:T(8,128)(2,1)S(1)}, u32[]{:S(2)}, u32[]{:S(2)}) collective-permute-start(bf16[80,3072]{1,0:T(8,128)(2,1)S(1)} %get-tuple-element.77), channel_id=1, source_target_pairs={{0,8},{4,12},{8,0},{12,4},{1,9},{5,13},{9,1},{13,5},{2,10},{6,14},... | collective-permute-start | bytes 1474568 | tf_op jit(solution)/shard_map/ppermute | solution.py:451
  111.0 10.4 %collective-permute-start.15 = (bf16[160,3072]{1,0:T(8,128)(2,1)S(1)}, bf16[160,3072]{1,0:T(8,128)(2,1)S(1)}, u32[]{:S(2)}, u32[]{:S(2)}) collective-permute-start(bf16[160,3072]{1,0:T(8,128)(2,1)S(1)} %get-tuple-element.76), channel_id=1, source_target_pairs={{0,4},{4,0},{8,12},{12,8},{1,5},{5,1},{9,13},{13,9},{2,6},{6,2},{1... | collective-permute-start | bytes 2949128 | tf_op jit(solution)/shard_map/ppermute | solution.py:446
  111.6 14.0 %collective-permute-start.18 = (bf16[80,3072]{1,0:T(8,128)(2,1)S(1)}, bf16[80,3072]{1,0:T(8,128)(2,1)S(1)}, u32[]{:S(2)}, u32[]{:S(2)}) collective-permute-start(bf16[80,3072]{1,0:T(8,128)(2,1)S(1)} %get-tuple-element.82), channel_id=1, source_target_pairs={{0,8},{4,12},{8,0},{12,4},{1,9},{5,13},{9,1},{13,5},{2,10},{6,14},... | collective-permute-start | bytes 1474568 | tf_op jit(solution)/shard_map/ppermute | solution.py:451
  121.1 12.7 %collective-permute-start.19 = (bf16[128,3072]{1,0:T(8,128)(2,1)S(1)}, bf16[128,3072]{1,0:T(8,128)(2,1)S(1)}, u32[]{:S(2)}, u32[]{:S(2)}) collective-permute-start(bf16[128,3072]{1,0:T(8,128)(2,1)S(1)} %get-tuple-element.85), channel_id=1, source_target_pairs={{0,4},{4,0},{8,12},{12,8},{1,5},{5,1},{9,13},{13,9},{2,6},{6,2},{1... | collective-permute-start | bytes 2359304 | tf_op jit(solution)/shard_map/ppermute | solution.py:446
  121.9 13.9 %collective-permute-start.17 = (bf16[80,3072]{1,0:T(8,128)(2,1)S(1)}, bf16[80,3072]{1,0:T(8,128)(2,1)S(1)}, u32[]{:S(2)}, u32[]{:S(2)}) collective-permute-start(bf16[80,3072]{1,0:T(8,128)(2,1)S(1)} %get-tuple-element.81), channel_id=1, source_target_pairs={{0,8},{4,12},{8,0},{12,4},{1,9},{5,13},{9,1},{13,5},{2,10},{6,14},... | collective-permute-start | bytes 1474568 | tf_op jit(solution)/shard_map/ppermute | solution.py:451
  133.8 13.2 %collective-permute-start.22 = (bf16[128,3072]{1,0:T(8,128)(2,1)S(1)}, bf16[128,3072]{1,0:T(8,128)(2,1)S(1)}, u32[]{:S(2)}, u32[]{:S(2)}) collective-permute-start(bf16[128,3072]{1,0:T(8,128)(2,1)S(1)} %get-tuple-element.94), channel_id=1, source_target_pairs={{0,4},{4,0},{8,12},{12,8},{1,5},{5,1},{9,13},{13,9},{2,6},{6,2},{1... | collective-permute-start | bytes 2359304 | tf_op jit(solution)/shard_map/ppermute | solution.py:446
  134.3 11.6 %collective-permute-start.20 = (bf16[64,3072]{1,0:T(8,128)(2,1)S(1)}, bf16[64,3072]{1,0:T(8,128)(2,1)S(1)}, u32[]{:S(2)}, u32[]{:S(2)}) collective-permute-start(bf16[64,3072]{1,0:T(8,128)(2,1)S(1)} %get-tuple-element.90), channel_id=1, source_target_pairs={{0,8},{4,12},{8,0},{12,4},{1,9},{5,13},{9,1},{13,5},{2,10},{6,14},... | collective-permute-start | bytes 1179656 | tf_op jit(solution)/shard_map/ppermute | solution.py:451
  146.9 2.3 %collective-permute-start.21 = (bf16[128,3072]{1,0:T(8,128)(2,1)S(1)}, bf16[128,3072]{1,0:T(8,128)(2,1)S(1)}, u32[]{:S(2)}, u32[]{:S(2)}) collective-permute-start(bf16[128,3072]{1,0:T(8,128)(2,1)S(1)} %get-tuple-element.93), channel_id=1, source_target_pairs={{0,4},{4,0},{8,12},{12,8},{1,5},{5,1},{9,13},{13,9},{2,6},{6,2},{1... | collective-permute-start | bytes 2359304 | tf_op jit(solution)/shard_map/ppermute | solution.py:459
  147.3 12.0 %collective-permute-start.24 = (bf16[64,3072]{1,0:T(8,128)(2,1)S(1)}, bf16[64,3072]{1,0:T(8,128)(2,1)S(1)}, u32[]{:S(2)}, u32[]{:S(2)}) collective-permute-start(bf16[64,3072]{1,0:T(8,128)(2,1)S(1)} %get-tuple-element.98), channel_id=1, source_target_pairs={{0,8},{4,12},{8,0},{12,4},{1,9},{5,13},{9,1},{13,5},{2,10},{6,14},... | collective-permute-start | bytes 1179656 | tf_op jit(solution)/shard_map/ppermute | solution.py:451
  149.6 17.7 %collective-permute-start.23 = (bf16[64,3072]{1,0:T(8,128)(2,1)S(1)}, bf16[64,3072]{1,0:T(8,128)(2,1)S(1)}, u32[]{:S(2)}, u32[]{:S(2)}) collective-permute-start(bf16[64,3072]{1,0:T(8,128)(2,1)S(1)} %get-tuple-element.97), channel_id=1, source_target_pairs={{0,8},{4,12},{8,0},{12,4},{1,9},{5,13},{9,1},{13,5},{2,10},{6,14},... | collective-permute-start | bytes 1179656 | tf_op jit(solution)/shard_map/ppermute | solution.py:451

commit v10 on v9

--- a/solution.py
+++ b/solution.py
@@ -351,7 +351,7 @@
     return pieces
 
 
-SHARES = ((9, 9), (6, 6, 6), (6, 6, 6))
+SHARES = ((12, 6), (6, 6, 6), (6, 6, 6))
 
 
 def chunk_sizes(block):
@@ -361,8 +361,8 @@
 
 
 ORDER = (
-    ("f0", "a0", "p00", "p01", "s00", "f1", "s01"),
-    ("a1", "t2", "p10", "p11-00", "f2", "s10", "p12-01", "s11"),
+    ("f0", "a0", "p00", "f1", "p01", "s00"),
+    ("a1", "t2", "p10", "s01", "p11-00", "f2", "s10", "p12-01", "s11"),
     ("a2", "p20-10", "s12", "p21-11", "s20", "p22-12+", "g20!"),
     ("s21!", "s22", "g21", "g22"),
 )
@@ -422,14 +422,14 @@
                 looked = look(chips, n_gx, block, 0, sizes[0], exclusive, place, onehot, depth_table, after)
                 cuts = sorted({(start, tile_of(width)) for each in pieces for start, width in each})
                 ready = later(weight, looked)
+                if exclusive:
+                    held[1][1] = swap(later(own[1], looked), 1)
                 leads = {(start, tile): ready[:, start:start + tile] for start, tile in cuts}
         if kind == "t":
             take(index, after[0])
         if kind == "a":
             rows = arrange(chips, exclusive, place, held[index], None if index else looked, after)
             after = [rows]
-            if exclusive and index == 0:
-                held[1][1] = swap(later(own[1], rows), 1)
         if kind == "p":
             start, width = pieces[index][int(item[2])]
             extra = {}

time: 169 us -> 172 us (1.018)
  starting transfers between devices: 22.5 us -> 25.8 us
    ppermute x6, waiting for transfers between devices: 11.1 us -> 17.3 us  [swap(): return lax.ppermute(array, 'gy', [(k, k ^ distance) for k in range(n_gy)])]
    ppermute x3, waiting for transfers between devices: 10.8 us -> 6.1 us  [local(): lax.ppermute(given, 'gy', [(0, 2), (1, 0), (2, 3), (3, 1)])]
    ppermute x8, starting transfers between devices: 6.86 us -> 10.5 us  [local(): lax.ppermute(away[(ahead - 1) * size:ahead * size], 'gx', across(ahead))]
  transfers between devices with their start and end apart: 25 -> 25, of which waited for: 12 -> 12; matrix products, arithmetic and copies ran while one was open for 4% -> 3% of each run, Pallas kernels for 53% -> 52%
where the time goes in v10:
time: 172 us
  Pallas kernels  90.8 us (53%)
  waiting for transfers between devices  46.5 us (27%)
  starting transfers between devices  25.8 us (15%)
  local copies, waits for them, and re-layouts  8.07 us (5%)
    pallas_call x8, Pallas kernels, product(): pl.pallas_call(functools.partial(product_kernel, start, tile, width // ti...  73.5 us
    ppermute x8, waiting for transfers between devices, local(): lax.ppermute(away[(ahead - 1) * size:ahead * size], 'gx', across(ahead))  22.8 us
    ppermute x6, waiting for transfers between devices, swap(): return lax.ppermute(array, 'gy', [(k, k ^ distance) for k in range(n_gy)])  17.3 us
    ppermute x8, starting transfers between devices, local(): lax.ppermute(away[(ahead - 1) * size:ahead * size], 'gx', across(ahead))  10.5 us
    ppermute x6, starting transfers between devices, swap(): return lax.ppermute(array, 'gy', [(k, k ^ distance) for k in range(n_gy)])  10.3 us
    ppermute x3, waiting for transfers between devices, local(): lax.ppermute(given, 'gy', [(0, 2), (1, 0), (2, 3), (3, 1)])  6.1 us
    slice x1, local copies, waits for them, and re-layouts, local(): ready[:, start:start + tile]  4.72 us
    ppermute x3, starting transfers between devices, local(): lax.ppermute(given, 'gy', [(0, 2), (1, 0), (2, 3), (3, 1)])  4.43 us
  transfers between devices with their start and end apart: 25, of which 12 were waited for; matrix products, arithmetic and copies ran while one was open for 3% of the time, Pallas kernels for 52%

profile of v10, /device:TPU:0, one launch (start us, length us, event | category | flops | bytes accessed | tf_op | source)
XLA Modules:
  0.0 171.6 jit_solution(4980815576731416630)
XLA Ops:
  1.0 4.1 %collective-permute-start.1 = (bf16[48,3584]{1,0:T(8,128)(2,1)S(1)}, bf16[48,3584]{1,0:T(8,128)(2,1)S(1)}, u32[]{:S(2)}, u32[]{:S(2)}) collective-permute-start(bf16[48,3584]{1,0:T(8,128)(2,1)S(1)} %slice.12.refs_0_), channel_id=1, source_target_pairs={{0,2},{1,3},{2,0},{3,1},{4,6},{5,7},{6,4},{7,5},{8,10},{9,11},{10,... | collective-permute-start | bytes 1032200 | tf_op jit(solution)/shard_map/ppermute | solution.py:384
  5.1 1.6 collective-permute-start
  7.5 2.0 %onehot.1.onehot_ref = bf16[768,256]{1,0:T(8,128)(2,1)S(1)} custom-call(s32[768,1]{1,0:T(8,128)S(1)} %broadcast_in_dim.4.parents_ref), custom_call_target="tpu_custom_call" | custom-call | flops 19327352832 | bytes 12582912 | tf_op jit(solution)/shard_map/onehot/pallas_call | solution.py:53
  9.6 1.5 copy-done.1
  11.1 2.0 %own.1 = (bf16[80,3584]{1,0:T(8,128)(2,1)S(1)}, bf16[64,3584]{1,0:T(8,128)(2,1)S(1)}) custom-call(s32[2]{0:T(128)S(1)} %pad_add_fusion.place_ref, bf16[768,256]{1,0:T(8,128)(2,1)S(1)} %onehot.1.onehot_ref, bf16[256,3584]{1,0:T(8,128)(2,1)S(1)} %copy-done.1, bf16[192,3584]{1,0:T(8,128)(2,1)S(1)} %copy-done), custom_call_target="tpu_custom_call" | custom-call | flops 2113929216 | bytes 24772608 | tf_op jit(solution)/shard_map/own/pallas_call | solution.py:159
  13.1 7.5 %collective-permute-done.1.far_ref.refs_2_ = bf16[48,3584]{1,0:T(8,128)(2,1)S(1)} collective-permute-done((bf16[48,3584]{1,0:T(8,128)(2,1)S(1)}, bf16[48,3584]{1,0:T(8,128)(2,1)S(1)}, u32[]{:S(2)}, u32[]{:S(2)}) %collective-permute-start.1) | collective-permute-done | bytes 344096 | tf_op jit(solution)/shard_map/ppermute | solution.py:384
  21.4 1.4 collective-permute-start.4
  22.8 2.4 %look.1.refs_4_ = bf16[192,3584]{1,0:T(8,128)(2,1)S(1)} custom-call(s32[2]{0:T(128)S(1)} %pad_add_fusion.place_ref, bf16[768,256]{1,0:T(8,128)(2,1)S(1)} %onehot.1.onehot_ref, bf16[256,3584]{1,0:T(8,128)(2,1)S(1)} %copy-done.2, bf16[48,3584]{1,0:T(8,128)(2,1)S(1)} %forward.3.refs_0_.refs_5_), custom_call_target="tpu_custom_call" | custom-call | flops 2818572288 | bytes 22020096 | tf_op jit(solution)/shard_map/look/pallas_call | solution.py:105
  25.2 2.5 %collective-permute-start.3 = (bf16[80,3584]{1,0:T(8,128)(2,1)S(1)}, bf16[80,3584]{1,0:T(8,128)(2,1)S(1)}, u32[]{:S(2)}, u32[]{:S(2)}) collective-permute-start(bf16[80,3584]{1,0:T(8,128)(2,1)S(1)} %get-tuple-element.57.refs_0_), channel_id=1, source_target_pairs={{0,2},{1,3},{2,0},{3,1},{4,6},{5,7},{6,4},{7,5},{8,10},{9,11},{10,... | collective-permute-start | bytes 1720328 | tf_op jit(solution)/shard_map/ppermute | solution.py:384
  28.3 4.7 %fusion = (bf16[3584,512]{1,0:T(8,128)(2,1)S(1)}, bf16[3584,512]{1,0:T(8,128)(2,1)S(1)}, bf16[3584,512]{1,0:T(8,128)(2,1)S(1)}) fusion(bf16[3584,9216]{1,0:T(8,128)(2,1)} %weight_ref.15), kind=kLoop, calls=%fused_computation.1 | loop fusion | bytes 22020096 | tf_op jit(solution)/shard_map/slice | solution.py:427
  34.0 13.9 %product.8 = (bf16[96,6144]{1,0:T(8,128)(2,1)S(1)}, bf16[96,6144]{1,0:T(8,128)(2,1)S(1)}) custom-call(bf16[192,3584]{1,0:T(8,128)(2,1)S(1)} %arrange.3.rows_ref.refs_0_, bf16[3584,512]{1,0:T(8,128)(2,1)S(1)} %get-tuple-element.105.lead_ref, bf16[3584,9216]{1,0:T(8,128)(2,1)} %weight_ref.15, bf16[192,3584]{1,0:T(8,128)(2,1)S(1)} %arrange.3.rows_ref.refs_0_), custom_call_target="tpu_custom_call" | custom-call | flops 67645734912 | bytes 382205952 | tf_op jit(solution)/shard_map/product/pallas_call | solution.py:281
  48.0 9.5 %collective-permute-done.3.far_ref.refs_2_ = bf16[80,3584]{1,0:T(8,128)(2,1)S(1)} collective-permute-done((bf16[80,3584]{1,0:T(8,128)(2,1)S(1)}, bf16[80,3584]{1,0:T(8,128)(2,1)S(1)}, u32[]{:S(2)}, u32[]{:S(2)}) %collective-permute-start.3) | collective-permute-done | bytes 573472 | tf_op jit(solution)/shard_map/ppermute | solution.py:384
  58.8 7.5 %product.9 = (bf16[96,3072]{1,0:T(8,128)(2,1)S(1)}, bf16[96,3072]{1,0:T(8,128)(2,1)S(1)}) custom-call(bf16[192,3584]{1,0:T(8,128)(2,1)S(1)} %arrange.3.rows_ref.refs_0_, bf16[3584,512]{1,0:T(8,128)(2,1)S(1)} %get-tuple-element.104.lead_ref, bf16[3584,9216]{1,0:T(8,128)(2,1)} %weight_ref.15, bf16[80,3584]{1,0:T(8,128)(2,1)S(1)} %forward.4.refs_0_), custom_call_target="tpu_custom_call" | custom-call | flops 33822867456 | bytes 196608000 | tf_op jit(solution)/shard_map/product/pallas_call | solution.py:281
  67.0 6.1 %collective-permute-done.5.refs_3_ = bf16[80,3584]{1,0:T(8,128)(2,1)S(1)} collective-permute-done((bf16[80,3584]{1,0:T(8,128)(2,1)S(1)}, bf16[80,3584]{1,0:T(8,128)(2,1)S(1)}, u32[]{:S(2)}, u32[]{:S(2)}) %collective-permute-start.5) | collective-permute-done | bytes 573472 | tf_op jit(solution)/shard_map/ppermute | solution.py:418
  73.8 1.2 collective-permute-start.8
  75.3 1.5 collective-permute-start.9
  76.8 9.0 %product.10 = (bf16[160,3072]{1,0:T(8,128)(2,1)S(1)}, bf16[160,3072]{1,0:T(8,128)(2,1)S(1)}) custom-call(bf16[320,3584]{1,0:T(8,128)(2,1)S(1)} %arrange.4.rows_ref.refs_0_, bf16[3584,512]{1,0:T(8,128)(2,1)S(1)} %get-tuple-element.105.lead_ref, bf16[3584,9216]{1,0:T(8,128)(2,1)} %weight_ref.15, bf16[320,3584]{1,0:T(8,128)(2,1)S(1)} %arrange.4.rows_ref.refs_0_), custom_call_target="tpu_custom_call" | custom-call | flops 56371445760 | bytes 210239488 | tf_op jit(solution)/shard_map/product/pallas_call | solution.py:281
  86.8 3.9 %collective-permute-done.9.refs_1_ = bf16[48,6144]{1,0:T(8,128)(2,1)S(1)} collective-permute-done((bf16[48,6144]{1,0:T(8,128)(2,1)S(1)}, bf16[48,6144]{1,0:T(8,128)(2,1)S(1)}, u32[]{:S(2)}, u32[]{:S(2)}) %collective-permute-start.9) | collective-permute-done | bytes 589856 | tf_op jit(solution)/shard_map/ppermute | solution.py:451
  90.7 9.3 %product.11 = (bf16[160,3072]{1,0:T(8,128)(2,1)S(1)}, bf16[160,3072]{1,0:T(8,128)(2,1)S(1)}, bf16[192,9216]{1,0:T(8,128)(2,1)}) custom-call(bf16[320,3584]{1,0:T(8,128)(2,1)S(1)} %arrange.4.rows_ref.refs_0_, bf16[3584,512]{1,0:T(8,128)(2,1)S(1)} %get-tuple-element.103.lead_ref, bf16[3584,9216]{1,0:T(8,128)(2,1)} %weight_ref.15, ...), custom_call_target="tpu_custom_call" | custom-call | flops 56371445760 | bytes 210239488 | tf_op jit(solution)/shard_map/product/pallas_call | solution.py:281
  100.7 2.3 %collective-permute-start.11 = (bf16[64,3584]{1,0:T(8,128)(2,1)S(1)}, bf16[64,3584]{1,0:T(8,128)(2,1)S(1)}, u32[]{:S(2)}, u32[]{:S(2)}) collective-permute-start(bf16[64,3584]{1,0:T(8,128)(2,1)S(1)} %forward.5.refs_0_), channel_id=1, source_target_pairs={{0,2},{1,0},{2,3},{3,1},{4,6},{5,4},{6,7},{7,5},{8,10},{9,8},{10,1... | collective-permute-start | bytes 1376264 | tf_op jit(solution)/shard_map/ppermute | solution.py:418
  103.5 1.8 %collective-permute-start.16 = (bf16[80,3072]{1,0:T(8,128)(2,1)S(1)}, bf16[80,3072]{1,0:T(8,128)(2,1)S(1)}, u32[]{:S(2)}, u32[]{:S(2)}) collective-permute-start(bf16[80,3072]{1,0:T(8,128)(2,1)S(1)} %get-tuple-element.77), channel_id=1, source_target_pairs={{0,8},{4,12},{8,0},{12,4},{1,9},{5,13},{9,1},{13,5},{2,10},{6,14},... | collective-permute-start | bytes 1474568 | tf_op jit(solution)/shard_map/ppermute | solution.py:451
  105.3 9.1 %product.12 = (bf16[160,3072]{1,0:T(8,128)(2,1)S(1)}, bf16[160,3072]{1,0:T(8,128)(2,1)S(1)}, bf16[192,9216]{1,0:T(8,128)(2,1)}) custom-call(bf16[320,3584]{1,0:T(8,128)(2,1)S(1)} %arrange.4.rows_ref.refs_0_, bf16[3584,512]{1,0:T(8,128)(2,1)S(1)} %get-tuple-element.104.lead_ref, bf16[3584,9216]{1,0:T(8,128)(2,1)} %weight_ref.15, ...), custom_call_target="tpu_custom_call", output_to_operand_aliasing={{2}: (5, {})} | custom-call | flops 56371445760 | bytes 210239488 | tf_op jit(solution)/shard_map/product/pallas_call | solution.py:281
  117.2 8.2 %product.13 = (bf16[128,3072]{1,0:T(8,128)(2,1)S(1)}, bf16[128,3072]{1,0:T(8,128)(2,1)S(1)}, bf16[192,9216]{1,0:T(8,128)(2,1)}) custom-call(bf16[256,3584]{1,0:T(8,128)(2,1)S(1)} %arrange.5.rows_ref.refs_3_, bf16[3584,512]{1,0:T(8,128)(2,1)S(1)} %get-tuple-element.105.lead_ref, bf16[3584,9216]{1,0:T(8,128)(2,1)} %weight_ref.15, ...), custom_call_target="tpu_custom_call", output_to_operand_aliasing={{2}: (5, {})} | custom-call | flops 45097156608 | bytes 203423744 | tf_op jit(solution)/shard_map/product/pallas_call | solution.py:281
  126.0 2.2 %collective-permute-start.17 = (bf16[80,3072]{1,0:T(8,128)(2,1)S(1)}, bf16[80,3072]{1,0:T(8,128)(2,1)S(1)}, u32[]{:S(2)}, u32[]{:S(2)}) collective-permute-start(bf16[80,3072]{1,0:T(8,128)(2,1)S(1)} %get-tuple-element.81), channel_id=1, source_target_pairs={{0,8},{4,12},{8,0},{12,4},{1,9},{5,13},{9,1},{13,5},{2,10},{6,14},... | collective-permute-start | bytes 1474568 | tf_op jit(solution)/shard_map/ppermute | solution.py:451
  128.7 8.2 %product.14 = (bf16[128,3072]{1,0:T(8,128)(2,1)S(1)}, bf16[128,3072]{1,0:T(8,128)(2,1)S(1)}, bf16[192,9216]{1,0:T(8,128)(2,1)}) custom-call(bf16[256,3584]{1,0:T(8,128)(2,1)S(1)} %arrange.5.rows_ref.refs_3_, bf16[3584,512]{1,0:T(8,128)(2,1)S(1)} %get-tuple-element.103.lead_ref, bf16[3584,9216]{1,0:T(8,128)(2,1)} %weight_ref.15, ...), custom_call_target="tpu_custom_call", output_to_operand_aliasing={{2}: (5, {})} | custom-call | flops 45097156608 | bytes 203423744 | tf_op jit(solution)/shard_map/product/pallas_call | solution.py:281
  138.3 1.8 %collective-permute-done.17.refs_1_ = bf16[80,3072]{1,0:T(8,128)(2,1)S(1)} collective-permute-done((bf16[80,3072]{1,0:T(8,128)(2,1)S(1)}, bf16[80,3072]{1,0:T(8,128)(2,1)S(1)}, u32[]{:S(2)}, u32[]{:S(2)}) %collective-permute-start.17) | collective-permute-done | bytes 491552 | tf_op jit(solution)/shard_map/ppermute | solution.py:451
  140.1 8.2 %product.15 = (bf16[128,3072]{1,0:T(8,128)(2,1)S(1)}, bf16[128,3072]{1,0:T(8,128)(2,1)S(1)}, bf16[192,9216]{1,0:T(8,128)(2,1)}) custom-call(bf16[256,3584]{1,0:T(8,128)(2,1)S(1)} %arrange.5.rows_ref.refs_3_, bf16[3584,512]{1,0:T(8,128)(2,1)S(1)} %get-tuple-element.104.lead_ref, bf16[3584,9216]{1,0:T(8,128)(2,1)} %weight_ref.15, ...), custom_call_target="tpu_custom_call", output_to_operand_aliasing={{2}: (5, {})} | custom-call | flops 45097156608 | bytes 203423744 | tf_op jit(solution)/shard_map/product/pallas_call | solution.py:281
  150.5 1.6 collective-permute-start.24
  152.8 1.6 collective-permute-start.23
  154.3 8.1 %collective-permute-done.24.refs_1_ = bf16[64,3072]{1,0:T(8,128)(2,1)S(1)} collective-permute-done((bf16[64,3072]{1,0:T(8,128)(2,1)S(1)}, bf16[64,3072]{1,0:T(8,128)(2,1)S(1)}, u32[]{:S(2)}, u32[]{:S(2)}) %collective-permute-start.24) | collective-permute-done | bytes 393248 | tf_op jit(solution)/shard_map/ppermute | solution.py:451
  163.6 6.9 %collective-permute-done.23.refs_1_ = bf16[64,3072]{1,0:T(8,128)(2,1)S(1)} collective-permute-done((bf16[64,3072]{1,0:T(8,128)(2,1)S(1)}, bf16[64,3072]{1,0:T(8,128)(2,1)S(1)}, u32[]{:S(2)}, u32[]{:S(2)}) %collective-permute-start.23) | collective-permute-done | bytes 393248 | tf_op jit(solution)/shard_map/ppermute | solution.py:451
  170.5 1.1 finish.5
  (56 shorter events, 18.3 us)
Async XLA Ops:
  1.0 19.6 %collective-permute-start.1 = (bf16[48,3584]{1,0:T(8,128)(2,1)S(1)}, bf16[48,3584]{1,0:T(8,128)(2,1)S(1)}, u32[]{:S(2)}, u32[]{:S(2)}) collective-permute-start(bf16[48,3584]{1,0:T(8,128)(2,1)S(1)} %slice.12.refs_0_), channel_id=1, source_target_pairs={{0,2},{1,3},{2,0},{3,1},{4,6},{5,7},{6,4},{7,5},{8,10},{9,11},{10,... | collective-permute-start | bytes 1032200 | tf_op jit(solution)/shard_map/ppermute | solution.py:384
  5.1 15.7 %collective-permute-start = (bf16[48,3584]{1,0:T(8,128)(2,1)S(1)}, bf16[48,3584]{1,0:T(8,128)(2,1)S(1)}, u32[]{:S(2)}, u32[]{:S(2)}) collective-permute-start(bf16[48,3584]{1,0:T(8,128)(2,1)S(1)} %slice.12.refs_0_), channel_id=1, source_target_pairs={{0,1},{1,0},{2,3},{3,2},{4,5},{5,4},{6,7},{7,6},{8,9},{9,8},{10,11... | collective-permute-start | bytes 1032200 | tf_op jit(solution)/shard_map/ppermute | solution.py:384
  7.5 2.1 %copy-start = (bf16[192,3584]{1,0:T(8,128)(2,1)S(1)}, bf16[192,3584]{1,0:T(8,128)(2,1)}, u32[]{:S(2)}) copy-start(bf16[192,3584]{1,0:T(8,128)(2,1)} %hidden_ref.1) | copy-start | bytes 4128772
  9.6 1.5 copy-start.1
  11.1 11.7 %copy-start.2 = (bf16[256,3584]{1,0:T(8,128)(2,1)S(1)}, bf16[256,3584]{1,0:T(8,128)(2,1)}, u32[]{:S(2)}) copy-start(bf16[256,3584]{1,0:T(8,128)(2,1)} %table_ref.3) | copy-start | bytes 5505028
  21.4 11.7 %collective-permute-start.4 = (bf16[48,3584]{1,0:T(8,128)(2,1)S(1)}, bf16[48,3584]{1,0:T(8,128)(2,1)S(1)}, u32[]{:S(2)}, u32[]{:S(2)}) collective-permute-start(bf16[48,3584]{1,0:T(8,128)(2,1)S(1)} %forward.3.refs_0_.refs_5_), channel_id=1, source_target_pairs={{0,2},{1,0},{2,3},{3,1},{4,6},{5,4},{6,7},{7,5},{8,10},{9,8},{10,1... | collective-permute-start | bytes 1032200 | tf_op jit(solution)/shard_map/ppermute | solution.py:418
  25.2 32.3 %collective-permute-start.3 = (bf16[80,3584]{1,0:T(8,128)(2,1)S(1)}, bf16[80,3584]{1,0:T(8,128)(2,1)S(1)}, u32[]{:S(2)}, u32[]{:S(2)}) collective-permute-start(bf16[80,3584]{1,0:T(8,128)(2,1)S(1)} %get-tuple-element.57.refs_0_), channel_id=1, source_target_pairs={{0,2},{1,3},{2,0},{3,1},{4,6},{5,7},{6,4},{7,5},{8,10},{9,11},{10,... | collective-permute-start | bytes 1720328 | tf_op jit(solution)/shard_map/ppermute | solution.py:384
  27.7 29.8 %collective-permute-start.2 = (bf16[80,3584]{1,0:T(8,128)(2,1)S(1)}, bf16[80,3584]{1,0:T(8,128)(2,1)S(1)}, u32[]{:S(2)}, u32[]{:S(2)}) collective-permute-start(bf16[80,3584]{1,0:T(8,128)(2,1)S(1)} %get-tuple-element.57.refs_0_), channel_id=1, source_target_pairs={{0,1},{1,0},{2,3},{3,2},{4,5},{5,4},{6,7},{7,6},{8,9},{9,8},{10,11... | collective-permute-start | bytes 1720328 | tf_op jit(solution)/shard_map/ppermute | solution.py:384
  47.9 18.5 %collective-permute-start.6 = (bf16[96,6144]{1,0:T(8,128)(2,1)S(1)}, bf16[96,6144]{1,0:T(8,128)(2,1)S(1)}, u32[]{:S(2)}, u32[]{:S(2)}) collective-permute-start(bf16[96,6144]{1,0:T(8,128)(2,1)S(1)} %get-tuple-element.60), channel_id=1, source_target_pairs={{0,4},{4,0},{8,12},{12,8},{1,5},{5,1},{9,13},{13,9},{2,6},{6,2},{1... | collective-permute-start | bytes 3538952 | tf_op jit(solution)/shard_map/ppermute | solution.py:446
  58.1 15.0 %collective-permute-start.5 = (bf16[80,3584]{1,0:T(8,128)(2,1)S(1)}, bf16[80,3584]{1,0:T(8,128)(2,1)S(1)}, u32[]{:S(2)}, u32[]{:S(2)}) collective-permute-start(bf16[80,3584]{1,0:T(8,128)(2,1)S(1)} %forward.4.refs_0_), channel_id=1, source_target_pairs={{0,2},{1,0},{2,3},{3,1},{4,6},{5,4},{6,7},{7,5},{8,10},{9,8},{10,1... | collective-permute-start | bytes 1720328 | tf_op jit(solution)/shard_map/ppermute | solution.py:418
  66.3 19.6 %collective-permute-start.10 = (bf16[96,3072]{1,0:T(8,128)(2,1)S(1)}, bf16[96,3072]{1,0:T(8,128)(2,1)S(1)}, u32[]{:S(2)}, u32[]{:S(2)}) collective-permute-start(bf16[96,3072]{1,0:T(8,128)(2,1)S(1)} %get-tuple-element.65), channel_id=1, source_target_pairs={{0,4},{4,0},{8,12},{12,8},{1,5},{5,1},{9,13},{13,9},{2,6},{6,2},{1... | collective-permute-start | bytes 1769480 | tf_op jit(solution)/shard_map/ppermute | solution.py:446
  73.8 26.3 %collective-permute-start.8 = (bf16[64,3584]{1,0:T(8,128)(2,1)S(1)}, bf16[64,3584]{1,0:T(8,128)(2,1)S(1)}, u32[]{:S(2)}, u32[]{:S(2)}) collective-permute-start(bf16[64,3584]{1,0:T(8,128)(2,1)S(1)} %get-tuple-element.63.refs_0_), channel_id=1, source_target_pairs={{0,2},{1,3},{2,0},{3,1},{4,6},{5,7},{6,4},{7,5},{8,10},{9,11},{10,... | collective-permute-start | bytes 1376264 | tf_op jit(solution)/shard_map/ppermute | solution.py:384
  75.1 25.0 %collective-permute-start.7 = (bf16[64,3584]{1,0:T(8,128)(2,1)S(1)}, bf16[64,3584]{1,0:T(8,128)(2,1)S(1)}, u32[]{:S(2)}, u32[]{:S(2)}) collective-permute-start(bf16[64,3584]{1,0:T(8,128)(2,1)S(1)} %get-tuple-element.63.refs_0_), channel_id=1, source_target_pairs={{0,1},{1,0},{2,3},{3,2},{4,5},{5,4},{6,7},{7,6},{8,9},{9,8},{10,11... | collective-permute-start | bytes 1376264 | tf_op jit(solution)/shard_map/ppermute | solution.py:384
  75.3 15.4 %collective-permute-start.9 = (bf16[48,6144]{1,0:T(8,128)(2,1)S(1)}, bf16[48,6144]{1,0:T(8,128)(2,1)S(1)}, u32[]{:S(2)}, u32[]{:S(2)}) collective-permute-start(bf16[48,6144]{1,0:T(8,128)(2,1)S(1)} %get-tuple-element.64), channel_id=1, source_target_pairs={{0,8},{4,12},{8,0},{12,4},{1,9},{5,13},{9,1},{13,5},{2,10},{6,14},... | collective-permute-start | bytes 1769480 | tf_op jit(solution)/shard_map/ppermute | solution.py:451
  86.2 19.1 %collective-permute-start.13 = (bf16[48,3072]{1,0:T(8,128)(2,1)S(1)}, bf16[48,3072]{1,0:T(8,128)(2,1)S(1)}, u32[]{:S(2)}, u32[]{:S(2)}) collective-permute-start(bf16[48,3072]{1,0:T(8,128)(2,1)S(1)} %get-tuple-element.70), channel_id=1, source_target_pairs={{0,8},{4,12},{8,0},{12,4},{1,9},{5,13},{9,1},{13,5},{2,10},{6,14},... | collective-permute-start | bytes 884744 | tf_op jit(solution)/shard_map/ppermute | solution.py:451
  86.8 16.2 %collective-permute-start.14 = (bf16[160,3072]{1,0:T(8,128)(2,1)S(1)}, bf16[160,3072]{1,0:T(8,128)(2,1)S(1)}, u32[]{:S(2)}, u32[]{:S(2)}) collective-permute-start(bf16[160,3072]{1,0:T(8,128)(2,1)S(1)} %get-tuple-element.72), channel_id=1, source_target_pairs={{0,4},{4,0},{8,12},{12,8},{1,5},{5,1},{9,13},{13,9},{2,6},{6,2},{1... | collective-permute-start | bytes 2949128 | tf_op jit(solution)/shard_map/ppermute | solution.py:446
  100.7 14.9 %collective-permute-start.11 = (bf16[64,3584]{1,0:T(8,128)(2,1)S(1)}, bf16[64,3584]{1,0:T(8,128)(2,1)S(1)}, u32[]{:S(2)}, u32[]{:S(2)}) collective-permute-start(bf16[64,3584]{1,0:T(8,128)(2,1)S(1)} %forward.5.refs_0_), channel_id=1, source_target_pairs={{0,2},{1,0},{2,3},{3,1},{4,6},{5,4},{6,7},{7,5},{8,10},{9,8},{10,1... | collective-permute-start | bytes 1376264 | tf_op jit(solution)/shard_map/ppermute | solution.py:418
  103.0 11.7 %collective-permute-start.12 = (bf16[160,3072]{1,0:T(8,128)(2,1)S(1)}, bf16[160,3072]{1,0:T(8,128)(2,1)S(1)}, u32[]{:S(2)}, u32[]{:S(2)}) collective-permute-start(bf16[160,3072]{1,0:T(8,128)(2,1)S(1)} %get-tuple-element.69), channel_id=1, source_target_pairs={{0,4},{4,0},{8,12},{12,8},{1,5},{5,1},{9,13},{13,9},{2,6},{6,2},{1... | collective-permute-start | bytes 2949128 | tf_op jit(solution)/shard_map/ppermute | solution.py:446
  103.5 13.7 %collective-permute-start.16 = (bf16[80,3072]{1,0:T(8,128)(2,1)S(1)}, bf16[80,3072]{1,0:T(8,128)(2,1)S(1)}, u32[]{:S(2)}, u32[]{:S(2)}) collective-permute-start(bf16[80,3072]{1,0:T(8,128)(2,1)S(1)} %get-tuple-element.77), channel_id=1, source_target_pairs={{0,8},{4,12},{8,0},{12,4},{1,9},{5,13},{9,1},{13,5},{2,10},{6,14},... | collective-permute-start | bytes 1474568 | tf_op jit(solution)/shard_map/ppermute | solution.py:451
  114.4 11.1 %collective-permute-start.15 = (bf16[160,3072]{1,0:T(8,128)(2,1)S(1)}, bf16[160,3072]{1,0:T(8,128)(2,1)S(1)}, u32[]{:S(2)}, u32[]{:S(2)}) collective-permute-start(bf16[160,3072]{1,0:T(8,128)(2,1)S(1)} %get-tuple-element.76), channel_id=1, source_target_pairs={{0,4},{4,0},{8,12},{12,8},{1,5},{5,1},{9,13},{13,9},{2,6},{6,2},{1... | collective-permute-start | bytes 2949128 | tf_op jit(solution)/shard_map/ppermute | solution.py:446
  115.2 13.5 %collective-permute-start.18 = (bf16[80,3072]{1,0:T(8,128)(2,1)S(1)}, bf16[80,3072]{1,0:T(8,128)(2,1)S(1)}, u32[]{:S(2)}, u32[]{:S(2)}) collective-permute-start(bf16[80,3072]{1,0:T(8,128)(2,1)S(1)} %get-tuple-element.82), channel_id=1, source_target_pairs={{0,8},{4,12},{8,0},{12,4},{1,9},{5,13},{9,1},{13,5},{2,10},{6,14},... | collective-permute-start | bytes 1474568 | tf_op jit(solution)/shard_map/ppermute | solution.py:451
  125.4 11.5 %collective-permute-start.19 = (bf16[128,3072]{1,0:T(8,128)(2,1)S(1)}, bf16[128,3072]{1,0:T(8,128)(2,1)S(1)}, u32[]{:S(2)}, u32[]{:S(2)}) collective-permute-start(bf16[128,3072]{1,0:T(8,128)(2,1)S(1)} %get-tuple-element.85), channel_id=1, source_target_pairs={{0,4},{4,0},{8,12},{12,8},{1,5},{5,1},{9,13},{13,9},{2,6},{6,2},{1... | collective-permute-start | bytes 2359304 | tf_op jit(solution)/shard_map/ppermute | solution.py:446
  126.0 14.0 %collective-permute-start.17 = (bf16[80,3072]{1,0:T(8,128)(2,1)S(1)}, bf16[80,3072]{1,0:T(8,128)(2,1)S(1)}, u32[]{:S(2)}, u32[]{:S(2)}) collective-permute-start(bf16[80,3072]{1,0:T(8,128)(2,1)S(1)} %get-tuple-element.81), channel_id=1, source_target_pairs={{0,8},{4,12},{8,0},{12,4},{1,9},{5,13},{9,1},{13,5},{2,10},{6,14},... | collective-permute-start | bytes 1474568 | tf_op jit(solution)/shard_map/ppermute | solution.py:451
  136.9 13.2 %collective-permute-start.22 = (bf16[128,3072]{1,0:T(8,128)(2,1)S(1)}, bf16[128,3072]{1,0:T(8,128)(2,1)S(1)}, u32[]{:S(2)}, u32[]{:S(2)}) collective-permute-start(bf16[128,3072]{1,0:T(8,128)(2,1)S(1)} %get-tuple-element.94), channel_id=1, source_target_pairs={{0,4},{4,0},{8,12},{12,8},{1,5},{5,1},{9,13},{13,9},{2,6},{6,2},{1... | collective-permute-start | bytes 2359304 | tf_op jit(solution)/shard_map/ppermute | solution.py:446
  137.4 11.6 %collective-permute-start.20 = (bf16[64,3072]{1,0:T(8,128)(2,1)S(1)}, bf16[64,3072]{1,0:T(8,128)(2,1)S(1)}, u32[]{:S(2)}, u32[]{:S(2)}) collective-permute-start(bf16[64,3072]{1,0:T(8,128)(2,1)S(1)} %get-tuple-element.90), channel_id=1, source_target_pairs={{0,8},{4,12},{8,0},{12,4},{1,9},{5,13},{9,1},{13,5},{2,10},{6,14},... | collective-permute-start | bytes 1179656 | tf_op jit(solution)/shard_map/ppermute | solution.py:451
  150.1 2.3 %collective-permute-start.21 = (bf16[128,3072]{1,0:T(8,128)(2,1)S(1)}, bf16[128,3072]{1,0:T(8,128)(2,1)S(1)}, u32[]{:S(2)}, u32[]{:S(2)}) collective-permute-start(bf16[128,3072]{1,0:T(8,128)(2,1)S(1)} %get-tuple-element.93), channel_id=1, source_target_pairs={{0,4},{4,0},{8,12},{12,8},{1,5},{5,1},{9,13},{13,9},{2,6},{6,2},{1... | collective-permute-start | bytes 2359304 | tf_op jit(solution)/shard_map/ppermute | solution.py:459
  150.5 12.0 %collective-permute-start.24 = (bf16[64,3072]{1,0:T(8,128)(2,1)S(1)}, bf16[64,3072]{1,0:T(8,128)(2,1)S(1)}, u32[]{:S(2)}, u32[]{:S(2)}) collective-permute-start(bf16[64,3072]{1,0:T(8,128)(2,1)S(1)} %get-tuple-element.98), channel_id=1, source_target_pairs={{0,8},{4,12},{8,0},{12,4},{1,9},{5,13},{9,1},{13,5},{2,10},{6,14},... | collective-permute-start | bytes 1179656 | tf_op jit(solution)/shard_map/ppermute | solution.py:451
  152.8 17.7 %collective-permute-start.23 = (bf16[64,3072]{1,0:T(8,128)(2,1)S(1)}, bf16[64,3072]{1,0:T(8,128)(2,1)S(1)}, u32[]{:S(2)}, u32[]{:S(2)}) collective-permute-start(bf16[64,3072]{1,0:T(8,128)(2,1)S(1)} %get-tuple-element.97), channel_id=1, source_target_pairs={{0,8},{4,12},{8,0},{12,4},{1,9},{5,13},{9,1},{13,5},{2,10},{6,14},... | collective-permute-start | bytes 1179656 | tf_op jit(solution)/shard_map/ppermute | solution.py:451

commit v11 on v10

--- a/solution.py
+++ b/solution.py
@@ -351,12 +351,12 @@
     return pieces
 
 
-SHARES = ((12, 6), (6, 6, 6), (6, 6, 6))
+SHARES = ((10, 8), (6, 6, 6), (6, 6, 6))
 
 
 def chunk_sizes(block):
     if block % 192 == 0:
-        return [block // 4, block * 5 // 12, block // 3]
+        return [block // 3, block * 5 // 12, block // 4]
     return [block // 3] * 3
 
 

time: 172 us -> 175 us (1.017)
  waiting for transfers between devices: 46.5 us -> 49.1 us
    ppermute x6, waiting for transfers between devices: 17.3 us -> 24.1 us  [swap(): return lax.ppermute(array, 'gy', [(k, k ^ distance) for k in range(n_gy)])]
    ppermute x3, waiting for transfers between devices: 6.1 us -> 4.06 us  [local(): lax.ppermute(given, 'gy', [(0, 2), (1, 0), (2, 3), (3, 1)])]
    ppermute x8, waiting for transfers between devices: 22.8 us -> 20.9 us  [local(): lax.ppermute(away[(ahead - 1) * size:ahead * size], 'gx', across(ahead))]
  transfers between devices with their start and end apart: 25 -> 25, of which waited for: 12 -> 11; matrix products, arithmetic and copies ran while one was open for 3% -> 4% of each run, Pallas kernels for 52% -> 51%
where the time goes in v11:
time: 175 us
  Pallas kernels  90.4 us (52%)
  waiting for transfers between devices  49.1 us (28%)
  starting transfers between devices  25.3 us (14%)
  local copies, waits for them, and re-layouts  9.33 us (5%)
    pallas_call x8, Pallas kernels, product(): pl.pallas_call(functools.partial(product_kernel, start, tile, width // ti...  73.4 us
    ppermute x6, waiting for transfers between devices, swap(): return lax.ppermute(array, 'gy', [(k, k ^ distance) for k in range(n_gy)])  24.1 us
    ppermute x8, waiting for transfers between devices, local(): lax.ppermute(away[(ahead - 1) * size:ahead * size], 'gx', across(ahead))  20.9 us
    ppermute x8, starting transfers between devices, local(): lax.ppermute(away[(ahead - 1) * size:ahead * size], 'gx', across(ahead))  10.7 us
    ppermute x6, starting transfers between devices, swap(): return lax.ppermute(array, 'gy', [(k, k ^ distance) for k in range(n_gy)])  10.3 us
    slice x1, local copies, waits for them, and re-layouts, local(): ready[:, start:start + tile]  5.93 us
    ppermute x3, waiting for transfers between devices, local(): lax.ppermute(given, 'gy', [(0, 2), (1, 0), (2, 3), (3, 1)])  4.06 us
    ppermute x3, starting transfers between devices, local(): lax.ppermute(given, 'gy', [(0, 2), (1, 0), (2, 3), (3, 1)])  3.79 us
  transfers between devices with their start and end apart: 25, of which 11 were waited for; matrix products, arithmetic and copies ran while one was open for 4% of the time, Pallas kernels for 51%

profile of v11, /device:TPU:0, one launch (start us, length us, event | category | flops | bytes accessed | tf_op | source)
XLA Modules:
  0.0 174.6 jit_solution(1816902657889391687)
XLA Ops:
  1.1 4.1 %collective-permute-start.1 = (bf16[64,3584]{1,0:T(8,128)(2,1)S(1)}, bf16[64,3584]{1,0:T(8,128)(2,1)S(1)}, u32[]{:S(2)}, u32[]{:S(2)}) collective-permute-start(bf16[64,3584]{1,0:T(8,128)(2,1)S(1)} %slice.15.refs_0_), channel_id=1, source_target_pairs={{0,2},{1,3},{2,0},{3,1},{4,6},{5,7},{6,4},{7,5},{8,10},{9,11},{10,... | collective-permute-start | bytes 1376264 | tf_op jit(solution)/shard_map/ppermute | solution.py:384
  5.2 1.6 collective-permute-start
  7.6 2.0 %onehot.1.onehot_ref = bf16[768,256]{1,0:T(8,128)(2,1)S(1)} custom-call(s32[768,1]{1,0:T(8,128)S(1)} %broadcast_in_dim.4.parents_ref), custom_call_target="tpu_custom_call" | custom-call | flops 19327352832 | bytes 12582912 | tf_op jit(solution)/shard_map/onehot/pallas_call | solution.py:53
  9.7 1.5 copy-done.1
  11.2 1.9 %own.1 = (bf16[80,3584]{1,0:T(8,128)(2,1)S(1)}, bf16[48,3584]{1,0:T(8,128)(2,1)S(1)}) custom-call(s32[2]{0:T(128)S(1)} %pad_add_fusion.place_ref, bf16[768,256]{1,0:T(8,128)(2,1)S(1)} %onehot.1.onehot_ref, bf16[256,3584]{1,0:T(8,128)(2,1)S(1)} %copy-done.1, bf16[192,3584]{1,0:T(8,128)(2,1)S(1)} %copy-done), custom_call_target="tpu_custom_call" | custom-call | flops 1879048192 | bytes 22020096 | tf_op jit(solution)/shard_map/own/pallas_call | solution.py:159
  13.1 12.5 %collective-permute-done.1.far_ref.refs_2_ = bf16[64,3584]{1,0:T(8,128)(2,1)S(1)} collective-permute-done((bf16[64,3584]{1,0:T(8,128)(2,1)S(1)}, bf16[64,3584]{1,0:T(8,128)(2,1)S(1)}, u32[]{:S(2)}, u32[]{:S(2)}) %collective-permute-start.1) | collective-permute-done | bytes 458784 | tf_op jit(solution)/shard_map/ppermute | solution.py:384
  26.4 1.4 collective-permute-start.4
  27.8 2.5 %look.1.refs_4_ = bf16[256,3584]{1,0:T(8,128)(2,1)S(1)} custom-call(s32[2]{0:T(128)S(1)} %pad_add_fusion.place_ref, bf16[768,256]{1,0:T(8,128)(2,1)S(1)} %onehot.1.onehot_ref, bf16[256,3584]{1,0:T(8,128)(2,1)S(1)} %copy-done.2, bf16[64,3584]{1,0:T(8,128)(2,1)S(1)} %forward.3.refs_0_.refs_5_), custom_call_target="tpu_custom_call" | custom-call | flops 3758096384 | bytes 29360128 | tf_op jit(solution)/shard_map/look/pallas_call | solution.py:105
  30.3 2.5 %collective-permute-start.3 = (bf16[80,3584]{1,0:T(8,128)(2,1)S(1)}, bf16[80,3584]{1,0:T(8,128)(2,1)S(1)}, u32[]{:S(2)}, u32[]{:S(2)}) collective-permute-start(bf16[80,3584]{1,0:T(8,128)(2,1)S(1)} %get-tuple-element.57.refs_0_), channel_id=1, source_target_pairs={{0,2},{1,3},{2,0},{3,1},{4,6},{5,7},{6,4},{7,5},{8,10},{9,11},{10,... | collective-permute-start | bytes 1720328 | tf_op jit(solution)/shard_map/ppermute | solution.py:384
  33.4 5.9 %fusion = (bf16[3584,512]{1,0:T(8,128)(2,1)S(1)}, bf16[3584,512]{1,0:T(8,128)(2,1)S(1)}, bf16[3584,512]{1,0:T(8,128)(2,1)S(1)}, bf16[3584,512]{1,0:T(8,128)(2,1)S(1)}) fusion(bf16[3584,9216]{1,0:T(8,128)(2,1)} %weight_ref.15), kind=kLoop, calls=%fused_computation.1 | loop fusion | bytes 29360128 | tf_op jit(solution)/shard_map/slice | solution.py:427
  41.0 12.5 %product.8 = (bf16[128,5120]{1,0:T(8,128)(2,1)S(1)}, bf16[128,5120]{1,0:T(8,128)(2,1)S(1)}) custom-call(bf16[256,3584]{1,0:T(8,128)(2,1)S(1)} %arrange.3.rows_ref.refs_0_, bf16[3584,512]{1,0:T(8,128)(2,1)S(1)} %get-tuple-element.106.lead_ref, bf16[3584,9216]{1,0:T(8,128)(2,1)} %weight_ref.15, bf16[256,3584]{1,0:T(8,128)(2,1)S(1)} %arrange.3.rows_ref.refs_0_), custom_call_target="tpu_custom_call" | custom-call | flops 75161927680 | bytes 329252864 | tf_op jit(solution)/shard_map/product/pallas_call | solution.py:281
  53.5 11.4 %collective-permute-done.3.far_ref.refs_2_ = bf16[80,3584]{1,0:T(8,128)(2,1)S(1)} collective-permute-done((bf16[80,3584]{1,0:T(8,128)(2,1)S(1)}, bf16[80,3584]{1,0:T(8,128)(2,1)S(1)}, u32[]{:S(2)}, u32[]{:S(2)}) %collective-permute-start.3) | collective-permute-done | bytes 573472 | tf_op jit(solution)/shard_map/ppermute | solution.py:384
  66.2 10.2 %product.9 = (bf16[128,4096]{1,0:T(8,128)(2,1)S(1)}, bf16[128,4096]{1,0:T(8,128)(2,1)S(1)}) custom-call(bf16[256,3584]{1,0:T(8,128)(2,1)S(1)} %arrange.3.rows_ref.refs_0_, bf16[3584,512]{1,0:T(8,128)(2,1)S(1)} %get-tuple-element.105.lead_ref, bf16[3584,9216]{1,0:T(8,128)(2,1)} %weight_ref.15, bf16[80,3584]{1,0:T(8,128)(2,1)S(1)} %forward.4.refs_0_), custom_call_target="tpu_custom_call" | custom-call | flops 60129542144 | bytes 266338304 | tf_op jit(solution)/shard_map/product/pallas_call | solution.py:281
  77.1 3.4 %collective-permute-done.5.refs_3_ = bf16[80,3584]{1,0:T(8,128)(2,1)S(1)} collective-permute-done((bf16[80,3584]{1,0:T(8,128)(2,1)S(1)}, bf16[80,3584]{1,0:T(8,128)(2,1)S(1)}, u32[]{:S(2)}, u32[]{:S(2)}) %collective-permute-start.5) | collective-permute-done | bytes 573472 | tf_op jit(solution)/shard_map/ppermute | solution.py:418
  81.2 1.2 collective-permute-start.8
  82.8 1.5 collective-permute-start.9
  84.3 9.0 %product.10 = (bf16[160,3072]{1,0:T(8,128)(2,1)S(1)}, bf16[160,3072]{1,0:T(8,128)(2,1)S(1)}) custom-call(bf16[320,3584]{1,0:T(8,128)(2,1)S(1)} %arrange.4.rows_ref.refs_0_, bf16[3584,512]{1,0:T(8,128)(2,1)S(1)} %get-tuple-element.106.lead_ref, bf16[3584,9216]{1,0:T(8,128)(2,1)} %weight_ref.15, bf16[320,3584]{1,0:T(8,128)(2,1)S(1)} %arrange.4.rows_ref.refs_0_), custom_call_target="tpu_custom_call" | custom-call | flops 56371445760 | bytes 210239488 | tf_op jit(solution)/shard_map/product/pallas_call | solution.py:281
  94.4 6.0 %collective-permute-done.9.refs_1_ = bf16[64,5120]{1,0:T(8,128)(2,1)S(1)} collective-permute-done((bf16[64,5120]{1,0:T(8,128)(2,1)S(1)}, bf16[64,5120]{1,0:T(8,128)(2,1)S(1)}, u32[]{:S(2)}, u32[]{:S(2)}) %collective-permute-start.9) | collective-permute-done | bytes 655392 | tf_op jit(solution)/shard_map/ppermute | solution.py:451
  100.4 9.6 %product.11 = (bf16[160,3072]{1,0:T(8,128)(2,1)S(1)}, bf16[160,3072]{1,0:T(8,128)(2,1)S(1)}, bf16[192,9216]{1,0:T(8,128)(2,1)}) custom-call(bf16[320,3584]{1,0:T(8,128)(2,1)S(1)} %arrange.4.rows_ref.refs_0_, bf16[3584,512]{1,0:T(8,128)(2,1)S(1)} %get-tuple-element.104.lead_ref, bf16[3584,9216]{1,0:T(8,128)(2,1)} %weight_ref.15, ...), custom_call_target="tpu_custom_call" | custom-call | flops 56371445760 | bytes 210239488 | tf_op jit(solution)/shard_map/product/pallas_call | solution.py:281
  110.6 1.7 collective-permute-start.11
  112.8 1.6 collective-permute-start.16
  114.4 9.1 %product.12 = (bf16[160,3072]{1,0:T(8,128)(2,1)S(1)}, bf16[160,3072]{1,0:T(8,128)(2,1)S(1)}, bf16[192,9216]{1,0:T(8,128)(2,1)}) custom-call(bf16[320,3584]{1,0:T(8,128)(2,1)S(1)} %arrange.4.rows_ref.refs_0_, bf16[3584,512]{1,0:T(8,128)(2,1)S(1)} %get-tuple-element.103.lead_ref, bf16[3584,9216]{1,0:T(8,128)(2,1)} %weight_ref.15, ...), custom_call_target="tpu_custom_call", output_to_operand_aliasing={{2}: (5, {})} | custom-call | flops 56371445760 | bytes 210239488 | tf_op jit(solution)/shard_map/product/pallas_call | solution.py:281
  126.5 7.7 %product.13 = (bf16[96,3072]{1,0:T(8,128)(2,1)S(1)}, bf16[96,3072]{1,0:T(8,128)(2,1)S(1)}, bf16[192,9216]{1,0:T(8,128)(2,1)}) custom-call(bf16[192,3584]{1,0:T(8,128)(2,1)S(1)} %arrange.5.rows_ref.refs_3_, bf16[3584,512]{1,0:T(8,128)(2,1)S(1)} %get-tuple-element.106.lead_ref, bf16[3584,9216]{1,0:T(8,128)(2,1)} %weight_ref.15, ...), custom_call_target="tpu_custom_call", output_to_operand_aliasing={{2}: (5, {})} | custom-call | flops 33822867456 | bytes 196608000 | tf_op jit(solution)/shard_map/product/pallas_call | solution.py:281
  134.8 1.8 %collective-permute-start.17 = (bf16[80,3072]{1,0:T(8,128)(2,1)S(1)}, bf16[80,3072]{1,0:T(8,128)(2,1)S(1)}, u32[]{:S(2)}, u32[]{:S(2)}) collective-permute-start(bf16[80,3072]{1,0:T(8,128)(2,1)S(1)} %get-tuple-element.81), channel_id=1, source_target_pairs={{0,8},{4,12},{8,0},{12,4},{1,9},{5,13},{9,1},{13,5},{2,10},{6,14},... | collective-permute-start | bytes 1474568 | tf_op jit(solution)/shard_map/ppermute | solution.py:451
  136.6 1.2 collective-permute-done.18.refs_1_
  137.7 7.7 %product.14 = (bf16[96,3072]{1,0:T(8,128)(2,1)S(1)}, bf16[96,3072]{1,0:T(8,128)(2,1)S(1)}, bf16[192,9216]{1,0:T(8,128)(2,1)}) custom-call(bf16[192,3584]{1,0:T(8,128)(2,1)S(1)} %arrange.5.rows_ref.refs_3_, bf16[3584,512]{1,0:T(8,128)(2,1)S(1)} %get-tuple-element.104.lead_ref, bf16[3584,9216]{1,0:T(8,128)(2,1)} %weight_ref.15, ...), custom_call_target="tpu_custom_call", output_to_operand_aliasing={{2}: (5, {})} | custom-call | flops 33822867456 | bytes 196608000 | tf_op jit(solution)/shard_map/product/pallas_call | solution.py:281
  146.7 1.7 collective-permute-done.17.refs_1_
  148.5 7.7 %product.15 = (bf16[96,3072]{1,0:T(8,128)(2,1)S(1)}, bf16[96,3072]{1,0:T(8,128)(2,1)S(1)}, bf16[192,9216]{1,0:T(8,128)(2,1)}) custom-call(bf16[192,3584]{1,0:T(8,128)(2,1)S(1)} %arrange.5.rows_ref.refs_3_, bf16[3584,512]{1,0:T(8,128)(2,1)S(1)} %get-tuple-element.103.lead_ref, bf16[3584,9216]{1,0:T(8,128)(2,1)} %weight_ref.15, ...), custom_call_target="tpu_custom_call", output_to_operand_aliasing={{2}: (5, {})} | custom-call | flops 33822867456 | bytes 196608000 | tf_op jit(solution)/shard_map/product/pallas_call | solution.py:281
  157.5 2.1 %collective-permute-start.24 = (bf16[48,3072]{1,0:T(8,128)(2,1)S(1)}, bf16[48,3072]{1,0:T(8,128)(2,1)S(1)}, u32[]{:S(2)}, u32[]{:S(2)}) collective-permute-start(bf16[48,3072]{1,0:T(8,128)(2,1)S(1)} %get-tuple-element.98), channel_id=1, source_target_pairs={{0,8},{4,12},{8,0},{12,4},{1,9},{5,13},{9,1},{13,5},{2,10},{6,14},... | collective-permute-start | bytes 884744 | tf_op jit(solution)/shard_map/ppermute | solution.py:451
  159.9 1.7 collective-permute-start.23
  161.6 5.9 %collective-permute-done.24.refs_1_ = bf16[48,3072]{1,0:T(8,128)(2,1)S(1)} collective-permute-done((bf16[48,3072]{1,0:T(8,128)(2,1)S(1)}, bf16[48,3072]{1,0:T(8,128)(2,1)S(1)}, u32[]{:S(2)}, u32[]{:S(2)}) %collective-permute-start.24) | collective-permute-done | bytes 294944 | tf_op jit(solution)/shard_map/ppermute | solution.py:451
  168.5 5.1 %collective-permute-done.23.refs_1_ = bf16[48,3072]{1,0:T(8,128)(2,1)S(1)} collective-permute-done((bf16[48,3072]{1,0:T(8,128)(2,1)S(1)}, bf16[48,3072]{1,0:T(8,128)(2,1)S(1)}, u32[]{:S(2)}, u32[]{:S(2)}) %collective-permute-start.23) | collective-permute-done | bytes 294944 | tf_op jit(solution)/shard_map/ppermute | solution.py:451
  (56 shorter events, 18.8 us)
Async XLA Ops:
  1.1 24.6 %collective-permute-start.1 = (bf16[64,3584]{1,0:T(8,128)(2,1)S(1)}, bf16[64,3584]{1,0:T(8,128)(2,1)S(1)}, u32[]{:S(2)}, u32[]{:S(2)}) collective-permute-start(bf16[64,3584]{1,0:T(8,128)(2,1)S(1)} %slice.15.refs_0_), channel_id=1, source_target_pairs={{0,2},{1,3},{2,0},{3,1},{4,6},{5,7},{6,4},{7,5},{8,10},{9,11},{10,... | collective-permute-start | bytes 1376264 | tf_op jit(solution)/shard_map/ppermute | solution.py:384
  5.2 20.6 %collective-permute-start = (bf16[64,3584]{1,0:T(8,128)(2,1)S(1)}, bf16[64,3584]{1,0:T(8,128)(2,1)S(1)}, u32[]{:S(2)}, u32[]{:S(2)}) collective-permute-start(bf16[64,3584]{1,0:T(8,128)(2,1)S(1)} %slice.15.refs_0_), channel_id=1, source_target_pairs={{0,1},{1,0},{2,3},{3,2},{4,5},{5,4},{6,7},{7,6},{8,9},{9,8},{10,11... | collective-permute-start | bytes 1376264 | tf_op jit(solution)/shard_map/ppermute | solution.py:384
  7.6 2.1 %copy-start = (bf16[192,3584]{1,0:T(8,128)(2,1)S(1)}, bf16[192,3584]{1,0:T(8,128)(2,1)}, u32[]{:S(2)}) copy-start(bf16[192,3584]{1,0:T(8,128)(2,1)} %hidden_ref.1) | copy-start | bytes 4128772
  9.7 1.5 copy-start.1
  11.2 16.6 %copy-start.2 = (bf16[256,3584]{1,0:T(8,128)(2,1)S(1)}, bf16[256,3584]{1,0:T(8,128)(2,1)}, u32[]{:S(2)}) copy-start(bf16[256,3584]{1,0:T(8,128)(2,1)} %table_ref.3) | copy-start | bytes 5505028
  26.4 13.6 %collective-permute-start.4 = (bf16[64,3584]{1,0:T(8,128)(2,1)S(1)}, bf16[64,3584]{1,0:T(8,128)(2,1)S(1)}, u32[]{:S(2)}, u32[]{:S(2)}) collective-permute-start(bf16[64,3584]{1,0:T(8,128)(2,1)S(1)} %forward.3.refs_0_.refs_5_), channel_id=1, source_target_pairs={{0,2},{1,0},{2,3},{3,1},{4,6},{5,4},{6,7},{7,5},{8,10},{9,8},{10,1... | collective-permute-start | bytes 1376264 | tf_op jit(solution)/shard_map/ppermute | solution.py:418
  30.3 34.7 %collective-permute-start.3 = (bf16[80,3584]{1,0:T(8,128)(2,1)S(1)}, bf16[80,3584]{1,0:T(8,128)(2,1)S(1)}, u32[]{:S(2)}, u32[]{:S(2)}) collective-permute-start(bf16[80,3584]{1,0:T(8,128)(2,1)S(1)} %get-tuple-element.57.refs_0_), channel_id=1, source_target_pairs={{0,2},{1,3},{2,0},{3,1},{4,6},{5,7},{6,4},{7,5},{8,10},{9,11},{10,... | collective-permute-start | bytes 1720328 | tf_op jit(solution)/shard_map/ppermute | solution.py:384
  32.8 32.2 %collective-permute-start.2 = (bf16[80,3584]{1,0:T(8,128)(2,1)S(1)}, bf16[80,3584]{1,0:T(8,128)(2,1)S(1)}, u32[]{:S(2)}, u32[]{:S(2)}) collective-permute-start(bf16[80,3584]{1,0:T(8,128)(2,1)S(1)} %get-tuple-element.57.refs_0_), channel_id=1, source_target_pairs={{0,1},{1,0},{2,3},{3,2},{4,5},{5,4},{6,7},{7,6},{8,9},{9,8},{10,11... | collective-permute-start | bytes 1720328 | tf_op jit(solution)/shard_map/ppermute | solution.py:384
  53.5 23.0 %collective-permute-start.6 = (bf16[128,5120]{1,0:T(8,128)(2,1)S(1)}, bf16[128,5120]{1,0:T(8,128)(2,1)S(1)}, u32[]{:S(2)}, u32[]{:S(2)}) collective-permute-start(bf16[128,5120]{1,0:T(8,128)(2,1)S(1)} %get-tuple-element.60), channel_id=1, source_target_pairs={{0,4},{4,0},{8,12},{12,8},{1,5},{5,1},{9,13},{13,9},{2,6},{6,2},{1... | collective-permute-start | bytes 3932168 | tf_op jit(solution)/shard_map/ppermute | solution.py:446
  65.6 15.0 %collective-permute-start.5 = (bf16[80,3584]{1,0:T(8,128)(2,1)S(1)}, bf16[80,3584]{1,0:T(8,128)(2,1)S(1)}, u32[]{:S(2)}, u32[]{:S(2)}) collective-permute-start(bf16[80,3584]{1,0:T(8,128)(2,1)S(1)} %forward.4.refs_0_), channel_id=1, source_target_pairs={{0,2},{1,0},{2,3},{3,1},{4,6},{5,4},{6,7},{7,5},{8,10},{9,8},{10,1... | collective-permute-start | bytes 1720328 | tf_op jit(solution)/shard_map/ppermute | solution.py:418
  76.4 16.9 %collective-permute-start.10 = (bf16[128,4096]{1,0:T(8,128)(2,1)S(1)}, bf16[128,4096]{1,0:T(8,128)(2,1)S(1)}, u32[]{:S(2)}, u32[]{:S(2)}) collective-permute-start(bf16[128,4096]{1,0:T(8,128)(2,1)S(1)} %get-tuple-element.65), channel_id=1, source_target_pairs={{0,4},{4,0},{8,12},{12,8},{1,5},{5,1},{9,13},{13,9},{2,6},{6,2},{1... | collective-permute-start | bytes 3145736 | tf_op jit(solution)/shard_map/ppermute | solution.py:446
  81.2 28.8 %collective-permute-start.8 = (bf16[48,3584]{1,0:T(8,128)(2,1)S(1)}, bf16[48,3584]{1,0:T(8,128)(2,1)S(1)}, u32[]{:S(2)}, u32[]{:S(2)}) collective-permute-start(bf16[48,3584]{1,0:T(8,128)(2,1)S(1)} %get-tuple-element.63.refs_0_), channel_id=1, source_target_pairs={{0,2},{1,3},{2,0},{3,1},{4,6},{5,7},{6,4},{7,5},{8,10},{9,11},{10,... | collective-permute-start | bytes 1032200 | tf_op jit(solution)/shard_map/ppermute | solution.py:384
  82.5 27.5 %collective-permute-start.7 = (bf16[48,3584]{1,0:T(8,128)(2,1)S(1)}, bf16[48,3584]{1,0:T(8,128)(2,1)S(1)}, u32[]{:S(2)}, u32[]{:S(2)}) collective-permute-start(bf16[48,3584]{1,0:T(8,128)(2,1)S(1)} %get-tuple-element.63.refs_0_), channel_id=1, source_target_pairs={{0,1},{1,0},{2,3},{3,2},{4,5},{5,4},{6,7},{7,6},{8,9},{9,8},{10,11... | collective-permute-start | bytes 1032200 | tf_op jit(solution)/shard_map/ppermute | solution.py:384
  82.8 17.7 %collective-permute-start.9 = (bf16[64,5120]{1,0:T(8,128)(2,1)S(1)}, bf16[64,5120]{1,0:T(8,128)(2,1)S(1)}, u32[]{:S(2)}, u32[]{:S(2)}) collective-permute-start(bf16[64,5120]{1,0:T(8,128)(2,1)S(1)} %get-tuple-element.64), channel_id=1, source_target_pairs={{0,8},{4,12},{8,0},{12,4},{1,9},{5,13},{9,1},{13,5},{2,10},{6,14},... | collective-permute-start | bytes 1966088 | tf_op jit(solution)/shard_map/ppermute | solution.py:451
  93.8 20.6 %collective-permute-start.13 = (bf16[64,4096]{1,0:T(8,128)(2,1)S(1)}, bf16[64,4096]{1,0:T(8,128)(2,1)S(1)}, u32[]{:S(2)}, u32[]{:S(2)}) collective-permute-start(bf16[64,4096]{1,0:T(8,128)(2,1)S(1)} %get-tuple-element.70), channel_id=1, source_target_pairs={{0,8},{4,12},{8,0},{12,4},{1,9},{5,13},{9,1},{13,5},{2,10},{6,14},... | collective-permute-start | bytes 1572872 | tf_op jit(solution)/shard_map/ppermute | solution.py:451
  94.4 17.9 %collective-permute-start.14 = (bf16[160,3072]{1,0:T(8,128)(2,1)S(1)}, bf16[160,3072]{1,0:T(8,128)(2,1)S(1)}, u32[]{:S(2)}, u32[]{:S(2)}) collective-permute-start(bf16[160,3072]{1,0:T(8,128)(2,1)S(1)} %get-tuple-element.72), channel_id=1, source_target_pairs={{0,4},{4,0},{8,12},{12,8},{1,5},{5,1},{9,13},{13,9},{2,6},{6,2},{1... | collective-permute-start | bytes 2949128 | tf_op jit(solution)/shard_map/ppermute | solution.py:446
  110.6 14.2 %collective-permute-start.11 = (bf16[48,3584]{1,0:T(8,128)(2,1)S(1)}, bf16[48,3584]{1,0:T(8,128)(2,1)S(1)}, u32[]{:S(2)}, u32[]{:S(2)}) collective-permute-start(bf16[48,3584]{1,0:T(8,128)(2,1)S(1)} %forward.5.refs_0_), channel_id=1, source_target_pairs={{0,2},{1,0},{2,3},{3,1},{4,6},{5,4},{6,7},{7,5},{8,10},{9,8},{10,1... | collective-permute-start | bytes 1032200 | tf_op jit(solution)/shard_map/ppermute | solution.py:418
  112.3 11.4 %collective-permute-start.12 = (bf16[160,3072]{1,0:T(8,128)(2,1)S(1)}, bf16[160,3072]{1,0:T(8,128)(2,1)S(1)}, u32[]{:S(2)}, u32[]{:S(2)}) collective-permute-start(bf16[160,3072]{1,0:T(8,128)(2,1)S(1)} %get-tuple-element.69), channel_id=1, source_target_pairs={{0,4},{4,0},{8,12},{12,8},{1,5},{5,1},{9,13},{13,9},{2,6},{6,2},{1... | collective-permute-start | bytes 2949128 | tf_op jit(solution)/shard_map/ppermute | solution.py:446
  112.8 13.7 %collective-permute-start.16 = (bf16[80,3072]{1,0:T(8,128)(2,1)S(1)}, bf16[80,3072]{1,0:T(8,128)(2,1)S(1)}, u32[]{:S(2)}, u32[]{:S(2)}) collective-permute-start(bf16[80,3072]{1,0:T(8,128)(2,1)S(1)} %get-tuple-element.77), channel_id=1, source_target_pairs={{0,8},{4,12},{8,0},{12,4},{1,9},{5,13},{9,1},{13,5},{2,10},{6,14},... | collective-permute-start | bytes 1474568 | tf_op jit(solution)/shard_map/ppermute | solution.py:451
  123.5 10.8 %collective-permute-start.15 = (bf16[160,3072]{1,0:T(8,128)(2,1)S(1)}, bf16[160,3072]{1,0:T(8,128)(2,1)S(1)}, u32[]{:S(2)}, u32[]{:S(2)}) collective-permute-start(bf16[160,3072]{1,0:T(8,128)(2,1)S(1)} %get-tuple-element.76), channel_id=1, source_target_pairs={{0,4},{4,0},{8,12},{12,8},{1,5},{5,1},{9,13},{13,9},{2,6},{6,2},{1... | collective-permute-start | bytes 2949128 | tf_op jit(solution)/shard_map/ppermute | solution.py:446
  124.2 13.5 %collective-permute-start.18 = (bf16[80,3072]{1,0:T(8,128)(2,1)S(1)}, bf16[80,3072]{1,0:T(8,128)(2,1)S(1)}, u32[]{:S(2)}, u32[]{:S(2)}) collective-permute-start(bf16[80,3072]{1,0:T(8,128)(2,1)S(1)} %get-tuple-element.82), channel_id=1, source_target_pairs={{0,8},{4,12},{8,0},{12,4},{1,9},{5,13},{9,1},{13,5},{2,10},{6,14},... | collective-permute-start | bytes 1474568 | tf_op jit(solution)/shard_map/ppermute | solution.py:451
  134.2 11.3 %collective-permute-start.19 = (bf16[96,3072]{1,0:T(8,128)(2,1)S(1)}, bf16[96,3072]{1,0:T(8,128)(2,1)S(1)}, u32[]{:S(2)}, u32[]{:S(2)}) collective-permute-start(bf16[96,3072]{1,0:T(8,128)(2,1)S(1)} %get-tuple-element.85), channel_id=1, source_target_pairs={{0,4},{4,0},{8,12},{12,8},{1,5},{5,1},{9,13},{13,9},{2,6},{6,2},{1... | collective-permute-start | bytes 1769480 | tf_op jit(solution)/shard_map/ppermute | solution.py:446
  134.8 13.7 %collective-permute-start.17 = (bf16[80,3072]{1,0:T(8,128)(2,1)S(1)}, bf16[80,3072]{1,0:T(8,128)(2,1)S(1)}, u32[]{:S(2)}, u32[]{:S(2)}) collective-permute-start(bf16[80,3072]{1,0:T(8,128)(2,1)S(1)} %get-tuple-element.81), channel_id=1, source_target_pairs={{0,8},{4,12},{8,0},{12,4},{1,9},{5,13},{9,1},{13,5},{2,10},{6,14},... | collective-permute-start | bytes 1474568 | tf_op jit(solution)/shard_map/ppermute | solution.py:451
  145.4 11.8 %collective-permute-start.22 = (bf16[96,3072]{1,0:T(8,128)(2,1)S(1)}, bf16[96,3072]{1,0:T(8,128)(2,1)S(1)}, u32[]{:S(2)}, u32[]{:S(2)}) collective-permute-start(bf16[96,3072]{1,0:T(8,128)(2,1)S(1)} %get-tuple-element.94), channel_id=1, source_target_pairs={{0,4},{4,0},{8,12},{12,8},{1,5},{5,1},{9,13},{13,9},{2,6},{6,2},{1... | collective-permute-start | bytes 1769480 | tf_op jit(solution)/shard_map/ppermute | solution.py:446
  145.8 10.3 %collective-permute-start.20 = (bf16[48,3072]{1,0:T(8,128)(2,1)S(1)}, bf16[48,3072]{1,0:T(8,128)(2,1)S(1)}, u32[]{:S(2)}, u32[]{:S(2)}) collective-permute-start(bf16[48,3072]{1,0:T(8,128)(2,1)S(1)} %get-tuple-element.90), channel_id=1, source_target_pairs={{0,8},{4,12},{8,0},{12,4},{1,9},{5,13},{9,1},{13,5},{2,10},{6,14},... | collective-permute-start | bytes 884744 | tf_op jit(solution)/shard_map/ppermute | solution.py:451
  157.2 2.4 %collective-permute-start.21 = (bf16[96,3072]{1,0:T(8,128)(2,1)S(1)}, bf16[96,3072]{1,0:T(8,128)(2,1)S(1)}, u32[]{:S(2)}, u32[]{:S(2)}) collective-permute-start(bf16[96,3072]{1,0:T(8,128)(2,1)S(1)} %get-tuple-element.93), channel_id=1, source_target_pairs={{0,4},{4,0},{8,12},{12,8},{1,5},{5,1},{9,13},{13,9},{2,6},{6,2},{1... | collective-permute-start | bytes 1769480 | tf_op jit(solution)/shard_map/ppermute | solution.py:459
  157.5 9.9 %collective-permute-start.24 = (bf16[48,3072]{1,0:T(8,128)(2,1)S(1)}, bf16[48,3072]{1,0:T(8,128)(2,1)S(1)}, u32[]{:S(2)}, u32[]{:S(2)}) collective-permute-start(bf16[48,3072]{1,0:T(8,128)(2,1)S(1)} %get-tuple-element.98), channel_id=1, source_target_pairs={{0,8},{4,12},{8,0},{12,4},{1,9},{5,13},{9,1},{13,5},{2,10},{6,14},... | collective-permute-start | bytes 884744 | tf_op jit(solution)/shard_map/ppermute | solution.py:451
  159.9 13.7 %collective-permute-start.23 = (bf16[48,3072]{1,0:T(8,128)(2,1)S(1)}, bf16[48,3072]{1,0:T(8,128)(2,1)S(1)}, u32[]{:S(2)}, u32[]{:S(2)}) collective-permute-start(bf16[48,3072]{1,0:T(8,128)(2,1)S(1)} %get-tuple-element.97), channel_id=1, source_target_pairs={{0,8},{4,12},{8,0},{12,4},{1,9},{5,13},{9,1},{13,5},{2,10},{6,14},... | collective-permute-start | bytes 884744 | tf_op jit(solution)/shard_map/ppermute | solution.py:451
